TPU v7x, 32 devices: a whole 2x2x4 slice. The times are simulated.
32 devices in a mesh: branch: 4 (over y, core), shard: 8 (over z, x).
Axes of the slice: x: 2, y: 2, z: 4, core: 2. Of those that a mesh axis runs over, the one named last changes fastest.
Arguments:
- tokens: bfloat16 [128, 4096], P(('branch', 'shard')), may hold values from -6 to 6
- routes: int32 [128, 2], P(('branch', 'shard')), may hold values from 0 to 3, all different within a row; in each aligned block of 4 rows (0 to 3, 4 to 7, ...) at most 3 rows name the same one
- mixing: float32 [128, 2], P(('branch', 'shard')), may hold values from 0.2 to 1
- gate_weight: bfloat16 [4, 4096, 14336], P('branch', 'shard'), may hold values from -0.09375 to 0.09375
- up_weight: bfloat16 [4, 4096, 14336], P('branch', 'shard'), may hold values from -0.09375 to 0.09375
- down_weight: bfloat16 [4, 14336, 4096], P('branch', 'shard'), may hold values from -0.046875 to 0.046875
- key_value: bfloat16 [4, 4096, 2048], P('branch', 'shard'), may hold values from -6 to 6
Outputs:
- mixed_out: bfloat16 [128, 4096], P(('branch', 'shard'))
- merged_kv: bfloat16 [4096, 2048], P('shard', 'branch')
Inputs may be any that keep to these rules, and one draw needn't show every extreme that they name: `routes`: in each block of the 4 tokens of one device no expert is named by more than 3 pairs, and in some block one expert is named by exactly 3; a token's two experts differ.
All inputs are finite; a program needn't handle non-finite values.
Results may differ from a plain program's by a relative error of at most 0.018.
Values may be sent and summed in bfloat16 or wider, within the bound.
No kernel may reach another device: no remote copies, remote signals or barrier semaphores. Data moves between devices by JAX's collectives and lax.ppermute only.
A program may use at most 192 MiB of HBM per device.

v0:
```python
import jax
import jax.numpy as jnp
from jax import lax
from jax.sharding import PartitionSpec as P


def local(tokens, routes, mixing, gate_weight, up_weight, down_weight, key_value):
    expert_count = lax.axis_size("branch")
    token_count = tokens.shape[0]
    capacity = max(2, (2 * token_count + expert_count - 1) // expert_count + 1)
    width = tokens.shape[1]
    pair_count = token_count * 2
    pair_ids = routes.reshape(pair_count)
    experts_row = jnp.arange(expert_count, dtype=jnp.int32)
    onehot = (pair_ids[:, None] == experts_row[None, :]).astype(jnp.int32)
    earlier = jnp.cumsum(onehot, axis=0) - onehot
    slots = jnp.sum(earlier * onehot, axis=1)
    cells = jnp.arange(expert_count * capacity, dtype=jnp.int32)
    placing = (pair_ids[None, :] == (cells // capacity)[:, None]) & (
        slots[None, :] == (cells % capacity)[:, None]
    )
    pair_tokens = jnp.repeat(tokens, 2, axis=0)
    outgoing = jnp.dot(
        placing.astype(jnp.bfloat16), pair_tokens, preferred_element_type=jnp.float32
    )
    outgoing = outgoing.astype(jnp.bfloat16).reshape(expert_count, capacity, width)
    pair_weights = placing.astype(jnp.float32).T * mixing.reshape(pair_count)[:, None]
    combine = jnp.sum(pair_weights.reshape(token_count, 2, expert_count * capacity), axis=1)
    gate_cols, up_cols = (
        lax.all_to_all(gate_weight, "shard", split_axis=2, concat_axis=1, tiled=True),
        lax.all_to_all(up_weight, "shard", split_axis=2, concat_axis=1, tiled=True),
    )
    gate_cols = gate_cols[0]
    up_cols = up_cols[0]
    down_rows = down_weight[0]
    spread = lax.all_gather(outgoing, "shard", axis=1, tiled=True)
    arrived = lax.all_to_all(spread, "branch", split_axis=0, concat_axis=0, tiled=True)
    rows = arrived.reshape(-1, width)
    gate = jnp.dot(rows, gate_cols, preferred_element_type=jnp.float32)
    upper = jnp.dot(rows, up_cols, preferred_element_type=jnp.float32)
    hidden = (jax.nn.silu(gate) * upper).astype(jnp.bfloat16)
    partial_value = jnp.dot(hidden, down_rows, preferred_element_type=jnp.float32).astype(
        jnp.bfloat16
    )
    partial_value = partial_value.reshape(arrived.shape)
    partial_back = lax.all_to_all(partial_value, "branch", split_axis=0, concat_axis=0, tiled=True)
    summed = lax.psum_scatter(
        partial_back.astype(jnp.float32).astype(jnp.bfloat16),
        "shard",
        scatter_dimension=1,
        tiled=True,
    )
    expert_flat = summed.reshape(expert_count * capacity, width).astype(jnp.float32)
    mixed_out = jnp.dot(
        combine, expert_flat, precision=lax.Precision.HIGHEST, preferred_element_type=jnp.float32
    )
    mixed_out = mixed_out.astype(jnp.bfloat16)
    local_kv = key_value[0].astype(jnp.float32)
    total = lax.psum(local_kv.astype(jnp.bfloat16), "branch").astype(jnp.float32)
    column_width = local_kv.shape[1] // expert_count
    owned = lax.dynamic_slice_in_dim(
        total, lax.axis_index("branch") * column_width, column_width, 1
    )
    merged_kv = (owned / expert_count).astype(jnp.bfloat16)
    return (mixed_out, merged_kv)


def solution(mesh):
    return jax.shard_map(
        local,
        mesh=mesh,
        in_specs=(
            P(("branch", "shard"), None),
            P(("branch", "shard"), None),
            P(("branch", "shard"), None),
            P("branch", "shard", None),
            P("branch", "shard", None),
            P("branch", "shard", None),
            P("branch", "shard", None),
        ),
        out_specs=(P(("branch", "shard"), None), P("shard", "branch")),
        check_vma=False,
    )
```

profile of v0, /device:TPU:0, one launch (start us, length us, event | category | flops | bytes accessed | tf_op | source)
XLA Modules:
  0.0 1090.9 jit_solution(4913683675111962432)
XLA Ops:
  7.2 59.9 %copy.58 = bf16[1,512,14336]{1,0,2:T(2,128)(2,1)} copy(bf16[1,512,14336]{2,1,0:T(8,128)(2,1)} %param.10) | data formatting | bytes 29360128 | tf_op args[3]
  67.1 0.5 broadcast.74
  67.6 93.9 %reduce.1 = bf16[14336,512]{1,0:T(8,128)(2,1)} reduce(bf16[14336,1,512]{2,1,0:T(2,128)(2,1)} %bitcast.28, bf16[]{:T(256)} %broadcast.74), dimensions={1}, to_apply=%bitcast.19.reduce_sub_computation | reduce | bytes 29360130
  161.5 16.2 %reshape.78 = bf16[8,2,458752]{2,1,0:T(2,128)(2,1)} reshape(bf16[14336,512]{1,0:T(8,128)(2,1)} %reduce.1) | data formatting | bytes 29360128
  177.7 7.3 all-to-all-start.1
  184.9 59.9 %copy.60 = bf16[1,512,14336]{1,0,2:T(2,128)(2,1)} copy(bf16[1,512,14336]{2,1,0:T(8,128)(2,1)} %param.11) | data formatting | bytes 29360128 | tf_op args[4]
  244.8 93.8 %reduce = bf16[14336,512]{1,0:T(8,128)(2,1)} reduce(bf16[14336,1,512]{2,1,0:T(2,128)(2,1)} %bitcast.29, bf16[]{:T(256)} %broadcast.74), dimensions={1}, to_apply=%bitcast.17.reduce_sub_computation | reduce | bytes 29360130
  338.7 16.2 %reshape.76 = bf16[8,2,458752]{2,1,0:T(2,128)(2,1)} reshape(bf16[14336,512]{1,0:T(8,128)(2,1)} %reduce) | data formatting | bytes 29360128
  354.9 148.1 %all-to-all-done.1 = bf16[8,2,458752]{2,1,0:T(2,128)(2,1)} async-done(((bf16[8,2,458752]{2,1,0:T(2,128)(2,1)}), bf16[8,2,458752]{2,1,0:T(2,128)(2,1)}, u32[]{:S(2)}, u32[]{:S(2)}) %all-to-all-start.1) | async-done | bytes 14680096 | tf_op jit(solution)/shard_map/all_to_all | solution.py:30
  503.0 5.5 all-to-all-start.2
  508.5 0.1 copy.54
  508.6 0.1 eq.64
  508.8 0.2 reduce_window_sum.11
  509.0 0.2 convolution_convert_fusion
  509.2 0.1 reshape.71
  509.3 0.1 copy.56
  509.4 337.9 %all_gather.3 = bf16[4,24,4096]{2,0,1:T(4,128)(2,1)S(1)} all-gather(bf16[4,3,4096]{2,0,1:T(4,128)(2,1)S(1)} %copy.56), channel_id=1, replica_groups=mesh['branch'=4,'shard'=8] {'shard'}, dimensions={1}, use_global_device_ids=true | all-gather | bytes 884736 | tf_op jit(solution)/shard_map/all_gather | solution.py:36
  847.3 1.4 copy.57
  848.7 0.0 all-to-all-done.2
  848.7 3.5 all-to-all-start
  852.2 0.0 all-reduce.4.cloned.1.call-start
  852.3 0.7 all-reduce.4.cloned.1.call-update
  852.9 0.3 all-reduce.6.cloned.1.call-start
  853.2 20.2 %reshape.79 = bf16[14336,1,512]{2,1,0:T(2,128)(2,1)} reshape(bf16[8,2,458752]{2,1,0:T(2,128)(2,1)} %all-to-all-done.1) | data formatting | bytes 29360128
  873.4 20.1 %copy.64 = bf16[1,512,14336]{1,2,0:T(8,128)(2,1)} copy(bf16[1,512,14336]{1,0,2:T(2,128)(2,1)} %bitcast.30) | data formatting | bytes 29360128
  893.5 18.8 %copy.59 = bf16[1,8,512,1792]{3,2,1,0:T(8,128)(2,1)} copy(bf16[1,8,512,1792]{2,3,1,0:T(8,128)(2,1)} %bitcast.34) | data formatting | bytes 29360128 | tf_op jit(solution)/shard_map/all_to_all | solution.py:30
  912.3 20.2 %reshape.77 = bf16[14336,1,512]{2,1,0:T(2,128)(2,1)} reshape(bf16[8,2,458752]{2,1,0:T(2,128)(2,1)} %all-to-all-done.2) | data formatting | bytes 29360128
  932.5 19.2 %copy.65 = bf16[1,512,14336]{1,2,0:T(8,128)(2,1)} copy(bf16[1,512,14336]{1,0,2:T(2,128)(2,1)} %bitcast.31) | data formatting | bytes 29360128
  951.7 18.8 %copy.61 = bf16[1,8,512,1792]{3,2,1,0:T(8,128)(2,1)} copy(bf16[1,8,512,1792]{2,3,1,0:T(8,128)(2,1)} %bitcast.35) | data formatting | bytes 29360128 | tf_op jit(solution)/shard_map/all_to_all | solution.py:31
  970.5 0.0 all-to-all-done
  970.5 7.6 fusion.21
  978.2 0.0 copy-start.3
  978.2 0.0 copy-start.2
  978.2 14.0 %fusion.2 = bf16[96,4096]{1,0:T(8,128)(2,1)S(1)} fusion(bf16[1,1792,4096]{2,1,0:T(8,128)(2,1)} %param.12, bf16[96,4096]{1,0:T(8,128)(2,1)S(1)} %bitcast.37, bf16[4096,1792]{1,0:T(8,128)(2,1)} %bitcast.33, f32[96,1792]{1,0:T(8,128)S(1)} %fusion.21), kind=kOutput, calls=%fused_computation.2 | convolution fusion | flops 2819997696 | bytes 31621120 | tf_op jit(solution)/shard_map/dot_general | solution.py:42
  992.2 14.6 %all_to_all.40 = bf16[4,24,4096]{2,1,0:T(8,128)(2,1)S(1)} all-to-all(bf16[4,24,4096]{2,1,0:T(8,128)(2,1)S(1)} %bitcast.38), channel_id=1, replica_groups=mesh['branch'=4,'shard'=8] {'branch'}, dimensions={0} | all-to-all | bytes 1572864 | tf_op jit(solution)/shard_map/all_to_all | solution.py:46
  1006.8 1.5 copy.62
  1008.3 0.0 all-reduce.6.cloned.1.call-update
  1008.3 0.1 eq.68
  1008.4 0.1 copy.55
  1008.5 0.6 dynamic-slice
  1009.8 0.1 select_reduce_fusion
  1009.8 0.0 all-reduce.4.cloned.1.call-done
  1009.9 1.9 multiply_convert_fusion
  1011.8 70.4 %all-reduce.6.cloned.1.call-done = bf16[4,24,4096]{2,0,1:T(4,128)(2,1)} async-done(((bf16[4,24,4096]{2,0,1:T(4,128)(2,1)}), bf16[4,24,4096]{2,0,1:T(4,128)(2,1)}) %all-reduce.6.cloned.1.call-update) | async-done | bytes 786448
  1082.1 0.9 constant_dynamic-slice_fusion
  1083.1 0.1 copy.63
  1083.2 0.1 reshape.74
  1083.3 0.8 convolution_convert_fusion.1
  (11 shorter events, 0.1 us)
Async XLA Ops:
  177.7 325.3 %all-to-all-start.1 = ((bf16[8,2,458752]{2,1,0:T(2,128)(2,1)}), bf16[8,2,458752]{2,1,0:T(2,128)(2,1)}, u32[]{:S(2)}, u32[]{:S(2)}) async-start(bf16[8,2,458752]{2,1,0:T(2,128)(2,1)} %reshape.78), calls=%async_computation.1 | async-start | bytes 29360128 | tf_op jit(solution)/shard_map/all_to_all | solution.py:30
  354.9 153.6 %copy-start.1 = (s32[4,2]{0,1:T(2,128)S(1)}, s32[4,2]{0,1:T(2,128)}, u32[]{:S(2)}) copy-start(s32[4,2]{0,1:T(2,128)} %param.8) | copy-start | bytes 100
  354.9 153.8 %copy-start = (bf16[4,4096]{1,0:T(4,128)(2,1)S(1)}, bf16[4,4096]{1,0:T(4,128)(2,1)}, u32[]{:S(2)}) copy-start(bf16[4,4096]{1,0:T(4,128)(2,1)} %param.7) | copy-start | bytes 98308
  503.0 345.7 %all-to-all-start.2 = ((bf16[8,2,458752]{2,1,0:T(2,128)(2,1)}), bf16[8,2,458752]{2,1,0:T(2,128)(2,1)}, u32[]{:S(2)}, u32[]{:S(2)}) async-start(bf16[8,2,458752]{2,1,0:T(2,128)(2,1)} %reshape.76), calls=%async_computation.2 | async-start | bytes 29360128 | tf_op jit(solution)/shard_map/all_to_all | solution.py:31
  848.7 121.8 %all-to-all-start = ((bf16[4,24,4096]{2,1,0:T(8,128)(2,1)}), bf16[4,24,4096]{2,1,0:T(8,128)(2,1)S(1)}, u32[]{:S(2)}, u32[]{:S(2)}) async-start(bf16[4,24,4096]{2,1,0:T(8,128)(2,1)} %copy.57), calls=%async_computation | async-start | bytes 1572864 | tf_op jit(solution)/shard_map/all_to_all | solution.py:37
  852.2 157.6 %all-reduce.4.cloned.1.call-start = ((), (), s32[]{:S(2)}) async-start(), calls=%async_computation.4 | async-start | bytes 4194304 | tf_op jit(solution)/shard_map/psum | solution.py:59
  852.9 229.2 %all-reduce.6.cloned.1.call-start = ((), (), s32[]{:S(2)}) async-start(), calls=%async_computation.5 | async-start | bytes 1572864
  978.2 30.4 %copy-start.3 = (u32[32]{0:T(128)S(1)}, u32[32]{0:T(128)}, u32[]{:S(2)}) copy-start(u32[32]{0:T(128)} %constant.52) | copy-start | bytes 388
  978.2 31.6 %copy-start.2 = (f32[4,2]{0,1:T(2,128)S(1)}, f32[4,2]{0,1:T(2,128)}, u32[]{:S(2)}) copy-start(f32[4,2]{0,1:T(2,128)} %param.9) | copy-start | bytes 100
Sparse Core Ops, SparseCore 0:
  855.4 51.7 all-reduce.3
  1008.4 73.6 all-reduce.5
where the time goes:
time: 1100 us; the launch traced here: 1090 us
  blocking collectives  352 us (32%)
  local copies, waits for them, and re-layouts  275 us (25%)
  waiting for transfers between devices  219 us (20%)
  other arithmetic  190 us (17%)
  matrix products  22.7 us (2%)
  starting transfers between devices  16.6 us (2%)
  between operations  14.8 us (1%)
    all_gather x1, blocking collectives, local(): spread = lax.all_gather(outgoing, 'shard', axis=1, tiled=True)  338 us
    unnamed x20, local copies, waits for them, and re-layouts  234 us
    unnamed x2, other arithmetic  188 us
    all_to_all x1, waiting for transfers between devices, local(): lax.all_to_all(gate_weight, 'shard', split_axis=2, concat_axis=1, tiled=T...  148 us
    unnamed x3, waiting for transfers between devices  71.1 us
  transfers between devices with their start and end apart: 5, of which 2 were waited for; matrix products, arithmetic and copies ran while one was open for 29% of the time, Pallas kernels for 0%

commit v1 on v0

v1 whole, which is shorter than its diff:
```python
import jax
import jax.numpy as jnp
from jax import lax
from jax.sharding import PartitionSpec as P


def route_cells(routes, experts, capacity):
    pairs = routes.shape[0] * 2
    pair_ids = routes.reshape(pairs)
    onehot = (pair_ids[:, None] == jnp.arange(experts, dtype=jnp.int32)[None, :]).astype(jnp.int32)
    earlier = jnp.cumsum(onehot, axis=0) - onehot
    slots = jnp.sum(earlier * onehot, axis=1)
    cells = jnp.arange(experts * capacity, dtype=jnp.int32)
    return (pair_ids[None, :] == (cells // capacity)[:, None]) & (
        slots[None, :] == (cells % capacity)[:, None]
    )


def local(tokens, routes, mixing, gate_weight, up_weight, down_weight, key_value):
    experts = lax.axis_size("branch")
    shards = lax.axis_size("shard")
    token_count, width = tokens.shape
    capacity = max(2, (2 * token_count + experts - 1) // experts + 1)
    depth = gate_weight.shape[1]
    slice_width = down_weight.shape[1]
    placing = route_cells(routes, experts, capacity)
    pair_tokens = jnp.repeat(tokens, 2, axis=0)
    outgoing = jnp.dot(
        placing.astype(jnp.bfloat16), pair_tokens, preferred_element_type=jnp.float32
    ).astype(jnp.bfloat16)
    outgoing = outgoing.reshape(experts, capacity, shards, depth).transpose(0, 2, 1, 3)
    outgoing = outgoing.reshape(experts * shards, capacity, depth)
    pair_weights = placing.astype(jnp.float32).T * mixing.reshape(token_count * 2)[:, None]
    combine = jnp.sum(pair_weights.reshape(token_count, 2, experts * capacity), axis=1)

    arrived = lax.all_to_all(
        outgoing, ("branch", "shard"), split_axis=0, concat_axis=0, tiled=True
    )
    rows = arrived.reshape(-1, depth)
    count = rows.shape[0]
    gate = jnp.dot(rows, gate_weight[0], preferred_element_type=jnp.float32).astype(jnp.bfloat16)
    upper = jnp.dot(rows, up_weight[0], preferred_element_type=jnp.float32).astype(jnp.bfloat16)
    both = jnp.concatenate([gate, upper], axis=0)
    own = lax.psum_scatter(both, "shard", scatter_dimension=1, tiled=True).astype(jnp.float32)
    hidden = (jax.nn.silu(own[:count]) * own[count:]).astype(jnp.bfloat16)
    partial = jnp.dot(hidden, down_weight[0], preferred_element_type=jnp.float32)
    partial = partial.astype(jnp.bfloat16).reshape(experts, shards, capacity, width)
    partial = partial.transpose(1, 0, 2, 3).reshape(shards * experts * capacity, width)
    summed = lax.psum_scatter(partial, "shard", scatter_dimension=0, tiled=True)
    back = lax.all_to_all(
        summed.reshape(experts, capacity, width), "branch", split_axis=0, concat_axis=0, tiled=True
    )
    expert_flat = back.reshape(experts * capacity, width).astype(jnp.float32)
    mixed_out = jnp.dot(
        combine, expert_flat, precision=lax.Precision.HIGHEST, preferred_element_type=jnp.float32
    ).astype(jnp.bfloat16)

    merged = lax.psum_scatter(key_value[0], "branch", scatter_dimension=1, tiled=True)
    merged_kv = (merged.astype(jnp.float32) / experts).astype(jnp.bfloat16)
    return mixed_out, merged_kv


def solution(mesh):
    return jax.shard_map(
        local,
        mesh=mesh,
        in_specs=(
            P(("branch", "shard"), None),
            P(("branch", "shard"), None),
            P(("branch", "shard"), None),
            P("branch", "shard", None),
            P("branch", "shard", None),
            P("branch", "shard", None),
            P("branch", "shard", None),
        ),
        out_specs=(P(("branch", "shard"), None), P("shard", "branch")),
        check_vma=False,
    )
```

time: 1100 us -> 210 us (0.19)
  blocking collectives: 352 us -> 44.3 us
  local copies, waits for them, and re-layouts: 275 us -> 7.58 us
  other arithmetic: 190 us -> 6.35 us
  waiting for transfers between devices: 219 us -> 110 us
    all_gather x1 -> x0, blocking collectives: 338 us -> none  [local(): spread = lax.all_gather(outgoing, 'shard', axis=1, tiled=True)]
    unnamed x20 -> x15, local copies, waits for them, and re-layouts: 234 us -> 3.69 us
    unnamed x2 -> x0, other arithmetic: 188 us -> none
    all_to_all x3 -> x1, waiting for transfers between devices: 148 us -> 2.65 us  [local(): lax.all_to_all(summed.reshape(experts, capacity, width), 'branch', split_...]
    reduce_scatter x0 -> x2, waiting for transfers between devices: none -> 104 us  [the longest x1 104 us: local(): lax.psum_scatter(both, 'shard', scatter_dimension=1, tiled=True)]
    unnamed x3 -> x4, waiting for transfers between devices: 71.1 us -> 3.11 us
    all_to_all x3 -> x0, local copies, waits for them, and re-layouts: 39.1 us -> none  [the longest x1 18.8 us: local(): lax.all_to_all(up_weight, 'shard', split_axis=2, concat_axis=1, tiled=True)]
    unnamed x0 -> x1, blocking collectives: none -> 29.5 us
  transfers between devices with their start and end apart: 5 -> 5, of which waited for: 2 -> 3; matrix products, arithmetic and copies ran while one was open for 29% -> 21% of each run, Pallas kernels for 0% -> 0%
where the time goes in v1:
time: 210 us; the launch traced here: 209 us
  waiting for transfers between devices  110 us (52%)
  blocking collectives  44.3 us (21%)
  matrix products  19 us (9%)
  between operations  14.9 us (7%)
  local copies, waits for them, and re-layouts  7.58 us (4%)
  starting transfers between devices  7.35 us (4%)
  other arithmetic  6.35 us (3%)
    reduce_scatter x1, waiting for transfers between devices, local(): lax.psum_scatter(both, 'shard', scatter_dimension=1, tiled=True)  104 us
    unnamed x1, blocking collectives  29.5 us
    all_to_all x1, blocking collectives, local(): lax.all_to_all(outgoing, ('branch', 'shard'), split_axis=0, concat_axis=0...  14.8 us
    dot_general x1, matrix products, local(): jnp.dot(rows, up_weight[0], preferred_element_type=jnp.float32)  7.76 us
    dot_general x1, matrix products, local(): jnp.dot(hidden, down_weight[0], preferred_element_type=jnp.float32)  7.65 us
  transfers between devices with their start and end apart: 5, of which 3 were waited for; matrix products, arithmetic and copies ran while one was open for 21% of the time, Pallas kernels for 0%

profile of v1, /device:TPU:0, one launch (start us, length us, event | category | flops | bytes accessed | tf_op | source)
XLA Modules:
  0.0 209.3 jit_solution(17064081493970906530)
XLA Ops:
  7.2 0.0 reduce-scatter.5.cloned.1.call-start
  7.2 0.8 copy.24
  8.0 0.1 eq.64
  8.1 0.2 reduce_window_sum.11
  8.3 0.8 broadcast_in_dim.2
  9.1 0.2 convolution_convert_fusion.2
  9.4 0.1 copy.27
  9.5 14.8 %all_to_all.10 = bf16[32,3,512]{2,1,0:T(4,128)(2,1)S(1)} all-to-all(bf16[32,3,512]{2,1,0:T(4,128)(2,1)S(1)} %copy.27), channel_id=1, replica_groups=mesh['branch'=4,'shard'=8] {'branch','shard'}, dimensions={0} | all-to-all | bytes 196608 | tf_op jit(solution)/shard_map/all_to_all | solution.py:36
  24.4 0.1 reshape.80
  24.5 0.0 copy-start
  24.5 7.8 %convolution_convert_fusion = bf16[96,14336]{1,0:T(8,128)(2,1)S(1)} fusion(bf16[96,512]{1,0:T(8,128)(2,1)S(1)} %reshape.80, bf16[1,512,14336]{2,1,0:T(8,128)(2,1)} %param.11), kind=kOutput, calls=%fused_computation | convolution fusion | flops 1410662400 | bytes 17530880 | tf_op jit(solution)/shard_map/dot_general | solution.py:42
  32.2 1.6 copy-done
  33.8 2.5 %convolution_convert_fusion.1 = bf16[96,14336]{1,0:T(8,128)(2,1)S(1)} fusion(bf16[96,512]{1,0:T(8,128)(2,1)S(1)} %reshape.80, bf16[1,512,14336]{2,1,0:T(8,128)(2,1)S(1)} %copy-done), kind=kOutput, calls=%fused_computation.1 | convolution fusion | flops 1410662400 | bytes 17530880 | tf_op jit(solution)/shard_map/dot_general | solution.py:41
  36.3 2.9 %pad_maximum_fusion = bf16[192,14336]{1,0:T(8,128)(2,1)} fusion(bf16[96,14336]{1,0:T(8,128)(2,1)S(1)} %convolution_convert_fusion, bf16[96,14336]{1,0:T(8,128)(2,1)S(1)} %convolution_convert_fusion.1), kind=kLoop, calls=%fused_computation.6 | loop fusion | flops 11010048 | bytes 11010048 | tf_op jit(solution)/shard_map/concatenate | solution.py:43
  39.3 0.0 reduce-scatter.5.cloned.1.call-update
  39.3 0.0 reduce-scatter.7.cloned.1.call-start
  39.3 0.7 reduce-scatter.7.cloned.1.call-update
  40.0 104.1 %reduce-scatter.5.cloned.1.call-done = bf16[192,1792]{1,0:T(8,128)(2,1)} async-done(((bf16[192,14336]{1,0:T(8,128)(2,1)}), bf16[192,1792]{1,0:T(8,128)(2,1)}) %reduce-scatter.5.cloned.1.call-update) | async-done | bytes 688144 | tf_op jit(solution)/shard_map/reduce_scatter | solution.py:44
  144.1 1.2 convert_element_type.39
  145.3 7.6 %fusion.5 = bf16[96,4096]{1,0:T(8,128)(2,1)S(1)} fusion(bf16[1,1792,4096]{2,1,0:T(8,128)(2,1)} %param.12, f32[192,1792]{1,0:T(8,128)S(1)} %convert_element_type.39), kind=kOutput, calls=%fused_computation.7 | convolution fusion | flops 1410711552 | bytes 16842752 | tf_op jit(solution)/shard_map/dot_general | solution.py:46
  153.0 0.0 copy-start.3
  153.0 0.0 copy-start.1
  153.0 0.0 copy-start.2
  153.0 0.5 reshape.81
  153.5 0.6 copy.28
  154.2 0.7 reshape.82
  154.9 29.5 %fusion = bf16[16,4096]{1,0:T(8,128)(2,1)S(1)} fusion(bf16[96,4096]{1,0:T(8,128)(2,1)S(1)} %reshape.82), kind=kCustom, calls=%all-reduce-scatter | all-reduce-scatter fusion | flops 524289 | bytes 918016
  184.4 1.9 collective-permute-start
  186.3 0.1 eq.68
  186.4 0.1 copy.25
  186.5 0.0 copy-done.3
  186.5 0.6 dynamic-slice.4
  187.8 2.0 collective-permute-start.1
  189.8 0.0 copy-done.1
  189.8 0.0 copy-done.2
  189.8 0.1 select_reduce_fusion
  189.9 2.4 %collective-permute-done.1 = bf16[12,4096]{1,0:T(8,128)(2,1)S(1)} collective-permute-done((bf16[12,4096]{1,0:T(8,128)(2,1)S(1)}, bf16[12,4096]{1,0:T(8,128)(2,1)S(1)}, u32[]{:S(2)}, u32[]{:S(2)}) %collective-permute-start.1) | collective-permute-done | bytes 98336
  192.3 0.0 collective-permute-done
  192.3 0.6 concatenate.4
  192.9 0.7 reshape.83
  193.7 3.3 %all-to-all-start.1 = ((bf16[4,3,4096]{2,1,0:T(4,128)(2,1)}), bf16[4,3,4096]{2,1,0:T(4,128)(2,1)S(1)}, u32[]{:S(2)}, u32[]{:S(2)}) async-start(bf16[4,3,4096]{2,1,0:T(4,128)(2,1)} %reshape.83), calls=%async_computation.2 | async-start | bytes 262144 | tf_op jit(solution)/shard_map/all_to_all | solution.py:50
  197.0 0.0 reduce-scatter.7.cloned.1.call-done
  197.0 1.9 multiply_convert_fusion
  198.9 2.6 %all-to-all-done.1 = bf16[4,3,4096]{2,1,0:T(4,128)(2,1)S(1)} async-done(((bf16[4,3,4096]{2,1,0:T(4,128)(2,1)}), bf16[4,3,4096]{2,1,0:T(4,128)(2,1)S(1)}, u32[]{:S(2)}, u32[]{:S(2)}) %all-to-all-start.1) | async-done | bytes 98336 | tf_op jit(solution)/shard_map/all_to_all | solution.py:50
  201.6 0.1 reshape.84
  201.7 0.8 convolution_convert_fusion.3
  (9 shorter events, 0.2 us)
Async XLA Ops:
  7.2 137.0 %reduce-scatter.5.cloned.1.call-start = ((), (), s32[]{:S(2)}) async-start(), calls=%async_computation.4 | async-start | bytes 6193152 | tf_op jit(solution)/shard_map/reduce_scatter | solution.py:44
  24.5 9.4 %copy-start = (bf16[1,512,14336]{2,1,0:T(8,128)(2,1)S(1)}, bf16[1,512,14336]{2,1,0:T(8,128)(2,1)}, u32[]{:S(2)}) copy-start(bf16[1,512,14336]{2,1,0:T(8,128)(2,1)} %param.10) | copy-start | bytes 44040196
  39.3 157.7 %reduce-scatter.7.cloned.1.call-start = ((), (), s32[]{:S(2)}) async-start(), calls=%async_computation.5 | async-start | bytes 2621440 | tf_op jit(solution)/shard_map/reduce_scatter | solution.py:58
  153.0 33.5 %copy-start.3 = (u32[32]{0:T(128)S(1)}, u32[32]{0:T(128)}, u32[]{:S(2)}) copy-start(u32[32]{0:T(128)} %constant.43) | copy-start | bytes 388
  153.0 36.8 %copy-start.1 = (s32[4,2]{0,1:T(2,128)S(1)}, s32[4,2]{0,1:T(2,128)}, u32[]{:S(2)}) copy-start(s32[4,2]{0,1:T(2,128)} %param.8) | copy-start | bytes 100
  153.0 36.8 %copy-start.2 = (f32[4,2]{0,1:T(2,128)S(1)}, f32[4,2]{0,1:T(2,128)}, u32[]{:S(2)}) copy-start(f32[4,2]{0,1:T(2,128)} %param.9) | copy-start | bytes 100
  184.4 7.9 %collective-permute-start = (bf16[16,4096]{1,0:T(8,128)(2,1)S(1)}, bf16[16,4096]{1,0:T(8,128)(2,1)S(1)}, u32[]{:S(2)}, u32[]{:S(2)}) collective-permute-start(bf16[16,4096]{1,0:T(8,128)(2,1)S(1)} %fusion), channel_id=1, source_target_pairs={{0,1},{1,2},{2,3},{3,4},{4,5},{5,6},{6,7},{8,9},{9,10},{10,11},{11... | collective-permute-start | bytes 393224
  187.8 4.5 %collective-permute-start.1 = (bf16[12,4096]{1,0:T(8,128)(2,1)S(1)}, bf16[12,4096]{1,0:T(8,128)(2,1)S(1)}, u32[]{:S(2)}, u32[]{:S(2)}) collective-permute-start(bf16[12,4096]{1,0:T(8,128)(2,1)S(1)} %slice.10), channel_id=1, source_target_pairs={{0,2},{1,3},{2,4},{3,5},{4,6},{5,7},{8,10},{9,11},{10,12},{11,13},... | collective-permute-start | bytes 294920
  193.7 7.9 %all-to-all-start.1 = ((bf16[4,3,4096]{2,1,0:T(4,128)(2,1)}), bf16[4,3,4096]{2,1,0:T(4,128)(2,1)S(1)}, u32[]{:S(2)}, u32[]{:S(2)}) async-start(bf16[4,3,4096]{2,1,0:T(4,128)(2,1)} %reshape.83), calls=%async_computation.2 | async-start | bytes 262144 | tf_op jit(solution)/shard_map/all_to_all | solution.py:50
Sparse Core Ops, SparseCore 0:
  39.4 104.6 reduce-scatter.4
  146.8 31.1 reduce-scatter.6

commit v2 on v1

v2 whole, which is shorter than its diff:
```python
import functools

import jax
import jax.numpy as jnp
from jax import lax
from jax.sharding import PartitionSpec as P

F32 = jnp.float32
BF16 = jnp.bfloat16


def ring_order(devices):
    places = [getattr(d, "coords", None) for d in devices]
    count = len(places)
    if any(p is None for p in places):
        return list(range(count))
    at = {(p[2], p[0]): i for i, p in enumerate(places)}
    zs, xs = sorted({k[0] for k in at}), sorted({k[1] for k in at})
    if len(at) != count or len(zs) * len(xs) != count or len(xs) < 2 or len(zs) % 2:
        return list(range(count))
    order = [at[(z, xs[0])] for z in zs]
    for i, z in enumerate(reversed(zs)):
        line = xs[1:] if i % 2 == 0 else list(reversed(xs[1:]))
        order += [at[(z, x)] for x in line]
    return order


def core_count(devices):
    places = [getattr(d, "coords", None) for d in devices]
    if any(p is None for p in places):
        return 1
    same = [tuple(p) == tuple(places[0]) for p in places]
    cores = sum(same)
    return cores if all(same[:cores]) and len(places) % cores == 0 else 1


def pick(x, index, axis):
    return lax.dynamic_index_in_dim(x, index, axis, keepdims=False)


def direct_sum(x, axis_name, me, count, target):
    total = pick(x, me, 0).astype(F32)
    for k in range(1, count):
        sent = pick(x, lax.rem(me + k, count), 0).astype(BF16)
        total = total + lax.ppermute(sent, axis_name, target(k)).astype(F32)
    return total


def branch_sum(x, cores):
    size = lax.axis_size("branch")
    chips = size // cores
    b = lax.axis_index("branch")
    core, chip = lax.rem(b, cores), lax.div(b, cores)
    x = jnp.swapaxes(x.reshape((chips, cores) + x.shape[1:]), 0, 1)
    x = direct_sum(
        x, "branch", core, cores,
        lambda k: [(i, i // cores * cores + (i + k) % cores) for i in range(size)],
    )
    return direct_sum(
        x, "branch", chip, chips,
        lambda k: [(i, (i + k * cores) % size) for i in range(size)],
    )


def cell_table(routes, mixing, experts, capacity):
    pairs = routes.shape[0] * 2
    ids = routes.reshape(pairs)
    order = jnp.arange(pairs, dtype=jnp.int32)
    same = (ids[:, None] == ids[None, :]) & (order[None, :] < order[:, None])
    slots = jnp.sum(same.astype(jnp.int32), axis=1)
    cells = jnp.arange(experts * capacity, dtype=jnp.int32)
    placing = cells[:, None] == (ids * capacity + slots)[None, :]
    number = jnp.sum(jnp.where(placing, order[None, :] // 2 + 1, 0), axis=1)
    weight = jnp.sum(jnp.where(placing, mixing.reshape(pairs)[None, :], 0.0), axis=1)
    return placing, number, weight


def local(order, cores, tokens, routes, mixing, gate_weight, up_weight, down_weight, key_value):
    experts = lax.axis_size("branch")
    shards = lax.axis_size("shard")
    token_count, width = tokens.shape
    capacity = max(2, (2 * token_count + experts - 1) // experts + 1)
    depth = gate_weight.shape[1]
    slice_width = down_weight.shape[1]
    count = experts * shards * capacity

    kv = key_value[0].reshape(key_value.shape[1], experts, -1).swapaxes(0, 1)
    merged_kv = (branch_sum(kv, cores) / experts).astype(BF16)

    placing, number, weight = cell_table(routes, mixing, experts, capacity)
    cells = jnp.dot(
        placing.astype(BF16), jnp.repeat(tokens, 2, axis=0), preferred_element_type=F32
    ).astype(BF16)
    high = weight.astype(BF16)
    low = (weight - high.astype(F32)).astype(BF16)
    extra = jnp.stack([number.astype(BF16), high, low], axis=1)
    extra = jnp.pad(extra, ((0, 0), (0, 125)))
    cells = jnp.concatenate([cells, extra], axis=1).reshape(experts, capacity, -1)
    cells = lax.all_to_all(cells, "branch", split_axis=0, concat_axis=0, tiled=True)
    cells = cells.reshape(experts * capacity, -1)
    body = cells[:, :width].reshape(experts * capacity, shards, depth).swapaxes(0, 1)
    tail = jnp.broadcast_to(cells[None, :, width:], (shards, experts * capacity, 128))
    cells = jnp.concatenate([body, tail], axis=2)
    cells = lax.all_to_all(cells, "shard", split_axis=0, concat_axis=0, tiled=True)
    cells = cells.reshape(count, depth + 128)
    rows = cells[:, :depth]
    number = cells[:, depth].astype(jnp.int32)
    weight = (cells[:, depth + 1].astype(F32) + cells[:, depth + 2].astype(F32))[:, None]

    gate = jnp.dot(rows, gate_weight[0], preferred_element_type=F32)
    upper = jnp.dot(rows, up_weight[0], preferred_element_type=F32)

    place = [0] * shards
    for i, s in enumerate(order):
        place[s] = i
    here = jnp.asarray(place, jnp.int32)[lax.axis_index("shard")]
    owner = jnp.asarray(order, jnp.int32)
    forth = [(order[i], order[(i + 1) % shards]) for i in range(shards)]
    back = [(b, a) for a, b in forth]

    def piece(x, step):
        who = owner[lax.rem(here + step + 2 * shards, shards)]
        return lax.dynamic_slice_in_dim(x, who * slice_width, slice_width, 1)

    gate_sum, up_sum = piece(gate, -1), piece(upper, 1)
    for t in range(1, shards):
        gate_in = lax.ppermute(gate_sum.astype(BF16), "shard", forth)
        up_in = lax.ppermute(up_sum.astype(BF16), "shard", back)
        gate_sum = gate_in.astype(F32) + piece(gate, -1 - t)
        up_sum = up_in.astype(F32) + piece(upper, 1 + t)

    hidden = (jax.nn.silu(gate_sum) * up_sum * weight).astype(BF16)
    cell = jnp.arange(count, dtype=jnp.int32)
    source = cell // capacity
    source = lax.rem(source, experts) * shards + source // experts
    target = jnp.where(number > 0, source * token_count + number - 1, -1)
    spread = target[:, None] == jnp.arange(experts * shards * token_count, dtype=jnp.int32)[None, :]
    hidden = lax.dot_general(
        spread.astype(BF16), hidden, (((0,), (0,)), ((), ())), preferred_element_type=F32
    ).astype(BF16)
    partial = jnp.dot(hidden, down_weight[0], preferred_element_type=F32)
    partial = branch_sum(partial.reshape(experts, shards * token_count, width), cores)
    partial = partial.astype(BF16).reshape(shards, token_count, width)
    partial = lax.all_to_all(partial, "shard", split_axis=0, concat_axis=0, tiled=True)
    mixed_out = jnp.sum(partial.astype(F32), axis=0).astype(BF16)
    return mixed_out, merged_kv


def solution(mesh):
    grid = mesh.devices
    order = ring_order(list(grid[0, :]))
    cores = core_count(list(grid[:, 0]))
    return jax.shard_map(
        functools.partial(local, order, cores),
        mesh=mesh,
        in_specs=(
            P(("branch", "shard"), None),
            P(("branch", "shard"), None),
            P(("branch", "shard"), None),
            P("branch", "shard", None),
            P("branch", "shard", None),
            P("branch", "shard", None),
            P("branch", "shard", None),
        ),
        out_specs=(P(("branch", "shard"), None), P("shard", "branch")),
        check_vma=False,
    )
```

time: 210 us -> 164 us (0.78)
  waiting for transfers between devices: 110 us -> 47.6 us
  blocking collectives: 44.3 us -> 8.75 us
  starting transfers between devices: 7.35 us -> 40.4 us
  local copies, waits for them, and re-layouts: 7.58 us -> 18.5 us
  between operations: 14.9 us -> 21.5 us
    reduce_scatter x2 -> x0, waiting for transfers between devices: 104 us -> none  [the longest x1 104 us: local(): lax.psum_scatter(both, 'shard', scatter_dimension=1, tiled=True)]
    ppermute x0 -> x18, waiting for transfers between devices: none -> 45.1 us  [the longest x7 26.9 us: local(): gate_in = lax.ppermute(gate_sum.astype(BF16), 'shard', forth)]
    unnamed x1 -> x0, blocking collectives: 29.5 us -> none
    ppermute x0 -> x18, starting transfers between devices: none -> 28.8 us  [the longest x7 13.4 us: local(): gate_in = lax.ppermute(gate_sum.astype(BF16), 'shard', forth)]
    all_to_all x1 -> x2, starting transfers between devices: 3.32 us -> 11.6 us  [the longest x1 5.83 us: local(): lax.all_to_all(partial, 'shard', split_axis=0, concat_axis=0, tiled=True)]
    all_to_all x1, blocking collectives: 14.8 us -> 8.75 us  [local(): lax.all_to_all(cells, 'branch', split_axis=0, concat_axis=0, tiled=True)]
    unnamed x2 -> x0, starting transfers between devices: 3.94 us -> none
    unnamed x15 -> x16, local copies, waits for them, and re-layouts: 3.69 us -> 7.58 us
  transfers between devices with their start and end apart: 5 -> 20, of which waited for: 3 -> 17; matrix products, arithmetic and copies ran while one was open for 21% -> 11% of each run, Pallas kernels for 0% -> 0%
where the time goes in v2:
time: 164 us; the launch traced here: 163 us
  waiting for transfers between devices  47.6 us (29%)
  starting transfers between devices  40.4 us (25%)
  between operations  21.5 us (13%)
  matrix products  19.9 us (12%)
  local copies, waits for them, and re-layouts  18.5 us (11%)
  blocking collectives  8.75 us (5%)
  other arithmetic  6.38 us (4%)
    ppermute x7, waiting for transfers between devices, local(): gate_in = lax.ppermute(gate_sum.astype(BF16), 'shard', forth)  26.9 us
    ppermute x7, starting transfers between devices, local(): gate_in = lax.ppermute(gate_sum.astype(BF16), 'shard', forth)  13.4 us
    ppermute x7, starting transfers between devices, local(): up_in = lax.ppermute(up_sum.astype(BF16), 'shard', back)  13.2 us
    ppermute x4, waiting for transfers between devices, direct_sum(): total = total + lax.ppermute(sent, axis_name, target(k)).astype(F32)  9.49 us
    ppermute x7, waiting for transfers between devices, local(): up_in = lax.ppermute(up_sum.astype(BF16), 'shard', back)  8.79 us
    all_to_all x1, blocking collectives, local(): lax.all_to_all(cells, 'branch', split_axis=0, concat_axis=0, tiled=True)  8.75 us
    dot_general x1, matrix products, local(): upper = jnp.dot(rows, up_weight[0], preferred_element_type=F32)  7.76 us
    unnamed x16, local copies, waits for them, and re-layouts  7.58 us
  transfers between devices with their start and end apart: 20, of which 17 were waited for; matrix products, arithmetic and copies ran while one was open for 11% of the time, Pallas kernels for 0%

profile of v2, /device:TPU:0, one launch (start us, length us, event | category | flops | bytes accessed | tf_op | source)
XLA Modules:
  0.0 163.0 jit_solution(11965654178277892005)
XLA Ops:
  4.1 8.8 %all_to_all.15 = bf16[4,3,4224]{2,1,0:T(4,128)(2,1)S(1)} all-to-all(bf16[4,3,4224]{2,1,0:T(4,128)(2,1)S(1)} %reshape.275), channel_id=1, replica_groups=mesh['branch'=4,'shard'=8] {'branch'}, dimensions={0} | all-to-all | bytes 202752 | tf_op jit(solution)/shard_map/all_to_all | solution.py:99
  13.8 5.8 %all-to-all-start.1 = ((bf16[8,12,640]{2,1,0:T(8,128)(2,1)}), bf16[8,12,640]{2,1,0:T(8,128)(2,1)S(1)}, u32[]{:S(2)}, u32[]{:S(2)}) async-start(bf16[8,12,640]{2,1,0:T(8,128)(2,1)} %copy.40), calls=%async_computation.1 | async-start | bytes 327680 | tf_op jit(solution)/shard_map/all_to_all | solution.py:104
  19.6 1.2 dynamic_slice.119
  31.3 2.0 %fusion.33 = (s32[1]{0:T(128)}, s32[1]{0:T(128)}, s32[1]{0:T(128)}, s32[1]{0:T(128)}, s32[1]{0:T(128)}, /*index=5*/s32[1]{0:T(128)}, s32[1]{0:T(128)}, s32[1]{0:...) fusion(s32[8]{0:T(128)} %constant.215.clone, ...), kind=kLoop, calls=%fused_computation.88 | loop fusion | bytes 192 | tf_op jit(solution)/shard_map/dynamic_slice | solution.py:122
  42.2 7.8 %fusion.2 = f32[96,14336]{1,0:T(8,128)S(1)} fusion(bf16[1,512,14336]{2,1,0:T(8,128)(2,1)} %param.13, bf16[96,640]{1,0:T(8,128)(2,1)S(1)} %reshape.278), kind=kOutput, calls=%fused_computation.2 | convolution fusion | flops 1409286144 | bytes 20283392 | tf_op jit(solution)/shard_map/dot_general | solution.py:111
  50.0 2.1 %collective-permute-start.7 = (bf16[96,1792]{1,0:T(8,128)(2,1)S(1)}, bf16[96,1792]{1,0:T(8,128)(2,1)S(1)}, u32[]{:S(2)}, u32[]{:S(2)}) collective-permute-start(bf16[96,1792]{1,0:T(8,128)(2,1)S(1)} %dynamic-slice_convert_fusion.2), channel_id=1, source_target_pairs={{2,0},{4,2},{6,4},{7,6},{5,7},{3,5},{1,3},{0,1},{10,8},{12,10},{14... | collective-permute-start | bytes 1032200 | tf_op jit(solution)/shard_map/ppermute | solution.py:128
  52.9 2.6 %fusion.4 = f32[96,14336]{1,0:T(8,128)S(1)} fusion(bf16[1,512,14336]{2,1,0:T(8,128)(2,1)S(1)} %copy-done.2, bf16[96,640]{1,0:T(8,128)(2,1)S(1)} %reshape.278), kind=kOutput, calls=%fused_computation.4 | convolution fusion | flops 1409286144 | bytes 20283392 | tf_op jit(solution)/shard_map/dot_general | solution.py:110
  55.6 2.1 %collective-permute-start = (bf16[96,1792]{1,0:T(8,128)(2,1)S(1)}, bf16[96,1792]{1,0:T(8,128)(2,1)S(1)}, u32[]{:S(2)}, u32[]{:S(2)}) collective-permute-start(bf16[96,1792]{1,0:T(8,128)(2,1)S(1)} %dynamic-slice_convert_fusion.3), channel_id=1, source_target_pairs={{0,2},{2,4},{4,6},{6,7},{7,5},{5,3},{3,1},{1,0},{8,10},{10,12},{12... | collective-permute-start | bytes 1032200 | tf_op jit(solution)/shard_map/ppermute | solution.py:127
  57.7 2.1 %collective-permute-done.7 = bf16[96,1792]{1,0:T(8,128)(2,1)S(1)} collective-permute-done((bf16[96,1792]{1,0:T(8,128)(2,1)S(1)}, bf16[96,1792]{1,0:T(8,128)(2,1)S(1)}, u32[]{:S(2)}, u32[]{:S(2)}) %collective-permute-start.7) | collective-permute-done | bytes 344096 | tf_op jit(solution)/shard_map/ppermute | solution.py:128
  59.9 1.8 %collective-permute-start.8 = (bf16[96,1792]{1,0:T(8,128)(2,1)S(1)}, bf16[96,1792]{1,0:T(8,128)(2,1)S(1)}, u32[]{:S(2)}, u32[]{:S(2)}) collective-permute-start(bf16[96,1792]{1,0:T(8,128)(2,1)S(1)} %add_convert_fusion.5), channel_id=1, source_target_pairs={{2,0},{4,2},{6,4},{7,6},{5,7},{3,5},{1,3},{0,1},{10,8},{12,10},{14... | collective-permute-start | bytes 1032200 | tf_op jit(solution)/shard_map/ppermute | solution.py:128
  61.7 3.7 %collective-permute-done = bf16[96,1792]{1,0:T(8,128)(2,1)S(1)} collective-permute-done((bf16[96,1792]{1,0:T(8,128)(2,1)S(1)}, bf16[96,1792]{1,0:T(8,128)(2,1)S(1)}, u32[]{:S(2)}, u32[]{:S(2)}) %collective-permute-start) | collective-permute-done | bytes 344096 | tf_op jit(solution)/shard_map/ppermute | solution.py:127
  65.5 1.8 %collective-permute-start.1 = (bf16[96,1792]{1,0:T(8,128)(2,1)S(1)}, bf16[96,1792]{1,0:T(8,128)(2,1)S(1)}, u32[]{:S(2)}, u32[]{:S(2)}) collective-permute-start(bf16[96,1792]{1,0:T(8,128)(2,1)S(1)} %add_convert_fusion.11), channel_id=1, source_target_pairs={{0,2},{2,4},{4,6},{6,7},{7,5},{5,3},{3,1},{1,0},{8,10},{10,12},{12... | collective-permute-start | bytes 1032200 | tf_op jit(solution)/shard_map/ppermute | solution.py:127
  67.3 1.5 collective-permute-done.8
  68.8 1.5 collective-permute-start.9
  70.3 4.1 %collective-permute-done.1 = bf16[96,1792]{1,0:T(8,128)(2,1)S(1)} collective-permute-done((bf16[96,1792]{1,0:T(8,128)(2,1)S(1)}, bf16[96,1792]{1,0:T(8,128)(2,1)S(1)}, u32[]{:S(2)}, u32[]{:S(2)}) %collective-permute-start.1) | collective-permute-done | bytes 344096 | tf_op jit(solution)/shard_map/ppermute | solution.py:127
  74.5 1.5 collective-permute-start.2
  75.9 1.1 collective-permute-done.9
  77.1 1.5 collective-permute-start.10
  78.6 4.1 %collective-permute-done.2 = bf16[96,1792]{1,0:T(8,128)(2,1)S(1)} collective-permute-done((bf16[96,1792]{1,0:T(8,128)(2,1)S(1)}, bf16[96,1792]{1,0:T(8,128)(2,1)S(1)}, u32[]{:S(2)}, u32[]{:S(2)}) %collective-permute-start.2) | collective-permute-done | bytes 344096 | tf_op jit(solution)/shard_map/ppermute | solution.py:127
  82.7 1.5 collective-permute-start.3
  84.1 1.2 collective-permute-done.10
  85.4 1.8 %collective-permute-start.11 = (bf16[96,1792]{1,0:T(8,128)(2,1)S(1)}, bf16[96,1792]{1,0:T(8,128)(2,1)S(1)}, u32[]{:S(2)}, u32[]{:S(2)}) collective-permute-start(bf16[96,1792]{1,0:T(8,128)(2,1)S(1)} %add_convert_fusion.2), channel_id=1, source_target_pairs={{2,0},{4,2},{6,4},{7,6},{5,7},{3,5},{1,3},{0,1},{10,8},{12,10},{14... | collective-permute-start | bytes 1032200 | tf_op jit(solution)/shard_map/ppermute | solution.py:128
  87.2 4.0 %collective-permute-done.3 = bf16[96,1792]{1,0:T(8,128)(2,1)S(1)} collective-permute-done((bf16[96,1792]{1,0:T(8,128)(2,1)S(1)}, bf16[96,1792]{1,0:T(8,128)(2,1)S(1)}, u32[]{:S(2)}, u32[]{:S(2)}) %collective-permute-start.3) | collective-permute-done | bytes 344096 | tf_op jit(solution)/shard_map/ppermute | solution.py:127
  91.3 1.8 %collective-permute-start.4 = (bf16[96,1792]{1,0:T(8,128)(2,1)S(1)}, bf16[96,1792]{1,0:T(8,128)(2,1)S(1)}, u32[]{:S(2)}, u32[]{:S(2)}) collective-permute-start(bf16[96,1792]{1,0:T(8,128)(2,1)S(1)} %add_convert_fusion.8), channel_id=1, source_target_pairs={{0,2},{2,4},{4,6},{6,7},{7,5},{5,3},{3,1},{1,0},{8,10},{10,12},{12... | collective-permute-start | bytes 1032200 | tf_op jit(solution)/shard_map/ppermute | solution.py:127
  93.1 1.3 collective-permute-done.11
  94.5 2.1 %collective-permute-start.12 = (bf16[96,1792]{1,0:T(8,128)(2,1)S(1)}, bf16[96,1792]{1,0:T(8,128)(2,1)S(1)}, u32[]{:S(2)}, u32[]{:S(2)}) collective-permute-start(bf16[96,1792]{1,0:T(8,128)(2,1)S(1)} %add_convert_fusion.1), channel_id=1, source_target_pairs={{2,0},{4,2},{6,4},{7,6},{5,7},{3,5},{1,3},{0,1},{10,8},{12,10},{14... | collective-permute-start | bytes 1032200 | tf_op jit(solution)/shard_map/ppermute | solution.py:128
  96.6 4.0 %collective-permute-done.4 = bf16[96,1792]{1,0:T(8,128)(2,1)S(1)} collective-permute-done((bf16[96,1792]{1,0:T(8,128)(2,1)S(1)}, bf16[96,1792]{1,0:T(8,128)(2,1)S(1)}, u32[]{:S(2)}, u32[]{:S(2)}) %collective-permute-start.4) | collective-permute-done | bytes 344096 | tf_op jit(solution)/shard_map/ppermute | solution.py:127
  100.7 2.2 %collective-permute-start.5 = (bf16[96,1792]{1,0:T(8,128)(2,1)S(1)}, bf16[96,1792]{1,0:T(8,128)(2,1)S(1)}, u32[]{:S(2)}, u32[]{:S(2)}) collective-permute-start(bf16[96,1792]{1,0:T(8,128)(2,1)S(1)} %add_convert_fusion.7), channel_id=1, source_target_pairs={{0,2},{2,4},{4,6},{6,7},{7,5},{5,3},{3,1},{1,0},{8,10},{10,12},{12... | collective-permute-start | bytes 1032200 | tf_op jit(solution)/shard_map/ppermute | solution.py:127
  102.8 1.5 collective-permute-done.12
  104.5 2.5 %collective-permute-start.13 = (bf16[96,1792]{1,0:T(8,128)(2,1)S(1)}, bf16[96,1792]{1,0:T(8,128)(2,1)S(1)}, u32[]{:S(2)}, u32[]{:S(2)}) collective-permute-start(bf16[96,1792]{1,0:T(8,128)(2,1)S(1)} %add_convert_fusion), channel_id=1, source_target_pairs={{2,0},{4,2},{6,4},{7,6},{5,7},{3,5},{1,3},{0,1},{10,8},{12,10},{14... | collective-permute-start | bytes 1032200 | tf_op jit(solution)/shard_map/ppermute | solution.py:128
  106.9 3.8 %collective-permute-done.5 = bf16[96,1792]{1,0:T(8,128)(2,1)S(1)} collective-permute-done((bf16[96,1792]{1,0:T(8,128)(2,1)S(1)}, bf16[96,1792]{1,0:T(8,128)(2,1)S(1)}, u32[]{:S(2)}, u32[]{:S(2)}) %collective-permute-start.5) | collective-permute-done | bytes 344096 | tf_op jit(solution)/shard_map/ppermute | solution.py:127
  110.8 2.7 %collective-permute-start.6 = (bf16[96,1792]{1,0:T(8,128)(2,1)S(1)}, bf16[96,1792]{1,0:T(8,128)(2,1)S(1)}, u32[]{:S(2)}, u32[]{:S(2)}) collective-permute-start(bf16[96,1792]{1,0:T(8,128)(2,1)S(1)} %add_convert_fusion.6), channel_id=1, source_target_pairs={{0,2},{2,4},{4,6},{6,7},{7,5},{5,3},{3,1},{1,0},{8,10},{10,12},{12... | collective-permute-start | bytes 1032200 | tf_op jit(solution)/shard_map/ppermute | solution.py:127
  115.1 3.2 %collective-permute-done.6 = bf16[96,1792]{1,0:T(8,128)(2,1)S(1)} collective-permute-done((bf16[96,1792]{1,0:T(8,128)(2,1)S(1)}, bf16[96,1792]{1,0:T(8,128)(2,1)S(1)}, u32[]{:S(2)}, u32[]{:S(2)}) %collective-permute-start.6) | collective-permute-done | bytes 344096 | tf_op jit(solution)/shard_map/ppermute | solution.py:127
  118.3 1.8 %convolution_convert_fusion.1 = bf16[128,1792]{1,0:T(8,128)(2,1)S(1)} fusion(f32[96,14336]{1,0:T(8,128)} %copy-done, s32[]{:T(128)S(6)} %select_n.202, bf16[96,1792]{1,0:T(8,128)(2,1)S(1)} %collective-permute-done.13, f32[96,14336]{1,0:T(8,128)} %copy-done.1, s32[]{:T(128)S(6)} %select_n.186, bf16[96,1792]{1,0:T(8,128)(2,1)S(1)} %collective-permute-done.6, ...), kind=kOutput, calls=%fused_computation.7 | convolution fusion | flops 46174208 | bytes 2523912 | tf_op jit(solution)/shard_map/dot_general | solution.py:138
  120.1 7.5 %fusion = f32[2,2,32,4096]{3,2,1,0:T(8,128)S(1)} fusion(bf16[2,2,32,1792]{3,2,1,0:T(8,128)(2,1)S(1)} %bitcast.92, bf16[1,1792,4096]{2,1,0:T(8,128)(2,1)} %param.14), kind=kOutput, calls=%fused_computation | convolution fusion | flops 1879048192 | bytes 17235968 | tf_op jit(solution)/shard_map/dot_general | solution.py:141
  127.6 1.3 copy-done.3
  128.9 0.8 fusion.8
  129.7 2.5 %copy.41 = bf16[1,512,2048]{1,2,0:T(8,128)(2,1)} copy(bf16[1,512,2048]{2,1,0:T(8,128)(2,1)S(1)} %copy-done.5) | data formatting | bytes 4194304 | tf_op args[6]
  132.2 2.8 %copy.42 = bf16[4,512,512]{2,1,0:T(8,128)(2,1)S(1)} copy(bf16[4,512,512]{1,2,0:T(8,128)(2,1)} %bitcast.91) | data formatting | bytes 4194304 | tf_op jit(solution)/shard_map/transpose | solution.py:87
  135.0 1.1 dynamic-slice_bitcast_fusion
  136.6 1.5 bitcast_add_fusion.1
  139.5 1.3 copy-done.4
  140.8 1.2 collective-permute-start.17
  142.0 5.3 %collective-permute-done.15 = bf16[32,4096]{1,0:T(8,128)(2,1)S(1)} collective-permute-done((bf16[32,4096]{1,0:T(8,128)(2,1)S(1)}, bf16[32,4096]{1,0:T(8,128)(2,1)S(1)}, u32[]{:S(2)}, u32[]{:S(2)}) %collective-permute-start.15) | collective-permute-done | bytes 262176 | tf_op jit(solution)/shard_map/ppermute | solution.py:45
  148.2 5.8 %all-to-all-start.2 = ((bf16[8,4,4096]{2,1,0:T(4,128)(2,1)}), bf16[8,4,4096]{2,1,0:T(4,128)(2,1)S(1)}, u32[]{:S(2)}, u32[]{:S(2)}) async-start(bf16[8,4,4096]{2,1,0:T(4,128)(2,1)} %reshape.279), calls=%async_computation.2 | async-start | bytes 524288 | tf_op jit(solution)/shard_map/all_to_all | solution.py:144
  154.1 3.6 %collective-permute-done.17 = bf16[512,512]{1,0:T(8,128)(2,1)S(1)} collective-permute-done((bf16[512,512]{1,0:T(8,128)(2,1)S(1)}, bf16[512,512]{1,0:T(8,128)(2,1)S(1)}, u32[]{:S(2)}, u32[]{:S(2)}) %collective-permute-start.17) | collective-permute-done | bytes 524320 | tf_op jit(solution)/shard_map/ppermute | solution.py:45
  157.7 2.2 %fusion.7 = bf16[512,512]{1,0:T(8,128)(2,1)} fusion(bf16[512,512]{1,0:T(8,128)(2,1)S(1)} %collective-permute-done.17, f32[2,512,512]{2,1,0:T(8,128)} %copy-done.4, s32[]{:T(128)S(6)} %select_n.205), kind=kLoop, calls=%fused_computation.11 | loop fusion | flops 1048576 | bytes 2097156 | tf_op jit(solution)/shard_map/convert_element_type | solution.py:88
  159.8 2.4 %all-to-all-done.2 = bf16[8,4,4096]{2,1,0:T(4,128)(2,1)S(1)} async-done(((bf16[8,4,4096]{2,1,0:T(4,128)(2,1)}), bf16[8,4,4096]{2,1,0:T(4,128)(2,1)S(1)}, u32[]{:S(2)}, u32[]{:S(2)}) %all-to-all-start.2) | async-done | bytes 262176 | tf_op jit(solution)/shard_map/all_to_all | solution.py:144
  (67 shorter events, 9.9 us)
Async XLA Ops:
  13.8 28.4 %all-to-all-start.1 = ((bf16[8,12,640]{2,1,0:T(8,128)(2,1)}), bf16[8,12,640]{2,1,0:T(8,128)(2,1)S(1)}, u32[]{:S(2)}, u32[]{:S(2)}) async-start(bf16[8,12,640]{2,1,0:T(8,128)(2,1)} %copy.40), calls=%async_computation.1 | async-start | bytes 327680 | tf_op jit(solution)/shard_map/all_to_all | solution.py:104
  42.2 10.7 %copy-start.2 = (bf16[1,512,14336]{2,1,0:T(8,128)(2,1)S(1)}, bf16[1,512,14336]{2,1,0:T(8,128)(2,1)}, u32[]{:S(2)}) copy-start(bf16[1,512,14336]{2,1,0:T(8,128)(2,1)} %param.12) | copy-start | bytes 44040196
  49.9 54.4 %copy-start = (f32[96,14336]{1,0:T(8,128)}, f32[96,14336]{1,0:T(8,128)S(1)}, u32[]{:S(2)}) copy-start(f32[96,14336]{1,0:T(8,128)S(1)} %fusion.2) | copy-start | bytes 16515076
  50.0 9.8 %collective-permute-start.7 = (bf16[96,1792]{1,0:T(8,128)(2,1)S(1)}, bf16[96,1792]{1,0:T(8,128)(2,1)S(1)}, u32[]{:S(2)}, u32[]{:S(2)}) collective-permute-start(bf16[96,1792]{1,0:T(8,128)(2,1)S(1)} %dynamic-slice_convert_fusion.2), channel_id=1, source_target_pairs={{2,0},{4,2},{6,4},{7,6},{5,7},{3,5},{1,3},{0,1},{10,8},{12,10},{14... | collective-permute-start | bytes 1032200 | tf_op jit(solution)/shard_map/ppermute | solution.py:128
  55.5 55.2 %copy-start.1 = (f32[96,14336]{1,0:T(8,128)}, f32[96,14336]{1,0:T(8,128)S(1)}, u32[]{:S(2)}) copy-start(f32[96,14336]{1,0:T(8,128)S(1)} %fusion.4) | copy-start | bytes 16515076
  55.6 9.8 %collective-permute-start = (bf16[96,1792]{1,0:T(8,128)(2,1)S(1)}, bf16[96,1792]{1,0:T(8,128)(2,1)S(1)}, u32[]{:S(2)}, u32[]{:S(2)}) collective-permute-start(bf16[96,1792]{1,0:T(8,128)(2,1)S(1)} %dynamic-slice_convert_fusion.3), channel_id=1, source_target_pairs={{0,2},{2,4},{4,6},{6,7},{7,5},{5,3},{3,1},{1,0},{8,10},{10,12},{12... | collective-permute-start | bytes 1032200 | tf_op jit(solution)/shard_map/ppermute | solution.py:127
  59.9 8.9 %collective-permute-start.8 = (bf16[96,1792]{1,0:T(8,128)(2,1)S(1)}, bf16[96,1792]{1,0:T(8,128)(2,1)S(1)}, u32[]{:S(2)}, u32[]{:S(2)}) collective-permute-start(bf16[96,1792]{1,0:T(8,128)(2,1)S(1)} %add_convert_fusion.5), channel_id=1, source_target_pairs={{2,0},{4,2},{6,4},{7,6},{5,7},{3,5},{1,3},{0,1},{10,8},{12,10},{14... | collective-permute-start | bytes 1032200 | tf_op jit(solution)/shard_map/ppermute | solution.py:128
  65.5 8.9 %collective-permute-start.1 = (bf16[96,1792]{1,0:T(8,128)(2,1)S(1)}, bf16[96,1792]{1,0:T(8,128)(2,1)S(1)}, u32[]{:S(2)}, u32[]{:S(2)}) collective-permute-start(bf16[96,1792]{1,0:T(8,128)(2,1)S(1)} %add_convert_fusion.11), channel_id=1, source_target_pairs={{0,2},{2,4},{4,6},{6,7},{7,5},{5,3},{3,1},{1,0},{8,10},{10,12},{12... | collective-permute-start | bytes 1032200 | tf_op jit(solution)/shard_map/ppermute | solution.py:127
  68.8 8.1 %collective-permute-start.9 = (bf16[96,1792]{1,0:T(8,128)(2,1)S(1)}, bf16[96,1792]{1,0:T(8,128)(2,1)S(1)}, u32[]{:S(2)}, u32[]{:S(2)}) collective-permute-start(bf16[96,1792]{1,0:T(8,128)(2,1)S(1)} %add_convert_fusion.4), channel_id=1, source_target_pairs={{2,0},{4,2},{6,4},{7,6},{5,7},{3,5},{1,3},{0,1},{10,8},{12,10},{14... | collective-permute-start | bytes 1032200 | tf_op jit(solution)/shard_map/ppermute | solution.py:128
  74.5 8.1 %collective-permute-start.2 = (bf16[96,1792]{1,0:T(8,128)(2,1)S(1)}, bf16[96,1792]{1,0:T(8,128)(2,1)S(1)}, u32[]{:S(2)}, u32[]{:S(2)}) collective-permute-start(bf16[96,1792]{1,0:T(8,128)(2,1)S(1)} %add_convert_fusion.10), channel_id=1, source_target_pairs={{0,2},{2,4},{4,6},{6,7},{7,5},{5,3},{3,1},{1,0},{8,10},{10,12},{12... | collective-permute-start | bytes 1032200 | tf_op jit(solution)/shard_map/ppermute | solution.py:127
  77.1 8.2 %collective-permute-start.10 = (bf16[96,1792]{1,0:T(8,128)(2,1)S(1)}, bf16[96,1792]{1,0:T(8,128)(2,1)S(1)}, u32[]{:S(2)}, u32[]{:S(2)}) collective-permute-start(bf16[96,1792]{1,0:T(8,128)(2,1)S(1)} %add_convert_fusion.3), channel_id=1, source_target_pairs={{2,0},{4,2},{6,4},{7,6},{5,7},{3,5},{1,3},{0,1},{10,8},{12,10},{14... | collective-permute-start | bytes 1032200 | tf_op jit(solution)/shard_map/ppermute | solution.py:128
  82.7 8.5 %collective-permute-start.3 = (bf16[96,1792]{1,0:T(8,128)(2,1)S(1)}, bf16[96,1792]{1,0:T(8,128)(2,1)S(1)}, u32[]{:S(2)}, u32[]{:S(2)}) collective-permute-start(bf16[96,1792]{1,0:T(8,128)(2,1)S(1)} %add_convert_fusion.9), channel_id=1, source_target_pairs={{0,2},{2,4},{4,6},{6,7},{7,5},{5,3},{3,1},{1,0},{8,10},{10,12},{12... | collective-permute-start | bytes 1032200 | tf_op jit(solution)/shard_map/ppermute | solution.py:127
  85.4 9.0 %collective-permute-start.11 = (bf16[96,1792]{1,0:T(8,128)(2,1)S(1)}, bf16[96,1792]{1,0:T(8,128)(2,1)S(1)}, u32[]{:S(2)}, u32[]{:S(2)}) collective-permute-start(bf16[96,1792]{1,0:T(8,128)(2,1)S(1)} %add_convert_fusion.2), channel_id=1, source_target_pairs={{2,0},{4,2},{6,4},{7,6},{5,7},{3,5},{1,3},{0,1},{10,8},{12,10},{14... | collective-permute-start | bytes 1032200 | tf_op jit(solution)/shard_map/ppermute | solution.py:128
  91.3 9.3 %collective-permute-start.4 = (bf16[96,1792]{1,0:T(8,128)(2,1)S(1)}, bf16[96,1792]{1,0:T(8,128)(2,1)S(1)}, u32[]{:S(2)}, u32[]{:S(2)}) collective-permute-start(bf16[96,1792]{1,0:T(8,128)(2,1)S(1)} %add_convert_fusion.8), channel_id=1, source_target_pairs={{0,2},{2,4},{4,6},{6,7},{7,5},{5,3},{3,1},{1,0},{8,10},{10,12},{12... | collective-permute-start | bytes 1032200 | tf_op jit(solution)/shard_map/ppermute | solution.py:127
  94.5 9.9 %collective-permute-start.12 = (bf16[96,1792]{1,0:T(8,128)(2,1)S(1)}, bf16[96,1792]{1,0:T(8,128)(2,1)S(1)}, u32[]{:S(2)}, u32[]{:S(2)}) collective-permute-start(bf16[96,1792]{1,0:T(8,128)(2,1)S(1)} %add_convert_fusion.1), channel_id=1, source_target_pairs={{2,0},{4,2},{6,4},{7,6},{5,7},{3,5},{1,3},{0,1},{10,8},{12,10},{14... | collective-permute-start | bytes 1032200 | tf_op jit(solution)/shard_map/ppermute | solution.py:128
  100.7 10.0 %collective-permute-start.5 = (bf16[96,1792]{1,0:T(8,128)(2,1)S(1)}, bf16[96,1792]{1,0:T(8,128)(2,1)S(1)}, u32[]{:S(2)}, u32[]{:S(2)}) collective-permute-start(bf16[96,1792]{1,0:T(8,128)(2,1)S(1)} %add_convert_fusion.7), channel_id=1, source_target_pairs={{0,2},{2,4},{4,6},{6,7},{7,5},{5,3},{3,1},{1,0},{8,10},{10,12},{12... | collective-permute-start | bytes 1032200 | tf_op jit(solution)/shard_map/ppermute | solution.py:127
  104.5 10.6 %collective-permute-start.13 = (bf16[96,1792]{1,0:T(8,128)(2,1)S(1)}, bf16[96,1792]{1,0:T(8,128)(2,1)S(1)}, u32[]{:S(2)}, u32[]{:S(2)}) collective-permute-start(bf16[96,1792]{1,0:T(8,128)(2,1)S(1)} %add_convert_fusion), channel_id=1, source_target_pairs={{2,0},{4,2},{6,4},{7,6},{5,7},{3,5},{1,3},{0,1},{10,8},{12,10},{14... | collective-permute-start | bytes 1032200 | tf_op jit(solution)/shard_map/ppermute | solution.py:128
  110.8 7.5 %collective-permute-start.6 = (bf16[96,1792]{1,0:T(8,128)(2,1)S(1)}, bf16[96,1792]{1,0:T(8,128)(2,1)S(1)}, u32[]{:S(2)}, u32[]{:S(2)}) collective-permute-start(bf16[96,1792]{1,0:T(8,128)(2,1)S(1)} %add_convert_fusion.6), channel_id=1, source_target_pairs={{0,2},{2,4},{4,6},{6,7},{7,5},{5,3},{3,1},{1,0},{8,10},{10,12},{12... | collective-permute-start | bytes 1032200 | tf_op jit(solution)/shard_map/ppermute | solution.py:127
  120.1 9.7 %copy-start.5 = (bf16[1,512,2048]{2,1,0:T(8,128)(2,1)S(1)}, bf16[1,512,2048]{2,1,0:T(8,128)(2,1)}, u32[]{:S(2)}) copy-start(bf16[1,512,2048]{2,1,0:T(8,128)(2,1)} %param.15) | copy-start | bytes 6291460
  127.6 1.3 copy-start.3
  129.7 6.9 %collective-permute-start.14 = (bf16[2,32,4096]{2,1,0:T(8,128)(2,1)}, bf16[2,32,4096]{2,1,0:T(8,128)(2,1)}, u32[]{:S(2)}, u32[]{:S(2)}) collective-permute-start(bf16[2,32,4096]{2,1,0:T(8,128)(2,1)} %fusion.8), channel_id=1, source_target_pairs={{0,8},{8,0},{16,24},{24,16},{1,9},{9,1},{17,25},{25,17},{2,10},{10... | collective-permute-start | bytes 1572872 | tf_op jit(solution)/shard_map/ppermute | solution.py:45
  136.1 3.0 %collective-permute-start.16 = (bf16[2,512,512]{2,1,0:T(8,128)(2,1)}, bf16[2,512,512]{2,1,0:T(8,128)(2,1)S(1)}, u32[]{:S(2)}, u32[]{:S(2)}) collective-permute-start(bf16[2,512,512]{2,1,0:T(8,128)(2,1)} %dynamic-slice_bitcast_fusion), channel_id=1, source_target_pairs={{0,8},{8,0},{16,24},{24,16},{1,9},{9,1},{17,25},{25,17},{2,10},{10... | collective-permute-start | bytes 3145736 | tf_op jit(solution)/shard_map/ppermute | solution.py:45
  138.1 9.2 %collective-permute-start.15 = (bf16[32,4096]{1,0:T(8,128)(2,1)S(1)}, bf16[32,4096]{1,0:T(8,128)(2,1)S(1)}, u32[]{:S(2)}, u32[]{:S(2)}) collective-permute-start(bf16[32,4096]{1,0:T(8,128)(2,1)S(1)} %fusion.12), channel_id=1, source_target_pairs={{0,16},{8,24},{16,0},{24,8},{1,17},{9,25},{17,1},{25,9},{2,18},{10... | collective-permute-start | bytes 786440 | tf_op jit(solution)/shard_map/ppermute | solution.py:45
  139.4 1.3 copy-start.4
  140.8 16.8 %collective-permute-start.17 = (bf16[512,512]{1,0:T(8,128)(2,1)S(1)}, bf16[512,512]{1,0:T(8,128)(2,1)S(1)}, u32[]{:S(2)}, u32[]{:S(2)}) collective-permute-start(bf16[512,512]{1,0:T(8,128)(2,1)S(1)} %fusion.9), channel_id=1, source_target_pairs={{0,16},{8,24},{16,0},{24,8},{1,17},{9,25},{17,1},{25,9},{2,18},{10... | collective-permute-start | bytes 1572872 | tf_op jit(solution)/shard_map/ppermute | solution.py:45
  148.2 14.0 %all-to-all-start.2 = ((bf16[8,4,4096]{2,1,0:T(4,128)(2,1)}), bf16[8,4,4096]{2,1,0:T(4,128)(2,1)S(1)}, u32[]{:S(2)}, u32[]{:S(2)}) async-start(bf16[8,4,4096]{2,1,0:T(4,128)(2,1)} %reshape.279), calls=%async_computation.2 | async-start | bytes 524288 | tf_op jit(solution)/shard_map/all_to_all | solution.py:144

commit v3 on v1

v3 whole, which is shorter than its diff:
```python
import functools

import jax
import jax.numpy as jnp
import numpy as np
from jax import lax
from jax.experimental import pallas as pl
from jax.experimental.pallas import tpu as pltpu
from jax.sharding import PartitionSpec as P

F32 = jnp.float32
BF16 = jnp.bfloat16
LANES = 128
VMEM_LIMIT = 40 * 1024 * 1024


def ring_order(devices):
    places = [getattr(d, "coords", None) for d in devices]
    count = len(places)
    if any(p is None for p in places):
        return list(range(count))
    at = {(p[2], p[0]): i for i, p in enumerate(places)}
    zs, xs = sorted({k[0] for k in at}), sorted({k[1] for k in at})
    if len(at) != count or len(zs) * len(xs) != count or len(xs) < 2 or len(zs) % 2:
        return list(range(count))
    order = [at[(z, xs[0])] for z in zs]
    for i, z in enumerate(reversed(zs)):
        line = xs[1:] if i % 2 == 0 else list(reversed(xs[1:]))
        order += [at[(z, x)] for x in line]
    return order


def core_count(devices):
    places = [getattr(d, "coords", None) for d in devices]
    if any(p is None for p in places):
        return 1
    same = [tuple(p) == tuple(places[0]) for p in places]
    cores = sum(same)
    return cores if all(same[:cores]) and len(places) % cores == 0 else 1


def turned(index, step, count):
    return lax.rem(index + step, jnp.int32(count))


def place_rows(tokens, routes, mixing, experts, capacity, shards):
    token_count, width = tokens.shape
    depth = width // shards
    padded = -(-capacity // 8) * 8

    def kernel(tokens_ref, routes_ref, mixing_ref, out_ref):
        ids = [routes_ref[p % 2, p // 2] for p in range(2 * token_count)]
        slots = []
        for p in range(2 * token_count):
            slot = jnp.int32(0)
            for q in range(p):
                slot = slot + jnp.where(ids[q] == ids[p], 1, 0)
            slots.append(slot)
        row = lax.broadcasted_iota(jnp.int32, (padded, LANES), 0)
        lane = lax.broadcasted_iota(jnp.int32, (padded, LANES), 1)
        values = tokens_ref[...].astype(F32)
        tails = []
        for p in range(2 * token_count):
            weight = jnp.full((padded, LANES), mixing_ref[p % 2, p // 2], F32)
            high = weight.astype(BF16).astype(F32)
            number = jnp.full((padded, LANES), float(p // 2 + 1), F32)
            tail = jnp.where(lane == 1, high, jnp.where(lane == 2, weight - high, 0.0))
            tails.append(jnp.where(lane == 0, number, tail))
        for e in range(experts):
            tail = jnp.zeros((padded, LANES), F32)
            body = jnp.zeros((padded, width), F32)
            for p in range(2 * token_count):
                slot = jnp.where(ids[p] == e, slots[p], -1)
                tail = jnp.where(row == slot, tails[p], tail)
                here = lax.broadcasted_iota(jnp.int32, (padded, width), 0) == slot
                t = p // 2
                body = jnp.where(here, jnp.broadcast_to(values[t : t + 1], (padded, width)), body)
            body, tail = body.astype(BF16)[:capacity], tail.astype(BF16)[:capacity]
            for s in range(shards):
                at = s * (depth + LANES)
                out_ref[e, :, at : at + depth] = body[:, s * depth : (s + 1) * depth]
                out_ref[e, :, at + depth : at + depth + LANES] = tail

    return pl.pallas_call(
        kernel,
        out_shape=jax.ShapeDtypeStruct((experts, capacity, shards * (depth + LANES)), BF16),
        in_specs=[
            pl.BlockSpec(memory_space=pltpu.VMEM),
            pl.BlockSpec(memory_space=pltpu.SMEM),
            pl.BlockSpec(memory_space=pltpu.SMEM),
        ],
        out_specs=pl.BlockSpec(memory_space=pltpu.VMEM),
        name="place_rows",
    )(tokens, routes.T, mixing.T)


def column_pieces(where, table, rows, gate_weight, up_weight, pieces, first, cuts, kind):
    count, depth = rows.shape
    shards = len(table) and int(np.sqrt(len(table) // 2))
    width = gate_weight.shape[2] // shards
    block = width // cuts
    chunk = block if block <= 256 else next(c for c in (256, 128) if block % c == 0)

    def kernel(where_ref, table_ref, rows_ref, gate_ref, up_ref, gate_out, up_out):
        held = rows_ref[...]
        for at in range(0, block, chunk):
            for ref, out in ((gate_ref, gate_out), (up_ref, up_out)):
                value = jnp.dot(held, ref[0, :, at : at + chunk], preferred_element_type=F32)
                out[0, :, at : at + chunk] = value.astype(kind)

    def weight_map(side):
        def index(i, j, where_ref, table_ref):
            return 0, 0, table_ref[(where_ref[1] * 2 + side) * shards + first + i] * cuts + j

        return index

    out = jax.ShapeDtypeStruct((pieces, count, width), kind)
    return pl.pallas_call(
        kernel,
        out_shape=(out, out),
        grid_spec=pltpu.PrefetchScalarGridSpec(
            num_scalar_prefetch=2,
            grid=(pieces, cuts),
            in_specs=[
                pl.BlockSpec((count, depth), lambda i, j, *_: (0, 0)),
                pl.BlockSpec((1, depth, block), weight_map(0)),
                pl.BlockSpec((1, depth, block), weight_map(1)),
            ],
            out_specs=[pl.BlockSpec((1, count, block), lambda i, j, *_: (i, 0, j))] * 2,
        ),
        compiler_params=pltpu.CompilerParams(vmem_limit_bytes=VMEM_LIMIT),
        cost_estimate=pl.CostEstimate(
            flops=4 * pieces * count * depth * width,
            bytes_accessed=4 * pieces * depth * width,
            transcendentals=0,
        ),
        name="column_pieces",
    )(where, jnp.asarray(table, jnp.int32), rows, gate_weight, up_weight)


def plain_pieces(here, table, rows, gate_weight, up_weight, shards):
    width = gate_weight.shape[2] // shards
    both = []
    for side, weight in enumerate((gate_weight, up_weight)):
        value = jnp.dot(rows, weight[0], preferred_element_type=F32)
        at = jnp.asarray(table, jnp.int32).reshape(shards, 2, shards)[here, side] * width
        both.append([lax.dynamic_slice_in_dim(value, at[t], width, 1) for t in range(shards)])
    return both


def turn_columns(where, x, cores, chips):
    rows, total = x.shape[1:]
    block = total // (cores * chips)

    def index(i, where_ref):
        b = where_ref[0]
        chip = turned(lax.div(b, jnp.int32(cores)), lax.rem(i, jnp.int32(chips)), chips)
        core = turned(lax.rem(b, jnp.int32(cores)), lax.div(i, jnp.int32(chips)), cores)
        return 0, 0, chip * cores + core

    def kernel(where_ref, in_ref, out_ref):
        out_ref[...] = in_ref[...]

    return pl.pallas_call(
        kernel,
        out_shape=jax.ShapeDtypeStruct((cores * chips, rows, block), x.dtype),
        grid_spec=pltpu.PrefetchScalarGridSpec(
            num_scalar_prefetch=1,
            grid=(cores * chips,),
            in_specs=[pl.BlockSpec((1, rows, block), index)],
            out_specs=pl.BlockSpec((1, rows, block), lambda i, *_: (i, 0, 0)),
        ),
        cost_estimate=pl.CostEstimate(flops=0, bytes_accessed=4 * rows * total, transcendentals=0),
        name="turn_columns",
    )(where, x)


def expert_outputs(where, gate_in, up_in, gate_own, up_own, tails, down_weight, sizes):
    experts, shards, cores, token_count, capacity = sizes
    chips = experts // cores
    count, slice_width = gate_in.shape
    width = down_weight.shape[2]
    total = experts * shards * token_count
    kept = total // cores
    block = 512 if width % 512 == 0 else width
    cell = np.arange(count)
    origin = np.zeros((count, LANES), np.float32)
    branch = cell % (experts * capacity) // capacity
    origin[:, 0] = branch // cores
    origin[:, 1] = branch % cores
    origin[:, 2] = cell // (experts * capacity) * token_count
    chunk = next(c for c in (256, 128, slice_width) if slice_width % c == 0)

    def kernel(where_ref, gate_ref, up_ref, gate_own_ref, up_own_ref, tail_ref, origin_ref, down_ref, *rest):
        hidden_ref = rest[-1]

        @pl.when(pl.program_id(0) == 0)
        def _():
            b = where_ref[0]
            tail = tail_ref[...].astype(F32)
            place = origin_ref[...]
            number, weight = tail[:, 0:1], tail[:, 1:2] + tail[:, 2:3]
            chip = place[:, 0:1] - lax.div(b, jnp.int32(cores)).astype(F32)
            core = place[:, 1:2] - lax.rem(b, jnp.int32(cores)).astype(F32)
            chip = jnp.where(chip < 0, chip + chips, chip)
            core = jnp.where(core < 0, core + cores, core)
            target = (core * chips + chip) * (shards * token_count) + place[:, 2:3] + number - 1.0
            target = jnp.where(number > 0, target, -1.0).astype(jnp.int32)
            spread = target == lax.broadcasted_iota(jnp.int32, (count, total), 1)
            spread = spread.astype(F32).astype(BF16)
            for at in range(0, slice_width, chunk):
                cut = slice(at, at + chunk)
                gate = gate_ref[:, cut].astype(F32) + gate_own_ref[:, cut]
                upper = up_ref[:, cut].astype(F32) + up_own_ref[:, cut]
                hidden = (gate / (1.0 + jnp.exp(-gate)) * upper * weight).astype(BF16)
                hidden_ref[:, cut] = lax.dot_general(
                    spread, hidden, (((0,), (0,)), ((), ())), preferred_element_type=F32
                ).astype(BF16)

        value = jnp.dot(hidden_ref[...], down_ref[0], preferred_element_type=F32)
        rest[0][...] = value[:kept]
        if cores > 1:
            rest[1][...] = value[kept:].astype(BF16)

    whole = pl.BlockSpec((count, slice_width), lambda j, *_: (0, 0))
    lanes = pl.BlockSpec((count, LANES), lambda j, *_: (0, 0))
    shapes = [jax.ShapeDtypeStruct((kept, width), F32)]
    specs = [pl.BlockSpec((kept, block), lambda j, *_: (0, j))]
    if cores > 1:
        shapes.append(jax.ShapeDtypeStruct((total - kept, width), BF16))
        specs.append(pl.BlockSpec((total - kept, block), lambda j, *_: (0, j)))
    return pl.pallas_call(
        kernel,
        out_shape=shapes,
        grid_spec=pltpu.PrefetchScalarGridSpec(
            num_scalar_prefetch=1,
            grid=(width // block,),
            in_specs=[
                whole, whole, whole, whole, lanes, lanes,
                pl.BlockSpec((1, slice_width, block), lambda j, *_: (0, 0, j)),
            ],
            out_specs=specs,
            scratch_shapes=[pltpu.VMEM((total, slice_width), BF16)],
        ),
        compiler_params=pltpu.CompilerParams(vmem_limit_bytes=VMEM_LIMIT),
        cost_estimate=pl.CostEstimate(
            flops=2 * total * slice_width * width,
            bytes_accessed=2 * slice_width * width,
            transcendentals=count * slice_width,
        ),
        name="expert_outputs",
    )(where, gate_in, up_in, gate_own, up_own, tails, jnp.asarray(origin), down_weight)


def core_target(size, cores, k):
    return [(i, i // cores * cores + (i + k) % cores) for i in range(size)]


def chip_target(size, cores, k):
    return [(i, (i + k * cores) % size) for i in range(size)]


def local(order, cores, tokens, routes, mixing, gate_weight, up_weight, down_weight, key_value):
    experts = lax.axis_size("branch")
    shards = lax.axis_size("shard")
    chips = experts // cores
    token_count, width = tokens.shape
    capacity = max(2, (2 * token_count + experts - 1) // experts + 1)
    depth = gate_weight.shape[1]
    slice_width = down_weight.shape[1]
    count = experts * shards * capacity
    where = jnp.stack([lax.axis_index("branch"), lax.axis_index("shard")]).astype(jnp.int32)

    place = np.argsort(np.asarray(order))
    table = np.zeros((shards, 2, shards), np.int32)
    for s in range(shards):
        for t in range(shards):
            table[s, 0, t] = order[(place[s] - 1 - t) % shards]
            table[s, 1, t] = order[(place[s] + 1 + t) % shards]
    table = table.reshape(-1)
    forth = [(order[i], order[(i + 1) % shards]) for i in range(shards)]
    back = [(b, a) for a, b in forth]

    cells = place_rows(tokens, routes, mixing, experts, capacity, shards)
    cells = lax.all_to_all(cells, "branch", split_axis=0, concat_axis=0, tiled=True)
    cells = cells.reshape(experts * capacity, shards, depth + LANES).swapaxes(0, 1)
    cells = lax.all_to_all(cells, "shard", split_axis=0, concat_axis=0, tiled=True)
    cells = cells.reshape(count, depth + LANES)
    rows, tails = cells[:, :depth], cells[:, depth:]

    kv = turn_columns(where, key_value, cores, chips)
    kv_rows, kv_block = kv.shape[1:]
    kv = kv.reshape(cores, chips, kv_rows, kv_block)

    if slice_width % LANES == 0:
        cuts = 2 if slice_width % (2 * LANES) == 0 else 1
        one = column_pieces(where, table, rows, gate_weight, up_weight, 1, 0, cuts, BF16)
        gate_sum, up_sum = one[0][0], one[1][0]
        gates, ups = column_pieces(
            where, table, rows, gate_weight, up_weight, shards - 1, 1, 1, F32
        )
    else:
        gates, ups = plain_pieces(where[1], table, rows, gate_weight, up_weight, shards)
        gate_sum, up_sum = gates.pop(0).astype(BF16), ups.pop(0).astype(BF16)

    kv_core = [
        lax.ppermute(kv[k], "branch", core_target(experts, cores, k)) for k in range(1, cores)
    ]
    kv_sum = None
    for t in range(1, shards):
        gate_in = lax.ppermute(gate_sum, "shard", forth)
        up_in = lax.ppermute(up_sum, "shard", back)
        if t == min(2, shards - 1):
            gate_in, kv_core = lax.optimization_barrier((gate_in, kv_core))
            kv_sum = kv[0].astype(F32) + sum(x.astype(F32) for x in kv_core)
            kv_chip = [
                lax.ppermute(kv_sum[k].astype(BF16), "branch", chip_target(experts, cores, k))
                for k in range(1, chips)
            ]
        if t == min(5, shards - 1):
            gate_in, kv_chip = lax.optimization_barrier((gate_in, kv_chip))
            kv_sum = kv_sum[0] + sum(x.astype(F32) for x in kv_chip)
            merged_kv = (kv_sum / experts).astype(BF16)
        if t < shards - 1:
            gate_sum = (gate_in.astype(F32) + gates[t - 1]).astype(BF16)
            up_sum = (up_in.astype(F32) + ups[t - 1]).astype(BF16)

    sizes = (experts, shards, cores, token_count, capacity)
    outputs = expert_outputs(
        where, gate_in, up_in, gates[shards - 2], ups[shards - 2], tails, down_weight, sizes
    )
    total = outputs[0].reshape(chips, shards * token_count, width)
    for k in range(1, cores):
        sent = outputs[1].reshape(cores - 1, chips, shards * token_count, width)[k - 1]
        total = total + lax.ppermute(sent, "branch", core_target(experts, cores, k)).astype(F32)
    mixed = total[0]
    for k in range(1, chips):
        sent = total[k].astype(BF16)
        mixed = mixed + lax.ppermute(sent, "branch", chip_target(experts, cores, k)).astype(F32)
    mixed = mixed.astype(BF16).reshape(shards, token_count, width)
    mixed = lax.all_to_all(mixed, "shard", split_axis=0, concat_axis=0, tiled=True)
    mixed_out = jnp.sum(mixed.astype(F32), axis=0).astype(BF16)
    return mixed_out, merged_kv


def solution(mesh):
    grid = mesh.devices
    order = ring_order(list(grid[0, :]))
    cores = core_count(list(grid[:, 0]))
    return jax.shard_map(
        functools.partial(local, order, cores),
        mesh=mesh,
        in_specs=(
            P(("branch", "shard"), None),
            P(("branch", "shard"), None),
            P(("branch", "shard"), None),
            P("branch", "shard", None),
            P("branch", "shard", None),
            P("branch", "shard", None),
            P("branch", "shard", None),
        ),
        out_specs=(P(("branch", "shard"), None), P("shard", "branch")),
        check_vma=False,
    )
```

time: 210 us -> 139 us (0.66)
  waiting for transfers between devices: 110 us -> 64.5 us
  blocking collectives: 44.3 us -> 9.22 us
  Pallas kernels: 0 us -> 31.3 us
  matrix products: 19 us -> 0 us
  starting transfers between devices: 7.35 us -> 25.6 us
  between operations: 14.9 us -> 0.87 us
  local copies, waits for them, and re-layouts: 7.58 us -> 3.8 us
  other arithmetic: 6.35 us -> 2.98 us
    reduce_scatter x2 -> x0, waiting for transfers between devices: 104 us -> none  [the longest x1 104 us: local(): lax.psum_scatter(both, 'shard', scatter_dimension=1, tiled=True)]
    ppermute x0 -> x18, waiting for transfers between devices: none -> 49.3 us  [the longest x7 38.2 us: local(): up_in = lax.ppermute(up_sum, 'shard', back)]
    pallas_call x0 -> x5, Pallas kernels: none -> 31.3 us  [the longest x2 15.3 us: column_pieces(): pl.pallas_call(kernel, out_shape=(out, out), grid_spec=pltpu.PrefetchScal...]
    unnamed x1 -> x0, blocking collectives: 29.5 us -> none
    dot_general x5 -> x0, matrix products: 19 us -> none  [the longest x1 7.76 us: local(): jnp.dot(rows, up_weight[0], preferred_element_type=jnp.float32)]
    ppermute x0 -> x18, starting transfers between devices: none -> 15.9 us  [the longest x7 7.76 us: local(): gate_in = lax.ppermute(gate_sum, 'shard', forth)]
    all_to_all x1 -> x2, waiting for transfers between devices: 2.65 us -> 15.1 us  [the longest x1 7.64 us: local(): lax.all_to_all(mixed, 'shard', split_axis=0, concat_axis=0, tiled=True)]
    all_to_all x1 -> x2, starting transfers between devices: 3.32 us -> 9.74 us  [the longest x1 6.33 us: local(): lax.all_to_all(cells, 'shard', split_axis=0, concat_axis=0, tiled=True)]
  transfers between devices with their start and end apart: 5 -> 20, of which waited for: 3 -> 12; matrix products, arithmetic and copies ran while one was open for 21% -> 3% of each run, Pallas kernels for 0% -> 12%
where the time goes in v3:
time: 139 us; the launch traced here: 138 us
  waiting for transfers between devices  64.5 us (46%)
  Pallas kernels  31.3 us (23%)
  starting transfers between devices  25.6 us (18%)
  blocking collectives  9.22 us (7%)
  local copies, waits for them, and re-layouts  3.8 us (3%)
  other arithmetic  2.98 us (2%)
    ppermute x7, waiting for transfers between devices, local(): up_in = lax.ppermute(up_sum, 'shard', back)  38.2 us
    pallas_call x2, Pallas kernels, column_pieces(): pl.pallas_call(kernel, out_shape=(out, out), grid_spec=pltpu.PrefetchScal...  15.3 us
    pallas_call x1, Pallas kernels, expert_outputs(): pl.pallas_call(kernel, out_shape=shapes, grid_spec=pltpu.PrefetchScalarGr...  9.84 us
    all_to_all x1, blocking collectives, local(): lax.all_to_all(cells, 'branch', split_axis=0, concat_axis=0, tiled=True)  9.22 us
    ppermute x1, waiting for transfers between devices, local(): lax.ppermute(sent, 'branch', chip_target(experts, cores, k)).astype(F32)  7.99 us
    ppermute x7, starting transfers between devices, local(): gate_in = lax.ppermute(gate_sum, 'shard', forth)  7.76 us
    all_to_all x1, waiting for transfers between devices, local(): lax.all_to_all(mixed, 'shard', split_axis=0, concat_axis=0, tiled=True)  7.64 us
    all_to_all x1, waiting for transfers between devices, local(): lax.all_to_all(cells, 'shard', split_axis=0, concat_axis=0, tiled=True)  7.5 us
  transfers between devices with their start and end apart: 20, of which 12 were waited for; matrix products, arithmetic and copies ran while one was open for 3% of the time, Pallas kernels for 12%

profile of v3, /device:TPU:0, one launch (start us, length us, event | category | flops | bytes accessed | tf_op | source)
XLA Modules:
  0.0 138.3 jit_solution(12973914479041345890)
XLA Ops:
  0.6 1.7 %place_rows.1 = bf16[4,3,5120]{2,1,0:T(4,128)(2,1)} custom-call(bf16[4,4096]{1,0:T(4,128)(2,1)} %tokens_ref.1, s32[2,4]{1,0:T(2,128)} %bitcast.84, f32[2,4]{1,0:T(2,128)} %bitcast.85), custom_call_target="tpu_custom_call" | custom-call | tf_op jit(solution)/shard_map/place_rows/pallas_call | solution.py:84
  2.4 9.2 %all_to_all.15 = bf16[4,3,5120]{2,1,0:T(4,128)(2,1)S(1)} all-to-all(bf16[4,3,5120]{2,1,0:T(4,128)(2,1)} %place_rows.1), channel_id=1, replica_groups=mesh['branch'=4,'shard'=8] {'branch'}, dimensions={0} | all-to-all | bytes 245760 | tf_op jit(solution)/shard_map/all_to_all | solution.py:285
  11.6 0.1 reshape.23
  11.7 0.7 copy.14
  12.4 6.3 %all-to-all-start.1 = ((bf16[8,12,640]{2,1,0:T(8,128)(2,1)}), bf16[8,12,640]{2,1,0:T(8,128)(2,1)S(1)}, u32[]{:S(2)}, u32[]{:S(2)}) async-start(bf16[8,12,640]{2,1,0:T(8,128)(2,1)} %copy.14), calls=%async_computation.1 | async-start | bytes 327680 | tf_op jit(solution)/shard_map/all_to_all | solution.py:287
  18.8 7.5 %all-to-all-done.1 = bf16[8,12,640]{2,1,0:T(8,128)(2,1)S(1)} async-done(((bf16[8,12,640]{2,1,0:T(8,128)(2,1)}), bf16[8,12,640]{2,1,0:T(8,128)(2,1)S(1)}, u32[]{:S(2)}, u32[]{:S(2)}) %all-to-all-start.1) | async-done | bytes 122912 | tf_op jit(solution)/shard_map/all_to_all | solution.py:287
  26.4 0.6 copy-done.3
  27.0 3.2 %column_pieces.2 = (bf16[1,96,1792]{2,1,0:T(8,128)(2,1)S(1)}, bf16[1,96,1792]{2,1,0:T(8,128)(2,1)S(1)}) custom-call(s32[2]{0:T(128)S(1)} %pad_add_fusion.where_ref, s32[128]{0:T(128)S(1)} %copy-done.3, bf16[96,512]{1,0:T(8,128)(2,1)S(1)} %slice.92.rows_ref, bf16[1,512,14336]{2,1,0:T(8,128)(2,1)} %gate_ref.3, bf16[1,512,14336]{2,1,0:T(8,128)(2,1)} %up_ref.3), custom_call_target="tpu_custom_call" | custom-call | flops 352321536 | bytes 3670016 | tf_op jit(solution)/shard_map/column_pieces/pallas_call | solution.py:118
  30.3 1.0 collective-permute-start.9
  31.3 4.5 %turn_columns.1 = bf16[4,512,512]{2,1,0:T(8,128)(2,1)} custom-call(s32[2]{0:T(128)} %copy-done.1, bf16[1,512,2048]{2,1,0:T(8,128)(2,1)} %in_ref.1), custom_call_target="tpu_custom_call" | custom-call | bytes 4194304 | tf_op jit(solution)/shard_map/turn_columns/pallas_call | solution.py:164
  35.8 1.3 slice.93
  37.2 1.1 collective-permute-start
  38.3 12.0 %column_pieces.3 = (f32[7,96,1792]{2,1,0:T(8,128)S(1)}, f32[7,96,1792]{2,1,0:T(8,128)S(1)}) custom-call(s32[2]{0:T(128)S(1)} %copy-done.2, s32[128]{0:T(128)S(1)} %copy-done.4, bf16[96,512]{1,0:T(8,128)(2,1)S(1)} %slice.92.rows_ref, bf16[1,512,14336]{2,1,0:T(8,128)(2,1)} %gate_ref.3, bf16[1,512,14336]{2,1,0:T(8,128)(2,1)} %up_ref.3), custom_call_target="tpu_custom_call" | custom-call | flops 2466250752 | bytes 25690112 | tf_op jit(solution)/shard_map/column_pieces/pallas_call | solution.py:118
  50.3 0.1 fusion.8
  50.4 1.0 collective-permute-start.10
  51.5 1.1 collective-permute-start.1
  52.6 8.0 %collective-permute-done.10 = bf16[96,1792]{1,0:T(8,128)(2,1)S(1)} collective-permute-done((bf16[96,1792]{1,0:T(8,128)(2,1)S(1)}, bf16[96,1792]{1,0:T(8,128)(2,1)S(1)}, u32[]{:S(2)}, u32[]{:S(2)}) %collective-permute-start.10) | collective-permute-done | bytes 344096 | tf_op jit(solution)/shard_map/ppermute | solution.py:312
  60.7 1.0 collective-permute-start.11
  61.7 0.1 fusion.13
  61.8 0.3 convert_add_fusion
  62.1 1.1 collective-permute-start.3
  63.3 0.4 collective-permute-start.6
  63.7 6.3 %collective-permute-done.11 = bf16[96,1792]{1,0:T(8,128)(2,1)S(1)} collective-permute-done((bf16[96,1792]{1,0:T(8,128)(2,1)S(1)}, bf16[96,1792]{1,0:T(8,128)(2,1)S(1)}, u32[]{:S(2)}, u32[]{:S(2)}) %collective-permute-start.11) | collective-permute-done | bytes 344096 | tf_op jit(solution)/shard_map/ppermute | solution.py:312
  70.1 1.0 collective-permute-start.12
  71.1 0.1 collective-permute-done.3
  71.2 1.1 collective-permute-start.4
  72.4 6.1 %collective-permute-done.12 = bf16[96,1792]{1,0:T(8,128)(2,1)S(1)} collective-permute-done((bf16[96,1792]{1,0:T(8,128)(2,1)S(1)}, bf16[96,1792]{1,0:T(8,128)(2,1)S(1)}, u32[]{:S(2)}, u32[]{:S(2)}) %collective-permute-start.12) | collective-permute-done | bytes 344096 | tf_op jit(solution)/shard_map/ppermute | solution.py:312
  78.6 1.0 collective-permute-start.13
  79.7 1.1 collective-permute-start.5
  80.8 6.0 %collective-permute-done.13 = bf16[96,1792]{1,0:T(8,128)(2,1)S(1)} collective-permute-done((bf16[96,1792]{1,0:T(8,128)(2,1)S(1)}, bf16[96,1792]{1,0:T(8,128)(2,1)S(1)}, u32[]{:S(2)}, u32[]{:S(2)}) %collective-permute-start.13) | collective-permute-done | bytes 344096 | tf_op jit(solution)/shard_map/ppermute | solution.py:312
  86.8 1.0 collective-permute-start.14
  87.9 1.1 collective-permute-start.7
  89.0 6.8 %collective-permute-done.14 = bf16[96,1792]{1,0:T(8,128)(2,1)S(1)} collective-permute-done((bf16[96,1792]{1,0:T(8,128)(2,1)S(1)}, bf16[96,1792]{1,0:T(8,128)(2,1)S(1)}, u32[]{:S(2)}, u32[]{:S(2)}) %collective-permute-start.14) | collective-permute-done | bytes 344096 | tf_op jit(solution)/shard_map/ppermute | solution.py:312
  95.9 1.0 collective-permute-start.15
  97.0 1.1 collective-permute-start.8
  98.1 0.1 slice_bitcast_fusion.1
  98.2 5.0 %collective-permute-done.15.up_ref = bf16[96,1792]{1,0:T(8,128)(2,1)S(1)} collective-permute-done((bf16[96,1792]{1,0:T(8,128)(2,1)S(1)}, bf16[96,1792]{1,0:T(8,128)(2,1)S(1)}, u32[]{:S(2)}, u32[]{:S(2)}) %collective-permute-start.15) | collective-permute-done | bytes 344096 | tf_op jit(solution)/shard_map/ppermute | solution.py:312
  103.2 1.1 collective-permute-done.8.gate_ref
  104.3 9.8 %expert_outputs.1 = (f32[64,4096]{1,0:T(8,128)S(1)}, bf16[64,4096]{1,0:T(8,128)(2,1)S(1)}) custom-call(s32[2]{0:T(128)S(1)} %copy-done.2, bf16[96,1792]{1,0:T(8,128)(2,1)S(1)} %collective-permute-done.8.gate_ref, bf16[96,1792]{1,0:T(8,128)(2,1)S(1)} %collective-permute-done.15.up_ref, f32[96,1792]{1,0:T(8,128)S(1)} %get-tuple-element.23.gate_own_ref, ...), custom_call_target="tpu_custom_call" | custom-call | flops 1879048192 | bytes 14680064 | tf_op jit(solution)/shard_map/expert_outputs/pallas_call | solution.py:232
  114.2 1.9 %collective-permute-done.16 = bf16[2,32,4096]{2,1,0:T(8,128)(2,1)S(1)} collective-permute-done((bf16[2,32,4096]{2,1,0:T(8,128)(2,1)S(1)}, bf16[2,32,4096]{2,1,0:T(8,128)(2,1)S(1)}, u32[]{:S(2)}, u32[]{:S(2)}) %collective-permute-start.16) | collective-permute-done | bytes 524320 | tf_op jit(solution)/shard_map/ppermute | solution.py:335
  116.1 0.1 convert_add_fusion.1
  116.2 0.4 collective-permute-start.17
  116.7 8.0 %collective-permute-done.17 = bf16[32,4096]{1,0:T(8,128)(2,1)S(1)} collective-permute-done((bf16[32,4096]{1,0:T(8,128)(2,1)S(1)}, bf16[32,4096]{1,0:T(8,128)(2,1)S(1)}, u32[]{:S(2)}, u32[]{:S(2)}) %collective-permute-start.17) | collective-permute-done | bytes 262176 | tf_op jit(solution)/shard_map/ppermute | solution.py:339
  124.7 0.8 reshape.26
  125.5 3.4 %all-to-all-start.2 = ((bf16[8,4,4096]{2,1,0:T(4,128)(2,1)}), bf16[8,4,4096]{2,1,0:T(4,128)(2,1)S(1)}, u32[]{:S(2)}, u32[]{:S(2)}) async-start(bf16[8,4,4096]{2,1,0:T(4,128)(2,1)} %reshape.26), calls=%async_computation.2 | async-start | bytes 524288 | tf_op jit(solution)/shard_map/all_to_all | solution.py:341
  128.9 1.0 fusion.2
  129.9 7.6 %all-to-all-done.2 = bf16[8,4,4096]{2,1,0:T(4,128)(2,1)S(1)} async-done(((bf16[8,4,4096]{2,1,0:T(4,128)(2,1)}), bf16[8,4,4096]{2,1,0:T(4,128)(2,1)S(1)}, u32[]{:S(2)}, u32[]{:S(2)}) %all-to-all-start.2) | async-done | bytes 262176 | tf_op jit(solution)/shard_map/all_to_all | solution.py:341
  137.5 0.7 reduce_sum.12
  (38 shorter events, 1.0 us)
Async XLA Ops:
  12.4 13.9 %all-to-all-start.1 = ((bf16[8,12,640]{2,1,0:T(8,128)(2,1)}), bf16[8,12,640]{2,1,0:T(8,128)(2,1)S(1)}, u32[]{:S(2)}, u32[]{:S(2)}) async-start(bf16[8,12,640]{2,1,0:T(8,128)(2,1)} %copy.14), calls=%async_computation.1 | async-start | bytes 327680 | tf_op jit(solution)/shard_map/all_to_all | solution.py:287
  18.8 11.4 %copy-start.1 = (s32[2]{0:T(128)}, s32[2]{0:T(128)S(1)}, u32[]{:S(2)}) copy-start(s32[2]{0:T(128)S(1)} %pad_add_fusion.where_ref) | copy-start | bytes 28
  26.4 0.7 copy-start.3
  30.2 8.0 %copy-start.4 = (s32[128]{0:T(128)S(1)}, s32[128]{0:T(128)}, u32[]{:S(2)}) copy-start(s32[128]{0:T(128)} %constant.18.clone.table_ref) | copy-start | bytes 1540
  30.3 8.0 %copy-start.2 = (s32[2]{0:T(128)S(1)}, s32[2]{0:T(128)}, u32[]{:S(2)}) copy-start(s32[2]{0:T(128)} %copy-done.1) | copy-start | bytes 28
  30.3 20.1 %collective-permute-start.9 = (bf16[96,1792]{1,0:T(8,128)(2,1)S(1)}, bf16[96,1792]{1,0:T(8,128)(2,1)S(1)}, u32[]{:S(2)}, u32[]{:S(2)}) collective-permute-start(bf16[96,1792]{1,0:T(8,128)(2,1)S(1)} %bitcast.82), channel_id=1, source_target_pairs={{2,0},{4,2},{6,4},{7,6},{5,7},{3,5},{1,3},{0,1},{10,8},{12,10},{14... | collective-permute-start | bytes 1032200 | tf_op jit(solution)/shard_map/ppermute | solution.py:312
  37.1 24.6 %collective-permute-start.2 = (bf16[2,512,512]{2,1,0:T(8,128)(2,1)S(1)}, bf16[2,512,512]{2,1,0:T(8,128)(2,1)S(1)}, u32[]{:S(2)}, u32[]{:S(2)}) collective-permute-start(bf16[2,512,512]{2,1,0:T(8,128)(2,1)S(1)} %slice.93), channel_id=1, source_target_pairs={{0,8},{8,0},{16,24},{24,16},{1,9},{9,1},{17,25},{25,17},{2,10},{10... | collective-permute-start | bytes 3145736 | tf_op jit(solution)/shard_map/ppermute | solution.py:307
  37.2 14.3 %collective-permute-start = (bf16[96,1792]{1,0:T(8,128)(2,1)S(1)}, bf16[96,1792]{1,0:T(8,128)(2,1)S(1)}, u32[]{:S(2)}, u32[]{:S(2)}) collective-permute-start(bf16[96,1792]{1,0:T(8,128)(2,1)S(1)} %bitcast.81), channel_id=1, source_target_pairs={{0,2},{2,4},{4,6},{6,7},{7,5},{5,3},{3,1},{1,0},{8,10},{10,12},{12... | collective-permute-start | bytes 1032200 | tf_op jit(solution)/shard_map/ppermute | solution.py:311
  50.3 11.5 %copy-start.5 = (bf16[4,512,512]{2,1,0:T(8,128)(2,1)S(1)}, bf16[4,512,512]{2,1,0:T(8,128)(2,1)}, u32[]{:S(2)}) copy-start(bf16[4,512,512]{2,1,0:T(8,128)(2,1)} %turn_columns.1) | copy-start | bytes 6291460
  50.4 10.2 %collective-permute-start.10 = (bf16[96,1792]{1,0:T(8,128)(2,1)S(1)}, bf16[96,1792]{1,0:T(8,128)(2,1)S(1)}, u32[]{:S(2)}, u32[]{:S(2)}) collective-permute-start(bf16[96,1792]{1,0:T(8,128)(2,1)S(1)} %fusion.8), channel_id=1, source_target_pairs={{2,0},{4,2},{6,4},{7,6},{5,7},{3,5},{1,3},{0,1},{10,8},{12,10},{14... | collective-permute-start | bytes 1032200 | tf_op jit(solution)/shard_map/ppermute | solution.py:312
  51.5 10.2 %collective-permute-start.1 = (bf16[96,1792]{1,0:T(8,128)(2,1)S(1)}, bf16[96,1792]{1,0:T(8,128)(2,1)S(1)}, u32[]{:S(2)}, u32[]{:S(2)}) collective-permute-start(bf16[96,1792]{1,0:T(8,128)(2,1)S(1)} %fusion.14), channel_id=1, source_target_pairs={{0,2},{2,4},{4,6},{6,7},{7,5},{5,3},{3,1},{1,0},{8,10},{10,12},{12... | collective-permute-start | bytes 1032200 | tf_op jit(solution)/shard_map/ppermute | solution.py:311
  60.7 9.3 %collective-permute-start.11 = (bf16[96,1792]{1,0:T(8,128)(2,1)S(1)}, bf16[96,1792]{1,0:T(8,128)(2,1)S(1)}, u32[]{:S(2)}, u32[]{:S(2)}) collective-permute-start(bf16[96,1792]{1,0:T(8,128)(2,1)S(1)} %fusion.7), channel_id=1, source_target_pairs={{2,0},{4,2},{6,4},{7,6},{5,7},{3,5},{1,3},{0,1},{10,8},{12,10},{14... | collective-permute-start | bytes 1032200 | tf_op jit(solution)/shard_map/ppermute | solution.py:312
  62.1 9.1 %collective-permute-start.3 = (bf16[96,1792]{1,0:T(8,128)(2,1)S(1)}, bf16[96,1792]{1,0:T(8,128)(2,1)S(1)}, u32[]{:S(2)}, u32[]{:S(2)}) collective-permute-start(bf16[96,1792]{1,0:T(8,128)(2,1)S(1)} %fusion.13), channel_id=1, source_target_pairs={{0,2},{2,4},{4,6},{6,7},{7,5},{5,3},{3,1},{1,0},{8,10},{10,12},{12... | collective-permute-start | bytes 1032200 | tf_op jit(solution)/shard_map/ppermute | solution.py:311
  63.3 24.5 %collective-permute-start.6 = (bf16[512,512]{1,0:T(8,128)(2,1)S(1)}, bf16[512,512]{1,0:T(8,128)(2,1)S(1)}, u32[]{:S(2)}, u32[]{:S(2)}) collective-permute-start(bf16[512,512]{1,0:T(8,128)(2,1)S(1)} %fusion.15), channel_id=1, source_target_pairs={{0,16},{8,24},{16,0},{24,8},{1,17},{9,25},{17,1},{25,9},{2,18},{10... | collective-permute-start | bytes 1572872 | tf_op jit(solution)/shard_map/ppermute | solution.py:317
  70.1 8.4 %collective-permute-start.12 = (bf16[96,1792]{1,0:T(8,128)(2,1)S(1)}, bf16[96,1792]{1,0:T(8,128)(2,1)S(1)}, u32[]{:S(2)}, u32[]{:S(2)}) collective-permute-start(bf16[96,1792]{1,0:T(8,128)(2,1)S(1)} %fusion.6), channel_id=1, source_target_pairs={{2,0},{4,2},{6,4},{7,6},{5,7},{3,5},{1,3},{0,1},{10,8},{12,10},{14... | collective-permute-start | bytes 1032200 | tf_op jit(solution)/shard_map/ppermute | solution.py:312
  71.2 8.3 %collective-permute-start.4 = (bf16[96,1792]{1,0:T(8,128)(2,1)S(1)}, bf16[96,1792]{1,0:T(8,128)(2,1)S(1)}, u32[]{:S(2)}, u32[]{:S(2)}) collective-permute-start(bf16[96,1792]{1,0:T(8,128)(2,1)S(1)} %fusion.12), channel_id=1, source_target_pairs={{0,2},{2,4},{4,6},{6,7},{7,5},{5,3},{3,1},{1,0},{8,10},{10,12},{12... | collective-permute-start | bytes 1032200 | tf_op jit(solution)/shard_map/ppermute | solution.py:311
  78.6 25.7 %copy-start = (f32[96,128]{1,0:T(8,128)S(1)}, f32[96,128]{1,0:T(8,128)}, u32[]{:S(2)}) copy-start(f32[96,128]{1,0:T(8,128)} %constant.19.clone.origin_ref) | copy-start | bytes 147460
  78.6 8.2 %collective-permute-start.13 = (bf16[96,1792]{1,0:T(8,128)(2,1)S(1)}, bf16[96,1792]{1,0:T(8,128)(2,1)S(1)}, u32[]{:S(2)}, u32[]{:S(2)}) collective-permute-start(bf16[96,1792]{1,0:T(8,128)(2,1)S(1)} %fusion.5), channel_id=1, source_target_pairs={{2,0},{4,2},{6,4},{7,6},{5,7},{3,5},{1,3},{0,1},{10,8},{12,10},{14... | collective-permute-start | bytes 1032200 | tf_op jit(solution)/shard_map/ppermute | solution.py:312
  79.7 8.2 %collective-permute-start.5 = (bf16[96,1792]{1,0:T(8,128)(2,1)S(1)}, bf16[96,1792]{1,0:T(8,128)(2,1)S(1)}, u32[]{:S(2)}, u32[]{:S(2)}) collective-permute-start(bf16[96,1792]{1,0:T(8,128)(2,1)S(1)} %fusion.11), channel_id=1, source_target_pairs={{0,2},{2,4},{4,6},{6,7},{7,5},{5,3},{3,1},{1,0},{8,10},{10,12},{12... | collective-permute-start | bytes 1032200 | tf_op jit(solution)/shard_map/ppermute | solution.py:311
  86.8 9.0 %collective-permute-start.14 = (bf16[96,1792]{1,0:T(8,128)(2,1)S(1)}, bf16[96,1792]{1,0:T(8,128)(2,1)S(1)}, u32[]{:S(2)}, u32[]{:S(2)}) collective-permute-start(bf16[96,1792]{1,0:T(8,128)(2,1)S(1)} %fusion.4), channel_id=1, source_target_pairs={{2,0},{4,2},{6,4},{7,6},{5,7},{3,5},{1,3},{0,1},{10,8},{12,10},{14... | collective-permute-start | bytes 1032200 | tf_op jit(solution)/shard_map/ppermute | solution.py:312
  87.9 9.0 %collective-permute-start.7 = (bf16[96,1792]{1,0:T(8,128)(2,1)S(1)}, bf16[96,1792]{1,0:T(8,128)(2,1)S(1)}, u32[]{:S(2)}, u32[]{:S(2)}) collective-permute-start(bf16[96,1792]{1,0:T(8,128)(2,1)S(1)} %fusion.10), channel_id=1, source_target_pairs={{0,2},{2,4},{4,6},{6,7},{7,5},{5,3},{3,1},{1,0},{8,10},{10,12},{12... | collective-permute-start | bytes 1032200 | tf_op jit(solution)/shard_map/ppermute | solution.py:311
  95.9 7.3 %collective-permute-start.15 = (bf16[96,1792]{1,0:T(8,128)(2,1)S(1)}, bf16[96,1792]{1,0:T(8,128)(2,1)S(1)}, u32[]{:S(2)}, u32[]{:S(2)}) collective-permute-start(bf16[96,1792]{1,0:T(8,128)(2,1)S(1)} %fusion.3), channel_id=1, source_target_pairs={{2,0},{4,2},{6,4},{7,6},{5,7},{3,5},{1,3},{0,1},{10,8},{12,10},{14... | collective-permute-start | bytes 1032200 | tf_op jit(solution)/shard_map/ppermute | solution.py:312
  97.0 7.3 %collective-permute-start.8 = (bf16[96,1792]{1,0:T(8,128)(2,1)S(1)}, bf16[96,1792]{1,0:T(8,128)(2,1)S(1)}, u32[]{:S(2)}, u32[]{:S(2)}) collective-permute-start(bf16[96,1792]{1,0:T(8,128)(2,1)S(1)} %fusion.9), channel_id=1, source_target_pairs={{0,2},{2,4},{4,6},{6,7},{7,5},{5,3},{3,1},{1,0},{8,10},{10,12},{12... | collective-permute-start | bytes 1032200 | tf_op jit(solution)/shard_map/ppermute | solution.py:311
  114.1 2.0 %collective-permute-start.16 = (bf16[2,32,4096]{2,1,0:T(8,128)(2,1)S(1)}, bf16[2,32,4096]{2,1,0:T(8,128)(2,1)S(1)}, u32[]{:S(2)}, u32[]{:S(2)}) collective-permute-start(bf16[2,32,4096]{2,1,0:T(8,128)(2,1)S(1)} %bitcast.80), channel_id=1, source_target_pairs={{0,8},{8,0},{16,24},{24,16},{1,9},{9,1},{17,25},{25,17},{2,10},{10... | collective-permute-start | bytes 1572872 | tf_op jit(solution)/shard_map/ppermute | solution.py:335
  116.2 8.4 %collective-permute-start.17 = (bf16[32,4096]{1,0:T(8,128)(2,1)S(1)}, bf16[32,4096]{1,0:T(8,128)(2,1)S(1)}, u32[]{:S(2)}, u32[]{:S(2)}) collective-permute-start(bf16[32,4096]{1,0:T(8,128)(2,1)S(1)} %fusion.18), channel_id=1, source_target_pairs={{0,16},{8,24},{16,0},{24,8},{1,17},{9,25},{17,1},{25,9},{2,18},{10... | collective-permute-start | bytes 786440 | tf_op jit(solution)/shard_map/ppermute | solution.py:339
  125.5 12.0 %all-to-all-start.2 = ((bf16[8,4,4096]{2,1,0:T(4,128)(2,1)}), bf16[8,4,4096]{2,1,0:T(4,128)(2,1)S(1)}, u32[]{:S(2)}, u32[]{:S(2)}) async-start(bf16[8,4,4096]{2,1,0:T(4,128)(2,1)} %reshape.26), calls=%async_computation.2 | async-start | bytes 524288 | tf_op jit(solution)/shard_map/all_to_all | solution.py:341

commit v4 on v3

v4 whole, which is shorter than its diff:
```python
import functools

import jax
import jax.numpy as jnp
import numpy as np
from jax import lax
from jax.experimental import pallas as pl
from jax.experimental.pallas import tpu as pltpu
from jax.sharding import PartitionSpec as P

F32 = jnp.float32
BF16 = jnp.bfloat16
LANES = 128
VMEM_LIMIT = 40 * 1024 * 1024


def ring_order(devices):
    places = [getattr(d, "coords", None) for d in devices]
    count = len(places)
    if any(p is None for p in places):
        return list(range(count))
    at = {(p[2], p[0]): i for i, p in enumerate(places)}
    zs, xs = sorted({k[0] for k in at}), sorted({k[1] for k in at})
    if len(at) != count or len(zs) * len(xs) != count or len(xs) < 2 or len(zs) % 2:
        return list(range(count))
    order = [at[(z, xs[0])] for z in zs]
    for i, z in enumerate(reversed(zs)):
        line = xs[1:] if i % 2 == 0 else list(reversed(xs[1:]))
        order += [at[(z, x)] for x in line]
    return order


def core_count(devices):
    places = [getattr(d, "coords", None) for d in devices]
    if any(p is None for p in places):
        return 1
    same = [tuple(p) == tuple(places[0]) for p in places]
    cores = sum(same)
    return cores if all(same[:cores]) and len(places) % cores == 0 else 1


def turned(index, step, count):
    return lax.rem(index + step, jnp.int32(count))


def place_rows(where, tokens, routes, mixing, experts, cores, capacity, shards):
    token_count, width = tokens.shape
    depth = width // shards
    chips = experts // cores
    padded = -(-capacity // 8) * 8

    def kernel(where_ref, tokens_ref, routes_ref, mixing_ref, *outs):
        b, s = where_ref[0], where_ref[1]
        chip, core = lax.div(b, jnp.int32(cores)), lax.rem(b, jnp.int32(cores))
        ids = [routes_ref[p % 2, p // 2] for p in range(2 * token_count)]
        slots = []
        for p in range(2 * token_count):
            slot = jnp.int32(0)
            for q in range(p):
                slot = slot + jnp.where(ids[q] == ids[p], 1, 0)
            slots.append(slot)
        row = lax.broadcasted_iota(jnp.int32, (padded, LANES), 0)
        lane = lax.broadcasted_iota(jnp.int32, (padded, LANES), 1)
        wide_row = lax.broadcasted_iota(jnp.int32, (padded, depth), 0)
        tails = []
        for p in range(2 * token_count):
            weight = jnp.full((padded, LANES), mixing_ref[p % 2, p // 2], F32)
            high = weight.astype(BF16).astype(F32)
            number = jnp.full((padded, LANES), float(p // 2 + 1), F32)
            tail = jnp.where(lane == 1, high, jnp.where(lane == 2, weight - high, 0.0))
            tails.append(jnp.where(lane == 0, number, tail))
        held = []
        for j in range(experts):
            e = turned(chip, j % chips, chips) * cores + turned(core, j // chips, cores)
            held.append([jnp.where(ids[p] == e, slots[p], -1) for p in range(2 * token_count)])
        for k in range(shards):
            first = pl.multiple_of(turned(s, k, shards) * depth, LANES)
            values = tokens_ref[:, pl.ds(first, depth)].astype(F32)
            at = k * (depth + LANES)
            for j in range(experts):
                body = jnp.zeros((padded, depth), F32)
                for p in range(2 * token_count):
                    value = jnp.broadcast_to(values[p // 2 : p // 2 + 1], (padded, depth))
                    body = jnp.where(wide_row == held[j][p], value, body)
                outs[j][:, at : at + depth] = body.astype(BF16)[:capacity]
        for j in range(experts):
            tail = jnp.zeros((padded, LANES), F32)
            for p in range(2 * token_count):
                tail = jnp.where(row == held[j][p], tails[p], tail)
            tail = tail.astype(BF16)[:capacity]
            for k in range(shards):
                at = k * (depth + LANES) + depth
                outs[j][:, at : at + LANES] = tail

    out = jax.ShapeDtypeStruct((capacity, shards * (depth + LANES)), BF16)
    return pl.pallas_call(
        kernel,
        out_shape=[out] * experts,
        in_specs=[
            pl.BlockSpec(memory_space=pltpu.SMEM),
            pl.BlockSpec(memory_space=pltpu.VMEM),
            pl.BlockSpec(memory_space=pltpu.SMEM),
            pl.BlockSpec(memory_space=pltpu.SMEM),
        ],
        out_specs=[pl.BlockSpec(memory_space=pltpu.VMEM)] * experts,
        name="place_rows",
    )(where, tokens, routes.T, mixing.T)


def gather_rows(where, blocks, depth):
    shards = len(blocks)
    group = blocks[0].shape[0]
    count = shards * group

    def kernel(where_ref, *refs):
        total = None
        row = lax.broadcasted_iota(jnp.int32, (count, group), 0)
        column = lax.broadcasted_iota(jnp.int32, (count, group), 1)
        for k in range(shards):
            at = turned(where_ref[1], shards - k, shards) * group
            moved = (row == column + at).astype(F32).astype(BF16)
            value = jnp.dot(moved, refs[k][...], preferred_element_type=F32)
            total = value if total is None else total + value
        total = total.astype(BF16)
        refs[shards][...] = total[:, :depth]
        refs[shards + 1][...] = total[:, depth:]

    return pl.pallas_call(
        kernel,
        out_shape=[
            jax.ShapeDtypeStruct((count, depth), BF16),
            jax.ShapeDtypeStruct((count, LANES), BF16),
        ],
        in_specs=[pl.BlockSpec(memory_space=pltpu.SMEM)]
        + [pl.BlockSpec(memory_space=pltpu.VMEM)] * shards,
        out_specs=[pl.BlockSpec(memory_space=pltpu.VMEM)] * 2,
        name="gather_rows",
    )(where, *blocks)


def column_pieces(where, table, rows, gate_weight, up_weight, shards, first, pieces, cuts, halves):
    count, depth = rows.shape
    width = gate_weight.shape[2] // shards
    block = width // cuts
    chunk = block if block <= 256 else next(c for c in (256, LANES) if block % c == 0)
    part = count // max(halves, 1)

    def kernel(where_ref, table_ref, rows_ref, gate_ref, up_ref, *outs):
        held = rows_ref[...]
        for at in range(0, block, chunk):
            for side, ref in enumerate((gate_ref, up_ref)):
                value = jnp.dot(held, ref[0, :, at : at + chunk], preferred_element_type=F32)
                value = value.astype(BF16)
                if not halves:
                    outs[side][0, :, at : at + chunk] = value
                for h in range(halves):
                    outs[side * halves + h][:, at : at + chunk] = value[h * part : (h + 1) * part]

    def weight_map(side):
        def index(i, j, where_ref, table_ref):
            return 0, 0, table_ref[(where_ref[1] * 2 + side) * shards + first + i] * cuts + j

        return index

    if halves:
        out_shape = [jax.ShapeDtypeStruct((part, width), BF16)] * (2 * halves)
        out_spec = pl.BlockSpec((part, block), lambda i, j, *_: (0, j))
    else:
        out_shape = [jax.ShapeDtypeStruct((pieces, count, width), BF16)] * 2
        out_spec = pl.BlockSpec((1, count, block), lambda i, j, *_: (i, 0, j))
    return pl.pallas_call(
        kernel,
        out_shape=out_shape,
        grid_spec=pltpu.PrefetchScalarGridSpec(
            num_scalar_prefetch=2,
            grid=(pieces, cuts),
            in_specs=[
                pl.BlockSpec((count, depth), lambda i, j, *_: (0, 0)),
                pl.BlockSpec((1, depth, block), weight_map(0)),
                pl.BlockSpec((1, depth, block), weight_map(1)),
            ],
            out_specs=[out_spec] * len(out_shape),
        ),
        compiler_params=pltpu.CompilerParams(vmem_limit_bytes=VMEM_LIMIT),
        cost_estimate=pl.CostEstimate(
            flops=4 * pieces * count * depth * width,
            bytes_accessed=4 * pieces * depth * width,
            transcendentals=0,
        ),
        name="column_pieces",
    )(where, table, rows, gate_weight, up_weight)


def plain_pieces(where, table, rows, gate_weight, up_weight, shards):
    width = gate_weight.shape[2] // shards
    both = []
    for side, weight in enumerate((gate_weight, up_weight)):
        value = jnp.dot(rows, weight[0], preferred_element_type=F32).astype(BF16)
        at = table.reshape(shards, 2, shards)[where[1], side] * width
        both.append([lax.dynamic_slice_in_dim(value, at[t], width, 1) for t in range(shards)])
    return both


def turn_columns(where, x, cores, chips):
    rows, total = x.shape[1:]
    block = total // (cores * chips)

    def index(k):
        def place(i, where_ref):
            b = where_ref[0]
            chip = turned(lax.div(b, jnp.int32(cores)), i, chips)
            return 0, 0, chip * cores + turned(lax.rem(b, jnp.int32(cores)), k, cores)

        return place

    def kernel(where_ref, *refs):
        for k in range(cores):
            refs[cores + k][...] = refs[k][...]

    return pl.pallas_call(
        kernel,
        out_shape=[jax.ShapeDtypeStruct((chips, rows, block), x.dtype)] * cores,
        grid_spec=pltpu.PrefetchScalarGridSpec(
            num_scalar_prefetch=1,
            grid=(chips,),
            in_specs=[pl.BlockSpec((1, rows, block), index(k)) for k in range(cores)],
            out_specs=[pl.BlockSpec((1, rows, block), lambda i, *_: (i, 0, 0))] * cores,
        ),
        cost_estimate=pl.CostEstimate(flops=0, bytes_accessed=4 * rows * total, transcendentals=0),
        name="turn_columns",
    )(where, *([x] * cores))


def hidden_rows(where, gate_in, up_in, gate_own, up_own, tails, base, total, shards, token_count):
    count, slice_width = gate_own.shape
    halves = len(gate_in)
    part = count // halves
    chunk = next(c for c in (256, LANES, slice_width) if slice_width % c == 0)

    def kernel(*refs):
        where_ref, refs = refs[0], refs[1:]
        gates, ups = refs[:halves], refs[halves : 2 * halves]
        gate_own_ref, up_own_ref, tail_ref, base_ref, out_ref = refs[2 * halves :]
        tail = tail_ref[...].astype(F32)
        number, weight = tail[:, 0:1], tail[:, 1:2] + tail[:, 2:3]
        shard = base_ref[...][:, 1:2] - where_ref[1].astype(F32)
        shard = jnp.where(shard < 0, shard + shards, shard)
        target = base_ref[...][:, 0:1] + shard * token_count + number
        target = jnp.where(number > 0, target, -1.0).astype(jnp.int32)
        spread = target == lax.broadcasted_iota(jnp.int32, (count, total), 1)
        spread = spread.astype(F32).astype(BF16)
        for at in range(0, slice_width, chunk):
            cut = slice(at, at + chunk)
            pieces = []
            for h in range(halves):
                line = slice(h * part, (h + 1) * part)
                gate = gates[h][:, cut].astype(F32) + gate_own_ref[line, cut].astype(F32)
                upper = ups[h][:, cut].astype(F32) + up_own_ref[line, cut].astype(F32)
                value = gate / (1.0 + jnp.exp(-gate)) * upper * weight[line]
                pieces.append(value.astype(BF16))
            hidden = jnp.concatenate(pieces, axis=0) if halves > 1 else pieces[0]
            out_ref[:, cut] = lax.dot_general(
                spread, hidden, (((0,), (0,)), ((), ())), preferred_element_type=F32
            ).astype(BF16)

    return pl.pallas_call(
        kernel,
        out_shape=jax.ShapeDtypeStruct((total, slice_width), BF16),
        cost_estimate=pl.CostEstimate(
            flops=2 * total * slice_width * count,
            bytes_accessed=8 * count * slice_width,
            transcendentals=count * slice_width,
        ),
        in_specs=[pl.BlockSpec(memory_space=pltpu.SMEM)]
        + [pl.BlockSpec(memory_space=pltpu.VMEM)] * (2 * halves + 4),
        out_specs=pl.BlockSpec(memory_space=pltpu.VMEM),
        compiler_params=pltpu.CompilerParams(vmem_limit_bytes=VMEM_LIMIT),
        name="hidden_rows",
    )(where, *gate_in, *up_in, gate_own, up_own, tails, base)


def down_half(hidden, down_weight, cores, half, halves):
    total, slice_width = hidden.shape
    width = down_weight.shape[2] // halves
    kept = total // cores
    block = 512 if width % 512 == 0 else width
    steps = width // block

    def kernel(hidden_ref, down_ref, *outs):
        value = jnp.dot(hidden_ref[...], down_ref[0], preferred_element_type=F32)
        outs[0][...] = value[:kept]
        for k in range(1, cores):
            outs[k][...] = value[k * kept : (k + 1) * kept].astype(BF16)

    shapes = [jax.ShapeDtypeStruct((kept, width), F32 if k == 0 else BF16) for k in range(cores)]
    return pl.pallas_call(
        kernel,
        out_shape=shapes,
        grid=(steps,),
        in_specs=[
            pl.BlockSpec((total, slice_width), lambda j: (0, 0)),
            pl.BlockSpec((1, slice_width, block), lambda j: (0, 0, half * steps + j)),
        ],
        out_specs=[pl.BlockSpec((kept, block), lambda j: (0, j))] * cores,
        compiler_params=pltpu.CompilerParams(vmem_limit_bytes=VMEM_LIMIT),
        cost_estimate=pl.CostEstimate(
            flops=2 * total * slice_width * width,
            bytes_accessed=2 * slice_width * width,
            transcendentals=0,
        ),
        name="down_half",
    )(hidden, down_weight)


def branch_target(size, cores, core_step, chip_step):
    chips = size // cores
    return [
        (i, (i // cores + chip_step) % chips * cores + (i + core_step) % cores)
        for i in range(size)
    ]


def shard_target(size, step):
    return [(i, (i + step) % size) for i in range(size)]


def local(order, cores, tokens, routes, mixing, gate_weight, up_weight, down_weight, key_value):
    experts = lax.axis_size("branch")
    shards = lax.axis_size("shard")
    chips = experts // cores
    token_count, width = tokens.shape
    capacity = max(2, (2 * token_count + experts - 1) // experts + 1)
    depth = gate_weight.shape[1]
    slice_width = down_weight.shape[1]
    group = experts * capacity
    count = shards * group
    halves = 2 if count % 32 == 0 and shards <= 8 else 1
    part = count // halves
    where = jnp.stack([lax.axis_index("branch"), lax.axis_index("shard")]).astype(jnp.int32)

    place = np.argsort(np.asarray(order))
    table = np.zeros((shards, 2, shards), np.int32)
    for s in range(shards):
        for t in range(shards):
            table[s, 0, t] = order[(place[s] - 1 - t) % shards]
            table[s, 1, t] = order[(place[s] + 1 + t) % shards]
    table = jnp.asarray(table.reshape(-1))
    forth = [(order[i], order[(i + 1) % shards]) for i in range(shards)]
    back = [(b, a) for a, b in forth]
    base = np.zeros((count, LANES), np.float32)
    for i in range(count):
        j = i % group // capacity
        core, chip = -(j // chips) % cores, -(j % chips) % chips
        base[i, 0] = (core * chips + chip) * shards * token_count - 1
        base[i, 1] = i // group
    base = jnp.asarray(base)

    cells = place_rows(where, tokens, routes, mixing, experts, cores, capacity, shards)
    cells, where, table, base = lax.optimization_barrier((cells, where, table, base))
    blocks = [cells[0]]
    for j in range(1, experts):
        target = branch_target(experts, cores, j // chips, j % chips)
        blocks.append(lax.ppermute(cells[j], "branch", target))
    kv = turn_columns(where, key_value, cores, chips)
    blocks, kv = lax.optimization_barrier((blocks, kv))
    blocks = jnp.concatenate(blocks, axis=0)
    cuts = jnp.split(blocks, shards, axis=1)
    for k in range(1, shards):
        cuts[k] = lax.ppermute(cuts[k], "shard", shard_target(shards, k))
    rows, tails = gather_rows(where, cuts, depth)
    kv_core = [
        lax.ppermute(kv[k], "branch", branch_target(experts, cores, k, 0))
        for k in range(1, cores)
    ]

    if slice_width % LANES == 0:
        cuts = 2 if slice_width % (2 * LANES) == 0 else 1
        one = column_pieces(
            where, table, rows, gate_weight, up_weight, shards, 0, 1, cuts, halves
        )
        gate_sum, up_sum = list(one[:halves]), list(one[halves:])
        gates, ups = column_pieces(
            where, table, rows, gate_weight, up_weight, shards, 1, shards - 1, 1, 0
        )
    else:
        gates, ups = plain_pieces(where, table, rows, gate_weight, up_weight, shards)
        gate_sum, up_sum = jnp.split(gates.pop(0), halves), jnp.split(ups.pop(0), halves)

    def added(arrived, own, h):
        own = own[h * part : (h + 1) * part]
        return (arrived.astype(F32) + own.astype(F32)).astype(BF16)

    for t in range(1, shards):
        for h in range(halves):
            gate_sum[h] = lax.ppermute(gate_sum[h], "shard", forth)
            up_sum[h] = lax.ppermute(up_sum[h], "shard", back)
        if t == min(2, shards - 1):
            gate_sum, kv_core = lax.optimization_barrier((gate_sum, kv_core))
            kv_sum = kv[0].astype(F32) + sum(x.astype(F32) for x in kv_core)
            kv_chip = [
                lax.ppermute(
                    kv_sum[k].astype(BF16), "branch", branch_target(experts, cores, 0, k)
                )
                for k in range(1, chips)
            ]
        if t == min(5, shards - 1):
            gate_sum, kv_chip = lax.optimization_barrier((gate_sum, kv_chip))
            kv_sum = kv_sum[0] + sum(x.astype(F32) for x in kv_chip)
            merged_kv = (kv_sum / experts).astype(BF16)
            gate_sum, merged_kv = lax.optimization_barrier((gate_sum, merged_kv))
        if t < shards - 1:
            for h in range(halves):
                gate_sum[h] = added(gate_sum[h], gates[t - 1], h)
                up_sum[h] = added(up_sum[h], ups[t - 1], h)

    total = experts * shards * token_count
    hidden = hidden_rows(
        where, gate_sum, up_sum, gates[shards - 2], ups[shards - 2], tails, base, total,
        shards, token_count,
    )
    mixed = []
    for half in range(2):
        outputs = down_half(hidden, down_weight, cores, half, 2)
        held = outputs[0].reshape(chips, shards * token_count, width // 2)
        for k in range(1, cores):
            sent = lax.ppermute(outputs[k], "branch", branch_target(experts, cores, k, 0))
            held = held + sent.astype(F32).reshape(held.shape)
        one = held[0]
        for k in range(1, chips):
            sent = lax.ppermute(
                held[k].astype(BF16), "branch", branch_target(experts, cores, 0, k)
            )
            one = one + sent.astype(F32)
        mixed.append(one)
    mixed = jnp.concatenate(mixed, axis=1).reshape(shards, token_count, width)
    mixed_out = mixed[0]
    for k in range(1, shards):
        sent = lax.ppermute(mixed[k].astype(BF16), "shard", shard_target(shards, k))
        mixed_out = mixed_out + sent.astype(F32)
    return mixed_out.astype(BF16), merged_kv


def solution(mesh):
    grid = mesh.devices
    order = ring_order(list(grid[0, :]))
    cores = core_count(list(grid[:, 0]))
    return jax.shard_map(
        functools.partial(local, order, cores),
        mesh=mesh,
        in_specs=(
            P(("branch", "shard"), None),
            P(("branch", "shard"), None),
            P(("branch", "shard"), None),
            P("branch", "shard", None),
            P("branch", "shard", None),
            P("branch", "shard", None),
            P("branch", "shard", None),
        ),
        out_specs=(P(("branch", "shard"), None), P("shard", "branch")),
        check_vma=False,
    )
```

time: 139 us -> 157 us (1.13)
  starting transfers between devices: 25.6 us -> 55.7 us
  blocking collectives: 9.22 us -> 0 us
  waiting for transfers between devices: 64.5 us -> 61.4 us
    ppermute x18 -> x51, starting transfers between devices: 15.9 us -> 55.7 us  [the longest x14 14.6 us: local(): up_sum[h] = lax.ppermute(up_sum[h], 'shard', back)]
    all_to_all x2 -> x0, waiting for transfers between devices: 15.1 us -> none  [the longest x1 7.64 us: local(): lax.all_to_all(mixed, 'shard', split_axis=0, concat_axis=0, tiled=True)]
    ppermute x18 -> x51, waiting for transfers between devices: 49.3 us -> 61.4 us  [the longest x14 34.3 us: local(): gate_sum[h] = lax.ppermute(gate_sum[h], 'shard', forth)]
    all_to_all x2 -> x0, starting transfers between devices: 9.74 us -> none  [the longest x1 6.33 us: local(): lax.all_to_all(cells, 'shard', split_axis=0, concat_axis=0, tiled=True)]
    all_to_all x1 -> x0, blocking collectives: 9.22 us -> none  [local(): lax.all_to_all(cells, 'branch', split_axis=0, concat_axis=0, tiled=True)]
    pallas_call x5 -> x8, Pallas kernels: 31.3 us -> 32.5 us  [the longest x2 15.3 us: column_pieces(): pl.pallas_call(kernel, out_shape=out_shape, grid_spec=pltpu.PrefetchScala...]
  transfers between devices with their start and end apart: 20 -> 51, of which waited for: 12 -> 27; matrix products, arithmetic and copies ran while one was open for 3% -> 2% of each run, Pallas kernels for 12% -> 13%
where the time goes in v4:
time: 157 us
  waiting for transfers between devices  61.4 us (39%)
  starting transfers between devices  55.7 us (35%)
  Pallas kernels  32.5 us (21%)
  other arithmetic  3.97 us (3%)
  local copies, waits for them, and re-layouts  2.34 us (1%)
    ppermute x14, waiting for transfers between devices, local(): gate_sum[h] = lax.ppermute(gate_sum[h], 'shard', forth)  34.3 us
    pallas_call x2, Pallas kernels, column_pieces(): pl.pallas_call(kernel, out_shape=out_shape, grid_spec=pltpu.PrefetchScala...  15.3 us
    ppermute x14, starting transfers between devices, local(): up_sum[h] = lax.ppermute(up_sum[h], 'shard', back)  14.6 us
    ppermute x7, starting transfers between devices, local(): cuts[k] = lax.ppermute(cuts[k], 'shard', shard_target(shards, k))  11.2 us
    ppermute x14, waiting for transfers between devices, local(): up_sum[h] = lax.ppermute(up_sum[h], 'shard', back)  10.8 us
    ppermute x14, starting transfers between devices, local(): gate_sum[h] = lax.ppermute(gate_sum[h], 'shard', forth)  10.6 us
    ppermute x7, starting transfers between devices, local(): sent = lax.ppermute(mixed[k].astype(BF16), 'shard', shard_target(shards, k))  9.73 us
    pallas_call x2, Pallas kernels, down_half(): pl.pallas_call(kernel, out_shape=shapes, grid=(steps,), in_specs=[pl.Bloc...  9.13 us
  transfers between devices with their start and end apart: 51, of which 27 were waited for; matrix products, arithmetic and copies ran while one was open for 2% of the time, Pallas kernels for 13%

profile of v4, /device:TPU:0, one launch (start us, length us, event | category | flops | bytes accessed | tf_op | source)
XLA Modules:
  0.0 156.9 jit_solution(16949658125494644586)
XLA Ops:
  1.3 1.8 %place_rows.1 = (bf16[3,5120]{1,0:T(4,128)(2,1)}, bf16[3,5120]{1,0:T(4,128)(2,1)}, bf16[3,5120]{1,0:T(4,128)(2,1)}, bf16[3,5120]{1,0:T(4,128)(2,1)}) custom-call(s32[2]{0:T(128)} %pad_add_fusion.where_ref.refs_0_, bf16[4,4096]{1,0:T(4,128)(2,1)} %tokens_ref.1, s32[2,4]{1,0:T(2,128)} %bitcast.90, f32[2,4]{1,0:T(2,128)} %bitcast.91), custom_call_target="tpu_custom_call" | custom-call | tf_op jit(solution)/shard_map/place_rows/pallas_call | solution.py:96
  3.1 3.0 %collective-permute-start = (bf16[3,5120]{1,0:T(4,128)(2,1)}, bf16[3,5120]{1,0:T(4,128)(2,1)S(1)}, u32[]{:S(2)}, u32[]{:S(2)}) collective-permute-start(bf16[3,5120]{1,0:T(4,128)(2,1)} %get-tuple-element.49), channel_id=1, source_target_pairs={{0,16},{8,24},{16,0},{24,8},{1,17},{9,25},{17,1},{25,9},{2,18},{10... | collective-permute-start | bytes 92168 | tf_op jit(solution)/shard_map/ppermute | solution.py:363
  6.3 3.3 %turn_columns.1 = (bf16[2,512,512]{2,1,0:T(8,128)(2,1)}, bf16[2,512,512]{2,1,0:T(8,128)(2,1)}) custom-call(s32[2]{0:T(128)} %pad_add_fusion.where_ref.refs_0_, bf16[1,512,2048]{2,1,0:T(8,128)(2,1)} %refs_1_.1, bf16[1,512,2048]{2,1,0:T(8,128)(2,1)} %refs_1_.1), custom_call_target="tpu_custom_call" | custom-call | bytes 4194304 | tf_op jit(solution)/shard_map/turn_columns/pallas_call | solution.py:220
  10.5 4.8 %collective-permute-start.9 = (bf16[12,640]{1,0:T(8,128)(2,1)S(1)}, bf16[12,640]{1,0:T(8,128)(2,1)S(1)}, u32[]{:S(2)}, u32[]{:S(2)}) collective-permute-start(bf16[12,640]{1,0:T(8,128)(2,1)S(1)} %get-tuple-element.113), channel_id=1, source_target_pairs={{0,7},{1,0},{2,1},{3,2},{4,3},{5,4},{6,5},{7,6},{8,15},{9,8},{10,9... | collective-permute-start | bytes 46088 | tf_op jit(solution)/shard_map/ppermute | solution.py:369
  15.7 3.0 %collective-permute-start.6 = (bf16[12,640]{1,0:T(8,128)(2,1)S(1)}, bf16[12,640]{1,0:T(8,128)(2,1)S(1)}, u32[]{:S(2)}, u32[]{:S(2)}) collective-permute-start(bf16[12,640]{1,0:T(8,128)(2,1)S(1)} %get-tuple-element.116), channel_id=1, source_target_pairs={{0,4},{1,5},{2,6},{3,7},{4,0},{5,1},{6,2},{7,3},{8,12},{9,13},{10,... | collective-permute-start | bytes 46088 | tf_op jit(solution)/shard_map/ppermute | solution.py:369
  18.8 1.8 %collective-permute-start.4 = (bf16[12,640]{1,0:T(8,128)(2,1)S(1)}, bf16[12,640]{1,0:T(8,128)(2,1)S(1)}, u32[]{:S(2)}, u32[]{:S(2)}) collective-permute-start(bf16[12,640]{1,0:T(8,128)(2,1)S(1)} %get-tuple-element.118), channel_id=1, source_target_pairs={{0,2},{1,3},{2,4},{3,5},{4,6},{5,7},{6,0},{7,1},{8,10},{9,11},{10,... | collective-permute-start | bytes 46088 | tf_op jit(solution)/shard_map/ppermute | solution.py:369
  21.7 2.6 %collective-permute-done.5.refs_3_ = bf16[12,640]{1,0:T(8,128)(2,1)S(1)} collective-permute-done((bf16[12,640]{1,0:T(8,128)(2,1)S(1)}, bf16[12,640]{1,0:T(8,128)(2,1)S(1)}, u32[]{:S(2)}, u32[]{:S(2)}) %collective-permute-start.5) | collective-permute-done | bytes 15392 | tf_op jit(solution)/shard_map/ppermute | solution.py:369
  25.5 1.6 %collective-permute-done.3.refs_1_ = bf16[12,640]{1,0:T(8,128)(2,1)S(1)} collective-permute-done((bf16[12,640]{1,0:T(8,128)(2,1)S(1)}, bf16[12,640]{1,0:T(8,128)(2,1)S(1)}, u32[]{:S(2)}, u32[]{:S(2)}) %collective-permute-start.3) | collective-permute-done | bytes 15392 | tf_op jit(solution)/shard_map/ppermute | solution.py:369
  27.7 1.9 %gather_rows.1 = (bf16[96,512]{1,0:T(8,128)(2,1)}, bf16[96,128]{1,0:T(8,128)(2,1)}) custom-call(s32[2]{0:T(128)} %pad_add_fusion.where_ref.refs_0_, bf16[12,640]{1,0:T(8,128)(2,1)} %get-tuple-element.120.refs_0_, bf16[12,640]{1,0:T(8,128)(2,1)} %copy-done.13, bf16[12,640]{1,0:T(8,128)(2,1)} %copy-done.12, bf16[12,640]{1,0:T(8,128)(2,1)} %copy-done.11, ...), custom_call_target="tpu_custom_call" | custom-call | tf_op jit(solution)/shard_map/gather_rows/pallas_call | solution.py:128
  30.5 3.2 %column_pieces.2 = (bf16[48,1792]{1,0:T(8,128)(2,1)S(1)}, bf16[48,1792]{1,0:T(8,128)(2,1)S(1)}, bf16[48,1792]{1,0:T(8,128)(2,1)S(1)}, bf16[48,1792]{1,0:T(8,128)(2,1)S(1)}) custom-call(s32[2]{0:T(128)S(1)} %copy-done.3, s32[128]{0:T(128)S(1)} %copy-done.4, bf16[96,512]{1,0:T(8,128)(2,1)S(1)} %copy-done, bf16[1,512,14336]{2,1,0:T(8,128)(2,1)} %gate_ref.3, ...), custom_call_target="tpu_custom_call" | custom-call | flops 352321536 | bytes 3670016 | tf_op jit(solution)/shard_map/column_pieces/pallas_call | solution.py:171
  34.3 12.1 %column_pieces.3 = (bf16[7,96,1792]{2,1,0:T(8,128)(2,1)S(1)}, bf16[7,96,1792]{2,1,0:T(8,128)(2,1)S(1)}) custom-call(s32[2]{0:T(128)S(1)} %copy-done.3, s32[128]{0:T(128)S(1)} %copy-done.4, bf16[96,512]{1,0:T(8,128)(2,1)S(1)} %copy-done, bf16[1,512,14336]{2,1,0:T(8,128)(2,1)} %gate_ref.3, bf16[1,512,14336]{2,1,0:T(8,128)(2,1)} %up_ref.3), custom_call_target="tpu_custom_call" | custom-call | flops 2466250752 | bytes 25690112 | tf_op jit(solution)/shard_map/column_pieces/pallas_call | solution.py:171
  48.0 3.9 %collective-permute-done.34 = bf16[48,1792]{1,0:T(8,128)(2,1)S(1)} collective-permute-done((bf16[48,1792]{1,0:T(8,128)(2,1)S(1)}, bf16[48,1792]{1,0:T(8,128)(2,1)S(1)}, u32[]{:S(2)}, u32[]{:S(2)}) %collective-permute-start.34) | collective-permute-done | bytes 172064 | tf_op jit(solution)/shard_map/ppermute | solution.py:396
  51.9 3.1 %collective-permute-done.27 = bf16[48,1792]{1,0:T(8,128)(2,1)S(1)} collective-permute-done((bf16[48,1792]{1,0:T(8,128)(2,1)S(1)}, bf16[48,1792]{1,0:T(8,128)(2,1)S(1)}, u32[]{:S(2)}, u32[]{:S(2)}) %collective-permute-start.27) | collective-permute-done | bytes 172064 | tf_op jit(solution)/shard_map/ppermute | solution.py:396
  58.0 1.2 collective-permute-start.12
  59.2 1.3 collective-permute-done.35
  60.5 2.2 %collective-permute-done.28 = bf16[48,1792]{1,0:T(8,128)(2,1)S(1)} collective-permute-done((bf16[48,1792]{1,0:T(8,128)(2,1)S(1)}, bf16[48,1792]{1,0:T(8,128)(2,1)S(1)}, u32[]{:S(2)}, u32[]{:S(2)}) %collective-permute-start.28) | collective-permute-done | bytes 172064 | tf_op jit(solution)/shard_map/ppermute | solution.py:396
  63.8 1.3 collective-permute-start.29
  65.1 2.9 %collective-permute-done.12 = bf16[48,1792]{1,0:T(8,128)(2,1)S(1)} collective-permute-done((bf16[48,1792]{1,0:T(8,128)(2,1)S(1)}, bf16[48,1792]{1,0:T(8,128)(2,1)S(1)}, u32[]{:S(2)}, u32[]{:S(2)}) %collective-permute-start.12) | collective-permute-done | bytes 172064 | tf_op jit(solution)/shard_map/ppermute | solution.py:395
  68.6 1.2 collective-permute-start.11
  71.2 1.4 collective-permute-start.30
  72.6 2.8 %collective-permute-done.13 = bf16[48,1792]{1,0:T(8,128)(2,1)S(1)} collective-permute-done((bf16[48,1792]{1,0:T(8,128)(2,1)S(1)}, bf16[48,1792]{1,0:T(8,128)(2,1)S(1)}, u32[]{:S(2)}, u32[]{:S(2)}) %collective-permute-start.13) | collective-permute-done | bytes 172064 | tf_op jit(solution)/shard_map/ppermute | solution.py:395
  75.4 2.6 %collective-permute-done.11 = bf16[48,1792]{1,0:T(8,128)(2,1)S(1)} collective-permute-done((bf16[48,1792]{1,0:T(8,128)(2,1)S(1)}, bf16[48,1792]{1,0:T(8,128)(2,1)S(1)}, u32[]{:S(2)}, u32[]{:S(2)}) %collective-permute-start.11) | collective-permute-done | bytes 172064 | tf_op jit(solution)/shard_map/ppermute | solution.py:395
  78.5 1.2 collective-permute-start.15
  80.0 5.4 %collective-permute-done.18 = bf16[48,1792]{1,0:T(8,128)(2,1)S(1)} collective-permute-done((bf16[48,1792]{1,0:T(8,128)(2,1)S(1)}, bf16[48,1792]{1,0:T(8,128)(2,1)S(1)}, u32[]{:S(2)}, u32[]{:S(2)}) %collective-permute-start.18) | collective-permute-done | bytes 172064 | tf_op jit(solution)/shard_map/ppermute | solution.py:395
  85.4 1.8 %collective-permute-done.15 = bf16[48,1792]{1,0:T(8,128)(2,1)S(1)} collective-permute-done((bf16[48,1792]{1,0:T(8,128)(2,1)S(1)}, bf16[48,1792]{1,0:T(8,128)(2,1)S(1)}, u32[]{:S(2)}, u32[]{:S(2)}) %collective-permute-start.15) | collective-permute-done | bytes 172064 | tf_op jit(solution)/shard_map/ppermute | solution.py:395
  88.6 1.8 %collective-permute-start.21 = (bf16[512,512]{1,0:T(8,128)(2,1)S(1)}, bf16[512,512]{1,0:T(8,128)(2,1)S(1)}, u32[]{:S(2)}, u32[]{:S(2)}) collective-permute-start(bf16[512,512]{1,0:T(8,128)(2,1)S(1)} %fusion.4), channel_id=1, source_target_pairs={{0,16},{8,24},{16,0},{24,8},{1,17},{9,25},{17,1},{25,9},{2,18},{10... | collective-permute-start | bytes 1572872 | tf_op jit(solution)/shard_map/ppermute | solution.py:401
  90.5 3.2 %collective-permute-done.19 = bf16[48,1792]{1,0:T(8,128)(2,1)S(1)} collective-permute-done((bf16[48,1792]{1,0:T(8,128)(2,1)S(1)}, bf16[48,1792]{1,0:T(8,128)(2,1)S(1)}, u32[]{:S(2)}, u32[]{:S(2)}) %collective-permute-start.19) | collective-permute-done | bytes 172064 | tf_op jit(solution)/shard_map/ppermute | solution.py:395
  93.6 1.8 %collective-permute-done.16 = bf16[48,1792]{1,0:T(8,128)(2,1)S(1)} collective-permute-done((bf16[48,1792]{1,0:T(8,128)(2,1)S(1)}, bf16[48,1792]{1,0:T(8,128)(2,1)S(1)}, u32[]{:S(2)}, u32[]{:S(2)}) %collective-permute-start.16) | collective-permute-done | bytes 172064 | tf_op jit(solution)/shard_map/ppermute | solution.py:395
  96.9 1.2 collective-permute-start.38
  98.1 1.7 %collective-permute-start.31 = (bf16[48,1792]{1,0:T(8,128)(2,1)S(1)}, bf16[48,1792]{1,0:T(8,128)(2,1)S(1)}, u32[]{:S(2)}, u32[]{:S(2)}) collective-permute-start(bf16[48,1792]{1,0:T(8,128)(2,1)S(1)} %get-tuple-element.85), channel_id=1, source_target_pairs={{2,0},{4,2},{6,4},{7,6},{5,7},{3,5},{1,3},{0,1},{10,8},{12,10},{14... | collective-permute-start | bytes 516104 | tf_op jit(solution)/shard_map/ppermute | solution.py:396
  99.8 1.2 collective-permute-done.20
  101.0 1.8 %collective-permute-done.17 = bf16[48,1792]{1,0:T(8,128)(2,1)S(1)} collective-permute-done((bf16[48,1792]{1,0:T(8,128)(2,1)S(1)}, bf16[48,1792]{1,0:T(8,128)(2,1)S(1)}, u32[]{:S(2)}, u32[]{:S(2)}) %collective-permute-start.17) | collective-permute-done | bytes 172064 | tf_op jit(solution)/shard_map/ppermute | solution.py:395
  106.4 1.7 %collective-permute-start.32 = (bf16[48,1792]{1,0:T(8,128)(2,1)S(1)}, bf16[48,1792]{1,0:T(8,128)(2,1)S(1)}, u32[]{:S(2)}, u32[]{:S(2)}) collective-permute-start(bf16[48,1792]{1,0:T(8,128)(2,1)S(1)} %get-tuple-element.83), channel_id=1, source_target_pairs={{2,0},{4,2},{6,4},{7,6},{5,7},{3,5},{1,3},{0,1},{10,8},{12,10},{14... | collective-permute-start | bytes 516104 | tf_op jit(solution)/shard_map/ppermute | solution.py:396
  108.2 1.3 collective-permute-done.24
  109.5 3.7 %collective-permute-done.22 = bf16[48,1792]{1,0:T(8,128)(2,1)S(1)} collective-permute-done((bf16[48,1792]{1,0:T(8,128)(2,1)S(1)}, bf16[48,1792]{1,0:T(8,128)(2,1)S(1)}, u32[]{:S(2)}, u32[]{:S(2)}) %collective-permute-start.22) | collective-permute-done | bytes 172064 | tf_op jit(solution)/shard_map/ppermute | solution.py:395
  113.6 1.2 collective-permute-start.23
  114.9 3.9 %collective-permute-done.25.refs_2_ = bf16[48,1792]{1,0:T(8,128)(2,1)S(1)} collective-permute-done((bf16[48,1792]{1,0:T(8,128)(2,1)S(1)}, bf16[48,1792]{1,0:T(8,128)(2,1)S(1)}, u32[]{:S(2)}, u32[]{:S(2)}) %collective-permute-start.25) | collective-permute-done | bytes 172064 | tf_op jit(solution)/shard_map/ppermute | solution.py:395
  118.7 1.8 %collective-permute-done.23.refs_1_ = bf16[48,1792]{1,0:T(8,128)(2,1)S(1)} collective-permute-done((bf16[48,1792]{1,0:T(8,128)(2,1)S(1)}, bf16[48,1792]{1,0:T(8,128)(2,1)S(1)}, u32[]{:S(2)}, u32[]{:S(2)}) %collective-permute-start.23) | collective-permute-done | bytes 172064 | tf_op jit(solution)/shard_map/ppermute | solution.py:395
  121.7 4.6 %down_half.3 = (f32[64,2048]{1,0:T(8,128)S(1)}, bf16[64,2048]{1,0:T(8,128)(2,1)S(1)}) custom-call(bf16[128,1792]{1,0:T(8,128)(2,1)S(1)} %hidden_rows.1.hidden_ref, bf16[1,1792,4096]{2,1,0:T(8,128)(2,1)} %down_ref.3), custom_call_target="tpu_custom_call" | custom-call | flops 939524096 | bytes 7340032 | tf_op jit(solution)/shard_map/down_half/pallas_call | solution.py:296
  126.4 4.6 %down_half.2 = (f32[64,2048]{1,0:T(8,128)S(1)}, bf16[64,2048]{1,0:T(8,128)(2,1)S(1)}) custom-call(bf16[128,1792]{1,0:T(8,128)(2,1)S(1)} %hidden_rows.1.hidden_ref, bf16[1,1792,4096]{2,1,0:T(8,128)(2,1)} %down_ref.3), custom_call_target="tpu_custom_call" | custom-call | flops 939524096 | bytes 7340032 | tf_op jit(solution)/shard_map/down_half/pallas_call | solution.py:296
  131.6 2.7 %collective-permute-start.43 = (bf16[32,2048]{1,0:T(8,128)(2,1)S(1)}, bf16[32,2048]{1,0:T(8,128)(2,1)S(1)}, u32[]{:S(2)}, u32[]{:S(2)}) collective-permute-start(bf16[32,2048]{1,0:T(8,128)(2,1)S(1)} %slice.333), channel_id=1, source_target_pairs={{0,16},{8,24},{16,0},{24,8},{1,17},{9,25},{17,1},{25,9},{2,18},{10... | collective-permute-start | bytes 393224 | tf_op jit(solution)/shard_map/ppermute | solution.py:430
  135.5 3.1 %collective-permute-done.43 = bf16[32,2048]{1,0:T(8,128)(2,1)S(1)} collective-permute-done((bf16[32,2048]{1,0:T(8,128)(2,1)S(1)}, bf16[32,2048]{1,0:T(8,128)(2,1)S(1)}, u32[]{:S(2)}, u32[]{:S(2)}) %collective-permute-start.43) | collective-permute-done | bytes 131104 | tf_op jit(solution)/shard_map/ppermute | solution.py:430
  138.6 2.2 %collective-permute-done.41 = bf16[32,2048]{1,0:T(8,128)(2,1)S(1)} collective-permute-done((bf16[32,2048]{1,0:T(8,128)(2,1)S(1)}, bf16[32,2048]{1,0:T(8,128)(2,1)S(1)}, u32[]{:S(2)}, u32[]{:S(2)}) %collective-permute-start.41) | collective-permute-done | bytes 131104 | tf_op jit(solution)/shard_map/ppermute | solution.py:430
  142.0 3.7 %collective-permute-start.50 = (bf16[4,4096]{1,0:T(4,128)(2,1)S(1)}, bf16[4,4096]{1,0:T(4,128)(2,1)S(1)}, u32[]{:S(2)}, u32[]{:S(2)}) collective-permute-start(bf16[4,4096]{1,0:T(4,128)(2,1)S(1)} %get-tuple-element.107), channel_id=1, source_target_pairs={{0,7},{1,0},{2,1},{3,2},{4,3},{5,4},{6,5},{7,6},{8,15},{9,8},{10,9... | collective-permute-start | bytes 98312 | tf_op jit(solution)/shard_map/ppermute | solution.py:438
  146.4 2.2 %collective-permute-start.47 = (bf16[4,4096]{1,0:T(4,128)(2,1)S(1)}, bf16[4,4096]{1,0:T(4,128)(2,1)S(1)}, u32[]{:S(2)}, u32[]{:S(2)}) collective-permute-start(bf16[4,4096]{1,0:T(4,128)(2,1)S(1)} %get-tuple-element.110), channel_id=1, source_target_pairs={{0,4},{1,5},{2,6},{3,7},{4,0},{5,1},{6,2},{7,3},{8,12},{9,13},{10,... | collective-permute-start | bytes 98312 | tf_op jit(solution)/shard_map/ppermute | solution.py:438
  148.9 1.8 %collective-permute-start.45 = (bf16[4,4096]{1,0:T(4,128)(2,1)S(1)}, bf16[4,4096]{1,0:T(4,128)(2,1)S(1)}, u32[]{:S(2)}, u32[]{:S(2)}) collective-permute-start(bf16[4,4096]{1,0:T(4,128)(2,1)S(1)} %get-tuple-element.112), channel_id=1, source_target_pairs={{0,2},{1,3},{2,4},{3,5},{4,6},{5,7},{6,0},{7,1},{8,10},{9,11},{10,... | collective-permute-start | bytes 98312 | tf_op jit(solution)/shard_map/ppermute | solution.py:438
  151.2 3.1 %collective-permute-done.46 = bf16[4,4096]{1,0:T(4,128)(2,1)S(1)} collective-permute-done((bf16[4,4096]{1,0:T(4,128)(2,1)S(1)}, bf16[4,4096]{1,0:T(4,128)(2,1)S(1)}, u32[]{:S(2)}, u32[]{:S(2)}) %collective-permute-start.46) | collective-permute-done | bytes 32800 | tf_op jit(solution)/shard_map/ppermute | solution.py:438
  154.4 1.8 %collective-permute-done.45 = bf16[4,4096]{1,0:T(4,128)(2,1)S(1)} collective-permute-done((bf16[4,4096]{1,0:T(4,128)(2,1)S(1)}, bf16[4,4096]{1,0:T(4,128)(2,1)S(1)}, u32[]{:S(2)}, u32[]{:S(2)}) %collective-permute-start.45) | collective-permute-done | bytes 32800 | tf_op jit(solution)/shard_map/ppermute | solution.py:438
  (120 shorter events, 28.3 us)
Async XLA Ops:
  3.1 6.5 %collective-permute-start = (bf16[3,5120]{1,0:T(4,128)(2,1)}, bf16[3,5120]{1,0:T(4,128)(2,1)S(1)}, u32[]{:S(2)}, u32[]{:S(2)}) collective-permute-start(bf16[3,5120]{1,0:T(4,128)(2,1)} %get-tuple-element.49), channel_id=1, source_target_pairs={{0,16},{8,24},{16,0},{24,8},{1,17},{9,25},{17,1},{25,9},{2,18},{10... | collective-permute-start | bytes 92168 | tf_op jit(solution)/shard_map/ppermute | solution.py:363
  10.5 8.3 %collective-permute-start.9 = (bf16[12,640]{1,0:T(8,128)(2,1)S(1)}, bf16[12,640]{1,0:T(8,128)(2,1)S(1)}, u32[]{:S(2)}, u32[]{:S(2)}) collective-permute-start(bf16[12,640]{1,0:T(8,128)(2,1)S(1)} %get-tuple-element.113), channel_id=1, source_target_pairs={{0,7},{1,0},{2,1},{3,2},{4,3},{5,4},{6,5},{7,6},{8,15},{9,8},{10,9... | collective-permute-start | bytes 46088 | tf_op jit(solution)/shard_map/ppermute | solution.py:369
  15.3 5.3 %collective-permute-start.8 = (bf16[12,640]{1,0:T(8,128)(2,1)S(1)}, bf16[12,640]{1,0:T(8,128)(2,1)S(1)}, u32[]{:S(2)}, u32[]{:S(2)}) collective-permute-start(bf16[12,640]{1,0:T(8,128)(2,1)S(1)} %get-tuple-element.114), channel_id=1, source_target_pairs={{0,6},{1,7},{2,0},{3,1},{4,2},{5,3},{6,4},{7,5},{8,14},{9,15},{10,... | collective-permute-start | bytes 46088 | tf_op jit(solution)/shard_map/ppermute | solution.py:369
  15.7 6.0 %collective-permute-start.7 = (bf16[12,640]{1,0:T(8,128)(2,1)S(1)}, bf16[12,640]{1,0:T(8,128)(2,1)S(1)}, u32[]{:S(2)}, u32[]{:S(2)}) collective-permute-start(bf16[12,640]{1,0:T(8,128)(2,1)S(1)} %get-tuple-element.115), channel_id=1, source_target_pairs={{0,5},{1,6},{2,7},{3,0},{4,1},{5,2},{6,3},{7,4},{8,13},{9,14},{10,... | collective-permute-start | bytes 46088 | tf_op jit(solution)/shard_map/ppermute | solution.py:369
  15.7 6.0 %collective-permute-start.6 = (bf16[12,640]{1,0:T(8,128)(2,1)S(1)}, bf16[12,640]{1,0:T(8,128)(2,1)S(1)}, u32[]{:S(2)}, u32[]{:S(2)}) collective-permute-start(bf16[12,640]{1,0:T(8,128)(2,1)S(1)} %get-tuple-element.116), channel_id=1, source_target_pairs={{0,4},{1,5},{2,6},{3,7},{4,0},{5,1},{6,2},{7,3},{8,12},{9,13},{10,... | collective-permute-start | bytes 46088 | tf_op jit(solution)/shard_map/ppermute | solution.py:369
  18.8 5.6 %collective-permute-start.5 = (bf16[12,640]{1,0:T(8,128)(2,1)S(1)}, bf16[12,640]{1,0:T(8,128)(2,1)S(1)}, u32[]{:S(2)}, u32[]{:S(2)}) collective-permute-start(bf16[12,640]{1,0:T(8,128)(2,1)S(1)} %get-tuple-element.117), channel_id=1, source_target_pairs={{0,3},{1,4},{2,5},{3,6},{4,7},{5,0},{6,1},{7,2},{8,11},{9,12},{10,... | collective-permute-start | bytes 46088 | tf_op jit(solution)/shard_map/ppermute | solution.py:369
  18.8 6.7 %collective-permute-start.4 = (bf16[12,640]{1,0:T(8,128)(2,1)S(1)}, bf16[12,640]{1,0:T(8,128)(2,1)S(1)}, u32[]{:S(2)}, u32[]{:S(2)}) collective-permute-start(bf16[12,640]{1,0:T(8,128)(2,1)S(1)} %get-tuple-element.118), channel_id=1, source_target_pairs={{0,2},{1,3},{2,4},{3,5},{4,6},{5,7},{6,0},{7,1},{8,10},{9,11},{10,... | collective-permute-start | bytes 46088 | tf_op jit(solution)/shard_map/ppermute | solution.py:369
  20.6 6.5 %collective-permute-start.3 = (bf16[12,640]{1,0:T(8,128)(2,1)S(1)}, bf16[12,640]{1,0:T(8,128)(2,1)S(1)}, u32[]{:S(2)}, u32[]{:S(2)}) collective-permute-start(bf16[12,640]{1,0:T(8,128)(2,1)S(1)} %get-tuple-element.119), channel_id=1, source_target_pairs={{0,1},{1,2},{2,3},{3,4},{4,5},{5,6},{6,7},{7,0},{8,9},{9,10},{10,1... | collective-permute-start | bytes 46088 | tf_op jit(solution)/shard_map/ppermute | solution.py:369
  33.7 12.6 %collective-permute-start.26 = (bf16[48,1792]{1,0:T(8,128)(2,1)S(1)}, bf16[48,1792]{1,0:T(8,128)(2,1)S(1)}, u32[]{:S(2)}, u32[]{:S(2)}) collective-permute-start(bf16[48,1792]{1,0:T(8,128)(2,1)S(1)} %get-tuple-element.72), channel_id=1, source_target_pairs={{2,0},{4,2},{6,4},{7,6},{5,7},{3,5},{1,3},{0,1},{10,8},{12,10},{14... | collective-permute-start | bytes 516104 | tf_op jit(solution)/shard_map/ppermute | solution.py:396
  33.8 12.6 %collective-permute-start.33 = (bf16[48,1792]{1,0:T(8,128)(2,1)S(1)}, bf16[48,1792]{1,0:T(8,128)(2,1)S(1)}, u32[]{:S(2)}, u32[]{:S(2)}) collective-permute-start(bf16[48,1792]{1,0:T(8,128)(2,1)S(1)} %get-tuple-element.74), channel_id=1, source_target_pairs={{2,0},{4,2},{6,4},{7,6},{5,7},{3,5},{1,3},{0,1},{10,8},{12,10},{14... | collective-permute-start | bytes 516104 | tf_op jit(solution)/shard_map/ppermute | solution.py:396
  46.5 5.5 %collective-permute-start.34 = (bf16[48,1792]{1,0:T(8,128)(2,1)S(1)}, bf16[48,1792]{1,0:T(8,128)(2,1)S(1)}, u32[]{:S(2)}, u32[]{:S(2)}) collective-permute-start(bf16[48,1792]{1,0:T(8,128)(2,1)S(1)} %get-tuple-element.92), channel_id=1, source_target_pairs={{2,0},{4,2},{6,4},{7,6},{5,7},{3,5},{1,3},{0,1},{10,8},{12,10},{14... | collective-permute-start | bytes 516104 | tf_op jit(solution)/shard_map/ppermute | solution.py:396
  47.4 7.6 %collective-permute-start.27 = (bf16[48,1792]{1,0:T(8,128)(2,1)S(1)}, bf16[48,1792]{1,0:T(8,128)(2,1)S(1)}, u32[]{:S(2)}, u32[]{:S(2)}) collective-permute-start(bf16[48,1792]{1,0:T(8,128)(2,1)S(1)} %get-tuple-element.93), channel_id=1, source_target_pairs={{2,0},{4,2},{6,4},{7,6},{5,7},{3,5},{1,3},{0,1},{10,8},{12,10},{14... | collective-permute-start | bytes 516104 | tf_op jit(solution)/shard_map/ppermute | solution.py:396
  55.1 5.5 %collective-permute-start.35 = (bf16[48,1792]{1,0:T(8,128)(2,1)S(1)}, bf16[48,1792]{1,0:T(8,128)(2,1)S(1)}, u32[]{:S(2)}, u32[]{:S(2)}) collective-permute-start(bf16[48,1792]{1,0:T(8,128)(2,1)S(1)} %get-tuple-element.90), channel_id=1, source_target_pairs={{2,0},{4,2},{6,4},{7,6},{5,7},{3,5},{1,3},{0,1},{10,8},{12,10},{14... | collective-permute-start | bytes 516104 | tf_op jit(solution)/shard_map/ppermute | solution.py:396
  56.0 6.7 %collective-permute-start.28 = (bf16[48,1792]{1,0:T(8,128)(2,1)S(1)}, bf16[48,1792]{1,0:T(8,128)(2,1)S(1)}, u32[]{:S(2)}, u32[]{:S(2)}) collective-permute-start(bf16[48,1792]{1,0:T(8,128)(2,1)S(1)} %get-tuple-element.91), channel_id=1, source_target_pairs={{2,0},{4,2},{6,4},{7,6},{5,7},{3,5},{1,3},{0,1},{10,8},{12,10},{14... | collective-permute-start | bytes 516104 | tf_op jit(solution)/shard_map/ppermute | solution.py:396
  57.0 21.0 %collective-permute-start.14 = (bf16[2,512,512]{2,1,0:T(8,128)(2,1)S(1)}, bf16[2,512,512]{2,1,0:T(8,128)(2,1)S(1)}, u32[]{:S(2)}, u32[]{:S(2)}) collective-permute-start(bf16[2,512,512]{2,1,0:T(8,128)(2,1)S(1)} %copy-done.14), channel_id=1, source_target_pairs={{0,8},{8,0},{16,24},{24,16},{1,9},{9,1},{17,25},{25,17},{2,10},{10... | collective-permute-start | bytes 3145736 | tf_op jit(solution)/shard_map/ppermute | solution.py:372
  57.1 8.1 %collective-permute-start.10 = (bf16[48,1792]{1,0:T(8,128)(2,1)S(1)}, bf16[48,1792]{1,0:T(8,128)(2,1)S(1)}, u32[]{:S(2)}, u32[]{:S(2)}) collective-permute-start(bf16[48,1792]{1,0:T(8,128)(2,1)S(1)} %get-tuple-element.59), channel_id=1, source_target_pairs={{0,2},{2,4},{4,6},{6,7},{7,5},{5,3},{3,1},{1,0},{8,10},{10,12},{12... | collective-permute-start | bytes 516104 | tf_op jit(solution)/shard_map/ppermute | solution.py:395
  58.0 10.0 %collective-permute-start.12 = (bf16[48,1792]{1,0:T(8,128)(2,1)S(1)}, bf16[48,1792]{1,0:T(8,128)(2,1)S(1)}, u32[]{:S(2)}, u32[]{:S(2)}) collective-permute-start(bf16[48,1792]{1,0:T(8,128)(2,1)S(1)} %get-tuple-element.61), channel_id=1, source_target_pairs={{0,2},{2,4},{4,6},{6,7},{7,5},{5,3},{3,1},{1,0},{8,10},{10,12},{12... | collective-permute-start | bytes 516104 | tf_op jit(solution)/shard_map/ppermute | solution.py:395
  62.8 7.0 %collective-permute-start.36 = (bf16[48,1792]{1,0:T(8,128)(2,1)S(1)}, bf16[48,1792]{1,0:T(8,128)(2,1)S(1)}, u32[]{:S(2)}, u32[]{:S(2)}) collective-permute-start(bf16[48,1792]{1,0:T(8,128)(2,1)S(1)} %get-tuple-element.88), channel_id=1, source_target_pairs={{2,0},{4,2},{6,4},{7,6},{5,7},{3,5},{1,3},{0,1},{10,8},{12,10},{14... | collective-permute-start | bytes 516104 | tf_op jit(solution)/shard_map/ppermute | solution.py:396
  63.8 6.3 %collective-permute-start.29 = (bf16[48,1792]{1,0:T(8,128)(2,1)S(1)}, bf16[48,1792]{1,0:T(8,128)(2,1)S(1)}, u32[]{:S(2)}, u32[]{:S(2)}) collective-permute-start(bf16[48,1792]{1,0:T(8,128)(2,1)S(1)} %get-tuple-element.89), channel_id=1, source_target_pairs={{2,0},{4,2},{6,4},{7,6},{5,7},{3,5},{1,3},{0,1},{10,8},{12,10},{14... | collective-permute-start | bytes 516104 | tf_op jit(solution)/shard_map/ppermute | solution.py:396
  68.1 7.3 %collective-permute-start.13 = (bf16[48,1792]{1,0:T(8,128)(2,1)S(1)}, bf16[48,1792]{1,0:T(8,128)(2,1)S(1)}, u32[]{:S(2)}, u32[]{:S(2)}) collective-permute-start(bf16[48,1792]{1,0:T(8,128)(2,1)S(1)} %get-tuple-element.104), channel_id=1, source_target_pairs={{0,2},{2,4},{4,6},{6,7},{7,5},{5,3},{3,1},{1,0},{8,10},{10,12},{12... | collective-permute-start | bytes 516104 | tf_op jit(solution)/shard_map/ppermute | solution.py:395
  68.6 9.4 %collective-permute-start.11 = (bf16[48,1792]{1,0:T(8,128)(2,1)S(1)}, bf16[48,1792]{1,0:T(8,128)(2,1)S(1)}, u32[]{:S(2)}, u32[]{:S(2)}) collective-permute-start(bf16[48,1792]{1,0:T(8,128)(2,1)S(1)} %get-tuple-element.105), channel_id=1, source_target_pairs={{0,2},{2,4},{4,6},{6,7},{7,5},{5,3},{3,1},{1,0},{8,10},{10,12},{12... | collective-permute-start | bytes 516104 | tf_op jit(solution)/shard_map/ppermute | solution.py:395
  70.2 26.7 %collective-permute-start.37 = (bf16[48,1792]{1,0:T(8,128)(2,1)S(1)}, bf16[48,1792]{1,0:T(8,128)(2,1)S(1)}, u32[]{:S(2)}, u32[]{:S(2)}) collective-permute-start(bf16[48,1792]{1,0:T(8,128)(2,1)S(1)} %get-tuple-element.86), channel_id=1, source_target_pairs={{2,0},{4,2},{6,4},{7,6},{5,7},{3,5},{1,3},{0,1},{10,8},{12,10},{14... | collective-permute-start | bytes 516104 | tf_op jit(solution)/shard_map/ppermute | solution.py:396
  71.2 25.6 %collective-permute-start.30 = (bf16[48,1792]{1,0:T(8,128)(2,1)S(1)}, bf16[48,1792]{1,0:T(8,128)(2,1)S(1)}, u32[]{:S(2)}, u32[]{:S(2)}) collective-permute-start(bf16[48,1792]{1,0:T(8,128)(2,1)S(1)} %get-tuple-element.87), channel_id=1, source_target_pairs={{2,0},{4,2},{6,4},{7,6},{5,7},{3,5},{1,3},{0,1},{10,8},{12,10},{14... | collective-permute-start | bytes 516104 | tf_op jit(solution)/shard_map/ppermute | solution.py:396
  78.1 7.2 %collective-permute-start.18 = (bf16[48,1792]{1,0:T(8,128)(2,1)S(1)}, bf16[48,1792]{1,0:T(8,128)(2,1)S(1)}, u32[]{:S(2)}, u32[]{:S(2)}) collective-permute-start(bf16[48,1792]{1,0:T(8,128)(2,1)S(1)} %get-tuple-element.102), channel_id=1, source_target_pairs={{0,2},{2,4},{4,6},{6,7},{7,5},{5,3},{3,1},{1,0},{8,10},{10,12},{12... | collective-permute-start | bytes 516104 | tf_op jit(solution)/shard_map/ppermute | solution.py:395
  78.5 8.7 %collective-permute-start.15 = (bf16[48,1792]{1,0:T(8,128)(2,1)S(1)}, bf16[48,1792]{1,0:T(8,128)(2,1)S(1)}, u32[]{:S(2)}, u32[]{:S(2)}) collective-permute-start(bf16[48,1792]{1,0:T(8,128)(2,1)S(1)} %get-tuple-element.103), channel_id=1, source_target_pairs={{0,2},{2,4},{4,6},{6,7},{7,5},{5,3},{3,1},{1,0},{8,10},{10,12},{12... | collective-permute-start | bytes 516104 | tf_op jit(solution)/shard_map/ppermute | solution.py:395
  87.3 6.3 %collective-permute-start.19 = (bf16[48,1792]{1,0:T(8,128)(2,1)S(1)}, bf16[48,1792]{1,0:T(8,128)(2,1)S(1)}, u32[]{:S(2)}, u32[]{:S(2)}) collective-permute-start(bf16[48,1792]{1,0:T(8,128)(2,1)S(1)} %get-tuple-element.100), channel_id=1, source_target_pairs={{0,2},{2,4},{4,6},{6,7},{7,5},{5,3},{3,1},{1,0},{8,10},{10,12},{12... | collective-permute-start | bytes 516104 | tf_op jit(solution)/shard_map/ppermute | solution.py:395
  87.6 7.8 %collective-permute-start.16 = (bf16[48,1792]{1,0:T(8,128)(2,1)S(1)}, bf16[48,1792]{1,0:T(8,128)(2,1)S(1)}, u32[]{:S(2)}, u32[]{:S(2)}) collective-permute-start(bf16[48,1792]{1,0:T(8,128)(2,1)S(1)} %get-tuple-element.101), channel_id=1, source_target_pairs={{0,2},{2,4},{4,6},{6,7},{7,5},{5,3},{3,1},{1,0},{8,10},{10,12},{12... | collective-permute-start | bytes 516104 | tf_op jit(solution)/shard_map/ppermute | solution.py:395
  88.6 14.2 %collective-permute-start.21 = (bf16[512,512]{1,0:T(8,128)(2,1)S(1)}, bf16[512,512]{1,0:T(8,128)(2,1)S(1)}, u32[]{:S(2)}, u32[]{:S(2)}) collective-permute-start(bf16[512,512]{1,0:T(8,128)(2,1)S(1)} %fusion.4), channel_id=1, source_target_pairs={{0,16},{8,24},{16,0},{24,8},{1,17},{9,25},{17,1},{25,9},{2,18},{10... | collective-permute-start | bytes 1572872 | tf_op jit(solution)/shard_map/ppermute | solution.py:401
  95.6 5.5 %collective-permute-start.20 = (bf16[48,1792]{1,0:T(8,128)(2,1)S(1)}, bf16[48,1792]{1,0:T(8,128)(2,1)S(1)}, u32[]{:S(2)}, u32[]{:S(2)}) collective-permute-start(bf16[48,1792]{1,0:T(8,128)(2,1)S(1)} %get-tuple-element.98), channel_id=1, source_target_pairs={{0,2},{2,4},{4,6},{6,7},{7,5},{5,3},{3,1},{1,0},{8,10},{10,12},{12... | collective-permute-start | bytes 516104 | tf_op jit(solution)/shard_map/ppermute | solution.py:395
  95.9 7.0 %collective-permute-start.17 = (bf16[48,1792]{1,0:T(8,128)(2,1)S(1)}, bf16[48,1792]{1,0:T(8,128)(2,1)S(1)}, u32[]{:S(2)}, u32[]{:S(2)}) collective-permute-start(bf16[48,1792]{1,0:T(8,128)(2,1)S(1)} %get-tuple-element.99), channel_id=1, source_target_pairs={{0,2},{2,4},{4,6},{6,7},{7,5},{5,3},{3,1},{1,0},{8,10},{10,12},{12... | collective-permute-start | bytes 516104 | tf_op jit(solution)/shard_map/ppermute | solution.py:395
  96.9 8.3 %collective-permute-start.38 = (bf16[48,1792]{1,0:T(8,128)(2,1)S(1)}, bf16[48,1792]{1,0:T(8,128)(2,1)S(1)}, u32[]{:S(2)}, u32[]{:S(2)}) collective-permute-start(bf16[48,1792]{1,0:T(8,128)(2,1)S(1)} %get-tuple-element.84), channel_id=1, source_target_pairs={{2,0},{4,2},{6,4},{7,6},{5,7},{3,5},{1,3},{0,1},{10,8},{12,10},{14... | collective-permute-start | bytes 516104 | tf_op jit(solution)/shard_map/ppermute | solution.py:396
  98.1 7.1 %collective-permute-start.31 = (bf16[48,1792]{1,0:T(8,128)(2,1)S(1)}, bf16[48,1792]{1,0:T(8,128)(2,1)S(1)}, u32[]{:S(2)}, u32[]{:S(2)}) collective-permute-start(bf16[48,1792]{1,0:T(8,128)(2,1)S(1)} %get-tuple-element.85), channel_id=1, source_target_pairs={{2,0},{4,2},{6,4},{7,6},{5,7},{3,5},{1,3},{0,1},{10,8},{12,10},{14... | collective-permute-start | bytes 516104 | tf_op jit(solution)/shard_map/ppermute | solution.py:396
  103.9 5.6 %collective-permute-start.24 = (bf16[48,1792]{1,0:T(8,128)(2,1)S(1)}, bf16[48,1792]{1,0:T(8,128)(2,1)S(1)}, u32[]{:S(2)}, u32[]{:S(2)}) collective-permute-start(bf16[48,1792]{1,0:T(8,128)(2,1)S(1)} %get-tuple-element.96), channel_id=1, source_target_pairs={{0,2},{2,4},{4,6},{6,7},{7,5},{5,3},{3,1},{1,0},{8,10},{10,12},{12... | collective-permute-start | bytes 516104 | tf_op jit(solution)/shard_map/ppermute | solution.py:395
  104.3 8.9 %collective-permute-start.22 = (bf16[48,1792]{1,0:T(8,128)(2,1)S(1)}, bf16[48,1792]{1,0:T(8,128)(2,1)S(1)}, u32[]{:S(2)}, u32[]{:S(2)}) collective-permute-start(bf16[48,1792]{1,0:T(8,128)(2,1)S(1)} %get-tuple-element.97), channel_id=1, source_target_pairs={{0,2},{2,4},{4,6},{6,7},{7,5},{5,3},{3,1},{1,0},{8,10},{10,12},{12... | collective-permute-start | bytes 516104 | tf_op jit(solution)/shard_map/ppermute | solution.py:395
  105.3 9.5 %collective-permute-start.39 = (bf16[48,1792]{1,0:T(8,128)(2,1)S(1)}, bf16[48,1792]{1,0:T(8,128)(2,1)S(1)}, u32[]{:S(2)}, u32[]{:S(2)}) collective-permute-start(bf16[48,1792]{1,0:T(8,128)(2,1)S(1)} %get-tuple-element.82), channel_id=1, source_target_pairs={{2,0},{4,2},{6,4},{7,6},{5,7},{3,5},{1,3},{0,1},{10,8},{12,10},{14... | collective-permute-start | bytes 516104 | tf_op jit(solution)/shard_map/ppermute | solution.py:396
  106.4 8.4 %collective-permute-start.32 = (bf16[48,1792]{1,0:T(8,128)(2,1)S(1)}, bf16[48,1792]{1,0:T(8,128)(2,1)S(1)}, u32[]{:S(2)}, u32[]{:S(2)}) collective-permute-start(bf16[48,1792]{1,0:T(8,128)(2,1)S(1)} %get-tuple-element.83), channel_id=1, source_target_pairs={{2,0},{4,2},{6,4},{7,6},{5,7},{3,5},{1,3},{0,1},{10,8},{12,10},{14... | collective-permute-start | bytes 516104 | tf_op jit(solution)/shard_map/ppermute | solution.py:396
  113.2 5.5 %collective-permute-start.25 = (bf16[48,1792]{1,0:T(8,128)(2,1)S(1)}, bf16[48,1792]{1,0:T(8,128)(2,1)S(1)}, u32[]{:S(2)}, u32[]{:S(2)}) collective-permute-start(bf16[48,1792]{1,0:T(8,128)(2,1)S(1)} %get-tuple-element.94), channel_id=1, source_target_pairs={{0,2},{2,4},{4,6},{6,7},{7,5},{5,3},{3,1},{1,0},{8,10},{10,12},{12... | collective-permute-start | bytes 516104 | tf_op jit(solution)/shard_map/ppermute | solution.py:395
  113.6 7.0 %collective-permute-start.23 = (bf16[48,1792]{1,0:T(8,128)(2,1)S(1)}, bf16[48,1792]{1,0:T(8,128)(2,1)S(1)}, u32[]{:S(2)}, u32[]{:S(2)}) collective-permute-start(bf16[48,1792]{1,0:T(8,128)(2,1)S(1)} %get-tuple-element.95), channel_id=1, source_target_pairs={{0,2},{2,4},{4,6},{6,7},{7,5},{5,3},{3,1},{1,0},{8,10},{10,12},{12... | collective-permute-start | bytes 516104 | tf_op jit(solution)/shard_map/ppermute | solution.py:395
  126.3 5.2 %collective-permute-start.42 = (bf16[64,2048]{1,0:T(8,128)(2,1)S(1)}, bf16[64,2048]{1,0:T(8,128)(2,1)S(1)}, u32[]{:S(2)}, u32[]{:S(2)}) collective-permute-start(bf16[64,2048]{1,0:T(8,128)(2,1)S(1)} %get-tuple-element.80), channel_id=1, source_target_pairs={{0,8},{8,0},{16,24},{24,16},{1,9},{9,1},{17,25},{25,17},{2,10},{10... | collective-permute-start | bytes 786440 | tf_op jit(solution)/shard_map/ppermute | solution.py:426
  131.6 7.0 %collective-permute-start.43 = (bf16[32,2048]{1,0:T(8,128)(2,1)S(1)}, bf16[32,2048]{1,0:T(8,128)(2,1)S(1)}, u32[]{:S(2)}, u32[]{:S(2)}) collective-permute-start(bf16[32,2048]{1,0:T(8,128)(2,1)S(1)} %slice.333), channel_id=1, source_target_pairs={{0,16},{8,24},{16,0},{24,8},{1,17},{9,25},{17,1},{25,9},{2,18},{10... | collective-permute-start | bytes 393224 | tf_op jit(solution)/shard_map/ppermute | solution.py:430
  134.4 6.4 %collective-permute-start.41 = (bf16[32,2048]{1,0:T(8,128)(2,1)S(1)}, bf16[32,2048]{1,0:T(8,128)(2,1)S(1)}, u32[]{:S(2)}, u32[]{:S(2)}) collective-permute-start(bf16[32,2048]{1,0:T(8,128)(2,1)S(1)} %slice.334), channel_id=1, source_target_pairs={{0,16},{8,24},{16,0},{24,8},{1,17},{9,25},{17,1},{25,9},{2,18},{10... | collective-permute-start | bytes 393224 | tf_op jit(solution)/shard_map/ppermute | solution.py:430
  140.9 7.7 %collective-permute-start.44 = (bf16[4,4096]{1,0:T(4,128)(2,1)S(1)}, bf16[4,4096]{1,0:T(4,128)(2,1)S(1)}, u32[]{:S(2)}, u32[]{:S(2)}) collective-permute-start(bf16[4,4096]{1,0:T(4,128)(2,1)S(1)} %get-tuple-element.106), channel_id=1, source_target_pairs={{0,1},{1,2},{2,3},{3,4},{4,5},{5,6},{6,7},{7,0},{8,9},{9,10},{10,1... | collective-permute-start | bytes 98312 | tf_op jit(solution)/shard_map/ppermute | solution.py:438
  142.0 6.9 %collective-permute-start.50 = (bf16[4,4096]{1,0:T(4,128)(2,1)S(1)}, bf16[4,4096]{1,0:T(4,128)(2,1)S(1)}, u32[]{:S(2)}, u32[]{:S(2)}) collective-permute-start(bf16[4,4096]{1,0:T(4,128)(2,1)S(1)} %get-tuple-element.107), channel_id=1, source_target_pairs={{0,7},{1,0},{2,1},{3,2},{4,3},{5,4},{6,5},{7,6},{8,15},{9,8},{10,9... | collective-permute-start | bytes 98312 | tf_op jit(solution)/shard_map/ppermute | solution.py:438
  145.7 5.0 %collective-permute-start.49 = (bf16[4,4096]{1,0:T(4,128)(2,1)S(1)}, bf16[4,4096]{1,0:T(4,128)(2,1)S(1)}, u32[]{:S(2)}, u32[]{:S(2)}) collective-permute-start(bf16[4,4096]{1,0:T(4,128)(2,1)S(1)} %get-tuple-element.108), channel_id=1, source_target_pairs={{0,6},{1,7},{2,0},{3,1},{4,2},{5,3},{6,4},{7,5},{8,14},{9,15},{10,... | collective-permute-start | bytes 98312 | tf_op jit(solution)/shard_map/ppermute | solution.py:438
  145.7 4.9 %collective-permute-start.48 = (bf16[4,4096]{1,0:T(4,128)(2,1)S(1)}, bf16[4,4096]{1,0:T(4,128)(2,1)S(1)}, u32[]{:S(2)}, u32[]{:S(2)}) collective-permute-start(bf16[4,4096]{1,0:T(4,128)(2,1)S(1)} %get-tuple-element.109), channel_id=1, source_target_pairs={{0,5},{1,6},{2,7},{3,0},{4,1},{5,2},{6,3},{7,4},{8,13},{9,14},{10,... | collective-permute-start | bytes 98312 | tf_op jit(solution)/shard_map/ppermute | solution.py:438
  146.4 4.8 %collective-permute-start.47 = (bf16[4,4096]{1,0:T(4,128)(2,1)S(1)}, bf16[4,4096]{1,0:T(4,128)(2,1)S(1)}, u32[]{:S(2)}, u32[]{:S(2)}) collective-permute-start(bf16[4,4096]{1,0:T(4,128)(2,1)S(1)} %get-tuple-element.110), channel_id=1, source_target_pairs={{0,4},{1,5},{2,6},{3,7},{4,0},{5,1},{6,2},{7,3},{8,12},{9,13},{10,... | collective-permute-start | bytes 98312 | tf_op jit(solution)/shard_map/ppermute | solution.py:438
  148.7 5.7 %collective-permute-start.46 = (bf16[4,4096]{1,0:T(4,128)(2,1)S(1)}, bf16[4,4096]{1,0:T(4,128)(2,1)S(1)}, u32[]{:S(2)}, u32[]{:S(2)}) collective-permute-start(bf16[4,4096]{1,0:T(4,128)(2,1)S(1)} %get-tuple-element.111), channel_id=1, source_target_pairs={{0,3},{1,4},{2,5},{3,6},{4,7},{5,0},{6,1},{7,2},{8,11},{9,12},{10,... | collective-permute-start | bytes 98312 | tf_op jit(solution)/shard_map/ppermute | solution.py:438
  148.9 7.3 %collective-permute-start.45 = (bf16[4,4096]{1,0:T(4,128)(2,1)S(1)}, bf16[4,4096]{1,0:T(4,128)(2,1)S(1)}, u32[]{:S(2)}, u32[]{:S(2)}) collective-permute-start(bf16[4,4096]{1,0:T(4,128)(2,1)S(1)} %get-tuple-element.112), channel_id=1, source_target_pairs={{0,2},{1,3},{2,4},{3,5},{4,6},{5,7},{6,0},{7,1},{8,10},{9,11},{10,... | collective-permute-start | bytes 98312 | tf_op jit(solution)/shard_map/ppermute | solution.py:438
  (18 other events, 190.6 us)

commit v5 on v3

v5 whole, which is shorter than its diff:
```python
import functools

import jax
import jax.numpy as jnp
import numpy as np
from jax import lax
from jax.experimental import pallas as pl
from jax.experimental.pallas import tpu as pltpu
from jax.sharding import PartitionSpec as P

F32 = jnp.float32
BF16 = jnp.bfloat16
LANES = 128
VMEM_LIMIT = 24 * 1024 * 1024
PIECES_LIMIT = 48 * 1024 * 1024


def ring_order(devices):
    places = [getattr(d, "coords", None) for d in devices]
    count = len(places)
    if any(p is None for p in places):
        return list(range(count))
    at = {(p[2], p[0]): i for i, p in enumerate(places)}
    zs, xs = sorted({k[0] for k in at}), sorted({k[1] for k in at})
    if len(at) != count or len(zs) * len(xs) != count or len(xs) < 2 or len(zs) % 2:
        return list(range(count))
    order = [at[(z, xs[0])] for z in zs]
    for i, z in enumerate(reversed(zs)):
        line = xs[1:] if i % 2 == 0 else list(reversed(xs[1:]))
        order += [at[(z, x)] for x in line]
    return order


def core_count(devices):
    places = [getattr(d, "coords", None) for d in devices]
    if any(p is None for p in places):
        return 1
    same = [tuple(p) == tuple(places[0]) for p in places]
    cores = sum(same)
    return cores if all(same[:cores]) and len(places) % cores == 0 else 1


def turned(index, step, count):
    return lax.rem(index + step, jnp.int32(count))


def place_rows(tokens, routes, mixing, experts, capacity, shards):
    token_count, width = tokens.shape
    depth = width // shards
    padded = -(-capacity // 8) * 8

    def kernel(tokens_ref, routes_ref, mixing_ref, out_ref):
        ids = [routes_ref[p % 2, p // 2] for p in range(2 * token_count)]
        slots = []
        for p in range(2 * token_count):
            slot = jnp.int32(0)
            for q in range(p):
                slot = slot + jnp.where(ids[q] == ids[p], 1, 0)
            slots.append(slot)
        row = lax.broadcasted_iota(jnp.int32, (padded, LANES), 0)
        lane = lax.broadcasted_iota(jnp.int32, (padded, LANES), 1)
        wide_row = lax.broadcasted_iota(jnp.int32, (padded, width), 0)
        values = tokens_ref[...].astype(F32)
        tails = []
        for p in range(2 * token_count):
            weight = jnp.full((padded, LANES), mixing_ref[p % 2, p // 2], F32)
            high = weight.astype(BF16).astype(F32)
            number = jnp.full((padded, LANES), float(p // 2 + 1), F32)
            tail = jnp.where(lane == 1, high, jnp.where(lane == 2, weight - high, 0.0))
            tails.append(jnp.where(lane == 0, number, tail))
        for e in range(experts):
            tail = jnp.zeros((padded, LANES), F32)
            body = jnp.zeros((padded, width), F32)
            for p in range(2 * token_count):
                slot = jnp.where(ids[p] == e, slots[p], -1)
                value = jnp.broadcast_to(values[p // 2 : p // 2 + 1], (padded, width))
                tail = jnp.where(row == slot, tails[p], tail)
                body = jnp.where(wide_row == slot, value, body)
            body, tail = body.astype(BF16)[:capacity], tail.astype(BF16)[:capacity]
            for s in range(shards):
                out_ref[e * shards + s, :, :depth] = body[:, s * depth : (s + 1) * depth]
                out_ref[e * shards + s, :, depth:] = tail

    return pl.pallas_call(
        kernel,
        out_shape=jax.ShapeDtypeStruct((experts * shards, capacity, depth + LANES), BF16),
        in_specs=[
            pl.BlockSpec(memory_space=pltpu.VMEM),
            pl.BlockSpec(memory_space=pltpu.SMEM),
            pl.BlockSpec(memory_space=pltpu.SMEM),
        ],
        out_specs=pl.BlockSpec(memory_space=pltpu.VMEM),
        name="place_rows",
    )(tokens, routes.T, mixing.T)


def column_pieces(where, table, rows, gate_weight, up_weight, shards, first, pieces, cuts):
    count, depth = rows.shape
    width = gate_weight.shape[2] // shards
    block = width // cuts

    def kernel(where_ref, table_ref, rows_ref, *refs):
        weights, outs = refs[: 2 * pieces], refs[2 * pieces :]
        for ref, out in zip(weights, outs):
            value = jnp.dot(rows_ref[...], ref[0], preferred_element_type=F32)
            out[...] = value.astype(BF16)

    def weight_map(side, i):
        def index(j, where_ref, table_ref):
            return 0, 0, table_ref[(where_ref[1] * 2 + side) * shards + first + i] * cuts + j

        return pl.BlockSpec((1, depth, block), index)

    both = [(side, i) for side in range(2) for i in range(pieces)]
    out = pl.pallas_call(
        kernel,
        out_shape=[jax.ShapeDtypeStruct((count, width), BF16)] * len(both),
        grid_spec=pltpu.PrefetchScalarGridSpec(
            num_scalar_prefetch=2,
            grid=(cuts,),
            in_specs=[pl.BlockSpec((count, depth), lambda j, *_: (0, 0))]
            + [weight_map(side, i) for side, i in both],
            out_specs=[pl.BlockSpec((count, block), lambda j, *_: (0, j))] * len(both),
        ),
        compiler_params=pltpu.CompilerParams(vmem_limit_bytes=PIECES_LIMIT),
        cost_estimate=pl.CostEstimate(
            flops=4 * pieces * count * depth * width,
            bytes_accessed=4 * pieces * depth * width,
            transcendentals=0,
        ),
        name="column_pieces",
    )(where, table, rows, *([gate_weight] * pieces + [up_weight] * pieces))
    return out[:pieces], out[pieces:]


def plain_pieces(where, table, rows, gate_weight, up_weight, shards):
    width = gate_weight.shape[2] // shards
    both = []
    for side, weight in enumerate((gate_weight, up_weight)):
        value = jnp.dot(rows, weight[0], preferred_element_type=F32).astype(BF16)
        at = table.reshape(shards, 2, shards)[where[1], side] * width
        both.append([lax.dynamic_slice_in_dim(value, at[t], width, 1) for t in range(shards)])
    return both


def turn_columns(where, x, cores, chips):
    rows, total = x.shape[1:]
    block = total // (cores * chips)

    def index(k):
        def place(i, where_ref):
            b = where_ref[0]
            chip = turned(lax.div(b, jnp.int32(cores)), i, chips)
            return 0, 0, chip * cores + turned(lax.rem(b, jnp.int32(cores)), k, cores)

        return place

    def kernel(where_ref, *refs):
        for k in range(cores):
            refs[cores + k][...] = refs[k][...]

    return pl.pallas_call(
        kernel,
        out_shape=[jax.ShapeDtypeStruct((chips, rows, block), x.dtype)] * cores,
        grid_spec=pltpu.PrefetchScalarGridSpec(
            num_scalar_prefetch=1,
            grid=(chips,),
            in_specs=[pl.BlockSpec((1, rows, block), index(k)) for k in range(cores)],
            out_specs=[pl.BlockSpec((1, rows, block), lambda i, *_: (i, 0, 0))] * cores,
        ),
        cost_estimate=pl.CostEstimate(flops=0, bytes_accessed=4 * rows * total, transcendentals=0),
        name="turn_columns",
    )(where, *([x] * cores))


def hidden_rows(where, gate_in, up_in, gate_own, up_own, tails, origin, sizes):
    experts, shards, cores, token_count = sizes
    chips = experts // cores
    total = experts * shards * token_count
    count, slice_width = gate_own.shape
    chunk = next(c for c in (256, LANES, slice_width) if slice_width % c == 0)

    def kernel(where_ref, gate_ref, up_ref, gate_own_ref, up_own_ref, tail_ref, origin_ref, out_ref):
        b = where_ref[0]
        tail = tail_ref[...].astype(F32)
        place = origin_ref[...]
        number, weight = tail[:, 0:1], tail[:, 1:2] + tail[:, 2:3]
        chip = place[:, 0:1] - lax.div(b, jnp.int32(cores)).astype(F32)
        core = place[:, 1:2] - lax.rem(b, jnp.int32(cores)).astype(F32)
        chip = jnp.where(chip < 0, chip + chips, chip)
        core = jnp.where(core < 0, core + cores, core)
        target = (core * chips + chip) * (shards * token_count) + place[:, 2:3] + number - 1.0
        target = jnp.where(number > 0, target, -1.0).astype(jnp.int32)
        spread = target == lax.broadcasted_iota(jnp.int32, (count, total), 1)
        spread = spread.astype(F32).astype(BF16)
        for at in range(0, slice_width, chunk):
            cut = slice(at, at + chunk)
            gate = gate_ref[:, cut].astype(F32) + gate_own_ref[:, cut].astype(F32)
            upper = up_ref[:, cut].astype(F32) + up_own_ref[:, cut].astype(F32)
            hidden = (gate / (1.0 + jnp.exp(-gate)) * upper * weight).astype(BF16)
            out_ref[:, cut] = lax.dot_general(
                spread, hidden, (((0,), (0,)), ((), ())), preferred_element_type=F32
            ).astype(BF16)

    return pl.pallas_call(
        kernel,
        out_shape=jax.ShapeDtypeStruct((total, slice_width), BF16),
        in_specs=[pl.BlockSpec(memory_space=pltpu.SMEM)]
        + [pl.BlockSpec(memory_space=pltpu.VMEM)] * 6,
        out_specs=pl.BlockSpec(memory_space=pltpu.VMEM),
        cost_estimate=pl.CostEstimate(
            flops=2 * total * slice_width * count,
            bytes_accessed=8 * count * slice_width,
            transcendentals=count * slice_width,
        ),
        compiler_params=pltpu.CompilerParams(vmem_limit_bytes=VMEM_LIMIT),
        name="hidden_rows",
    )(where, gate_in, up_in, gate_own, up_own, tails, origin)


def hold(where, x, parts):
    rows = x.shape[1] // parts

    def kernel(where_ref, in_ref, out_ref, sems):
        copies = [
            pltpu.make_async_copy(
                in_ref.at[:, pl.ds(i * rows, rows)], out_ref.at[:, pl.ds(i * rows, rows)], sems.at[i]
            )
            for i in range(parts)
        ]
        for copy in copies:
            copy.start()
        for copy in copies:
            copy.wait()

    return pl.pallas_call(
        kernel,
        out_shape=jax.ShapeDtypeStruct(x.shape, x.dtype),
        in_specs=[pl.BlockSpec(memory_space=pltpu.SMEM), pl.BlockSpec(memory_space=pl.ANY)],
        out_specs=pl.BlockSpec(memory_space=pl.ANY),
        scratch_shapes=[pltpu.SemaphoreType.DMA((parts,))],
        cost_estimate=pl.CostEstimate(
            flops=0, bytes_accessed=2 * x.size * x.dtype.itemsize, transcendentals=0
        ),
        name="hold",
    )(where, x)


def branch_target(size, cores, core_step, chip_step):
    chips = size // cores
    return [
        (i, (i // cores + chip_step) % chips * cores + (i + core_step) % cores)
        for i in range(size)
    ]


def local(order, cores, tokens, routes, mixing, gate_weight, up_weight, down_weight, key_value):
    experts = lax.axis_size("branch")
    shards = lax.axis_size("shard")
    chips = experts // cores
    token_count, width = tokens.shape
    capacity = max(2, (2 * token_count + experts - 1) // experts + 1)
    depth = gate_weight.shape[1]
    slice_width = down_weight.shape[1]
    count = experts * shards * capacity
    kept = chips * shards * token_count
    sizes = (experts, shards, cores, token_count)
    where = jnp.stack([lax.axis_index("branch"), lax.axis_index("shard")]).astype(jnp.int32)

    place = np.argsort(np.asarray(order))
    table = np.zeros((shards, 2, shards), np.int32)
    for s in range(shards):
        for t in range(shards):
            table[s, 0, t] = order[(place[s] - 1 - t) % shards]
            table[s, 1, t] = order[(place[s] + 1 + t) % shards]
    table = jnp.asarray(table.reshape(-1))
    forth = [(order[i], order[(i + 1) % shards]) for i in range(shards)]
    back = [(b, a) for a, b in forth]
    source = np.arange(count) // capacity
    origin = np.zeros((count, LANES), np.float32)
    origin[:, 0] = source // shards // cores
    origin[:, 1] = source // shards % cores
    origin[:, 2] = source % shards * token_count
    origin = jnp.asarray(origin)

    cells = place_rows(tokens, routes, mixing, experts, capacity, shards)
    cells, where, table, origin = lax.optimization_barrier((cells, where, table, origin))
    cells = lax.all_to_all(cells, ("branch", "shard"), split_axis=0, concat_axis=0, tiled=True)
    cells = cells.reshape(count, depth + LANES)
    rows, tails = cells[:, :depth], cells[:, depth:]

    sliced = slice_width % LANES == 0
    if sliced:
        cuts = 2 if slice_width % (2 * LANES) == 0 else 1
        gates, ups = column_pieces(where, table, rows, gate_weight, up_weight, shards, 0, 1, cuts)
    else:
        gates, ups = plain_pieces(where, table, rows, gate_weight, up_weight, shards)
    gate_sum, up_sum = gates[0], ups[0]
    last = shards - 1
    for t in range(1, shards):
        now, gate_sum, up_sum = lax.optimization_barrier((where, gate_sum, up_sum))
        gate_in = lax.ppermute(gate_sum, "shard", forth)
        up_in = lax.ppermute(up_sum, "shard", back)
        if sliced and len(gates) < shards:
            more = column_pieces(
                now, table, rows, gate_weight, up_weight, shards, len(gates),
                min(2, shards - len(gates)), 1,
            )
            gates, ups = gates + more[0], ups + more[1]
            gate_in, up_in, gates, ups = lax.optimization_barrier((gate_in, up_in, gates, ups))
        if t == min(4, last):
            kv = turn_columns(now, key_value, cores, chips)
            kv_core = [
                lax.ppermute(kv[k], "branch", branch_target(experts, cores, k, 0))
                for k in range(1, cores)
            ]
            gate_in, kv = lax.optimization_barrier((gate_in, kv))
        if t == min(5, last):
            gate_in, kv_core = lax.optimization_barrier((gate_in, kv_core))
            kv_sum = kv[0].astype(F32) + sum(x.astype(F32) for x in kv_core)
            kv_chip = [
                lax.ppermute(
                    kv_sum[k].astype(BF16), "branch", branch_target(experts, cores, 0, k)
                )
                for k in range(1, chips)
            ]
        if t == min(6, last):
            down_here = hold(now, down_weight, 8 if slice_width % LANES == 0 else 1)
            gate_in, down_here = lax.optimization_barrier((gate_in, down_here))
        if t == last:
            gate_in, kv_chip = lax.optimization_barrier((gate_in, kv_chip))
            kv_sum = kv_sum[0] + sum(x.astype(F32) for x in kv_chip)
            merged_kv = (kv_sum / experts).astype(BF16)
            gate_in, merged_kv = lax.optimization_barrier((gate_in, merged_kv))
        else:
            gate_sum = (gate_in.astype(F32) + gates[t].astype(F32)).astype(BF16)
            up_sum = (up_in.astype(F32) + ups[t].astype(F32)).astype(BF16)

    hidden = hidden_rows(where, gate_in, up_in, gates[last], ups[last], tails, origin, sizes)
    sent = []
    for k in range(1, cores):
        part = jnp.dot(
            hidden[k * kept : (k + 1) * kept], down_here[0], preferred_element_type=F32
        ).astype(BF16)
        sent.append(lax.ppermute(part, "branch", branch_target(experts, cores, k, 0)))
    mixed = jnp.dot(hidden[:kept], down_here[0], preferred_element_type=F32)
    mixed, sent = lax.optimization_barrier((mixed, sent))
    mixed = mixed + sum(x.astype(F32) for x in sent)
    mixed = mixed.reshape(chips, shards * token_count, width)
    total = mixed[0]
    for k in range(1, chips):
        part = lax.ppermute(mixed[k].astype(BF16), "branch", branch_target(experts, cores, 0, k))
        total = total + part.astype(F32)
    total = total.astype(BF16).reshape(shards, token_count, width)
    total = lax.all_to_all(total, "shard", split_axis=0, concat_axis=0, tiled=True)
    return jnp.sum(total.astype(F32), axis=0).astype(BF16), merged_kv


def solution(mesh):
    grid = mesh.devices
    order = ring_order(list(grid[0, :]))
    cores = core_count(list(grid[:, 0]))
    return jax.shard_map(
        functools.partial(local, order, cores),
        mesh=mesh,
        in_specs=(
            P(("branch", "shard"), None),
            P(("branch", "shard"), None),
            P(("branch", "shard"), None),
            P("branch", "shard", None),
            P("branch", "shard", None),
            P("branch", "shard", None),
            P("branch", "shard", None),
        ),
        out_specs=(P(("branch", "shard"), None), P("shard", "branch")),
        check_vma=False,
    )
```

time: 139 us -> 574 us (4.13)
  Pallas kernels: 31.3 us -> 474 us
  waiting for transfers between devices: 64.5 us -> 31.3 us
  blocking collectives: 9.22 us -> 27.2 us
  matrix products: 0 us -> 10.5 us
  starting transfers between devices: 25.6 us -> 16.7 us
  other arithmetic: 2.98 us -> 10 us
    pallas_call x5 -> x9, Pallas kernels: 31.3 us -> 474 us  [the longest x1 447 us: hold(): pl.pallas_call(kernel, out_shape=jax.ShapeDtypeStruct(x.shape, x.dtype),...]
    ppermute x7, waiting for transfers between devices: 38.2 us -> 10.5 us  [local(): up_in = lax.ppermute(up_sum, 'shard', back)]
    all_to_all x1 -> x2, blocking collectives: 9.22 us -> 27.2 us  [the longest x1 15.2 us: local(): lax.all_to_all(cells, ('branch', 'shard'), split_axis=0, concat_axis=0, t...]
    all_to_all x2 -> x0, waiting for transfers between devices: 15.1 us -> none  [the longest x1 7.64 us: local(): lax.all_to_all(mixed, 'shard', split_axis=0, concat_axis=0, tiled=True)]
    ppermute x7, waiting for transfers between devices: 1.19 us -> 13.1 us  [local(): gate_in = lax.ppermute(gate_sum, 'shard', forth)]
    dot_general x0 -> x2, matrix products: none -> 10.5 us  [the longest x1 7.88 us: local(): jnp.dot(hidden[k * kept:(k + 1) * kept], down_here[0], preferred_element_...]
    all_to_all x2 -> x0, starting transfers between devices: 9.74 us -> none  [the longest x1 6.33 us: local(): lax.all_to_all(cells, 'shard', split_axis=0, concat_axis=0, tiled=True)]
    convert_element_type x13 -> x12, other arithmetic: 0.79 us -> 6.62 us  [the longest x6 3.54 us: local(): up_sum = (up_in.astype(F32) + ups[t].astype(F32)).astype(BF16)]
  transfers between devices with their start and end apart: 20 -> 18, of which waited for: 12 -> 10; matrix products, arithmetic and copies ran while one was open for 3% -> 2% of each run, Pallas kernels for 12% -> 82%
where the time goes in v5:
time: 574 us
  Pallas kernels  474 us (83%)
  waiting for transfers between devices  31.3 us (5%)
  blocking collectives  27.2 us (5%)
  starting transfers between devices  16.7 us (3%)
  matrix products  10.5 us (2%)
  other arithmetic  10 us (2%)
    pallas_call x1, Pallas kernels, hold(): pl.pallas_call(kernel, out_shape=jax.ShapeDtypeStruct(x.shape, x.dtype),...  447 us
    pallas_call x5, Pallas kernels, column_pieces(): pl.pallas_call(kernel, out_shape=[jax.ShapeDtypeStruct((count, width), BF...  21.4 us
    all_to_all x1, blocking collectives, local(): lax.all_to_all(cells, ('branch', 'shard'), split_axis=0, concat_axis=0, t...  15.2 us
    ppermute x7, waiting for transfers between devices, local(): gate_in = lax.ppermute(gate_sum, 'shard', forth)  13.1 us
    all_to_all x1, blocking collectives, local(): lax.all_to_all(total, 'shard', split_axis=0, concat_axis=0, tiled=True)  12 us
  transfers between devices with their start and end apart: 18, of which 10 were waited for; matrix products, arithmetic and copies ran while one was open for 2% of the time, Pallas kernels for 82%

profile of v5, /device:TPU:0, one launch (start us, length us, event | category | flops | bytes accessed | tf_op | source)
XLA Modules:
  0.0 573.7 jit_solution(18330445763439850820)
XLA Ops:
  0.7 1.7 place_rows.1
  2.5 15.2 %all_to_all.10 = bf16[32,3,640]{2,1,0:T(4,128)(2,1)S(1)} all-to-all(bf16[32,3,640]{2,1,0:T(4,128)(2,1)} %place_rows.1), channel_id=1, replica_groups=mesh['branch'=4,'shard'=8] {'branch','shard'}, dimensions={0} | all-to-all | bytes 245760 | tf_op jit(solution)/shard_map/all_to_all | solution.py:288
  17.8 0.6 copy-done.4
  18.5 3.1 column_pieces.5
  21.5 1.4 collective-permute-start
  23.0 0.7 collective-permute-start.1
  23.6 5.0 column_pieces.6
  28.6 3.1 collective-permute-done
  31.7 1.1 collective-permute-done.1
  32.9 0.9 collective-permute-start.2
  33.9 1.1 collective-permute-start.3
  35.0 5.0 column_pieces.7
  40.0 1.9 collective-permute-done.2
  41.9 0.6 collective-permute-done.3
  42.7 0.7 collective-permute-start.4
  43.3 1.4 collective-permute-start.5
  44.8 5.0 column_pieces.8
  49.8 0.7 collective-permute-done.4
  50.9 0.8 add_convert_fusion.7
  51.7 0.8 add_convert_fusion.6
  53.1 1.5 collective-permute-start.7
  54.5 3.3 turn_columns.1
  57.9 0.6 copy-done.2
  58.5 3.3 column_pieces.9
  61.9 1.1 add_convert_fusion.4
  63.0 1.4 collective-permute-start.10
  64.4 0.7 collective-permute-start.8
  65.1 8.4 %collective-permute-done.10 = bf16[96,1792]{1,0:T(8,128)(2,1)S(1)} collective-permute-done((bf16[96,1792]{1,0:T(8,128)(2,1)S(1)}, bf16[96,1792]{1,0:T(8,128)(2,1)S(1)}, u32[]{:S(2)}, u32[]{:S(2)}) %collective-permute-start.10) | collective-permute-done | bytes 344096 | tf_op jit(solution)/shard_map/ppermute | solution.py:303
  73.6 0.9 collective-permute-done.8
  74.6 0.8 add_convert_fusion.3
  75.4 0.7 collective-permute-start.11
  76.1 1.3 collective-permute-start.12
  77.8 1.3 copy-done.7
  79.2 1.0 collective-permute-start.14
  80.1 446.5 %hold.1 = bf16[1,1792,4096]{2,1,0:T(8,128)(2,1)} custom-call(s32[2]{0:T(128)} %copy-done.1, bf16[1,1792,4096]{2,1,0:T(8,128)(2,1)} %in_ref.1), custom_call_target="tpu_custom_call" | custom-call | bytes 29360128 | tf_op jit(solution)/shard_map/hold/pallas_call | solution.py:236
  526.7 1.2 add_convert_fusion.1
  527.9 1.3 add_convert_fusion
  529.3 0.6 collective-permute-start.13
  529.9 1.5 collective-permute-start.15
  531.4 6.5 %collective-permute-done.13.gate_ref = bf16[96,1792]{1,0:T(8,128)(2,1)S(1)} collective-permute-done((bf16[96,1792]{1,0:T(8,128)(2,1)S(1)}, bf16[96,1792]{1,0:T(8,128)(2,1)S(1)}, u32[]{:S(2)}, u32[]{:S(2)}) %collective-permute-start.13) | collective-permute-done | bytes 344096 | tf_op jit(solution)/shard_map/ppermute | solution.py:302
  537.9 2.2 fusion.9
  540.1 1.2 hidden_rows.1
  541.3 7.9 %fusion.4 = bf16[64,4096]{1,0:T(8,128)(2,1)S(1)} fusion(bf16[1,1792,4096]{2,1,0:T(8,128)(2,1)} %hold.1, bf16[128,1792]{1,0:T(8,128)(2,1)S(1)} %hidden_rows.1), kind=kOutput, calls=%fused_computation.4 | convolution fusion | flops 939786240 | bytes 15433728 | tf_op jit(solution)/shard_map/dot_general | solution.py:342
  549.3 2.7 fusion.2
  552.1 1.2 collective-permute-start.17
  553.3 7.6 %collective-permute-done.17 = bf16[32,4096]{1,0:T(8,128)(2,1)S(1)} collective-permute-done((bf16[32,4096]{1,0:T(8,128)(2,1)S(1)}, bf16[32,4096]{1,0:T(8,128)(2,1)S(1)}, u32[]{:S(2)}, u32[]{:S(2)}) %collective-permute-start.17) | collective-permute-done | bytes 262176 | tf_op jit(solution)/shard_map/ppermute | solution.py:352
  561.0 12.0 %all_to_all.11 = bf16[8,4,4096]{2,1,0:T(4,128)(2,1)S(1)} all-to-all(bf16[8,4,4096]{2,1,0:T(4,128)(2,1)S(1)} %reshape.17), channel_id=1, replica_groups=mesh['branch'=4,'shard'=8] {'shard'}, dimensions={0} | all-to-all | bytes 524288 | tf_op jit(solution)/shard_map/all_to_all | solution.py:355
  573.0 0.7 reduce_sum.12
  (42 shorter events, 2.5 us)
Async XLA Ops:
  0.7 44.1 %copy-start.1 = (s32[2]{0:T(128)}, s32[2]{0:T(128)S(1)}, u32[]{:S(2)}) copy-start(s32[2]{0:T(128)S(1)} %pad_add_fusion.where_ref) | copy-start | bytes 28
  17.8 0.7 copy-start.4
  21.5 10.2 %collective-permute-start = (bf16[96,1792]{1,0:T(8,128)(2,1)S(1)}, bf16[96,1792]{1,0:T(8,128)(2,1)S(1)}, u32[]{:S(2)}, u32[]{:S(2)}) collective-permute-start(bf16[96,1792]{1,0:T(8,128)(2,1)S(1)} %get-tuple-element.94), channel_id=1, source_target_pairs={{0,2},{2,4},{4,6},{6,7},{7,5},{5,3},{3,1},{1,0},{8,10},{10,12},{12... | collective-permute-start | bytes 1032200 | tf_op jit(solution)/shard_map/ppermute | solution.py:302
  23.0 9.8 %collective-permute-start.1 = (bf16[96,1792]{1,0:T(8,128)(2,1)S(1)}, bf16[96,1792]{1,0:T(8,128)(2,1)S(1)}, u32[]{:S(2)}, u32[]{:S(2)}) collective-permute-start(bf16[96,1792]{1,0:T(8,128)(2,1)S(1)} %get-tuple-element.95), channel_id=1, source_target_pairs={{2,0},{4,2},{6,4},{7,6},{5,7},{3,5},{1,3},{0,1},{10,8},{12,10},{14... | collective-permute-start | bytes 1032200 | tf_op jit(solution)/shard_map/ppermute | solution.py:303
  32.9 9.0 %collective-permute-start.2 = (bf16[96,1792]{1,0:T(8,128)(2,1)S(1)}, bf16[96,1792]{1,0:T(8,128)(2,1)S(1)}, u32[]{:S(2)}, u32[]{:S(2)}) collective-permute-start(bf16[96,1792]{1,0:T(8,128)(2,1)S(1)} %get-tuple-element.105), channel_id=1, source_target_pairs={{0,2},{2,4},{4,6},{6,7},{7,5},{5,3},{3,1},{1,0},{8,10},{10,12},{12... | collective-permute-start | bytes 1032200 | tf_op jit(solution)/shard_map/ppermute | solution.py:302
  33.9 8.7 %collective-permute-start.3 = (bf16[96,1792]{1,0:T(8,128)(2,1)S(1)}, bf16[96,1792]{1,0:T(8,128)(2,1)S(1)}, u32[]{:S(2)}, u32[]{:S(2)}) collective-permute-start(bf16[96,1792]{1,0:T(8,128)(2,1)S(1)} %get-tuple-element.106), channel_id=1, source_target_pairs={{2,0},{4,2},{6,4},{7,6},{5,7},{3,5},{1,3},{0,1},{10,8},{12,10},{14... | collective-permute-start | bytes 1032200 | tf_op jit(solution)/shard_map/ppermute | solution.py:303
  42.7 15.2 %copy-start.5 = (s32[128]{0:T(128)S(1)}, s32[128]{0:T(128)}, u32[]{:S(2)}) copy-start(s32[128]{0:T(128)} %constant.18.clone.table_ref) | copy-start | bytes 1540
  42.7 7.8 %collective-permute-start.4 = (bf16[96,1792]{1,0:T(8,128)(2,1)S(1)}, bf16[96,1792]{1,0:T(8,128)(2,1)S(1)}, u32[]{:S(2)}, u32[]{:S(2)}) collective-permute-start(bf16[96,1792]{1,0:T(8,128)(2,1)S(1)} %add_convert_fusion.9), channel_id=1, source_target_pairs={{0,2},{2,4},{4,6},{6,7},{7,5},{5,3},{3,1},{1,0},{8,10},{10,12},{12... | collective-permute-start | bytes 1032200 | tf_op jit(solution)/shard_map/ppermute | solution.py:302
  43.3 7.6 %collective-permute-start.5 = (bf16[96,1792]{1,0:T(8,128)(2,1)S(1)}, bf16[96,1792]{1,0:T(8,128)(2,1)S(1)}, u32[]{:S(2)}, u32[]{:S(2)}) collective-permute-start(bf16[96,1792]{1,0:T(8,128)(2,1)S(1)} %add_convert_fusion.8), channel_id=1, source_target_pairs={{2,0},{4,2},{6,4},{7,6},{5,7},{3,5},{1,3},{0,1},{10,8},{12,10},{14... | collective-permute-start | bytes 1032200 | tf_op jit(solution)/shard_map/ppermute | solution.py:303
  52.5 9.3 %collective-permute-start.6 = (bf16[96,1792]{1,0:T(8,128)(2,1)}, bf16[96,1792]{1,0:T(8,128)(2,1)S(1)}, u32[]{:S(2)}, u32[]{:S(2)}) collective-permute-start(bf16[96,1792]{1,0:T(8,128)(2,1)} %add_convert_fusion.7), channel_id=1, source_target_pairs={{0,2},{2,4},{4,6},{6,7},{7,5},{5,3},{3,1},{1,0},{8,10},{10,12},{12... | collective-permute-start | bytes 1032200 | tf_op jit(solution)/shard_map/ppermute | solution.py:302
  53.1 8.8 %collective-permute-start.7 = (bf16[96,1792]{1,0:T(8,128)(2,1)}, bf16[96,1792]{1,0:T(8,128)(2,1)}, u32[]{:S(2)}, u32[]{:S(2)}) collective-permute-start(bf16[96,1792]{1,0:T(8,128)(2,1)} %add_convert_fusion.6), channel_id=1, source_target_pairs={{2,0},{4,2},{6,4},{7,6},{5,7},{3,5},{1,3},{0,1},{10,8},{12,10},{14... | collective-permute-start | bytes 1032200 | tf_op jit(solution)/shard_map/ppermute | solution.py:303
  57.8 16.7 %collective-permute-start.9 = (bf16[2,512,512]{2,1,0:T(8,128)(2,1)}, bf16[2,512,512]{2,1,0:T(8,128)(2,1)S(1)}, u32[]{:S(2)}, u32[]{:S(2)}) collective-permute-start(bf16[2,512,512]{2,1,0:T(8,128)(2,1)} %get-tuple-element.146), channel_id=1, source_target_pairs={{0,8},{8,0},{16,24},{24,16},{1,9},{9,1},{17,25},{25,17},{2,10},{10... | collective-permute-start | bytes 3145736 | tf_op jit(solution)/shard_map/ppermute | solution.py:314
  57.9 0.7 copy-start.2
  58.5 18.9 %copy-start.8 = (bf16[2,512,512]{2,1,0:T(8,128)(2,1)S(1)}, bf16[2,512,512]{2,1,0:T(8,128)(2,1)}, u32[]{:S(2)}) copy-start(bf16[2,512,512]{2,1,0:T(8,128)(2,1)} %get-tuple-element.163) | copy-start | bytes 3145732
  63.0 10.5 %collective-permute-start.10 = (bf16[96,1792]{1,0:T(8,128)(2,1)S(1)}, bf16[96,1792]{1,0:T(8,128)(2,1)S(1)}, u32[]{:S(2)}, u32[]{:S(2)}) collective-permute-start(bf16[96,1792]{1,0:T(8,128)(2,1)S(1)} %add_convert_fusion.4), channel_id=1, source_target_pairs={{2,0},{4,2},{6,4},{7,6},{5,7},{3,5},{1,3},{0,1},{10,8},{12,10},{14... | collective-permute-start | bytes 1032200 | tf_op jit(solution)/shard_map/ppermute | solution.py:303
  64.4 10.2 %collective-permute-start.8 = (bf16[96,1792]{1,0:T(8,128)(2,1)S(1)}, bf16[96,1792]{1,0:T(8,128)(2,1)S(1)}, u32[]{:S(2)}, u32[]{:S(2)}) collective-permute-start(bf16[96,1792]{1,0:T(8,128)(2,1)S(1)} %add_convert_fusion.5), channel_id=1, source_target_pairs={{0,2},{2,4},{4,6},{6,7},{7,5},{5,3},{3,1},{1,0},{8,10},{10,12},{12... | collective-permute-start | bytes 1032200 | tf_op jit(solution)/shard_map/ppermute | solution.py:302
  75.4 451.3 %collective-permute-start.11 = (bf16[96,1792]{1,0:T(8,128)(2,1)}, bf16[96,1792]{1,0:T(8,128)(2,1)}, u32[]{:S(2)}, u32[]{:S(2)}) collective-permute-start(bf16[96,1792]{1,0:T(8,128)(2,1)} %add_convert_fusion.3), channel_id=1, source_target_pairs={{0,2},{2,4},{4,6},{6,7},{7,5},{5,3},{3,1},{1,0},{8,10},{10,12},{12... | collective-permute-start | bytes 1032200 | tf_op jit(solution)/shard_map/ppermute | solution.py:302
  76.1 451.8 %collective-permute-start.12 = (bf16[96,1792]{1,0:T(8,128)(2,1)S(1)}, bf16[96,1792]{1,0:T(8,128)(2,1)}, u32[]{:S(2)}, u32[]{:S(2)}) collective-permute-start(bf16[96,1792]{1,0:T(8,128)(2,1)S(1)} %add_convert_fusion.2), channel_id=1, source_target_pairs={{2,0},{4,2},{6,4},{7,6},{5,7},{3,5},{1,3},{0,1},{10,8},{12,10},{14... | collective-permute-start | bytes 1032200 | tf_op jit(solution)/shard_map/ppermute | solution.py:303
  77.8 1.3 copy-start.7
  79.1 460.9 %copy-start = (f32[96,128]{1,0:T(8,128)S(1)}, f32[96,128]{1,0:T(8,128)}, u32[]{:S(2)}) copy-start(f32[96,128]{1,0:T(8,128)} %constant.19.clone.origin_ref) | copy-start | bytes 147460
  79.2 460.9 %copy-start.3 = (s32[2]{0:T(128)S(1)}, s32[2]{0:T(128)}, u32[]{:S(2)}) copy-start(s32[2]{0:T(128)} %copy-done.1) | copy-start | bytes 28
  79.2 452.2 %collective-permute-start.14 = (bf16[512,512]{1,0:T(8,128)(2,1)S(1)}, bf16[512,512]{1,0:T(8,128)(2,1)S(1)}, u32[]{:S(2)}, u32[]{:S(2)}) collective-permute-start(bf16[512,512]{1,0:T(8,128)(2,1)S(1)} %fusion.10), channel_id=1, source_target_pairs={{0,16},{8,24},{16,0},{24,8},{1,17},{9,25},{17,1},{25,9},{2,18},{10... | collective-permute-start | bytes 1572872 | tf_op jit(solution)/shard_map/ppermute | solution.py:322
  526.7 22.6 %copy-start.6 = (bf16[1,1792,4096]{2,1,0:T(8,128)(2,1)S(1)}, bf16[1,1792,4096]{2,1,0:T(8,128)(2,1)}, u32[]{:S(2)}) copy-start(bf16[1,1792,4096]{2,1,0:T(8,128)(2,1)} %hold.1) | copy-start | bytes 44040196
  529.3 8.6 %collective-permute-start.13 = (bf16[96,1792]{1,0:T(8,128)(2,1)S(1)}, bf16[96,1792]{1,0:T(8,128)(2,1)S(1)}, u32[]{:S(2)}, u32[]{:S(2)}) collective-permute-start(bf16[96,1792]{1,0:T(8,128)(2,1)S(1)} %add_convert_fusion.1), channel_id=1, source_target_pairs={{0,2},{2,4},{4,6},{6,7},{7,5},{5,3},{3,1},{1,0},{8,10},{10,12},{12... | collective-permute-start | bytes 1032200 | tf_op jit(solution)/shard_map/ppermute | solution.py:302
  529.9 10.2 %collective-permute-start.15 = (bf16[96,1792]{1,0:T(8,128)(2,1)S(1)}, bf16[96,1792]{1,0:T(8,128)(2,1)S(1)}, u32[]{:S(2)}, u32[]{:S(2)}) collective-permute-start(bf16[96,1792]{1,0:T(8,128)(2,1)S(1)} %add_convert_fusion), channel_id=1, source_target_pairs={{2,0},{4,2},{6,4},{7,6},{5,7},{3,5},{1,3},{0,1},{10,8},{12,10},{14... | collective-permute-start | bytes 1032200 | tf_op jit(solution)/shard_map/ppermute | solution.py:303
  549.2 2.8 collective-permute-start.16
  552.1 8.8 %collective-permute-start.17 = (bf16[32,4096]{1,0:T(8,128)(2,1)S(1)}, bf16[32,4096]{1,0:T(8,128)(2,1)S(1)}, u32[]{:S(2)}, u32[]{:S(2)}) collective-permute-start(bf16[32,4096]{1,0:T(8,128)(2,1)S(1)} %slice.62), channel_id=1, source_target_pairs={{0,16},{8,24},{16,0},{24,8},{1,17},{9,25},{17,1},{25,9},{2,18},{10... | collective-permute-start | bytes 786440 | tf_op jit(solution)/shard_map/ppermute | solution.py:352

commit v6 on v5

--- a/solution.py
+++ b/solution.py
@@ -11,8 +11,7 @@
 F32 = jnp.float32
 BF16 = jnp.bfloat16
 LANES = 128
-VMEM_LIMIT = 24 * 1024 * 1024
-PIECES_LIMIT = 48 * 1024 * 1024
+VMEM_LIMIT = 48 * 1024 * 1024
 
 
 def ring_order(devices):
@@ -94,43 +93,45 @@
     )(tokens, routes.T, mixing.T)
 
 
-def column_pieces(where, table, rows, gate_weight, up_weight, shards, first, pieces, cuts):
+def row_parts(rows):
+    return 4 if rows % 64 == 0 else 1
+
+
+def column_piece(where, table, rows, gate_weight, up_weight, shards, step, cuts):
     count, depth = rows.shape
     width = gate_weight.shape[2] // shards
     block = width // cuts
+    parts = row_parts(depth)
 
     def kernel(where_ref, table_ref, rows_ref, *refs):
-        weights, outs = refs[: 2 * pieces], refs[2 * pieces :]
-        for ref, out in zip(weights, outs):
-            value = jnp.dot(rows_ref[...], ref[0], preferred_element_type=F32)
-            out[...] = value.astype(BF16)
-
-    def weight_map(side, i):
+        for side in range(2):
+            weight = [ref[0] for ref in refs[side * parts : (side + 1) * parts]]
+            weight = jnp.concatenate(weight, axis=0) if parts > 1 else weight[0]
+            value = jnp.dot(rows_ref[...], weight, preferred_element_type=F32)
+            refs[2 * parts + side][...] = value.astype(BF16)
+
+    def weight_block(side, part):
         def index(j, where_ref, table_ref):
-            return 0, 0, table_ref[(where_ref[1] * 2 + side) * shards + first + i] * cuts + j
-
-        return pl.BlockSpec((1, depth, block), index)
-
-    both = [(side, i) for side in range(2) for i in range(pieces)]
-    out = pl.pallas_call(
+            return 0, part, table_ref[(where_ref[1] * 2 + side) * shards + step] * cuts + j
+
+        return pl.BlockSpec((1, depth // parts, block), index)
+
+    return pl.pallas_call(
         kernel,
-        out_shape=[jax.ShapeDtypeStruct((count, width), BF16)] * len(both),
+        out_shape=[jax.ShapeDtypeStruct((count, width), BF16)] * 2,
         grid_spec=pltpu.PrefetchScalarGridSpec(
             num_scalar_prefetch=2,
             grid=(cuts,),
             in_specs=[pl.BlockSpec((count, depth), lambda j, *_: (0, 0))]
-            + [weight_map(side, i) for side, i in both],
-            out_specs=[pl.BlockSpec((count, block), lambda j, *_: (0, j))] * len(both),
-        ),
-        compiler_params=pltpu.CompilerParams(vmem_limit_bytes=PIECES_LIMIT),
+            + [weight_block(side, part) for side in range(2) for part in range(parts)],
+            out_specs=[pl.BlockSpec((count, block), lambda j, *_: (0, j))] * 2,
+        ),
+        compiler_params=pltpu.CompilerParams(vmem_limit_bytes=VMEM_LIMIT),
         cost_estimate=pl.CostEstimate(
-            flops=4 * pieces * count * depth * width,
-            bytes_accessed=4 * pieces * depth * width,
-            transcendentals=0,
-        ),
-        name="column_pieces",
-    )(where, table, rows, *([gate_weight] * pieces + [up_weight] * pieces))
-    return out[:pieces], out[pieces:]
+            flops=4 * count * depth * width, bytes_accessed=4 * depth * width, transcendentals=0
+        ),
+        name="column_piece",
+    )(where, table, rows, *([gate_weight] * parts + [up_weight] * parts))
 
 
 def plain_pieces(where, table, rows, gate_weight, up_weight, shards):
@@ -173,77 +174,82 @@
     )(where, *([x] * cores))
 
 
-def hidden_rows(where, gate_in, up_in, gate_own, up_own, tails, origin, sizes):
+def expert_outputs(where, gate_in, up_in, gate_own, up_own, tails, origin, down_weight, sizes):
     experts, shards, cores, token_count = sizes
     chips = experts // cores
+    count, slice_width = gate_in.shape
+    width = down_weight.shape[2]
     total = experts * shards * token_count
-    count, slice_width = gate_own.shape
-    chunk = next(c for c in (256, LANES, slice_width) if slice_width % c == 0)
-
-    def kernel(where_ref, gate_ref, up_ref, gate_own_ref, up_own_ref, tail_ref, origin_ref, out_ref):
-        b = where_ref[0]
-        tail = tail_ref[...].astype(F32)
-        place = origin_ref[...]
-        number, weight = tail[:, 0:1], tail[:, 1:2] + tail[:, 2:3]
-        chip = place[:, 0:1] - lax.div(b, jnp.int32(cores)).astype(F32)
-        core = place[:, 1:2] - lax.rem(b, jnp.int32(cores)).astype(F32)
-        chip = jnp.where(chip < 0, chip + chips, chip)
-        core = jnp.where(core < 0, core + cores, core)
-        target = (core * chips + chip) * (shards * token_count) + place[:, 2:3] + number - 1.0
-        target = jnp.where(number > 0, target, -1.0).astype(jnp.int32)
-        spread = target == lax.broadcasted_iota(jnp.int32, (count, total), 1)
-        spread = spread.astype(F32).astype(BF16)
-        for at in range(0, slice_width, chunk):
-            cut = slice(at, at + chunk)
-            gate = gate_ref[:, cut].astype(F32) + gate_own_ref[:, cut].astype(F32)
-            upper = up_ref[:, cut].astype(F32) + up_own_ref[:, cut].astype(F32)
-            hidden = (gate / (1.0 + jnp.exp(-gate)) * upper * weight).astype(BF16)
-            out_ref[:, cut] = lax.dot_general(
-                spread, hidden, (((0,), (0,)), ((), ())), preferred_element_type=F32
-            ).astype(BF16)
-
+    kept = total // cores
+    block = 512 if width % 512 == 0 else width
+    parts = row_parts(slice_width)
+    chunk = next(c for c in (256, 128, slice_width) if slice_width % c == 0)
+
+    def kernel(where_ref, gate_ref, up_ref, gate_own_ref, up_own_ref, tail_ref, origin_ref, *rest):
+        hidden_ref = rest[-1]
+        weights, outs = rest[:parts], rest[parts:-1]
+
+        @pl.when(pl.program_id(0) == 0)
+        def _():
+            b = where_ref[0]
+            tail = tail_ref[...].astype(F32)
+            place = origin_ref[...]
+            number, weight = tail[:, 0:1], tail[:, 1:2] + tail[:, 2:3]
+            chip = place[:, 0:1] - lax.div(b, jnp.int32(cores)).astype(F32)
+            core = place[:, 1:2] - lax.rem(b, jnp.int32(cores)).astype(F32)
+            chip = jnp.where(chip < 0, chip + chips, chip)
+            core = jnp.where(core < 0, core + cores, core)
+            target = (core * chips + chip) * (shards * token_count) + place[:, 2:3] + number - 1.0
+            target = jnp.where(number > 0, target, -1.0).astype(jnp.int32)
+            spread = target == lax.broadcasted_iota(jnp.int32, (count, total), 1)
+            spread = spread.astype(F32).astype(BF16)
+            for at in range(0, slice_width, chunk):
+                cut = slice(at, at + chunk)
+                gate = gate_ref[:, cut].astype(F32) + gate_own_ref[:, cut].astype(F32)
+                upper = up_ref[:, cut].astype(F32) + up_own_ref[:, cut].astype(F32)
+                hidden = (gate / (1.0 + jnp.exp(-gate)) * upper * weight).astype(BF16)
+                hidden_ref[:, cut] = lax.dot_general(
+                    spread, hidden, (((0,), (0,)), ((), ())), preferred_element_type=F32
+                ).astype(BF16)
+
+        weight = [ref[0] for ref in weights]
+        weight = jnp.concatenate(weight, axis=0) if parts > 1 else weight[0]
+        value = jnp.dot(hidden_ref[...], weight, preferred_element_type=F32)
+        outs[0][...] = value[:kept]
+        if cores > 1:
+            outs[1][...] = value[kept:].astype(BF16)
+
+    def weight_block(part):
+        return pl.BlockSpec((1, slice_width // parts, block), lambda j, *_: (0, part, j))
+
+    whole = pl.BlockSpec((count, slice_width), lambda j, *_: (0, 0))
+    lanes = pl.BlockSpec((count, LANES), lambda j, *_: (0, 0))
+    shapes = [jax.ShapeDtypeStruct((kept, width), F32)]
+    specs = [pl.BlockSpec((kept, block), lambda j, *_: (0, j))]
+    if cores > 1:
+        shapes.append(jax.ShapeDtypeStruct((total - kept, width), BF16))
+        specs.append(pl.BlockSpec((total - kept, block), lambda j, *_: (0, j)))
     return pl.pallas_call(
         kernel,
-        out_shape=jax.ShapeDtypeStruct((total, slice_width), BF16),
-        in_specs=[pl.BlockSpec(memory_space=pltpu.SMEM)]
-        + [pl.BlockSpec(memory_space=pltpu.VMEM)] * 6,
-        out_specs=pl.BlockSpec(memory_space=pltpu.VMEM),
+        out_shape=shapes,
+        grid_spec=pltpu.PrefetchScalarGridSpec(
+            num_scalar_prefetch=1,
+            grid=(width // block,),
+            in_specs=[
+                whole, whole, whole, whole, lanes, lanes,
+            ]
+            + [weight_block(part) for part in range(parts)],
+            out_specs=specs,
+            scratch_shapes=[pltpu.VMEM((total, slice_width), BF16)],
+        ),
+        compiler_params=pltpu.CompilerParams(vmem_limit_bytes=VMEM_LIMIT),
         cost_estimate=pl.CostEstimate(
-            flops=2 * total * slice_width * count,
-            bytes_accessed=8 * count * slice_width,
+            flops=2 * total * slice_width * width,
+            bytes_accessed=2 * slice_width * width,
             transcendentals=count * slice_width,
         ),
-        compiler_params=pltpu.CompilerParams(vmem_limit_bytes=VMEM_LIMIT),
-        name="hidden_rows",
-    )(where, gate_in, up_in, gate_own, up_own, tails, origin)
-
-
-def hold(where, x, parts):
-    rows = x.shape[1] // parts
-
-    def kernel(where_ref, in_ref, out_ref, sems):
-        copies = [
-            pltpu.make_async_copy(
-                in_ref.at[:, pl.ds(i * rows, rows)], out_ref.at[:, pl.ds(i * rows, rows)], sems.at[i]
-            )
-            for i in range(parts)
-        ]
-        for copy in copies:
-            copy.start()
-        for copy in copies:
-            copy.wait()
-
-    return pl.pallas_call(
-        kernel,
-        out_shape=jax.ShapeDtypeStruct(x.shape, x.dtype),
-        in_specs=[pl.BlockSpec(memory_space=pltpu.SMEM), pl.BlockSpec(memory_space=pl.ANY)],
-        out_specs=pl.BlockSpec(memory_space=pl.ANY),
-        scratch_shapes=[pltpu.SemaphoreType.DMA((parts,))],
-        cost_estimate=pl.CostEstimate(
-            flops=0, bytes_accessed=2 * x.size * x.dtype.itemsize, transcendentals=0
-        ),
-        name="hold",
-    )(where, x)
+        name="expert_outputs",
+    )(where, gate_in, up_in, gate_own, up_own, tails, origin, *([down_weight] * parts))
 
 
 def branch_target(size, cores, core_step, chip_step):
@@ -263,7 +269,6 @@
     depth = gate_weight.shape[1]
     slice_width = down_weight.shape[1]
     count = experts * shards * capacity
-    kept = chips * shards * token_count
     sizes = (experts, shards, cores, token_count)
     where = jnp.stack([lax.axis_index("branch"), lax.axis_index("shard")]).astype(jnp.int32)
 
@@ -292,7 +297,8 @@
     sliced = slice_width % LANES == 0
     if sliced:
         cuts = 2 if slice_width % (2 * LANES) == 0 else 1
-        gates, ups = column_pieces(where, table, rows, gate_weight, up_weight, shards, 0, 1, cuts)
+        one = column_piece(where, table, rows, gate_weight, up_weight, shards, 0, cuts)
+        gates, ups = [one[0]], [one[1]]
     else:
         gates, ups = plain_pieces(where, table, rows, gate_weight, up_weight, shards)
     gate_sum, up_sum = gates[0], ups[0]
@@ -301,21 +307,19 @@
         now, gate_sum, up_sum = lax.optimization_barrier((where, gate_sum, up_sum))
         gate_in = lax.ppermute(gate_sum, "shard", forth)
         up_in = lax.ppermute(up_sum, "shard", back)
-        if sliced and len(gates) < shards:
-            more = column_pieces(
-                now, table, rows, gate_weight, up_weight, shards, len(gates),
-                min(2, shards - len(gates)), 1,
-            )
-            gates, ups = gates + more[0], ups + more[1]
-            gate_in, up_in, gates, ups = lax.optimization_barrier((gate_in, up_in, gates, ups))
-        if t == min(4, last):
+        if sliced:
+            one = column_piece(now, table, rows, gate_weight, up_weight, shards, t, cuts)
+            gate_in, up_in, one = lax.optimization_barrier((gate_in, up_in, one))
+            gates.append(one[0])
+            ups.append(one[1])
+        if t == 1:
             kv = turn_columns(now, key_value, cores, chips)
             kv_core = [
                 lax.ppermute(kv[k], "branch", branch_target(experts, cores, k, 0))
                 for k in range(1, cores)
             ]
             gate_in, kv = lax.optimization_barrier((gate_in, kv))
-        if t == min(5, last):
+        if t == min(2, last):
             gate_in, kv_core = lax.optimization_barrier((gate_in, kv_core))
             kv_sum = kv[0].astype(F32) + sum(x.astype(F32) for x in kv_core)
             kv_chip = [
@@ -324,29 +328,23 @@
                 )
                 for k in range(1, chips)
             ]
-        if t == min(6, last):
-            down_here = hold(now, down_weight, 8 if slice_width % LANES == 0 else 1)
-            gate_in, down_here = lax.optimization_barrier((gate_in, down_here))
-        if t == last:
+        if t == min(5, last):
             gate_in, kv_chip = lax.optimization_barrier((gate_in, kv_chip))
             kv_sum = kv_sum[0] + sum(x.astype(F32) for x in kv_chip)
             merged_kv = (kv_sum / experts).astype(BF16)
             gate_in, merged_kv = lax.optimization_barrier((gate_in, merged_kv))
-        else:
+        if t < last:
             gate_sum = (gate_in.astype(F32) + gates[t].astype(F32)).astype(BF16)
             up_sum = (up_in.astype(F32) + ups[t].astype(F32)).astype(BF16)
 
-    hidden = hidden_rows(where, gate_in, up_in, gates[last], ups[last], tails, origin, sizes)
-    sent = []
+    outputs = expert_outputs(
+        where, gate_in, up_in, gates[last], ups[last], tails, origin, down_weight, sizes
+    )
+    mixed = outputs[0].reshape(chips, shards * token_count, width)
     for k in range(1, cores):
-        part = jnp.dot(
-            hidden[k * kept : (k + 1) * kept], down_here[0], preferred_element_type=F32
-        ).astype(BF16)
-        sent.append(lax.ppermute(part, "branch", branch_target(experts, cores, k, 0)))
-    mixed = jnp.dot(hidden[:kept], down_here[0], preferred_element_type=F32)
-    mixed, sent = lax.optimization_barrier((mixed, sent))
-    mixed = mixed + sum(x.astype(F32) for x in sent)
-    mixed = mixed.reshape(chips, shards * token_count, width)
+        sent = outputs[1].reshape(cores - 1, chips, shards * token_count, width)[k - 1]
+        part = lax.ppermute(sent, "branch", branch_target(experts, cores, k, 0))
+        mixed = mixed + part.astype(F32)
     total = mixed[0]
     for k in range(1, chips):
         part = lax.ppermute(mixed[k].astype(BF16), "branch", branch_target(experts, cores, 0, k))

time: 574 us -> 127 us (0.22)
  Pallas kernels: 474 us -> 41.4 us
  matrix products: 10.5 us -> 0 us
  other arithmetic: 10 us -> 3.21 us
    pallas_call x7 -> x9, Pallas kernels: 469 us -> 36.3 us  [the longest x8 26.6 us: column_piece(): pl.pallas_call(kernel, out_shape=[jax.ShapeDtypeStruct((count, width), BF...]
    dot_general x2 -> x0, matrix products: 10.5 us -> none  [the longest x1 7.88 us: local(): jnp.dot(hidden[k * kept:(k + 1) * kept], down_here[0], preferred_element_...]
  transfers between devices with their start and end apart: 18 -> 18, of which waited for: 10 -> 15; matrix products, arithmetic and copies ran while one was open for 2% -> 1% of each run, Pallas kernels for 82% -> 21%
where the time goes in v6:
time: 127 us; the launch traced here: 126 us
  Pallas kernels  41.4 us (33%)
  waiting for transfers between devices  35.7 us (28%)
  blocking collectives  26.6 us (21%)
  starting transfers between devices  16.3 us (13%)
  other arithmetic  3.21 us (3%)
  local copies, waits for them, and re-layouts  1.77 us (1%)
    pallas_call x8, Pallas kernels, column_piece(): pl.pallas_call(kernel, out_shape=[jax.ShapeDtypeStruct((count, width), BF...  26.6 us
    ppermute x7, waiting for transfers between devices, local(): gate_in = lax.ppermute(gate_sum, 'shard', forth)  18.2 us
    all_to_all x1, blocking collectives, local(): lax.all_to_all(cells, ('branch', 'shard'), split_axis=0, concat_axis=0, t...  15.2 us
    all_to_all x1, blocking collectives, local(): lax.all_to_all(total, 'shard', split_axis=0, concat_axis=0, tiled=True)  11.4 us
    pallas_call x1, Pallas kernels, expert_outputs(): pl.pallas_call(kernel, out_shape=shapes, grid_spec=pltpu.PrefetchScalarGr...  9.7 us
    ppermute x7, starting transfers between devices, local(): gate_in = lax.ppermute(gate_sum, 'shard', forth)  8.84 us
    ppermute x1, waiting for transfers between devices, local(): lax.ppermute(mixed[k].astype(BF16), 'branch', branch_target(experts, core...  8.33 us
    ppermute x7, waiting for transfers between devices, local(): up_in = lax.ppermute(up_sum, 'shard', back)  7.29 us
  transfers between devices with their start and end apart: 18, of which 15 were waited for; matrix products, arithmetic and copies ran while one was open for 1% of the time, Pallas kernels for 21%

profile of v6, /device:TPU:0, one launch (start us, length us, event | category | flops | bytes accessed | tf_op | source)
XLA Modules:
  0.0 125.9 jit_solution(12939101300301235727)
XLA Ops:
  0.7 1.7 %place_rows.1 = bf16[32,3,640]{2,1,0:T(4,128)(2,1)} custom-call(bf16[4,4096]{1,0:T(4,128)(2,1)} %tokens_ref.1, s32[2,4]{1,0:T(2,128)} %bitcast.26, f32[2,4]{1,0:T(2,128)} %bitcast.27), custom_call_target="tpu_custom_call" | custom-call | tf_op jit(solution)/shard_map/place_rows/pallas_call | solution.py:83
  2.5 15.2 %all_to_all.10 = bf16[32,3,640]{2,1,0:T(4,128)(2,1)S(1)} all-to-all(bf16[32,3,640]{2,1,0:T(4,128)(2,1)} %place_rows.1), channel_id=1, replica_groups=mesh['branch'=4,'shard'=8] {'branch','shard'}, dimensions={0} | all-to-all | bytes 245760 | tf_op jit(solution)/shard_map/all_to_all | solution.py:293
  17.8 0.7 copy-done.3
  18.5 3.3 %column_piece.8 = (bf16[96,1792]{1,0:T(8,128)(2,1)S(1)}, bf16[96,1792]{1,0:T(8,128)(2,1)S(1)}) custom-call(s32[2]{0:T(128)S(1)} %pad_add_fusion.where_ref, s32[128]{0:T(128)S(1)} %copy-done.3, bf16[96,512]{1,0:T(8,128)(2,1)S(1)} %slice.26.rows_ref, bf16[1,512,14336]{2,1,0:T(8,128)(2,1)} %refs_3_.15, bf16[1,512,14336]{2,1,0:T(8,128)(2,1)} %refs_3_.15, ...), custom_call_target="tpu_custom_call" | custom-call | flops 352321536 | bytes 3670016 | tf_op jit(solution)/shard_map/column_piece/pallas_call | solution.py:119
  21.9 1.4 %collective-permute-start = (bf16[96,1792]{1,0:T(8,128)(2,1)S(1)}, bf16[96,1792]{1,0:T(8,128)(2,1)S(1)}, u32[]{:S(2)}, u32[]{:S(2)}) collective-permute-start(bf16[96,1792]{1,0:T(8,128)(2,1)S(1)} %get-tuple-element.88), channel_id=1, source_target_pairs={{0,2},{2,4},{4,6},{6,7},{7,5},{5,3},{3,1},{1,0},{8,10},{10,12},{12... | collective-permute-start | bytes 1032200 | tf_op jit(solution)/shard_map/ppermute | solution.py:308
  23.3 0.7 collective-permute-start.1
  24.0 3.3 %turn_columns.1 = (bf16[2,512,512]{2,1,0:T(8,128)(2,1)}, bf16[2,512,512]{2,1,0:T(8,128)(2,1)}) custom-call(s32[2]{0:T(128)} %copy-done, bf16[1,512,2048]{2,1,0:T(8,128)(2,1)} %refs_1_.11, bf16[1,512,2048]{2,1,0:T(8,128)(2,1)} %refs_1_.11), custom_call_target="tpu_custom_call" | custom-call | bytes 4194304 | tf_op jit(solution)/shard_map/turn_columns/pallas_call | solution.py:163
  27.3 3.3 %column_piece.9 = (bf16[96,1792]{1,0:T(8,128)(2,1)S(1)}, bf16[96,1792]{1,0:T(8,128)(2,1)S(1)}) custom-call(s32[2]{0:T(128)S(1)} %copy-done.1, s32[128]{0:T(128)S(1)} %copy-done.4, bf16[96,512]{1,0:T(8,128)(2,1)S(1)} %slice.26.rows_ref, bf16[1,512,14336]{2,1,0:T(8,128)(2,1)} %refs_3_.15, bf16[1,512,14336]{2,1,0:T(8,128)(2,1)} %refs_3_.15, ...), custom_call_target="tpu_custom_call" | custom-call | flops 352321536 | bytes 3670016 | tf_op jit(solution)/shard_map/column_piece/pallas_call | solution.py:119
  30.6 1.4 %collective-permute-done = bf16[96,1792]{1,0:T(8,128)(2,1)S(1)} collective-permute-done((bf16[96,1792]{1,0:T(8,128)(2,1)S(1)}, bf16[96,1792]{1,0:T(8,128)(2,1)S(1)}, u32[]{:S(2)}, u32[]{:S(2)}) %collective-permute-start) | collective-permute-done | bytes 344096 | tf_op jit(solution)/shard_map/ppermute | solution.py:308
  32.1 1.1 collective-permute-done.1
  33.1 0.2 add_convert_fusion.10
  33.3 0.9 collective-permute-start.2
  34.2 1.1 collective-permute-start.3
  35.4 3.3 %column_piece.10 = (bf16[96,1792]{1,0:T(8,128)(2,1)S(1)}, bf16[96,1792]{1,0:T(8,128)(2,1)S(1)}) custom-call(s32[2]{0:T(128)S(1)} %copy-done.1, s32[128]{0:T(128)S(1)} %copy-done.4, bf16[96,512]{1,0:T(8,128)(2,1)S(1)} %slice.26.rows_ref, bf16[1,512,14336]{2,1,0:T(8,128)(2,1)} %refs_3_.15, bf16[1,512,14336]{2,1,0:T(8,128)(2,1)} %refs_3_.15, ...), custom_call_target="tpu_custom_call" | custom-call | flops 352321536 | bytes 3670016 | tf_op jit(solution)/shard_map/column_piece/pallas_call | solution.py:119
  38.7 3.6 %collective-permute-done.2 = bf16[96,1792]{1,0:T(8,128)(2,1)S(1)} collective-permute-done((bf16[96,1792]{1,0:T(8,128)(2,1)S(1)}, bf16[96,1792]{1,0:T(8,128)(2,1)S(1)}, u32[]{:S(2)}, u32[]{:S(2)}) %collective-permute-start.2) | collective-permute-done | bytes 344096 | tf_op jit(solution)/shard_map/ppermute | solution.py:308
  42.2 0.6 collective-permute-done.3
  43.0 0.7 collective-permute-start.5
  43.7 1.4 %collective-permute-start.6 = (bf16[96,1792]{1,0:T(8,128)(2,1)S(1)}, bf16[96,1792]{1,0:T(8,128)(2,1)S(1)}, u32[]{:S(2)}, u32[]{:S(2)}) collective-permute-start(bf16[96,1792]{1,0:T(8,128)(2,1)S(1)} %add_convert_fusion.8), channel_id=1, source_target_pairs={{2,0},{4,2},{6,4},{7,6},{5,7},{3,5},{1,3},{0,1},{10,8},{12,10},{14... | collective-permute-start | bytes 1032200 | tf_op jit(solution)/shard_map/ppermute | solution.py:309
  45.1 3.3 %column_piece.11 = (bf16[96,1792]{1,0:T(8,128)(2,1)S(1)}, bf16[96,1792]{1,0:T(8,128)(2,1)S(1)}) custom-call(s32[2]{0:T(128)S(1)} %copy-done.1, s32[128]{0:T(128)S(1)} %copy-done.4, bf16[96,512]{1,0:T(8,128)(2,1)S(1)} %slice.26.rows_ref, bf16[1,512,14336]{2,1,0:T(8,128)(2,1)} %refs_3_.15, bf16[1,512,14336]{2,1,0:T(8,128)(2,1)} %refs_3_.15, ...), custom_call_target="tpu_custom_call" | custom-call | flops 352321536 | bytes 3670016 | tf_op jit(solution)/shard_map/column_piece/pallas_call | solution.py:119
  48.5 2.4 %collective-permute-done.5 = bf16[96,1792]{1,0:T(8,128)(2,1)S(1)} collective-permute-done((bf16[96,1792]{1,0:T(8,128)(2,1)S(1)}, bf16[96,1792]{1,0:T(8,128)(2,1)S(1)}, u32[]{:S(2)}, u32[]{:S(2)}) %collective-permute-start.5) | collective-permute-done | bytes 344096 | tf_op jit(solution)/shard_map/ppermute | solution.py:308
  50.8 0.6 collective-permute-done.6
  51.6 0.5 collective-permute-start.7
  52.0 1.6 %collective-permute-start.8 = (bf16[96,1792]{1,0:T(8,128)(2,1)S(1)}, bf16[96,1792]{1,0:T(8,128)(2,1)S(1)}, u32[]{:S(2)}, u32[]{:S(2)}) collective-permute-start(bf16[96,1792]{1,0:T(8,128)(2,1)S(1)} %add_convert_fusion.6), channel_id=1, source_target_pairs={{2,0},{4,2},{6,4},{7,6},{5,7},{3,5},{1,3},{0,1},{10,8},{12,10},{14... | collective-permute-start | bytes 1032200 | tf_op jit(solution)/shard_map/ppermute | solution.py:309
  53.7 0.3 convert_add_fusion
  54.0 0.7 collective-permute-start.11
  54.7 3.3 %column_piece.12 = (bf16[96,1792]{1,0:T(8,128)(2,1)S(1)}, bf16[96,1792]{1,0:T(8,128)(2,1)S(1)}) custom-call(s32[2]{0:T(128)S(1)} %copy-done.1, s32[128]{0:T(128)S(1)} %copy-done.4, bf16[96,512]{1,0:T(8,128)(2,1)S(1)} %slice.26.rows_ref, bf16[1,512,14336]{2,1,0:T(8,128)(2,1)} %refs_3_.15, bf16[1,512,14336]{2,1,0:T(8,128)(2,1)} %refs_3_.15, ...), custom_call_target="tpu_custom_call" | custom-call | flops 352321536 | bytes 3670016 | tf_op jit(solution)/shard_map/column_piece/pallas_call | solution.py:119
  58.0 2.1 %collective-permute-done.7 = bf16[96,1792]{1,0:T(8,128)(2,1)S(1)} collective-permute-done((bf16[96,1792]{1,0:T(8,128)(2,1)S(1)}, bf16[96,1792]{1,0:T(8,128)(2,1)S(1)}, u32[]{:S(2)}, u32[]{:S(2)}) %collective-permute-start.7) | collective-permute-done | bytes 344096 | tf_op jit(solution)/shard_map/ppermute | solution.py:308
  60.3 0.9 collective-permute-start.9
  61.2 1.5 %collective-permute-start.10 = (bf16[96,1792]{1,0:T(8,128)(2,1)S(1)}, bf16[96,1792]{1,0:T(8,128)(2,1)S(1)}, u32[]{:S(2)}, u32[]{:S(2)}) collective-permute-start(bf16[96,1792]{1,0:T(8,128)(2,1)S(1)} %add_convert_fusion.4), channel_id=1, source_target_pairs={{2,0},{4,2},{6,4},{7,6},{5,7},{3,5},{1,3},{0,1},{10,8},{12,10},{14... | collective-permute-start | bytes 1032200 | tf_op jit(solution)/shard_map/ppermute | solution.py:309
  62.7 3.3 %column_piece.13 = (bf16[96,1792]{1,0:T(8,128)(2,1)S(1)}, bf16[96,1792]{1,0:T(8,128)(2,1)S(1)}) custom-call(s32[2]{0:T(128)S(1)} %copy-done.1, s32[128]{0:T(128)S(1)} %copy-done.4, bf16[96,512]{1,0:T(8,128)(2,1)S(1)} %slice.26.rows_ref, bf16[1,512,14336]{2,1,0:T(8,128)(2,1)} %refs_3_.15, bf16[1,512,14336]{2,1,0:T(8,128)(2,1)} %refs_3_.15, ...), custom_call_target="tpu_custom_call" | custom-call | flops 352321536 | bytes 3670016 | tf_op jit(solution)/shard_map/column_piece/pallas_call | solution.py:119
  66.1 2.8 %collective-permute-done.9 = bf16[96,1792]{1,0:T(8,128)(2,1)S(1)} collective-permute-done((bf16[96,1792]{1,0:T(8,128)(2,1)S(1)}, bf16[96,1792]{1,0:T(8,128)(2,1)S(1)}, u32[]{:S(2)}, u32[]{:S(2)}) %collective-permute-start.9) | collective-permute-done | bytes 344096 | tf_op jit(solution)/shard_map/ppermute | solution.py:308
  68.8 0.1 collective-permute-done.10
  69.0 1.0 fusion.2
  70.1 2.7 %collective-permute-start.12 = (bf16[96,1792]{1,0:T(8,128)(2,1)S(1)}, bf16[96,1792]{1,0:T(8,128)(2,1)S(1)}, u32[]{:S(2)}, u32[]{:S(2)}) collective-permute-start(bf16[96,1792]{1,0:T(8,128)(2,1)S(1)} %add_convert_fusion.3), channel_id=1, source_target_pairs={{0,2},{2,4},{4,6},{6,7},{7,5},{5,3},{3,1},{1,0},{8,10},{10,12},{12... | collective-permute-start | bytes 1032200 | tf_op jit(solution)/shard_map/ppermute | solution.py:308
  72.8 3.3 %column_piece.14 = (bf16[96,1792]{1,0:T(8,128)(2,1)S(1)}, bf16[96,1792]{1,0:T(8,128)(2,1)S(1)}) custom-call(s32[2]{0:T(128)S(1)} %copy-done.1, s32[128]{0:T(128)S(1)} %copy-done.4, bf16[96,512]{1,0:T(8,128)(2,1)S(1)} %slice.26.rows_ref, bf16[1,512,14336]{2,1,0:T(8,128)(2,1)} %refs_3_.15, bf16[1,512,14336]{2,1,0:T(8,128)(2,1)} %refs_3_.15, ...), custom_call_target="tpu_custom_call" | custom-call | flops 352321536 | bytes 3670016 | tf_op jit(solution)/shard_map/column_piece/pallas_call | solution.py:119
  76.2 4.8 %collective-permute-done.12 = bf16[96,1792]{1,0:T(8,128)(2,1)S(1)} collective-permute-done((bf16[96,1792]{1,0:T(8,128)(2,1)S(1)}, bf16[96,1792]{1,0:T(8,128)(2,1)S(1)}, u32[]{:S(2)}, u32[]{:S(2)}) %collective-permute-start.12) | collective-permute-done | bytes 344096 | tf_op jit(solution)/shard_map/ppermute | solution.py:308
  81.0 3.2 %collective-permute-done.13 = bf16[96,1792]{1,0:T(8,128)(2,1)S(1)} collective-permute-done((bf16[96,1792]{1,0:T(8,128)(2,1)S(1)}, bf16[96,1792]{1,0:T(8,128)(2,1)S(1)}, u32[]{:S(2)}, u32[]{:S(2)}) %collective-permute-start.13) | collective-permute-done | bytes 344096 | tf_op jit(solution)/shard_map/ppermute | solution.py:309
  84.3 1.8 %collective-permute-start.14 = (bf16[96,1792]{1,0:T(8,128)(2,1)S(1)}, bf16[96,1792]{1,0:T(8,128)(2,1)S(1)}, u32[]{:S(2)}, u32[]{:S(2)}) collective-permute-start(bf16[96,1792]{1,0:T(8,128)(2,1)S(1)} %add_convert_fusion.1), channel_id=1, source_target_pairs={{0,2},{2,4},{4,6},{6,7},{7,5},{5,3},{3,1},{1,0},{8,10},{10,12},{12... | collective-permute-start | bytes 1032200 | tf_op jit(solution)/shard_map/ppermute | solution.py:308
  86.1 0.3 collective-permute-start.15
  86.4 0.7 slice.29.tail_ref
  87.1 3.3 %column_piece.15 = (bf16[96,1792]{1,0:T(8,128)(2,1)S(1)}, bf16[96,1792]{1,0:T(8,128)(2,1)S(1)}) custom-call(s32[2]{0:T(128)S(1)} %copy-done.1, s32[128]{0:T(128)S(1)} %copy-done.4, bf16[96,512]{1,0:T(8,128)(2,1)S(1)} %slice.26.rows_ref, bf16[1,512,14336]{2,1,0:T(8,128)(2,1)} %refs_3_.15, bf16[1,512,14336]{2,1,0:T(8,128)(2,1)} %refs_3_.15, ...), custom_call_target="tpu_custom_call" | custom-call | flops 352321536 | bytes 3670016 | tf_op jit(solution)/shard_map/column_piece/pallas_call | solution.py:119
  90.5 1.1 collective-permute-done.14.gate_ref
  91.6 1.7 %collective-permute-done.15.up_ref = bf16[96,1792]{1,0:T(8,128)(2,1)S(1)} collective-permute-done((bf16[96,1792]{1,0:T(8,128)(2,1)S(1)}, bf16[96,1792]{1,0:T(8,128)(2,1)S(1)}, u32[]{:S(2)}, u32[]{:S(2)}) %collective-permute-start.15) | collective-permute-done | bytes 344096 | tf_op jit(solution)/shard_map/ppermute | solution.py:309
  93.4 9.7 %expert_outputs.1 = (f32[64,4096]{1,0:T(8,128)S(1)}, bf16[64,4096]{1,0:T(8,128)(2,1)S(1)}) custom-call(s32[2]{0:T(128)S(1)} %copy-done.1, bf16[96,1792]{1,0:T(8,128)(2,1)S(1)} %collective-permute-done.14.gate_ref, bf16[96,1792]{1,0:T(8,128)(2,1)S(1)} %collective-permute-done.15.up_ref, bf16[96,1792]{1,0:T(8,128)(2,1)S(1)} %get-tuple-element.158.gate_own_ref, ...), custom_call_target="tpu_custom_call" | custom-call | flops 1879048192 | bytes 14680064 | tf_op jit(solution)/shard_map/expert_outputs/pallas_call | solution.py:232
  103.2 1.9 %collective-permute-done.16 = bf16[2,32,4096]{2,1,0:T(8,128)(2,1)S(1)} collective-permute-done((bf16[2,32,4096]{2,1,0:T(8,128)(2,1)S(1)}, bf16[2,32,4096]{2,1,0:T(8,128)(2,1)S(1)}, u32[]{:S(2)}, u32[]{:S(2)}) %collective-permute-start.16) | collective-permute-done | bytes 524320 | tf_op jit(solution)/shard_map/ppermute | solution.py:346
  105.3 8.3 %collective-permute-done.17 = bf16[32,4096]{1,0:T(8,128)(2,1)S(1)} collective-permute-done((bf16[32,4096]{1,0:T(8,128)(2,1)S(1)}, bf16[32,4096]{1,0:T(8,128)(2,1)S(1)}, u32[]{:S(2)}, u32[]{:S(2)}) %collective-permute-start.17) | collective-permute-done | bytes 262176 | tf_op jit(solution)/shard_map/ppermute | solution.py:350
  113.8 11.4 %all_to_all.11 = bf16[8,4,4096]{2,1,0:T(4,128)(2,1)S(1)} all-to-all(bf16[8,4,4096]{2,1,0:T(4,128)(2,1)S(1)} %reshape.17), channel_id=1, replica_groups=mesh['branch'=4,'shard'=8] {'shard'}, dimensions={0} | all-to-all | bytes 524288 | tf_op jit(solution)/shard_map/all_to_all | solution.py:353
  125.2 0.7 reduce_sum.12
  (38 shorter events, 1.6 us)
Async XLA Ops:
  0.7 21.1 %copy-start = (s32[2]{0:T(128)}, s32[2]{0:T(128)S(1)}, u32[]{:S(2)}) copy-start(s32[2]{0:T(128)S(1)} %pad_add_fusion.where_ref) | copy-start | bytes 28
  17.8 4.1 %copy-start.6 = (bf16[96,640]{1,0:T(8,128)(2,1)}, bf16[96,640]{1,0:T(8,128)(2,1)S(1)}, u32[]{:S(2)}) copy-start(bf16[96,640]{1,0:T(8,128)(2,1)S(1)} %reshape.15) | copy-start | bytes 368644
  17.8 0.7 copy-start.3
  21.9 5.4 %copy-start.1 = (s32[2]{0:T(128)S(1)}, s32[2]{0:T(128)}, u32[]{:S(2)}) copy-start(s32[2]{0:T(128)} %copy-done) | copy-start | bytes 28
  21.9 5.4 %copy-start.4 = (s32[128]{0:T(128)S(1)}, s32[128]{0:T(128)}, u32[]{:S(2)}) copy-start(s32[128]{0:T(128)} %constant.18.clone.table_ref) | copy-start | bytes 1540
  21.9 10.2 %collective-permute-start = (bf16[96,1792]{1,0:T(8,128)(2,1)S(1)}, bf16[96,1792]{1,0:T(8,128)(2,1)S(1)}, u32[]{:S(2)}, u32[]{:S(2)}) collective-permute-start(bf16[96,1792]{1,0:T(8,128)(2,1)S(1)} %get-tuple-element.88), channel_id=1, source_target_pairs={{0,2},{2,4},{4,6},{6,7},{7,5},{5,3},{3,1},{1,0},{8,10},{10,12},{12... | collective-permute-start | bytes 1032200 | tf_op jit(solution)/shard_map/ppermute | solution.py:308
  23.3 9.8 %collective-permute-start.1 = (bf16[96,1792]{1,0:T(8,128)(2,1)S(1)}, bf16[96,1792]{1,0:T(8,128)(2,1)S(1)}, u32[]{:S(2)}, u32[]{:S(2)}) collective-permute-start(bf16[96,1792]{1,0:T(8,128)(2,1)S(1)} %get-tuple-element.89), channel_id=1, source_target_pairs={{2,0},{4,2},{6,4},{7,6},{5,7},{3,5},{1,3},{0,1},{10,8},{12,10},{14... | collective-permute-start | bytes 1032200 | tf_op jit(solution)/shard_map/ppermute | solution.py:309
  27.3 15.7 %collective-permute-start.4 = (bf16[2,512,512]{2,1,0:T(8,128)(2,1)}, bf16[2,512,512]{2,1,0:T(8,128)(2,1)S(1)}, u32[]{:S(2)}, u32[]{:S(2)}) collective-permute-start(bf16[2,512,512]{2,1,0:T(8,128)(2,1)} %get-tuple-element.95), channel_id=1, source_target_pairs={{0,8},{8,0},{16,24},{24,16},{1,9},{9,1},{17,25},{25,17},{2,10},{10... | collective-permute-start | bytes 3145736 | tf_op jit(solution)/shard_map/ppermute | solution.py:318
  33.3 9.0 %collective-permute-start.2 = (bf16[96,1792]{1,0:T(8,128)(2,1)S(1)}, bf16[96,1792]{1,0:T(8,128)(2,1)S(1)}, u32[]{:S(2)}, u32[]{:S(2)}) collective-permute-start(bf16[96,1792]{1,0:T(8,128)(2,1)S(1)} %get-tuple-element.100), channel_id=1, source_target_pairs={{0,2},{2,4},{4,6},{6,7},{7,5},{5,3},{3,1},{1,0},{8,10},{10,12},{12... | collective-permute-start | bytes 1032200 | tf_op jit(solution)/shard_map/ppermute | solution.py:308
  34.2 8.6 %collective-permute-start.3 = (bf16[96,1792]{1,0:T(8,128)(2,1)S(1)}, bf16[96,1792]{1,0:T(8,128)(2,1)S(1)}, u32[]{:S(2)}, u32[]{:S(2)}) collective-permute-start(bf16[96,1792]{1,0:T(8,128)(2,1)S(1)} %get-tuple-element.101), channel_id=1, source_target_pairs={{2,0},{4,2},{6,4},{7,6},{5,7},{3,5},{1,3},{0,1},{10,8},{12,10},{14... | collective-permute-start | bytes 1032200 | tf_op jit(solution)/shard_map/ppermute | solution.py:309
  43.0 7.8 %collective-permute-start.5 = (bf16[96,1792]{1,0:T(8,128)(2,1)S(1)}, bf16[96,1792]{1,0:T(8,128)(2,1)S(1)}, u32[]{:S(2)}, u32[]{:S(2)}) collective-permute-start(bf16[96,1792]{1,0:T(8,128)(2,1)S(1)} %add_convert_fusion.9), channel_id=1, source_target_pairs={{0,2},{2,4},{4,6},{6,7},{7,5},{5,3},{3,1},{1,0},{8,10},{10,12},{12... | collective-permute-start | bytes 1032200 | tf_op jit(solution)/shard_map/ppermute | solution.py:308
  43.7 7.7 %collective-permute-start.6 = (bf16[96,1792]{1,0:T(8,128)(2,1)S(1)}, bf16[96,1792]{1,0:T(8,128)(2,1)S(1)}, u32[]{:S(2)}, u32[]{:S(2)}) collective-permute-start(bf16[96,1792]{1,0:T(8,128)(2,1)S(1)} %add_convert_fusion.8), channel_id=1, source_target_pairs={{2,0},{4,2},{6,4},{7,6},{5,7},{3,5},{1,3},{0,1},{10,8},{12,10},{14... | collective-permute-start | bytes 1032200 | tf_op jit(solution)/shard_map/ppermute | solution.py:309
  48.4 5.2 %copy-start.5 = (bf16[2,512,512]{2,1,0:T(8,128)(2,1)S(1)}, bf16[2,512,512]{2,1,0:T(8,128)(2,1)}, u32[]{:S(2)}) copy-start(bf16[2,512,512]{2,1,0:T(8,128)(2,1)} %get-tuple-element.134) | copy-start | bytes 3145732
  51.6 8.5 %collective-permute-start.7 = (bf16[96,1792]{1,0:T(8,128)(2,1)S(1)}, bf16[96,1792]{1,0:T(8,128)(2,1)S(1)}, u32[]{:S(2)}, u32[]{:S(2)}) collective-permute-start(bf16[96,1792]{1,0:T(8,128)(2,1)S(1)} %add_convert_fusion.7), channel_id=1, source_target_pairs={{0,2},{2,4},{4,6},{6,7},{7,5},{5,3},{3,1},{1,0},{8,10},{10,12},{12... | collective-permute-start | bytes 1032200 | tf_op jit(solution)/shard_map/ppermute | solution.py:308
  52.0 8.1 %collective-permute-start.8 = (bf16[96,1792]{1,0:T(8,128)(2,1)S(1)}, bf16[96,1792]{1,0:T(8,128)(2,1)S(1)}, u32[]{:S(2)}, u32[]{:S(2)}) collective-permute-start(bf16[96,1792]{1,0:T(8,128)(2,1)S(1)} %add_convert_fusion.6), channel_id=1, source_target_pairs={{2,0},{4,2},{6,4},{7,6},{5,7},{3,5},{1,3},{0,1},{10,8},{12,10},{14... | collective-permute-start | bytes 1032200 | tf_op jit(solution)/shard_map/ppermute | solution.py:309
  54.0 14.9 %collective-permute-start.11 = (bf16[512,512]{1,0:T(8,128)(2,1)S(1)}, bf16[512,512]{1,0:T(8,128)(2,1)S(1)}, u32[]{:S(2)}, u32[]{:S(2)}) collective-permute-start(bf16[512,512]{1,0:T(8,128)(2,1)S(1)} %fusion.3), channel_id=1, source_target_pairs={{0,16},{8,24},{16,0},{24,8},{1,17},{9,25},{17,1},{25,9},{2,18},{10... | collective-permute-start | bytes 1572872 | tf_op jit(solution)/shard_map/ppermute | solution.py:326
  60.3 8.5 %collective-permute-start.9 = (bf16[96,1792]{1,0:T(8,128)(2,1)S(1)}, bf16[96,1792]{1,0:T(8,128)(2,1)S(1)}, u32[]{:S(2)}, u32[]{:S(2)}) collective-permute-start(bf16[96,1792]{1,0:T(8,128)(2,1)S(1)} %add_convert_fusion.5), channel_id=1, source_target_pairs={{0,2},{2,4},{4,6},{6,7},{7,5},{5,3},{3,1},{1,0},{8,10},{10,12},{12... | collective-permute-start | bytes 1032200 | tf_op jit(solution)/shard_map/ppermute | solution.py:308
  61.2 7.8 %collective-permute-start.10 = (bf16[96,1792]{1,0:T(8,128)(2,1)S(1)}, bf16[96,1792]{1,0:T(8,128)(2,1)S(1)}, u32[]{:S(2)}, u32[]{:S(2)}) collective-permute-start(bf16[96,1792]{1,0:T(8,128)(2,1)S(1)} %add_convert_fusion.4), channel_id=1, source_target_pairs={{2,0},{4,2},{6,4},{7,6},{5,7},{3,5},{1,3},{0,1},{10,8},{12,10},{14... | collective-permute-start | bytes 1032200 | tf_op jit(solution)/shard_map/ppermute | solution.py:309
  70.1 10.9 %collective-permute-start.12 = (bf16[96,1792]{1,0:T(8,128)(2,1)S(1)}, bf16[96,1792]{1,0:T(8,128)(2,1)S(1)}, u32[]{:S(2)}, u32[]{:S(2)}) collective-permute-start(bf16[96,1792]{1,0:T(8,128)(2,1)S(1)} %add_convert_fusion.3), channel_id=1, source_target_pairs={{0,2},{2,4},{4,6},{6,7},{7,5},{5,3},{3,1},{1,0},{8,10},{10,12},{12... | collective-permute-start | bytes 1032200 | tf_op jit(solution)/shard_map/ppermute | solution.py:308
  72.8 11.3 %collective-permute-start.13 = (bf16[96,1792]{1,0:T(8,128)(2,1)S(1)}, bf16[96,1792]{1,0:T(8,128)(2,1)S(1)}, u32[]{:S(2)}, u32[]{:S(2)}) collective-permute-start(bf16[96,1792]{1,0:T(8,128)(2,1)S(1)} %add_convert_fusion.2), channel_id=1, source_target_pairs={{2,0},{4,2},{6,4},{7,6},{5,7},{3,5},{1,3},{0,1},{10,8},{12,10},{14... | collective-permute-start | bytes 1032200 | tf_op jit(solution)/shard_map/ppermute | solution.py:309
  84.3 7.3 %collective-permute-start.14 = (bf16[96,1792]{1,0:T(8,128)(2,1)S(1)}, bf16[96,1792]{1,0:T(8,128)(2,1)S(1)}, u32[]{:S(2)}, u32[]{:S(2)}) collective-permute-start(bf16[96,1792]{1,0:T(8,128)(2,1)S(1)} %add_convert_fusion.1), channel_id=1, source_target_pairs={{0,2},{2,4},{4,6},{6,7},{7,5},{5,3},{3,1},{1,0},{8,10},{10,12},{12... | collective-permute-start | bytes 1032200 | tf_op jit(solution)/shard_map/ppermute | solution.py:308
  86.1 7.2 %collective-permute-start.15 = (bf16[96,1792]{1,0:T(8,128)(2,1)S(1)}, bf16[96,1792]{1,0:T(8,128)(2,1)S(1)}, u32[]{:S(2)}, u32[]{:S(2)}) collective-permute-start(bf16[96,1792]{1,0:T(8,128)(2,1)S(1)} %add_convert_fusion), channel_id=1, source_target_pairs={{2,0},{4,2},{6,4},{7,6},{5,7},{3,5},{1,3},{0,1},{10,8},{12,10},{14... | collective-permute-start | bytes 1032200 | tf_op jit(solution)/shard_map/ppermute | solution.py:309
  87.1 6.2 %copy-start.2 = (f32[96,128]{1,0:T(8,128)S(1)}, f32[96,128]{1,0:T(8,128)}, u32[]{:S(2)}) copy-start(f32[96,128]{1,0:T(8,128)} %constant.19.clone.origin_ref) | copy-start | bytes 147460
  103.1 2.0 %collective-permute-start.16 = (bf16[2,32,4096]{2,1,0:T(8,128)(2,1)S(1)}, bf16[2,32,4096]{2,1,0:T(8,128)(2,1)S(1)}, u32[]{:S(2)}, u32[]{:S(2)}) collective-permute-start(bf16[2,32,4096]{2,1,0:T(8,128)(2,1)S(1)} %bitcast.25), channel_id=1, source_target_pairs={{0,8},{8,0},{16,24},{24,16},{1,9},{9,1},{17,25},{25,17},{2,10},{10... | collective-permute-start | bytes 1572872 | tf_op jit(solution)/shard_map/ppermute | solution.py:346
  105.2 8.4 %collective-permute-start.17 = (bf16[32,4096]{1,0:T(8,128)(2,1)S(1)}, bf16[32,4096]{1,0:T(8,128)(2,1)S(1)}, u32[]{:S(2)}, u32[]{:S(2)}) collective-permute-start(bf16[32,4096]{1,0:T(8,128)(2,1)S(1)} %fusion.6), channel_id=1, source_target_pairs={{0,16},{8,24},{16,0},{24,8},{1,17},{9,25},{17,1},{25,9},{2,18},{10... | collective-permute-start | bytes 786440 | tf_op jit(solution)/shard_map/ppermute | solution.py:350

commit v7 on v6

--- a/solution.py
+++ b/solution.py
@@ -28,6 +28,16 @@
         line = xs[1:] if i % 2 == 0 else list(reversed(xs[1:]))
         order += [at[(z, x)] for x in line]
     return order
+
+
+def grid_columns(devices):
+    places = [getattr(d, "coords", None) for d in devices]
+    if any(p is None for p in places):
+        return 1
+    columns = len({p[0] for p in places})
+    line = sorted(range(len(places)), key=lambda i: (places[i][2], places[i][0]))
+    whole = len({(p[2], p[0]) for p in places}) == len(places)
+    return columns if whole and line == list(range(len(places))) and len(places) % columns == 0 else 1
 
 
 def core_count(devices):
@@ -175,72 +185,91 @@
 
 
 def expert_outputs(where, gate_in, up_in, gate_own, up_own, tails, origin, down_weight, sizes):
-    experts, shards, cores, token_count = sizes
-    chips = experts // cores
+    experts, shards, cores, columns, token_count = sizes
+    chips, lines = experts // cores, shards // columns
     count, slice_width = gate_in.shape
     width = down_weight.shape[2]
     total = experts * shards * token_count
     kept = total // cores
-    block = 512 if width % 512 == 0 else width
-    parts = row_parts(slice_width)
-    chunk = next(c for c in (256, 128, slice_width) if slice_width % c == 0)
-
-    def kernel(where_ref, gate_ref, up_ref, gate_own_ref, up_own_ref, tail_ref, origin_ref, *rest):
-        hidden_ref = rest[-1]
-        weights, outs = rest[:parts], rest[parts:-1]
-
-        @pl.when(pl.program_id(0) == 0)
+    block = 256 if slice_width % 256 == 0 else slice_width
+    steps = slice_width // block
+    chunk = 512 if width % 512 == 0 else width
+
+    def kernel(where_ref, gate_ref, up_ref, gate_own_ref, up_own_ref, tail_ref, origin_ref, down_ref, *rest):
+        outs, spread_ref, sum_ref = rest[:-2], rest[-2], rest[-1]
+        step = pl.program_id(0)
+        tail = tail_ref[...].astype(F32)
+        weight = tail[:, 1:2] + tail[:, 2:3]
+
+        @pl.when(step == 0)
         def _():
-            b = where_ref[0]
-            tail = tail_ref[...].astype(F32)
-            place = origin_ref[...]
-            number, weight = tail[:, 0:1], tail[:, 1:2] + tail[:, 2:3]
-            chip = place[:, 0:1] - lax.div(b, jnp.int32(cores)).astype(F32)
-            core = place[:, 1:2] - lax.rem(b, jnp.int32(cores)).astype(F32)
-            chip = jnp.where(chip < 0, chip + chips, chip)
-            core = jnp.where(core < 0, core + cores, core)
-            target = (core * chips + chip) * (shards * token_count) + place[:, 2:3] + number - 1.0
+            b, s = where_ref[0], where_ref[1]
+            mine = (
+                lax.rem(b, jnp.int32(cores)), lax.div(b, jnp.int32(cores)),
+                lax.rem(s, jnp.int32(columns)), lax.div(s, jnp.int32(columns)),
+            )
+            number, place = tail[:, 0:1], origin_ref[...]
+            target = jnp.zeros((count, 1), F32)
+            for i, size in enumerate((cores, chips, columns, lines)):
+                away = place[:, i : i + 1] - mine[i].astype(F32)
+                target = target * size + jnp.where(away < 0, away + size, away)
+            target = target * token_count + number - 1.0
             target = jnp.where(number > 0, target, -1.0).astype(jnp.int32)
             spread = target == lax.broadcasted_iota(jnp.int32, (count, total), 1)
-            spread = spread.astype(F32).astype(BF16)
-            for at in range(0, slice_width, chunk):
+            spread_ref[...] = spread.astype(F32).astype(BF16)
+
+        gate = gate_ref[...].astype(F32) + gate_own_ref[...].astype(F32)
+        upper = up_ref[...].astype(F32) + up_own_ref[...].astype(F32)
+        hidden = (gate / (1.0 + jnp.exp(-gate)) * upper * weight).astype(BF16)
+        hidden = lax.dot_general(
+            spread_ref[...], hidden, (((0,), (0,)), ((), ())), preferred_element_type=F32
+        ).astype(BF16)
+
+        def add(first):
+            for at in range(0, width, chunk):
                 cut = slice(at, at + chunk)
-                gate = gate_ref[:, cut].astype(F32) + gate_own_ref[:, cut].astype(F32)
-                upper = up_ref[:, cut].astype(F32) + up_own_ref[:, cut].astype(F32)
-                hidden = (gate / (1.0 + jnp.exp(-gate)) * upper * weight).astype(BF16)
-                hidden_ref[:, cut] = lax.dot_general(
-                    spread, hidden, (((0,), (0,)), ((), ())), preferred_element_type=F32
-                ).astype(BF16)
-
-        weight = [ref[0] for ref in weights]
-        weight = jnp.concatenate(weight, axis=0) if parts > 1 else weight[0]
-        value = jnp.dot(hidden_ref[...], weight, preferred_element_type=F32)
-        outs[0][...] = value[:kept]
+                value = jnp.dot(hidden, down_ref[0, :, cut], preferred_element_type=F32)
+                if first:
+                    outs[0][:, cut] = value[:kept]
+                    if cores > 1:
+                        sum_ref[:, cut] = value[kept:]
+                else:
+                    outs[0][:, cut] += value[:kept]
+                    if cores > 1:
+                        sum_ref[:, cut] += value[kept:]
+
+        pl.when(step == 0)(lambda: add(True))
+        pl.when(step > 0)(lambda: add(False))
         if cores > 1:
-            outs[1][...] = value[kept:].astype(BF16)
-
-    def weight_block(part):
-        return pl.BlockSpec((1, slice_width // parts, block), lambda j, *_: (0, part, j))
-
-    whole = pl.BlockSpec((count, slice_width), lambda j, *_: (0, 0))
+
+            @pl.when(step == steps - 1)
+            def _():
+                for at in range(0, width, chunk):
+                    cut = slice(at, at + chunk)
+                    outs[1][:, cut] = sum_ref[:, cut].astype(BF16)
+
+    part = pl.BlockSpec((count, block), lambda j, *_: (0, j))
     lanes = pl.BlockSpec((count, LANES), lambda j, *_: (0, 0))
     shapes = [jax.ShapeDtypeStruct((kept, width), F32)]
-    specs = [pl.BlockSpec((kept, block), lambda j, *_: (0, j))]
+    specs = [pl.BlockSpec((kept, width), lambda j, *_: (0, 0))]
     if cores > 1:
         shapes.append(jax.ShapeDtypeStruct((total - kept, width), BF16))
-        specs.append(pl.BlockSpec((total - kept, block), lambda j, *_: (0, j)))
+        specs.append(pl.BlockSpec((total - kept, width), lambda j, *_: (0, 0)))
     return pl.pallas_call(
         kernel,
         out_shape=shapes,
         grid_spec=pltpu.PrefetchScalarGridSpec(
             num_scalar_prefetch=1,
-            grid=(width // block,),
+            grid=(steps,),
             in_specs=[
-                whole, whole, whole, whole, lanes, lanes,
-            ]
-            + [weight_block(part) for part in range(parts)],
+                part, part, part, part, lanes, lanes,
+                pl.BlockSpec((1, block, width), lambda j, *_: (0, j, 0)),
+            ],
             out_specs=specs,
-            scratch_shapes=[pltpu.VMEM((total, slice_width), BF16)],
+            scratch_shapes=[
+                pltpu.VMEM((count, total), BF16),
+                pltpu.VMEM((max(total - kept, 8), width), F32),
+            ],
         ),
         compiler_params=pltpu.CompilerParams(vmem_limit_bytes=VMEM_LIMIT),
         cost_estimate=pl.CostEstimate(
@@ -249,7 +278,7 @@
             transcendentals=count * slice_width,
         ),
         name="expert_outputs",
-    )(where, gate_in, up_in, gate_own, up_own, tails, origin, *([down_weight] * parts))
+    )(where, gate_in, up_in, gate_own, up_own, tails, origin, down_weight)
 
 
 def branch_target(size, cores, core_step, chip_step):
@@ -260,7 +289,22 @@
     ]
 
 
-def local(order, cores, tokens, routes, mixing, gate_weight, up_weight, down_weight, key_value):
+def shard_target(size, columns, x_step, z_step):
+    lines = size // columns
+    return [
+        (i, (i // columns + z_step) % lines * columns + (i + x_step) % columns)
+        for i in range(size)
+    ]
+
+
+def direct_sum(x, axis_name, target):
+    total = x[0]
+    for k in range(1, x.shape[0]):
+        total = total + lax.ppermute(x[k].astype(BF16), axis_name, target(k)).astype(F32)
+    return total
+
+
+def local(order, cores, columns, tokens, routes, mixing, gate_weight, up_weight, down_weight, key_value):
     experts = lax.axis_size("branch")
     shards = lax.axis_size("shard")
     chips = experts // cores
@@ -269,7 +313,8 @@
     depth = gate_weight.shape[1]
     slice_width = down_weight.shape[1]
     count = experts * shards * capacity
-    sizes = (experts, shards, cores, token_count)
+    lines = shards // columns
+    sizes = (experts, shards, cores, columns, token_count)
     where = jnp.stack([lax.axis_index("branch"), lax.axis_index("shard")]).astype(jnp.int32)
 
     place = np.argsort(np.asarray(order))
@@ -283,9 +328,10 @@
     back = [(b, a) for a, b in forth]
     source = np.arange(count) // capacity
     origin = np.zeros((count, LANES), np.float32)
-    origin[:, 0] = source // shards // cores
-    origin[:, 1] = source // shards % cores
-    origin[:, 2] = source % shards * token_count
+    origin[:, 0] = source // shards % cores
+    origin[:, 1] = source // shards // cores
+    origin[:, 2] = source % shards % columns
+    origin[:, 3] = source % shards // columns
     origin = jnp.asarray(origin)
 
     cells = place_rows(tokens, routes, mixing, experts, capacity, shards)
@@ -304,12 +350,11 @@
     gate_sum, up_sum = gates[0], ups[0]
     last = shards - 1
     for t in range(1, shards):
-        now, gate_sum, up_sum = lax.optimization_barrier((where, gate_sum, up_sum))
+        now, gate_sum = lax.optimization_barrier((where, gate_sum))
         gate_in = lax.ppermute(gate_sum, "shard", forth)
         up_in = lax.ppermute(up_sum, "shard", back)
         if sliced:
             one = column_piece(now, table, rows, gate_weight, up_weight, shards, t, cuts)
-            gate_in, up_in, one = lax.optimization_barrier((gate_in, up_in, one))
             gates.append(one[0])
             ups.append(one[1])
         if t == 1:
@@ -340,26 +385,36 @@
     outputs = expert_outputs(
         where, gate_in, up_in, gates[last], ups[last], tails, origin, down_weight, sizes
     )
-    mixed = outputs[0].reshape(chips, shards * token_count, width)
+    mixed = outputs[0]
     for k in range(1, cores):
-        sent = outputs[1].reshape(cores - 1, chips, shards * token_count, width)[k - 1]
+        sent = outputs[1].reshape(cores - 1, -1, width)[k - 1]
         part = lax.ppermute(sent, "branch", branch_target(experts, cores, k, 0))
         mixed = mixed + part.astype(F32)
-    total = mixed[0]
-    for k in range(1, chips):
-        part = lax.ppermute(mixed[k].astype(BF16), "branch", branch_target(experts, cores, 0, k))
-        total = total + part.astype(F32)
-    total = total.astype(BF16).reshape(shards, token_count, width)
-    total = lax.all_to_all(total, "shard", split_axis=0, concat_axis=0, tiled=True)
-    return jnp.sum(total.astype(F32), axis=0).astype(BF16), merged_kv
+
+    def over_chips(x):
+        return direct_sum(x, "branch", lambda k: branch_target(experts, cores, 0, k))
+
+    def over_columns(x):
+        return direct_sum(x, "shard", lambda k: shard_target(shards, columns, k, 0))
+
+    def over_lines(x):
+        return direct_sum(x, "shard", lambda k: shard_target(shards, columns, 0, k))
+
+    mixed = mixed.reshape(chips, columns, lines * token_count, width)
+    left = over_chips(mixed[..., : width // 2])
+    right = over_columns(mixed[..., width // 2 :].swapaxes(0, 1))
+    left, right = over_columns(left), over_chips(right)
+    mixed = jnp.concatenate([left, right], axis=1).reshape(lines, token_count, width)
+    return over_lines(mixed).astype(BF16), merged_kv
 
 
 def solution(mesh):
     grid = mesh.devices
     order = ring_order(list(grid[0, :]))
     cores = core_count(list(grid[:, 0]))
+    columns = grid_columns(list(grid[0, :]))
     return jax.shard_map(
-        functools.partial(local, order, cores),
+        functools.partial(local, order, cores, columns),
         mesh=mesh,
         in_specs=(
             P(("branch", "shard"), None),

time: 127 us -> 122 us (0.961)
  starting transfers between devices: 16.3 us -> 28.3 us
  blocking collectives: 26.6 us -> 15.2 us
  waiting for transfers between devices: 35.7 us -> 30 us
    ppermute x7, waiting for transfers between devices: 18.2 us -> 6.4 us  [local(): gate_in = lax.ppermute(gate_sum, 'shard', forth)]
    all_to_all x1 -> x0, blocking collectives: 11.4 us -> none  [local(): lax.all_to_all(total, 'shard', split_axis=0, concat_axis=0, tiled=True)]
    ppermute x1 -> x7, starting transfers between devices: 0.07 us -> 8.04 us  [direct_sum(): lax.ppermute(x[k].astype(BF16), axis_name, target(k)).astype(F32)]
    ppermute x7, starting transfers between devices: 6.68 us -> 12.1 us  [local(): up_in = lax.ppermute(up_sum, 'shard', back)]
    ppermute x1 -> x7, waiting for transfers between devices: 8.33 us -> 11.8 us  [direct_sum(): lax.ppermute(x[k].astype(BF16), axis_name, target(k)).astype(F32)]
    ppermute x7, waiting for transfers between devices: 7.29 us -> 9.88 us  [local(): up_in = lax.ppermute(up_sum, 'shard', back)]
    ppermute x7, starting transfers between devices: 8.84 us -> 7.27 us  [local(): gate_in = lax.ppermute(gate_sum, 'shard', forth)]
  transfers between devices with their start and end apart: 18 -> 24, of which waited for: 15 -> 17; matrix products, arithmetic and copies ran while one was open for 1% -> 3% of each run, Pallas kernels for 21% -> 22%
where the time goes in v7:
time: 122 us
  Pallas kernels  42 us (34%)
  waiting for transfers between devices  30 us (25%)
  starting transfers between devices  28.3 us (23%)
  blocking collectives  15.2 us (12%)
  other arithmetic  3.16 us (3%)
  local copies, waits for them, and re-layouts  2.35 us (2%)
    pallas_call x8, Pallas kernels, column_piece(): pl.pallas_call(kernel, out_shape=[jax.ShapeDtypeStruct((count, width), BF...  26.5 us
    all_to_all x1, blocking collectives, local(): lax.all_to_all(cells, ('branch', 'shard'), split_axis=0, concat_axis=0, t...  15.2 us
    ppermute x7, starting transfers between devices, local(): up_in = lax.ppermute(up_sum, 'shard', back)  12.1 us
    ppermute x7, waiting for transfers between devices, direct_sum(): lax.ppermute(x[k].astype(BF16), axis_name, target(k)).astype(F32)  11.8 us
    pallas_call x1, Pallas kernels, expert_outputs(): pl.pallas_call(kernel, out_shape=shapes, grid_spec=pltpu.PrefetchScalarGr...  10.4 us
    ppermute x7, waiting for transfers between devices, local(): up_in = lax.ppermute(up_sum, 'shard', back)  9.88 us
    ppermute x7, starting transfers between devices, direct_sum(): lax.ppermute(x[k].astype(BF16), axis_name, target(k)).astype(F32)  8.04 us
    ppermute x7, starting transfers between devices, local(): gate_in = lax.ppermute(gate_sum, 'shard', forth)  7.27 us
  transfers between devices with their start and end apart: 24, of which 17 were waited for; matrix products, arithmetic and copies ran while one was open for 3% of the time, Pallas kernels for 22%

profile of v7, /device:TPU:0, one launch (start us, length us, event | category | flops | bytes accessed | tf_op | source)
XLA Modules:
  0.0 121.9 jit_solution(1913473976156787637)
XLA Ops:
  0.7 1.7 %place_rows.1 = bf16[32,3,640]{2,1,0:T(4,128)(2,1)} custom-call(bf16[4,4096]{1,0:T(4,128)(2,1)} %tokens_ref.1, s32[2,4]{1,0:T(2,128)} %bitcast.44, f32[2,4]{1,0:T(2,128)} %bitcast.45), custom_call_target="tpu_custom_call" | custom-call | tf_op jit(solution)/shard_map/place_rows/pallas_call | solution.py:93
  2.5 15.2 %all_to_all.5 = bf16[32,3,640]{2,1,0:T(4,128)(2,1)S(1)} all-to-all(bf16[32,3,640]{2,1,0:T(4,128)(2,1)} %place_rows.1), channel_id=1, replica_groups=mesh['branch'=4,'shard'=8] {'branch','shard'}, dimensions={0} | all-to-all | bytes 245760 | tf_op jit(solution)/shard_map/all_to_all | solution.py:339
  18.4 0.6 copy-done.3
  19.1 3.3 %column_piece.8 = (bf16[96,1792]{1,0:T(8,128)(2,1)S(1)}, bf16[96,1792]{1,0:T(8,128)(2,1)S(1)}) custom-call(s32[2]{0:T(128)S(1)} %pad_add_fusion.where_ref, s32[128]{0:T(128)S(1)} %copy-done.3, bf16[96,512]{1,0:T(8,128)(2,1)S(1)} %slice.83.rows_ref, bf16[1,512,14336]{2,1,0:T(8,128)(2,1)} %refs_3_.15, bf16[1,512,14336]{2,1,0:T(8,128)(2,1)} %refs_3_.15, ...), custom_call_target="tpu_custom_call" | custom-call | flops 352321536 | bytes 3670016 | tf_op jit(solution)/shard_map/column_piece/pallas_call | solution.py:129
  22.4 1.6 %collective-permute-start.9 = (bf16[96,1792]{1,0:T(8,128)(2,1)S(1)}, bf16[96,1792]{1,0:T(8,128)(2,1)S(1)}, u32[]{:S(2)}, u32[]{:S(2)}) collective-permute-start(bf16[96,1792]{1,0:T(8,128)(2,1)S(1)} %get-tuple-element.80), channel_id=1, source_target_pairs={{2,0},{4,2},{6,4},{7,6},{5,7},{3,5},{1,3},{0,1},{10,8},{12,10},{14... | collective-permute-start | bytes 1032200 | tf_op jit(solution)/shard_map/ppermute | solution.py:355
  24.5 3.3 %turn_columns.1 = (bf16[2,512,512]{2,1,0:T(8,128)(2,1)}, bf16[2,512,512]{2,1,0:T(8,128)(2,1)}) custom-call(s32[2]{0:T(128)} %copy-done, bf16[1,512,2048]{2,1,0:T(8,128)(2,1)} %refs_1_.10, bf16[1,512,2048]{2,1,0:T(8,128)(2,1)} %refs_1_.10), custom_call_target="tpu_custom_call" | custom-call | bytes 4194304 | tf_op jit(solution)/shard_map/turn_columns/pallas_call | solution.py:173
  27.8 3.3 %column_piece.9 = (bf16[96,1792]{1,0:T(8,128)(2,1)S(1)}, bf16[96,1792]{1,0:T(8,128)(2,1)S(1)}) custom-call(s32[2]{0:T(128)S(1)} %copy-done.1, s32[128]{0:T(128)S(1)} %copy-done.4, bf16[96,512]{1,0:T(8,128)(2,1)S(1)} %slice.83.rows_ref, bf16[1,512,14336]{2,1,0:T(8,128)(2,1)} %refs_3_.15, bf16[1,512,14336]{2,1,0:T(8,128)(2,1)} %refs_3_.15, ...), custom_call_target="tpu_custom_call" | custom-call | flops 352321536 | bytes 3670016 | tf_op jit(solution)/shard_map/column_piece/pallas_call | solution.py:129
  31.2 1.4 %collective-permute-done.9 = bf16[96,1792]{1,0:T(8,128)(2,1)S(1)} collective-permute-done((bf16[96,1792]{1,0:T(8,128)(2,1)S(1)}, bf16[96,1792]{1,0:T(8,128)(2,1)S(1)}, u32[]{:S(2)}, u32[]{:S(2)}) %collective-permute-start.9) | collective-permute-done | bytes 344096 | tf_op jit(solution)/shard_map/ppermute | solution.py:355
  32.7 1.5 %collective-permute-start.10 = (bf16[96,1792]{1,0:T(8,128)(2,1)S(1)}, bf16[96,1792]{1,0:T(8,128)(2,1)S(1)}, u32[]{:S(2)}, u32[]{:S(2)}) collective-permute-start(bf16[96,1792]{1,0:T(8,128)(2,1)S(1)} %add_convert_fusion.5), channel_id=1, source_target_pairs={{2,0},{4,2},{6,4},{7,6},{5,7},{3,5},{1,3},{0,1},{10,8},{12,10},{14... | collective-permute-start | bytes 1032200 | tf_op jit(solution)/shard_map/ppermute | solution.py:355
  34.9 3.3 %column_piece.10 = (bf16[96,1792]{1,0:T(8,128)(2,1)S(1)}, bf16[96,1792]{1,0:T(8,128)(2,1)S(1)}) custom-call(s32[2]{0:T(128)S(1)} %copy-done.1, s32[128]{0:T(128)S(1)} %copy-done.4, bf16[96,512]{1,0:T(8,128)(2,1)S(1)} %slice.83.rows_ref, bf16[1,512,14336]{2,1,0:T(8,128)(2,1)} %refs_3_.15, bf16[1,512,14336]{2,1,0:T(8,128)(2,1)} %refs_3_.15, ...), custom_call_target="tpu_custom_call" | custom-call | flops 352321536 | bytes 3670016 | tf_op jit(solution)/shard_map/column_piece/pallas_call | solution.py:129
  38.2 3.8 %collective-permute-done.10 = bf16[96,1792]{1,0:T(8,128)(2,1)S(1)} collective-permute-done((bf16[96,1792]{1,0:T(8,128)(2,1)S(1)}, bf16[96,1792]{1,0:T(8,128)(2,1)S(1)}, u32[]{:S(2)}, u32[]{:S(2)}) %collective-permute-start.10) | collective-permute-done | bytes 344096 | tf_op jit(solution)/shard_map/ppermute | solution.py:355
  42.1 1.5 %collective-permute-start.11 = (bf16[96,1792]{1,0:T(8,128)(2,1)S(1)}, bf16[96,1792]{1,0:T(8,128)(2,1)S(1)}, u32[]{:S(2)}, u32[]{:S(2)}) collective-permute-start(bf16[96,1792]{1,0:T(8,128)(2,1)S(1)} %add_convert_fusion.4), channel_id=1, source_target_pairs={{2,0},{4,2},{6,4},{7,6},{5,7},{3,5},{1,3},{0,1},{10,8},{12,10},{14... | collective-permute-start | bytes 1032200 | tf_op jit(solution)/shard_map/ppermute | solution.py:355
  43.7 0.6 collective-permute-start.3
  44.3 3.3 %column_piece.11 = (bf16[96,1792]{1,0:T(8,128)(2,1)S(1)}, bf16[96,1792]{1,0:T(8,128)(2,1)S(1)}) custom-call(s32[2]{0:T(128)S(1)} %copy-done.1, s32[128]{0:T(128)S(1)} %copy-done.4, bf16[96,512]{1,0:T(8,128)(2,1)S(1)} %slice.83.rows_ref, bf16[1,512,14336]{2,1,0:T(8,128)(2,1)} %refs_3_.15, bf16[1,512,14336]{2,1,0:T(8,128)(2,1)} %refs_3_.15, ...), custom_call_target="tpu_custom_call" | custom-call | flops 352321536 | bytes 3670016 | tf_op jit(solution)/shard_map/column_piece/pallas_call | solution.py:129
  47.7 2.9 %collective-permute-done.11 = bf16[96,1792]{1,0:T(8,128)(2,1)S(1)} collective-permute-done((bf16[96,1792]{1,0:T(8,128)(2,1)S(1)}, bf16[96,1792]{1,0:T(8,128)(2,1)S(1)}, u32[]{:S(2)}, u32[]{:S(2)}) %collective-permute-start.11) | collective-permute-done | bytes 344096 | tf_op jit(solution)/shard_map/ppermute | solution.py:355
  50.6 1.4 %collective-permute-start.12 = (bf16[96,1792]{1,0:T(8,128)(2,1)S(1)}, bf16[96,1792]{1,0:T(8,128)(2,1)S(1)}, u32[]{:S(2)}, u32[]{:S(2)}) collective-permute-start(bf16[96,1792]{1,0:T(8,128)(2,1)S(1)} %add_convert_fusion.3), channel_id=1, source_target_pairs={{2,0},{4,2},{6,4},{7,6},{5,7},{3,5},{1,3},{0,1},{10,8},{12,10},{14... | collective-permute-start | bytes 1032200 | tf_op jit(solution)/shard_map/ppermute | solution.py:355
  52.4 0.7 collective-permute-start.6
  53.2 1.5 %collective-permute-start.4 = (bf16[96,1792]{1,0:T(8,128)(2,1)S(1)}, bf16[96,1792]{1,0:T(8,128)(2,1)S(1)}, u32[]{:S(2)}, u32[]{:S(2)}) collective-permute-start(bf16[96,1792]{1,0:T(8,128)(2,1)S(1)} %add_convert_fusion.9), channel_id=1, source_target_pairs={{0,2},{2,4},{4,6},{6,7},{7,5},{5,3},{3,1},{1,0},{8,10},{10,12},{12... | collective-permute-start | bytes 1032200 | tf_op jit(solution)/shard_map/ppermute | solution.py:354
  54.8 3.3 %column_piece.12 = (bf16[96,1792]{1,0:T(8,128)(2,1)S(1)}, bf16[96,1792]{1,0:T(8,128)(2,1)S(1)}) custom-call(s32[2]{0:T(128)S(1)} %copy-done.1, s32[128]{0:T(128)S(1)} %copy-done.4, bf16[96,512]{1,0:T(8,128)(2,1)S(1)} %slice.83.rows_ref, bf16[1,512,14336]{2,1,0:T(8,128)(2,1)} %refs_3_.15, bf16[1,512,14336]{2,1,0:T(8,128)(2,1)} %refs_3_.15, ...), custom_call_target="tpu_custom_call" | custom-call | flops 352321536 | bytes 3670016 | tf_op jit(solution)/shard_map/column_piece/pallas_call | solution.py:129
  58.6 1.7 %collective-permute-start.13 = (bf16[96,1792]{1,0:T(8,128)(2,1)S(1)}, bf16[96,1792]{1,0:T(8,128)(2,1)S(1)}, u32[]{:S(2)}, u32[]{:S(2)}) collective-permute-start(bf16[96,1792]{1,0:T(8,128)(2,1)S(1)} %add_convert_fusion.2), channel_id=1, source_target_pairs={{2,0},{4,2},{6,4},{7,6},{5,7},{3,5},{1,3},{0,1},{10,8},{12,10},{14... | collective-permute-start | bytes 1032200 | tf_op jit(solution)/shard_map/ppermute | solution.py:355
  60.3 1.4 %collective-permute-done.4 = bf16[96,1792]{1,0:T(8,128)(2,1)S(1)} collective-permute-done((bf16[96,1792]{1,0:T(8,128)(2,1)S(1)}, bf16[96,1792]{1,0:T(8,128)(2,1)S(1)}, u32[]{:S(2)}, u32[]{:S(2)}) %collective-permute-start.4) | collective-permute-done | bytes 344096 | tf_op jit(solution)/shard_map/ppermute | solution.py:354
  61.8 1.4 %collective-permute-start.5 = (bf16[96,1792]{1,0:T(8,128)(2,1)S(1)}, bf16[96,1792]{1,0:T(8,128)(2,1)S(1)}, u32[]{:S(2)}, u32[]{:S(2)}) collective-permute-start(bf16[96,1792]{1,0:T(8,128)(2,1)S(1)} %add_convert_fusion.8), channel_id=1, source_target_pairs={{0,2},{2,4},{4,6},{6,7},{7,5},{5,3},{3,1},{1,0},{8,10},{10,12},{12... | collective-permute-start | bytes 1032200 | tf_op jit(solution)/shard_map/ppermute | solution.py:354
  63.2 3.3 %column_piece.13 = (bf16[96,1792]{1,0:T(8,128)(2,1)S(1)}, bf16[96,1792]{1,0:T(8,128)(2,1)S(1)}) custom-call(s32[2]{0:T(128)S(1)} %copy-done.1, s32[128]{0:T(128)S(1)} %copy-done.4, bf16[96,512]{1,0:T(8,128)(2,1)S(1)} %slice.83.rows_ref, bf16[1,512,14336]{2,1,0:T(8,128)(2,1)} %refs_3_.15, bf16[1,512,14336]{2,1,0:T(8,128)(2,1)} %refs_3_.15, ...), custom_call_target="tpu_custom_call" | custom-call | flops 352321536 | bytes 3670016 | tf_op jit(solution)/shard_map/column_piece/pallas_call | solution.py:129
  67.2 1.9 %collective-permute-start.14 = (bf16[96,1792]{1,0:T(8,128)(2,1)S(1)}, bf16[96,1792]{1,0:T(8,128)(2,1)S(1)}, u32[]{:S(2)}, u32[]{:S(2)}) collective-permute-start(bf16[96,1792]{1,0:T(8,128)(2,1)S(1)} %add_convert_fusion.1), channel_id=1, source_target_pairs={{2,0},{4,2},{6,4},{7,6},{5,7},{3,5},{1,3},{0,1},{10,8},{12,10},{14... | collective-permute-start | bytes 1032200 | tf_op jit(solution)/shard_map/ppermute | solution.py:355
  69.1 0.9 collective-permute-done.5
  70.0 1.0 fusion.2
  71.1 1.3 %collective-permute-start.7 = (bf16[96,1792]{1,0:T(8,128)(2,1)S(1)}, bf16[96,1792]{1,0:T(8,128)(2,1)S(1)}, u32[]{:S(2)}, u32[]{:S(2)}) collective-permute-start(bf16[96,1792]{1,0:T(8,128)(2,1)S(1)} %add_convert_fusion.7), channel_id=1, source_target_pairs={{0,2},{2,4},{4,6},{6,7},{7,5},{5,3},{3,1},{1,0},{8,10},{10,12},{12... | collective-permute-start | bytes 1032200 | tf_op jit(solution)/shard_map/ppermute | solution.py:354
  72.4 3.3 %column_piece.14 = (bf16[96,1792]{1,0:T(8,128)(2,1)S(1)}, bf16[96,1792]{1,0:T(8,128)(2,1)S(1)}) custom-call(s32[2]{0:T(128)S(1)} %copy-done.1, s32[128]{0:T(128)S(1)} %copy-done.4, bf16[96,512]{1,0:T(8,128)(2,1)S(1)} %slice.83.rows_ref, bf16[1,512,14336]{2,1,0:T(8,128)(2,1)} %refs_3_.15, bf16[1,512,14336]{2,1,0:T(8,128)(2,1)} %refs_3_.15, ...), custom_call_target="tpu_custom_call" | custom-call | flops 352321536 | bytes 3670016 | tf_op jit(solution)/shard_map/column_piece/pallas_call | solution.py:129
  75.7 0.8 collective-permute-done.14
  76.6 2.5 %collective-permute-start.15 = (bf16[96,1792]{1,0:T(8,128)(2,1)S(1)}, bf16[96,1792]{1,0:T(8,128)(2,1)S(1)}, u32[]{:S(2)}, u32[]{:S(2)}) collective-permute-start(bf16[96,1792]{1,0:T(8,128)(2,1)S(1)} %add_convert_fusion), channel_id=1, source_target_pairs={{2,0},{4,2},{6,4},{7,6},{5,7},{3,5},{1,3},{0,1},{10,8},{12,10},{14... | collective-permute-start | bytes 1032200 | tf_op jit(solution)/shard_map/ppermute | solution.py:355
  79.1 2.1 %collective-permute-done.7 = bf16[96,1792]{1,0:T(8,128)(2,1)S(1)} collective-permute-done((bf16[96,1792]{1,0:T(8,128)(2,1)S(1)}, bf16[96,1792]{1,0:T(8,128)(2,1)S(1)}, u32[]{:S(2)}, u32[]{:S(2)}) %collective-permute-start.7) | collective-permute-done | bytes 344096 | tf_op jit(solution)/shard_map/ppermute | solution.py:354
  81.3 1.2 collective-permute-start.8
  82.5 0.7 slice.86.tail_ref
  83.2 3.3 %column_piece.15 = (bf16[96,1792]{1,0:T(8,128)(2,1)S(1)}, bf16[96,1792]{1,0:T(8,128)(2,1)S(1)}) custom-call(s32[2]{0:T(128)S(1)} %copy-done.1, s32[128]{0:T(128)S(1)} %copy-done.4, bf16[96,512]{1,0:T(8,128)(2,1)S(1)} %slice.83.rows_ref, bf16[1,512,14336]{2,1,0:T(8,128)(2,1)} %refs_3_.15, bf16[1,512,14336]{2,1,0:T(8,128)(2,1)} %refs_3_.15, ...), custom_call_target="tpu_custom_call" | custom-call | flops 352321536 | bytes 3670016 | tf_op jit(solution)/shard_map/column_piece/pallas_call | solution.py:129
  86.6 2.0 %collective-permute-done.8.gate_ref = bf16[96,1792]{1,0:T(8,128)(2,1)S(1)} collective-permute-done((bf16[96,1792]{1,0:T(8,128)(2,1)S(1)}, bf16[96,1792]{1,0:T(8,128)(2,1)S(1)}, u32[]{:S(2)}, u32[]{:S(2)}) %collective-permute-start.8) | collective-permute-done | bytes 344096 | tf_op jit(solution)/shard_map/ppermute | solution.py:354
  88.6 10.4 %expert_outputs.1 = (f32[64,4096]{1,0:T(8,128)S(1)}, bf16[64,4096]{1,0:T(8,128)(2,1)S(1)}) custom-call(s32[2]{0:T(128)S(1)} %copy-done.1, bf16[96,1792]{1,0:T(8,128)(2,1)S(1)} %collective-permute-done.8.gate_ref, bf16[96,1792]{1,0:T(8,128)(2,1)S(1)} %collective-permute-done.15.up_ref, bf16[96,1792]{1,0:T(8,128)(2,1)S(1)} %get-tuple-element.88.gate_own_ref, ...), custom_call_target="tpu_custom_call" | custom-call | flops 1879048192 | bytes 14680064 | tf_op jit(solution)/shard_map/expert_outputs/pallas_call | solution.py:258
  99.1 1.9 %collective-permute-done.16 = bf16[64,4096]{1,0:T(8,128)(2,1)S(1)} collective-permute-done((bf16[64,4096]{1,0:T(8,128)(2,1)S(1)}, bf16[64,4096]{1,0:T(8,128)(2,1)S(1)}, u32[]{:S(2)}, u32[]{:S(2)}) %collective-permute-start.16) | collective-permute-done | bytes 524320 | tf_op jit(solution)/shard_map/ppermute | solution.py:391
  101.2 1.6 %collective-permute-start.17 = (bf16[2,16,2048]{2,1,0:T(8,128)(2,1)S(1)}, bf16[2,16,2048]{2,1,0:T(8,128)(2,1)S(1)}, u32[]{:S(2)}, u32[]{:S(2)}) collective-permute-start(bf16[2,16,2048]{2,1,0:T(8,128)(2,1)S(1)} %fusion.7), channel_id=1, source_target_pairs={{0,16},{8,24},{16,0},{24,8},{1,17},{9,25},{17,1},{25,9},{2,18},{10... | collective-permute-start | bytes 393224 | tf_op jit(solution)/shard_map/ppermute | solution.py:303
  102.8 0.8 collective-permute-start.19
  103.5 3.3 %collective-permute-done.17 = bf16[2,16,2048]{2,1,0:T(8,128)(2,1)S(1)} collective-permute-done((bf16[2,16,2048]{2,1,0:T(8,128)(2,1)S(1)}, bf16[2,16,2048]{2,1,0:T(8,128)(2,1)S(1)}, u32[]{:S(2)}, u32[]{:S(2)}) %collective-permute-start.17) | collective-permute-done | bytes 131104 | tf_op jit(solution)/shard_map/ppermute | solution.py:303
  106.8 0.8 collective-permute-start.18
  108.1 1.1 collective-permute-start.20
  109.2 2.0 %collective-permute-done.18 = bf16[16,2048]{1,0:T(8,128)(2,1)S(1)} collective-permute-done((bf16[16,2048]{1,0:T(8,128)(2,1)S(1)}, bf16[16,2048]{1,0:T(8,128)(2,1)S(1)}, u32[]{:S(2)}, u32[]{:S(2)}) %collective-permute-start.18) | collective-permute-done | bytes 65568 | tf_op jit(solution)/shard_map/ppermute | solution.py:303
  111.2 1.3 %collective-permute-done.20 = bf16[16,2048]{1,0:T(8,128)(2,1)S(1)} collective-permute-done((bf16[16,2048]{1,0:T(8,128)(2,1)S(1)}, bf16[16,2048]{1,0:T(8,128)(2,1)S(1)}, u32[]{:S(2)}, u32[]{:S(2)}) %collective-permute-start.20) | collective-permute-done | bytes 65568 | tf_op jit(solution)/shard_map/ppermute | solution.py:303
  113.1 3.3 %collective-permute-start.23 = (bf16[4,4096]{1,0:T(4,128)(2,1)S(1)}, bf16[4,4096]{1,0:T(4,128)(2,1)S(1)}, u32[]{:S(2)}, u32[]{:S(2)}) collective-permute-start(bf16[4,4096]{1,0:T(4,128)(2,1)S(1)} %get-tuple-element.95), channel_id=1, source_target_pairs={{0,6},{1,7},{2,0},{3,1},{4,2},{5,3},{6,4},{7,5},{8,14},{9,15},{10,... | collective-permute-start | bytes 98312 | tf_op jit(solution)/shard_map/ppermute | solution.py:303
  116.4 2.0 %collective-permute-done.21 = bf16[4,4096]{1,0:T(4,128)(2,1)S(1)} collective-permute-done((bf16[4,4096]{1,0:T(4,128)(2,1)S(1)}, bf16[4,4096]{1,0:T(4,128)(2,1)S(1)}, u32[]{:S(2)}, u32[]{:S(2)}) %collective-permute-start.21) | collective-permute-done | bytes 32800 | tf_op jit(solution)/shard_map/ppermute | solution.py:303
  118.4 2.8 %collective-permute-done.22 = bf16[4,4096]{1,0:T(4,128)(2,1)S(1)} collective-permute-done((bf16[4,4096]{1,0:T(4,128)(2,1)S(1)}, bf16[4,4096]{1,0:T(4,128)(2,1)S(1)}, u32[]{:S(2)}, u32[]{:S(2)}) %collective-permute-start.22) | collective-permute-done | bytes 32800 | tf_op jit(solution)/shard_map/ppermute | solution.py:303
  121.2 0.7 fusion.17
  (58 shorter events, 5.8 us)
Async XLA Ops:
  0.7 21.7 %copy-start = (s32[2]{0:T(128)}, s32[2]{0:T(128)S(1)}, u32[]{:S(2)}) copy-start(s32[2]{0:T(128)S(1)} %pad_add_fusion.where_ref) | copy-start | bytes 28
  17.8 0.6 copy-start.6
  18.4 0.7 copy-start.3
  22.4 10.2 %collective-permute-start.9 = (bf16[96,1792]{1,0:T(8,128)(2,1)S(1)}, bf16[96,1792]{1,0:T(8,128)(2,1)S(1)}, u32[]{:S(2)}, u32[]{:S(2)}) collective-permute-start(bf16[96,1792]{1,0:T(8,128)(2,1)S(1)} %get-tuple-element.80), channel_id=1, source_target_pairs={{2,0},{4,2},{6,4},{7,6},{5,7},{3,5},{1,3},{0,1},{10,8},{12,10},{14... | collective-permute-start | bytes 1032200 | tf_op jit(solution)/shard_map/ppermute | solution.py:355
  24.0 3.8 %copy-start.1 = (s32[2]{0:T(128)S(1)}, s32[2]{0:T(128)}, u32[]{:S(2)}) copy-start(s32[2]{0:T(128)} %copy-done) | copy-start | bytes 28
  24.0 3.8 %copy-start.4 = (s32[128]{0:T(128)S(1)}, s32[128]{0:T(128)}, u32[]{:S(2)}) copy-start(s32[128]{0:T(128)} %constant.15.clone.table_ref) | copy-start | bytes 1540
  24.0 10.2 %collective-permute-start = (bf16[96,1792]{1,0:T(8,128)(2,1)S(1)}, bf16[96,1792]{1,0:T(8,128)(2,1)S(1)}, u32[]{:S(2)}, u32[]{:S(2)}) collective-permute-start(bf16[96,1792]{1,0:T(8,128)(2,1)S(1)} %get-tuple-element.52), channel_id=1, source_target_pairs={{0,2},{2,4},{4,6},{6,7},{7,5},{5,3},{3,1},{1,0},{8,10},{10,12},{12... | collective-permute-start | bytes 1032200 | tf_op jit(solution)/shard_map/ppermute | solution.py:354
  27.8 15.8 %collective-permute-start.2 = (bf16[2,512,512]{2,1,0:T(8,128)(2,1)}, bf16[2,512,512]{2,1,0:T(8,128)(2,1)S(1)}, u32[]{:S(2)}, u32[]{:S(2)}) collective-permute-start(bf16[2,512,512]{2,1,0:T(8,128)(2,1)} %get-tuple-element.55), channel_id=1, source_target_pairs={{0,8},{8,0},{16,24},{24,16},{1,9},{9,1},{17,25},{25,17},{2,10},{10... | collective-permute-start | bytes 3145736 | tf_op jit(solution)/shard_map/ppermute | solution.py:363
  32.7 9.3 %collective-permute-start.10 = (bf16[96,1792]{1,0:T(8,128)(2,1)S(1)}, bf16[96,1792]{1,0:T(8,128)(2,1)S(1)}, u32[]{:S(2)}, u32[]{:S(2)}) collective-permute-start(bf16[96,1792]{1,0:T(8,128)(2,1)S(1)} %add_convert_fusion.5), channel_id=1, source_target_pairs={{2,0},{4,2},{6,4},{7,6},{5,7},{3,5},{1,3},{0,1},{10,8},{12,10},{14... | collective-permute-start | bytes 1032200 | tf_op jit(solution)/shard_map/ppermute | solution.py:355
  34.3 9.3 %collective-permute-start.1 = (bf16[96,1792]{1,0:T(8,128)(2,1)S(1)}, bf16[96,1792]{1,0:T(8,128)(2,1)S(1)}, u32[]{:S(2)}, u32[]{:S(2)}) collective-permute-start(bf16[96,1792]{1,0:T(8,128)(2,1)S(1)} %add_convert_fusion.11), channel_id=1, source_target_pairs={{0,2},{2,4},{4,6},{6,7},{7,5},{5,3},{3,1},{1,0},{8,10},{10,12},{12... | collective-permute-start | bytes 1032200 | tf_op jit(solution)/shard_map/ppermute | solution.py:354
  42.1 8.4 %collective-permute-start.11 = (bf16[96,1792]{1,0:T(8,128)(2,1)S(1)}, bf16[96,1792]{1,0:T(8,128)(2,1)S(1)}, u32[]{:S(2)}, u32[]{:S(2)}) collective-permute-start(bf16[96,1792]{1,0:T(8,128)(2,1)S(1)} %add_convert_fusion.4), channel_id=1, source_target_pairs={{2,0},{4,2},{6,4},{7,6},{5,7},{3,5},{1,3},{0,1},{10,8},{12,10},{14... | collective-permute-start | bytes 1032200 | tf_op jit(solution)/shard_map/ppermute | solution.py:355
  43.7 8.4 %copy-start.5 = (bf16[2,512,512]{2,1,0:T(8,128)(2,1)S(1)}, bf16[2,512,512]{2,1,0:T(8,128)(2,1)}, u32[]{:S(2)}) copy-start(bf16[2,512,512]{2,1,0:T(8,128)(2,1)} %get-tuple-element.69) | copy-start | bytes 3145732
  43.7 9.5 %collective-permute-start.3 = (bf16[96,1792]{1,0:T(8,128)(2,1)S(1)}, bf16[96,1792]{1,0:T(8,128)(2,1)S(1)}, u32[]{:S(2)}, u32[]{:S(2)}) collective-permute-start(bf16[96,1792]{1,0:T(8,128)(2,1)S(1)} %add_convert_fusion.10), channel_id=1, source_target_pairs={{0,2},{2,4},{4,6},{6,7},{7,5},{5,3},{3,1},{1,0},{8,10},{10,12},{12... | collective-permute-start | bytes 1032200 | tf_op jit(solution)/shard_map/ppermute | solution.py:354
  50.6 7.9 %collective-permute-start.12 = (bf16[96,1792]{1,0:T(8,128)(2,1)S(1)}, bf16[96,1792]{1,0:T(8,128)(2,1)S(1)}, u32[]{:S(2)}, u32[]{:S(2)}) collective-permute-start(bf16[96,1792]{1,0:T(8,128)(2,1)S(1)} %add_convert_fusion.3), channel_id=1, source_target_pairs={{2,0},{4,2},{6,4},{7,6},{5,7},{3,5},{1,3},{0,1},{10,8},{12,10},{14... | collective-permute-start | bytes 1032200 | tf_op jit(solution)/shard_map/ppermute | solution.py:355
  52.4 16.7 %collective-permute-start.6 = (bf16[512,512]{1,0:T(8,128)(2,1)S(1)}, bf16[512,512]{1,0:T(8,128)(2,1)S(1)}, u32[]{:S(2)}, u32[]{:S(2)}) collective-permute-start(bf16[512,512]{1,0:T(8,128)(2,1)S(1)} %fusion.3), channel_id=1, source_target_pairs={{0,16},{8,24},{16,0},{24,8},{1,17},{9,25},{17,1},{25,9},{2,18},{10... | collective-permute-start | bytes 1572872 | tf_op jit(solution)/shard_map/ppermute | solution.py:371
  53.2 8.4 %collective-permute-start.4 = (bf16[96,1792]{1,0:T(8,128)(2,1)S(1)}, bf16[96,1792]{1,0:T(8,128)(2,1)S(1)}, u32[]{:S(2)}, u32[]{:S(2)}) collective-permute-start(bf16[96,1792]{1,0:T(8,128)(2,1)S(1)} %add_convert_fusion.9), channel_id=1, source_target_pairs={{0,2},{2,4},{4,6},{6,7},{7,5},{5,3},{3,1},{1,0},{8,10},{10,12},{12... | collective-permute-start | bytes 1032200 | tf_op jit(solution)/shard_map/ppermute | solution.py:354
  58.6 8.5 %collective-permute-start.13 = (bf16[96,1792]{1,0:T(8,128)(2,1)S(1)}, bf16[96,1792]{1,0:T(8,128)(2,1)S(1)}, u32[]{:S(2)}, u32[]{:S(2)}) collective-permute-start(bf16[96,1792]{1,0:T(8,128)(2,1)S(1)} %add_convert_fusion.2), channel_id=1, source_target_pairs={{2,0},{4,2},{6,4},{7,6},{5,7},{3,5},{1,3},{0,1},{10,8},{12,10},{14... | collective-permute-start | bytes 1032200 | tf_op jit(solution)/shard_map/ppermute | solution.py:355
  61.8 8.3 %collective-permute-start.5 = (bf16[96,1792]{1,0:T(8,128)(2,1)S(1)}, bf16[96,1792]{1,0:T(8,128)(2,1)S(1)}, u32[]{:S(2)}, u32[]{:S(2)}) collective-permute-start(bf16[96,1792]{1,0:T(8,128)(2,1)S(1)} %add_convert_fusion.8), channel_id=1, source_target_pairs={{0,2},{2,4},{4,6},{6,7},{7,5},{5,3},{3,1},{1,0},{8,10},{10,12},{12... | collective-permute-start | bytes 1032200 | tf_op jit(solution)/shard_map/ppermute | solution.py:354
  67.2 9.3 %collective-permute-start.14 = (bf16[96,1792]{1,0:T(8,128)(2,1)S(1)}, bf16[96,1792]{1,0:T(8,128)(2,1)S(1)}, u32[]{:S(2)}, u32[]{:S(2)}) collective-permute-start(bf16[96,1792]{1,0:T(8,128)(2,1)S(1)} %add_convert_fusion.1), channel_id=1, source_target_pairs={{2,0},{4,2},{6,4},{7,6},{5,7},{3,5},{1,3},{0,1},{10,8},{12,10},{14... | collective-permute-start | bytes 1032200 | tf_op jit(solution)/shard_map/ppermute | solution.py:355
  71.1 10.1 %collective-permute-start.7 = (bf16[96,1792]{1,0:T(8,128)(2,1)S(1)}, bf16[96,1792]{1,0:T(8,128)(2,1)S(1)}, u32[]{:S(2)}, u32[]{:S(2)}) collective-permute-start(bf16[96,1792]{1,0:T(8,128)(2,1)S(1)} %add_convert_fusion.7), channel_id=1, source_target_pairs={{0,2},{2,4},{4,6},{6,7},{7,5},{5,3},{3,1},{1,0},{8,10},{10,12},{12... | collective-permute-start | bytes 1032200 | tf_op jit(solution)/shard_map/ppermute | solution.py:354
  76.6 9.9 %collective-permute-start.15 = (bf16[96,1792]{1,0:T(8,128)(2,1)S(1)}, bf16[96,1792]{1,0:T(8,128)(2,1)S(1)}, u32[]{:S(2)}, u32[]{:S(2)}) collective-permute-start(bf16[96,1792]{1,0:T(8,128)(2,1)S(1)} %add_convert_fusion), channel_id=1, source_target_pairs={{2,0},{4,2},{6,4},{7,6},{5,7},{3,5},{1,3},{0,1},{10,8},{12,10},{14... | collective-permute-start | bytes 1032200 | tf_op jit(solution)/shard_map/ppermute | solution.py:355
  81.3 7.3 %collective-permute-start.8 = (bf16[96,1792]{1,0:T(8,128)(2,1)S(1)}, bf16[96,1792]{1,0:T(8,128)(2,1)S(1)}, u32[]{:S(2)}, u32[]{:S(2)}) collective-permute-start(bf16[96,1792]{1,0:T(8,128)(2,1)S(1)} %add_convert_fusion.6), channel_id=1, source_target_pairs={{0,2},{2,4},{4,6},{6,7},{7,5},{5,3},{3,1},{1,0},{8,10},{10,12},{12... | collective-permute-start | bytes 1032200 | tf_op jit(solution)/shard_map/ppermute | solution.py:354
  83.2 5.4 %copy-start.2 = (f32[96,128]{1,0:T(8,128)S(1)}, f32[96,128]{1,0:T(8,128)}, u32[]{:S(2)}) copy-start(f32[96,128]{1,0:T(8,128)} %constant.16.clone.origin_ref) | copy-start | bytes 147460
  99.0 2.0 %collective-permute-start.16 = (bf16[64,4096]{1,0:T(8,128)(2,1)S(1)}, bf16[64,4096]{1,0:T(8,128)(2,1)S(1)}, u32[]{:S(2)}, u32[]{:S(2)}) collective-permute-start(bf16[64,4096]{1,0:T(8,128)(2,1)S(1)} %get-tuple-element.92), channel_id=1, source_target_pairs={{0,8},{8,0},{16,24},{24,16},{1,9},{9,1},{17,25},{25,17},{2,10},{10... | collective-permute-start | bytes 1572872 | tf_op jit(solution)/shard_map/ppermute | solution.py:391
  101.2 5.6 %collective-permute-start.17 = (bf16[2,16,2048]{2,1,0:T(8,128)(2,1)S(1)}, bf16[2,16,2048]{2,1,0:T(8,128)(2,1)S(1)}, u32[]{:S(2)}, u32[]{:S(2)}) collective-permute-start(bf16[2,16,2048]{2,1,0:T(8,128)(2,1)S(1)} %fusion.7), channel_id=1, source_target_pairs={{0,16},{8,24},{16,0},{24,8},{1,17},{9,25},{17,1},{25,9},{2,18},{10... | collective-permute-start | bytes 393224 | tf_op jit(solution)/shard_map/ppermute | solution.py:303
  102.8 5.3 %collective-permute-start.19 = (bf16[2,16,2048]{2,1,0:T(8,128)(2,1)S(1)}, bf16[2,16,2048]{2,1,0:T(8,128)(2,1)S(1)}, u32[]{:S(2)}, u32[]{:S(2)}) collective-permute-start(bf16[2,16,2048]{2,1,0:T(8,128)(2,1)S(1)} %fusion.8), channel_id=1, source_target_pairs={{0,1},{1,0},{2,3},{3,2},{4,5},{5,4},{6,7},{7,6},{8,9},{9,8},{10,11... | collective-permute-start | bytes 393224 | tf_op jit(solution)/shard_map/ppermute | solution.py:303
  106.8 4.3 %collective-permute-start.18 = (bf16[16,2048]{1,0:T(8,128)(2,1)S(1)}, bf16[16,2048]{1,0:T(8,128)(2,1)S(1)}, u32[]{:S(2)}, u32[]{:S(2)}) collective-permute-start(bf16[16,2048]{1,0:T(8,128)(2,1)S(1)} %fusion.11), channel_id=1, source_target_pairs={{0,1},{1,0},{2,3},{3,2},{4,5},{5,4},{6,7},{7,6},{8,9},{9,8},{10,11... | collective-permute-start | bytes 196616 | tf_op jit(solution)/shard_map/ppermute | solution.py:303
  108.1 4.3 %collective-permute-start.20 = (bf16[16,2048]{1,0:T(8,128)(2,1)S(1)}, bf16[16,2048]{1,0:T(8,128)(2,1)S(1)}, u32[]{:S(2)}, u32[]{:S(2)}) collective-permute-start(bf16[16,2048]{1,0:T(8,128)(2,1)S(1)} %fusion.12), channel_id=1, source_target_pairs={{0,16},{8,24},{16,0},{24,8},{1,17},{9,25},{17,1},{25,9},{2,18},{10... | collective-permute-start | bytes 196616 | tf_op jit(solution)/shard_map/ppermute | solution.py:303
  112.5 5.9 %collective-permute-start.21 = (bf16[4,4096]{1,0:T(4,128)(2,1)S(1)}, bf16[4,4096]{1,0:T(4,128)(2,1)S(1)}, u32[]{:S(2)}, u32[]{:S(2)}) collective-permute-start(bf16[4,4096]{1,0:T(4,128)(2,1)S(1)} %get-tuple-element.94), channel_id=1, source_target_pairs={{0,2},{1,3},{2,4},{3,5},{4,6},{5,7},{6,0},{7,1},{8,10},{9,11},{10,... | collective-permute-start | bytes 98312 | tf_op jit(solution)/shard_map/ppermute | solution.py:303
  113.1 5.3 %collective-permute-start.23 = (bf16[4,4096]{1,0:T(4,128)(2,1)S(1)}, bf16[4,4096]{1,0:T(4,128)(2,1)S(1)}, u32[]{:S(2)}, u32[]{:S(2)}) collective-permute-start(bf16[4,4096]{1,0:T(4,128)(2,1)S(1)} %get-tuple-element.95), channel_id=1, source_target_pairs={{0,6},{1,7},{2,0},{3,1},{4,2},{5,3},{6,4},{7,5},{8,14},{9,15},{10,... | collective-permute-start | bytes 98312 | tf_op jit(solution)/shard_map/ppermute | solution.py:303
  116.4 4.8 %collective-permute-start.22 = (bf16[4,4096]{1,0:T(4,128)(2,1)S(1)}, bf16[4,4096]{1,0:T(4,128)(2,1)S(1)}, u32[]{:S(2)}, u32[]{:S(2)}) collective-permute-start(bf16[4,4096]{1,0:T(4,128)(2,1)S(1)} %get-tuple-element.96), channel_id=1, source_target_pairs={{0,4},{1,5},{2,6},{3,7},{4,0},{5,1},{6,2},{7,3},{8,12},{9,13},{10,... | collective-permute-start | bytes 98312 | tf_op jit(solution)/shard_map/ppermute | solution.py:303

commit v8 on v5

--- a/solution.py
+++ b/solution.py
@@ -11,8 +11,8 @@
 F32 = jnp.float32
 BF16 = jnp.bfloat16
 LANES = 128
-VMEM_LIMIT = 24 * 1024 * 1024
-PIECES_LIMIT = 48 * 1024 * 1024
+VMEM_LIMIT = 40 * 1024 * 1024
+HIDDEN_LIMIT = 24 * 1024 * 1024
 
 
 def ring_order(devices):
@@ -29,6 +29,16 @@
         line = xs[1:] if i % 2 == 0 else list(reversed(xs[1:]))
         order += [at[(z, x)] for x in line]
     return order
+
+
+def grid_columns(devices):
+    places = [getattr(d, "coords", None) for d in devices]
+    if any(p is None for p in places):
+        return 1
+    columns = len({p[0] for p in places})
+    line = sorted(range(len(places)), key=lambda i: (places[i][2], places[i][0]))
+    whole = len({(p[2], p[0]) for p in places}) == len(places)
+    return columns if whole and line == list(range(len(places))) and len(places) % columns == 0 else 1
 
 
 def core_count(devices):
@@ -122,7 +132,7 @@
             + [weight_map(side, i) for side, i in both],
             out_specs=[pl.BlockSpec((count, block), lambda j, *_: (0, j))] * len(both),
         ),
-        compiler_params=pltpu.CompilerParams(vmem_limit_bytes=PIECES_LIMIT),
+        compiler_params=pltpu.CompilerParams(vmem_limit_bytes=VMEM_LIMIT),
         cost_estimate=pl.CostEstimate(
             flops=4 * pieces * count * depth * width,
             bytes_accessed=4 * pieces * depth * width,
@@ -173,23 +183,29 @@
     )(where, *([x] * cores))
 
 
-def hidden_rows(where, gate_in, up_in, gate_own, up_own, tails, origin, sizes):
-    experts, shards, cores, token_count = sizes
-    chips = experts // cores
+def hidden_rows(where, gate_in, up_in, gate_own, up_own, tails, origin, sizes, parts):
+    experts, shards, cores, columns, token_count = sizes
+    chips, lines = experts // cores, shards // columns
     total = experts * shards * token_count
+    kept = total // cores
     count, slice_width = gate_own.shape
-    chunk = next(c for c in (256, LANES, slice_width) if slice_width % c == 0)
-
-    def kernel(where_ref, gate_ref, up_ref, gate_own_ref, up_own_ref, tail_ref, origin_ref, out_ref):
-        b = where_ref[0]
+    cut_width = slice_width // parts
+    chunk = next(c for c in (256, LANES, cut_width) if cut_width % c == 0)
+
+    def kernel(where_ref, gate_ref, up_ref, gate_own_ref, up_own_ref, tail_ref, origin_ref, *outs):
+        b, s = where_ref[0], where_ref[1]
+        mine = (
+            lax.rem(b, jnp.int32(cores)), lax.div(b, jnp.int32(cores)),
+            lax.rem(s, jnp.int32(columns)), jnp.int32(0),
+        )
         tail = tail_ref[...].astype(F32)
+        number, weight = tail[:, 0:1], tail[:, 1:2] + tail[:, 2:3]
         place = origin_ref[...]
-        number, weight = tail[:, 0:1], tail[:, 1:2] + tail[:, 2:3]
-        chip = place[:, 0:1] - lax.div(b, jnp.int32(cores)).astype(F32)
-        core = place[:, 1:2] - lax.rem(b, jnp.int32(cores)).astype(F32)
-        chip = jnp.where(chip < 0, chip + chips, chip)
-        core = jnp.where(core < 0, core + cores, core)
-        target = (core * chips + chip) * (shards * token_count) + place[:, 2:3] + number - 1.0
+        target = jnp.zeros((count, 1), F32)
+        for i, size in enumerate((cores, chips, columns, lines)):
+            away = place[:, i : i + 1] - mine[i].astype(F32)
+            target = target * size + jnp.where(away < 0, away + size, away)
+        target = target * token_count + number - 1.0
         target = jnp.where(number > 0, target, -1.0).astype(jnp.int32)
         spread = target == lax.broadcasted_iota(jnp.int32, (count, total), 1)
         spread = spread.astype(F32).astype(BF16)
@@ -198,52 +214,35 @@
             gate = gate_ref[:, cut].astype(F32) + gate_own_ref[:, cut].astype(F32)
             upper = up_ref[:, cut].astype(F32) + up_own_ref[:, cut].astype(F32)
             hidden = (gate / (1.0 + jnp.exp(-gate)) * upper * weight).astype(BF16)
-            out_ref[:, cut] = lax.dot_general(
+            hidden = lax.dot_general(
                 spread, hidden, (((0,), (0,)), ((), ())), preferred_element_type=F32
             ).astype(BF16)
-
+            part, to = at // cut_width, at % cut_width
+            if cores > 1:
+                outs[part][:, to : to + chunk] = hidden[kept:]
+            outs[len(outs) - parts + part][:, to : to + chunk] = hidden[:kept]
+
+    shapes = [jax.ShapeDtypeStruct((kept, cut_width), BF16)] * parts
+    if cores > 1:
+        shapes = [jax.ShapeDtypeStruct((total - kept, cut_width), BF16)] * parts + shapes
     return pl.pallas_call(
         kernel,
-        out_shape=jax.ShapeDtypeStruct((total, slice_width), BF16),
+        out_shape=shapes,
         in_specs=[pl.BlockSpec(memory_space=pltpu.SMEM)]
         + [pl.BlockSpec(memory_space=pltpu.VMEM)] * 6,
-        out_specs=pl.BlockSpec(memory_space=pltpu.VMEM),
+        out_specs=[pl.BlockSpec(memory_space=pltpu.VMEM)] * len(shapes),
         cost_estimate=pl.CostEstimate(
             flops=2 * total * slice_width * count,
             bytes_accessed=8 * count * slice_width,
             transcendentals=count * slice_width,
         ),
-        compiler_params=pltpu.CompilerParams(vmem_limit_bytes=VMEM_LIMIT),
+        compiler_params=pltpu.CompilerParams(vmem_limit_bytes=HIDDEN_LIMIT),
         name="hidden_rows",
     )(where, gate_in, up_in, gate_own, up_own, tails, origin)
 
 
-def hold(where, x, parts):
-    rows = x.shape[1] // parts
-
-    def kernel(where_ref, in_ref, out_ref, sems):
-        copies = [
-            pltpu.make_async_copy(
-                in_ref.at[:, pl.ds(i * rows, rows)], out_ref.at[:, pl.ds(i * rows, rows)], sems.at[i]
-            )
-            for i in range(parts)
-        ]
-        for copy in copies:
-            copy.start()
-        for copy in copies:
-            copy.wait()
-
-    return pl.pallas_call(
-        kernel,
-        out_shape=jax.ShapeDtypeStruct(x.shape, x.dtype),
-        in_specs=[pl.BlockSpec(memory_space=pltpu.SMEM), pl.BlockSpec(memory_space=pl.ANY)],
-        out_specs=pl.BlockSpec(memory_space=pl.ANY),
-        scratch_shapes=[pltpu.SemaphoreType.DMA((parts,))],
-        cost_estimate=pl.CostEstimate(
-            flops=0, bytes_accessed=2 * x.size * x.dtype.itemsize, transcendentals=0
-        ),
-        name="hold",
-    )(where, x)
+def down_product(hidden, weights):
+    return sum(jnp.dot(h, w, preferred_element_type=F32) for h, w in zip(hidden, weights))
 
 
 def branch_target(size, cores, core_step, chip_step):
@@ -254,7 +253,22 @@
     ]
 
 
-def local(order, cores, tokens, routes, mixing, gate_weight, up_weight, down_weight, key_value):
+def shard_target(size, columns, x_step, z_step):
+    lines = size // columns
+    return [
+        (i, (i // columns + z_step) % lines * columns + (i + x_step) % columns)
+        for i in range(size)
+    ]
+
+
+def direct_sum(x, axis_name, target):
+    total = x[0]
+    for k in range(1, x.shape[0]):
+        total = total + lax.ppermute(x[k].astype(BF16), axis_name, target(k)).astype(F32)
+    return total
+
+
+def local(order, cores, columns, tokens, routes, mixing, gate_weight, up_weight, down_weight, key_value):
     experts = lax.axis_size("branch")
     shards = lax.axis_size("shard")
     chips = experts // cores
@@ -263,8 +277,8 @@
     depth = gate_weight.shape[1]
     slice_width = down_weight.shape[1]
     count = experts * shards * capacity
-    kept = chips * shards * token_count
-    sizes = (experts, shards, cores, token_count)
+    lines = shards // columns
+    sizes = (experts, shards, cores, columns, token_count)
     where = jnp.stack([lax.axis_index("branch"), lax.axis_index("shard")]).astype(jnp.int32)
 
     place = np.argsort(np.asarray(order))
@@ -278,9 +292,10 @@
     back = [(b, a) for a, b in forth]
     source = np.arange(count) // capacity
     origin = np.zeros((count, LANES), np.float32)
-    origin[:, 0] = source // shards // cores
-    origin[:, 1] = source // shards % cores
-    origin[:, 2] = source % shards * token_count
+    origin[:, 0] = source // shards % cores
+    origin[:, 1] = source // shards // cores
+    origin[:, 2] = source % shards % columns
+    origin[:, 3] = source % shards // columns
     origin = jnp.asarray(origin)
 
     cells = place_rows(tokens, routes, mixing, experts, capacity, shards)
@@ -297,25 +312,26 @@
         gates, ups = plain_pieces(where, table, rows, gate_weight, up_weight, shards)
     gate_sum, up_sum = gates[0], ups[0]
     last = shards - 1
+    parts = 1
+    weights = [down_weight[0]]
     for t in range(1, shards):
-        now, gate_sum, up_sum = lax.optimization_barrier((where, gate_sum, up_sum))
+        now, gate_sum = lax.optimization_barrier((where, gate_sum))
         gate_in = lax.ppermute(gate_sum, "shard", forth)
         up_in = lax.ppermute(up_sum, "shard", back)
         if sliced and len(gates) < shards:
             more = column_pieces(
                 now, table, rows, gate_weight, up_weight, shards, len(gates),
-                min(2, shards - len(gates)), 1,
+                1 if t == 1 else min(2, shards - len(gates)), 1,
             )
             gates, ups = gates + more[0], ups + more[1]
-            gate_in, up_in, gates, ups = lax.optimization_barrier((gate_in, up_in, gates, ups))
-        if t == min(4, last):
+        if t == 1:
             kv = turn_columns(now, key_value, cores, chips)
             kv_core = [
                 lax.ppermute(kv[k], "branch", branch_target(experts, cores, k, 0))
                 for k in range(1, cores)
             ]
             gate_in, kv = lax.optimization_barrier((gate_in, kv))
-        if t == min(5, last):
+        if t == min(2, last):
             gate_in, kv_core = lax.optimization_barrier((gate_in, kv_core))
             kv_sum = kv[0].astype(F32) + sum(x.astype(F32) for x in kv_core)
             kv_chip = [
@@ -324,44 +340,55 @@
                 )
                 for k in range(1, chips)
             ]
-        if t == min(6, last):
-            down_here = hold(now, down_weight, 8 if slice_width % LANES == 0 else 1)
-            gate_in, down_here = lax.optimization_barrier((gate_in, down_here))
-        if t == last:
+        if t == min(5, last):
             gate_in, kv_chip = lax.optimization_barrier((gate_in, kv_chip))
             kv_sum = kv_sum[0] + sum(x.astype(F32) for x in kv_chip)
             merged_kv = (kv_sum / experts).astype(BF16)
             gate_in, merged_kv = lax.optimization_barrier((gate_in, merged_kv))
-        else:
+        if t < last:
             gate_sum = (gate_in.astype(F32) + gates[t].astype(F32)).astype(BF16)
             up_sum = (up_in.astype(F32) + ups[t].astype(F32)).astype(BF16)
 
-    hidden = hidden_rows(where, gate_in, up_in, gates[last], ups[last], tails, origin, sizes)
+    hidden = hidden_rows(
+        where, gate_in, up_in, gates[last], ups[last], tails, origin, sizes, parts
+    )
     sent = []
-    for k in range(1, cores):
-        part = jnp.dot(
-            hidden[k * kept : (k + 1) * kept], down_here[0], preferred_element_type=F32
-        ).astype(BF16)
-        sent.append(lax.ppermute(part, "branch", branch_target(experts, cores, k, 0)))
-    mixed = jnp.dot(hidden[:kept], down_here[0], preferred_element_type=F32)
+    if cores > 1:
+        others = down_product(hidden[:parts], weights).astype(BF16)
+        others = others.reshape(cores - 1, -1, width)
+        sent = [
+            lax.ppermute(others[k - 1], "branch", branch_target(experts, cores, k, 0))
+            for k in range(1, cores)
+        ]
+    mixed = down_product(hidden[-parts:], weights)
     mixed, sent = lax.optimization_barrier((mixed, sent))
     mixed = mixed + sum(x.astype(F32) for x in sent)
-    mixed = mixed.reshape(chips, shards * token_count, width)
-    total = mixed[0]
-    for k in range(1, chips):
-        part = lax.ppermute(mixed[k].astype(BF16), "branch", branch_target(experts, cores, 0, k))
-        total = total + part.astype(F32)
-    total = total.astype(BF16).reshape(shards, token_count, width)
-    total = lax.all_to_all(total, "shard", split_axis=0, concat_axis=0, tiled=True)
-    return jnp.sum(total.astype(F32), axis=0).astype(BF16), merged_kv
+
+    def over_chips(x):
+        return direct_sum(x, "branch", lambda k: branch_target(experts, cores, 0, k))
+
+    def over_columns(x):
+        return direct_sum(x, "shard", lambda k: shard_target(shards, columns, k, 0))
+
+    mixed = mixed.reshape(chips, columns, lines * token_count, width)
+    left = over_chips(mixed[..., : width // 2])
+    right = over_columns(mixed[..., width // 2 :].swapaxes(0, 1))
+    left, right = over_columns(left), over_chips(right)
+    mixed = jnp.concatenate([left, right], axis=1).reshape(lines, token_count, width)
+    groups = [[z * columns + x for z in range(lines)] for x in range(columns)]
+    mixed = lax.all_to_all(
+        mixed.astype(BF16), "shard", split_axis=0, concat_axis=0, axis_index_groups=groups, tiled=True
+    )
+    return jnp.sum(mixed.astype(F32), axis=0).astype(BF16), merged_kv
 
 
 def solution(mesh):
     grid = mesh.devices
     order = ring_order(list(grid[0, :]))
     cores = core_count(list(grid[:, 0]))
+    columns = grid_columns(list(grid[0, :]))
     return jax.shard_map(
-        functools.partial(local, order, cores),
+        functools.partial(local, order, cores, columns),
         mesh=mesh,
         in_specs=(
             P(("branch", "shard"), None),

time: 574 us -> 124 us (0.22)
  Pallas kernels: 474 us -> 28.4 us
  waiting for transfers between devices: 31.3 us -> 41 us
  other arithmetic: 10 us -> 3.19 us
    pallas_call x2 -> x1, Pallas kernels: 448 us -> 1.17 us  [hidden_rows(): pl.pallas_call(kernel, out_shape=shapes, in_specs=[pl.BlockSpec(memory_sp...]
    ppermute x7, waiting for transfers between devices: 13.1 us -> 21.2 us  [local(): gate_in = lax.ppermute(gate_sum, 'shard', forth)]
  transfers between devices with their start and end apart: 18 -> 21, of which waited for: 10 -> 13; matrix products, arithmetic and copies ran while one was open for 2% -> 4% of each run, Pallas kernels for 82% -> 18%
where the time goes in v8:
time: 124 us; the launch traced here: 123 us
  waiting for transfers between devices  41 us (33%)
  Pallas kernels  28.4 us (23%)
  blocking collectives  24 us (19%)
  starting transfers between devices  18.6 us (15%)
  matrix products  5.42 us (4%)
  other arithmetic  3.19 us (3%)
  local copies, waits for them, and re-layouts  1.67 us (1%)
    pallas_call x5, Pallas kernels, column_pieces(): pl.pallas_call(kernel, out_shape=[jax.ShapeDtypeStruct((count, width), BF...  22.2 us
    ppermute x7, waiting for transfers between devices, local(): gate_in = lax.ppermute(gate_sum, 'shard', forth)  21.2 us
    all_to_all x1, blocking collectives, local(): lax.all_to_all(cells, ('branch', 'shard'), split_axis=0, concat_axis=0, t...  15.2 us
    ppermute x7, waiting for transfers between devices, local(): up_in = lax.ppermute(up_sum, 'shard', back)  11.1 us
    ppermute x7, starting transfers between devices, local(): up_in = lax.ppermute(up_sum, 'shard', back)  10.7 us
    all_to_all x1, blocking collectives, local(): lax.all_to_all(mixed.astype(BF16), 'shard', split_axis=0, concat_axis=0,...  8.79 us
    ppermute x4, waiting for transfers between devices, direct_sum(): lax.ppermute(x[k].astype(BF16), axis_name, target(k)).astype(F32)  8.71 us
    dot_general x2, matrix products, down_product(): jnp.dot(h, w, preferred_element_type=F32)  5.42 us
  transfers between devices with their start and end apart: 21, of which 13 were waited for; matrix products, arithmetic and copies ran while one was open for 4% of the time, Pallas kernels for 18%

profile of v8, /device:TPU:0, one launch (start us, length us, event | category | flops | bytes accessed | tf_op | source)
XLA Modules:
  0.0 123.3 jit_solution(9661807868946861651)
XLA Ops:
  0.7 1.7 %place_rows.1 = bf16[32,3,640]{2,1,0:T(4,128)(2,1)} custom-call(bf16[4,4096]{1,0:T(4,128)(2,1)} %tokens_ref.1, s32[2,4]{1,0:T(2,128)} %bitcast.61, f32[2,4]{1,0:T(2,128)} %bitcast.62), custom_call_target="tpu_custom_call" | custom-call | tf_op jit(solution)/shard_map/place_rows/pallas_call | solution.py:94
  2.5 15.2 %all_to_all.10 = bf16[32,3,640]{2,1,0:T(4,128)(2,1)S(1)} all-to-all(bf16[32,3,640]{2,1,0:T(4,128)(2,1)} %place_rows.1), channel_id=1, replica_groups=mesh['branch'=4,'shard'=8] {'branch','shard'}, dimensions={0} | all-to-all | bytes 245760 | tf_op jit(solution)/shard_map/all_to_all | solution.py:303
  17.7 0.1 reshape.17
  17.8 0.6 copy-done.3
  18.5 3.1 %column_pieces.5 = (bf16[96,1792]{1,0:T(8,128)(2,1)S(1)}, bf16[96,1792]{1,0:T(8,128)(2,1)S(1)}) custom-call(s32[2]{0:T(128)S(1)} %pad_add_fusion.where_ref, s32[128]{0:T(128)S(1)} %copy-done.3, bf16[96,512]{1,0:T(8,128)(2,1)S(1)} %slice.60.rows_ref, bf16[1,512,14336]{2,1,0:T(8,128)(2,1)} %refs_1_.11, bf16[1,512,14336]{2,1,0:T(8,128)(2,1)} %refs_3_.5), custom_call_target="tpu_custom_call" | custom-call | flops 352321536 | bytes 3670016 | tf_op jit(solution)/shard_map/column_pieces/pallas_call | solution.py:125
  21.6 1.6 %collective-permute-start.9 = (bf16[96,1792]{1,0:T(8,128)(2,1)S(1)}, bf16[96,1792]{1,0:T(8,128)(2,1)S(1)}, u32[]{:S(2)}, u32[]{:S(2)}) collective-permute-start(bf16[96,1792]{1,0:T(8,128)(2,1)S(1)} %get-tuple-element.77), channel_id=1, source_target_pairs={{2,0},{4,2},{6,4},{7,6},{5,7},{3,5},{1,3},{0,1},{10,8},{12,10},{14... | collective-permute-start | bytes 1032200 | tf_op jit(solution)/shard_map/ppermute | solution.py:320
  23.1 0.5 collective-permute-start
  23.6 3.3 %turn_columns.1 = (bf16[2,512,512]{2,1,0:T(8,128)(2,1)}, bf16[2,512,512]{2,1,0:T(8,128)(2,1)}) custom-call(s32[2]{0:T(128)} %copy-done.1, bf16[1,512,2048]{2,1,0:T(8,128)(2,1)} %refs_1_.7, bf16[1,512,2048]{2,1,0:T(8,128)(2,1)} %refs_1_.7), custom_call_target="tpu_custom_call" | custom-call | bytes 4194304 | tf_op jit(solution)/shard_map/turn_columns/pallas_call | solution.py:172
  27.0 0.6 copy-done.2
  27.6 3.3 %column_pieces.6 = (bf16[96,1792]{1,0:T(8,128)(2,1)S(1)}, bf16[96,1792]{1,0:T(8,128)(2,1)S(1)}) custom-call(s32[2]{0:T(128)S(1)} %copy-done.2, s32[128]{0:T(128)S(1)} %copy-done.4, bf16[96,512]{1,0:T(8,128)(2,1)S(1)} %slice.60.rows_ref, bf16[1,512,14336]{2,1,0:T(8,128)(2,1)} %refs_1_.11, bf16[1,512,14336]{2,1,0:T(8,128)(2,1)} %refs_3_.5), custom_call_target="tpu_custom_call" | custom-call | flops 352321536 | bytes 3670016 | tf_op jit(solution)/shard_map/column_pieces/pallas_call | solution.py:125
  31.0 0.8 collective-permute-done.9
  31.8 1.5 %collective-permute-start.10 = (bf16[96,1792]{1,0:T(8,128)(2,1)S(1)}, bf16[96,1792]{1,0:T(8,128)(2,1)S(1)}, u32[]{:S(2)}, u32[]{:S(2)}) collective-permute-start(bf16[96,1792]{1,0:T(8,128)(2,1)S(1)} %add_convert_fusion.5), channel_id=1, source_target_pairs={{2,0},{4,2},{6,4},{7,6},{5,7},{3,5},{1,3},{0,1},{10,8},{12,10},{14... | collective-permute-start | bytes 1032200 | tf_op jit(solution)/shard_map/ppermute | solution.py:320
  33.4 5.0 %column_pieces.7 = (bf16[96,1792]{1,0:T(8,128)(2,1)S(1)}, bf16[96,1792]{1,0:T(8,128)(2,1)S(1)}, bf16[96,1792]{1,0:T(8,128)(2,1)S(1)}, bf16[96,1792]{1,0:T(8,128)(2,1)S(1)}) custom-call(s32[2]{0:T(128)S(1)} %copy-done.2, s32[128]{0:T(128)S(1)} %copy-done.4, bf16[96,512]{1,0:T(8,128)(2,1)S(1)} %slice.60.rows_ref, bf16[1,512,14336]{2,1,0:T(8,128)(2,1)} %refs_1_.11, ...), custom_call_target="tpu_custom_call" | custom-call | flops 704643072 | bytes 7340032 | tf_op jit(solution)/shard_map/column_pieces/pallas_call | solution.py:125
  38.5 3.1 %collective-permute-done.10 = bf16[96,1792]{1,0:T(8,128)(2,1)S(1)} collective-permute-done((bf16[96,1792]{1,0:T(8,128)(2,1)S(1)}, bf16[96,1792]{1,0:T(8,128)(2,1)S(1)}, u32[]{:S(2)}, u32[]{:S(2)}) %collective-permute-start.10) | collective-permute-done | bytes 344096 | tf_op jit(solution)/shard_map/ppermute | solution.py:320
  41.7 1.6 %collective-permute-start.11 = (bf16[96,1792]{1,0:T(8,128)(2,1)S(1)}, bf16[96,1792]{1,0:T(8,128)(2,1)S(1)}, u32[]{:S(2)}, u32[]{:S(2)}) collective-permute-start(bf16[96,1792]{1,0:T(8,128)(2,1)S(1)} %add_convert_fusion.4), channel_id=1, source_target_pairs={{2,0},{4,2},{6,4},{7,6},{5,7},{3,5},{1,3},{0,1},{10,8},{12,10},{14... | collective-permute-start | bytes 1032200 | tf_op jit(solution)/shard_map/ppermute | solution.py:320
  43.2 0.5 collective-permute-start.1
  43.7 6.8 %collective-permute-done.11 = bf16[96,1792]{1,0:T(8,128)(2,1)S(1)} collective-permute-done((bf16[96,1792]{1,0:T(8,128)(2,1)S(1)}, bf16[96,1792]{1,0:T(8,128)(2,1)S(1)}, u32[]{:S(2)}, u32[]{:S(2)}) %collective-permute-start.11) | collective-permute-done | bytes 344096 | tf_op jit(solution)/shard_map/ppermute | solution.py:320
  50.6 1.6 %collective-permute-start.12 = (bf16[96,1792]{1,0:T(8,128)(2,1)S(1)}, bf16[96,1792]{1,0:T(8,128)(2,1)S(1)}, u32[]{:S(2)}, u32[]{:S(2)}) collective-permute-start(bf16[96,1792]{1,0:T(8,128)(2,1)S(1)} %add_convert_fusion.3), channel_id=1, source_target_pairs={{2,0},{4,2},{6,4},{7,6},{5,7},{3,5},{1,3},{0,1},{10,8},{12,10},{14... | collective-permute-start | bytes 1032200 | tf_op jit(solution)/shard_map/ppermute | solution.py:320
  52.3 0.5 collective-permute-start.3
  52.8 0.3 convert_add_fusion
  53.2 1.2 collective-permute-start.6
  54.4 5.0 %column_pieces.8 = (bf16[96,1792]{1,0:T(8,128)(2,1)S(1)}, bf16[96,1792]{1,0:T(8,128)(2,1)S(1)}, bf16[96,1792]{1,0:T(8,128)(2,1)S(1)}, bf16[96,1792]{1,0:T(8,128)(2,1)S(1)}) custom-call(s32[2]{0:T(128)S(1)} %copy-done.2, s32[128]{0:T(128)S(1)} %copy-done.4, bf16[96,512]{1,0:T(8,128)(2,1)S(1)} %slice.60.rows_ref, bf16[1,512,14336]{2,1,0:T(8,128)(2,1)} %refs_1_.11, ...), custom_call_target="tpu_custom_call" | custom-call | flops 704643072 | bytes 7340032 | tf_op jit(solution)/shard_map/column_pieces/pallas_call | solution.py:125
  59.4 1.1 collective-permute-done.3
  60.5 0.5 collective-permute-start.4
  61.2 1.6 %collective-permute-start.13 = (bf16[96,1792]{1,0:T(8,128)(2,1)S(1)}, bf16[96,1792]{1,0:T(8,128)(2,1)S(1)}, u32[]{:S(2)}, u32[]{:S(2)}) collective-permute-start(bf16[96,1792]{1,0:T(8,128)(2,1)S(1)} %add_convert_fusion.2), channel_id=1, source_target_pairs={{2,0},{4,2},{6,4},{7,6},{5,7},{3,5},{1,3},{0,1},{10,8},{12,10},{14... | collective-permute-start | bytes 1032200 | tf_op jit(solution)/shard_map/ppermute | solution.py:320
  62.8 5.8 %column_pieces.9 = (bf16[96,1792]{1,0:T(8,128)(2,1)S(1)}, bf16[96,1792]{1,0:T(8,128)(2,1)S(1)}, bf16[96,1792]{1,0:T(8,128)(2,1)S(1)}, bf16[96,1792]{1,0:T(8,128)(2,1)S(1)}) custom-call(s32[2]{0:T(128)S(1)} %copy-done.2, s32[128]{0:T(128)S(1)} %copy-done.4, bf16[96,512]{1,0:T(8,128)(2,1)S(1)} %slice.60.rows_ref, bf16[1,512,14336]{2,1,0:T(8,128)(2,1)} %refs_1_.11, ...), custom_call_target="tpu_custom_call" | custom-call | flops 704643072 | bytes 7340032 | tf_op jit(solution)/shard_map/column_pieces/pallas_call | solution.py:125
  68.7 0.6 collective-permute-start.5
  69.3 0.4 collective-permute-done.13
  69.8 1.4 %collective-permute-start.14 = (bf16[96,1792]{1,0:T(8,128)(2,1)S(1)}, bf16[96,1792]{1,0:T(8,128)(2,1)S(1)}, u32[]{:S(2)}, u32[]{:S(2)}) collective-permute-start(bf16[96,1792]{1,0:T(8,128)(2,1)S(1)} %add_convert_fusion.1), channel_id=1, source_target_pairs={{2,0},{4,2},{6,4},{7,6},{5,7},{3,5},{1,3},{0,1},{10,8},{12,10},{14... | collective-permute-start | bytes 1032200 | tf_op jit(solution)/shard_map/ppermute | solution.py:320
  71.2 5.7 %collective-permute-done.5 = bf16[96,1792]{1,0:T(8,128)(2,1)S(1)} collective-permute-done((bf16[96,1792]{1,0:T(8,128)(2,1)S(1)}, bf16[96,1792]{1,0:T(8,128)(2,1)S(1)}, u32[]{:S(2)}, u32[]{:S(2)}) %collective-permute-start.5) | collective-permute-done | bytes 344096 | tf_op jit(solution)/shard_map/ppermute | solution.py:319
  76.9 1.0 fusion.9
  77.9 0.7 collective-permute-start.7
  78.8 1.4 %collective-permute-start.15 = (bf16[96,1792]{1,0:T(8,128)(2,1)S(1)}, bf16[96,1792]{1,0:T(8,128)(2,1)S(1)}, u32[]{:S(2)}, u32[]{:S(2)}) collective-permute-start(bf16[96,1792]{1,0:T(8,128)(2,1)S(1)} %add_convert_fusion), channel_id=1, source_target_pairs={{2,0},{4,2},{6,4},{7,6},{5,7},{3,5},{1,3},{0,1},{10,8},{12,10},{14... | collective-permute-start | bytes 1032200 | tf_op jit(solution)/shard_map/ppermute | solution.py:320
  80.1 7.9 %collective-permute-done.7 = bf16[96,1792]{1,0:T(8,128)(2,1)S(1)} collective-permute-done((bf16[96,1792]{1,0:T(8,128)(2,1)S(1)}, bf16[96,1792]{1,0:T(8,128)(2,1)S(1)}, u32[]{:S(2)}, u32[]{:S(2)}) %collective-permute-start.7) | collective-permute-done | bytes 344096 | tf_op jit(solution)/shard_map/ppermute | solution.py:319
  88.1 1.0 collective-permute-start.8
  89.1 6.5 %collective-permute-done.8.gate_ref = bf16[96,1792]{1,0:T(8,128)(2,1)S(1)} collective-permute-done((bf16[96,1792]{1,0:T(8,128)(2,1)S(1)}, bf16[96,1792]{1,0:T(8,128)(2,1)S(1)}, u32[]{:S(2)}, u32[]{:S(2)}) %collective-permute-start.8) | collective-permute-done | bytes 344096 | tf_op jit(solution)/shard_map/ppermute | solution.py:319
  95.6 1.2 hidden_rows.1
  96.8 2.7 %fusion.4 = bf16[64,4096]{1,0:T(8,128)(2,1)S(1)} fusion(bf16[64,1792]{1,0:T(8,128)(2,1)S(1)} %get-tuple-element.88, bf16[1,1792,4096]{2,1,0:T(8,128)(2,1)S(1)} %bitcast.57), kind=kOutput, calls=%fused_computation.4 | convolution fusion | flops 939786240 | bytes 15433728 | tf_op jit(solution)/shard_map/dot_general | solution.py:245
  99.6 2.7 %fusion.2 = f32[64,4096]{1,0:T(8,128)S(1)} fusion(bf16[64,1792]{1,0:T(8,128)(2,1)S(1)} %get-tuple-element.87, bf16[1,1792,4096]{2,1,0:T(8,128)(2,1)S(1)} %bitcast.57), kind=kOutput, calls=%fused_computation.2 | convolution fusion | flops 939524096 | bytes 15958016 | tf_op jit(solution)/shard_map/dot_general | solution.py:245
  102.4 0.1 convert_add_fusion.1
  102.5 1.1 collective-permute-start.17
  103.7 4.8 %collective-permute-done.17 = bf16[2,16,2048]{2,1,0:T(8,128)(2,1)S(1)} collective-permute-done((bf16[2,16,2048]{2,1,0:T(8,128)(2,1)S(1)}, bf16[2,16,2048]{2,1,0:T(8,128)(2,1)S(1)}, u32[]{:S(2)}, u32[]{:S(2)}) %collective-permute-start.17) | collective-permute-done | bytes 131104 | tf_op jit(solution)/shard_map/ppermute | solution.py:267
  108.6 0.7 collective-permute-done.19
  109.4 1.1 collective-permute-start.20
  110.4 2.4 %collective-permute-done.18 = bf16[16,2048]{1,0:T(8,128)(2,1)S(1)} collective-permute-done((bf16[16,2048]{1,0:T(8,128)(2,1)S(1)}, bf16[16,2048]{1,0:T(8,128)(2,1)S(1)}, u32[]{:S(2)}, u32[]{:S(2)}) %collective-permute-start.18) | collective-permute-done | bytes 65568 | tf_op jit(solution)/shard_map/ppermute | solution.py:267
  112.9 0.8 collective-permute-done.20
  113.8 8.8 %all_to_all.11 = bf16[4,4,4096]{2,1,0:T(4,128)(2,1)S(1)} all-to-all(bf16[4,4,4096]{2,1,0:T(4,128)(2,1)S(1)} %convert_element_type.215), channel_id=1, replica_groups={{0,2,4,6},{1,3,5,7},{8,10,12,14},{9,11,13,15},{16,18,20,22},{17,19,21,2..., dimensions={0} | all-to-all | bytes 262144 | tf_op jit(solution)/shard_map/all_to_all | solution.py:379
  122.6 0.7 reduce_sum.12
  (59 shorter events, 1.7 us)
Async XLA Ops:
  0.7 20.8 %copy-start.1 = (s32[2]{0:T(128)}, s32[2]{0:T(128)S(1)}, u32[]{:S(2)}) copy-start(s32[2]{0:T(128)S(1)} %pad_add_fusion.where_ref) | copy-start | bytes 28
  17.8 0.7 copy-start.3
  18.5 8.5 %copy-start.4 = (s32[128]{0:T(128)S(1)}, s32[128]{0:T(128)}, u32[]{:S(2)}) copy-start(s32[128]{0:T(128)} %constant.18.clone.table_ref) | copy-start | bytes 1540
  21.6 10.2 %collective-permute-start.9 = (bf16[96,1792]{1,0:T(8,128)(2,1)S(1)}, bf16[96,1792]{1,0:T(8,128)(2,1)S(1)}, u32[]{:S(2)}, u32[]{:S(2)}) collective-permute-start(bf16[96,1792]{1,0:T(8,128)(2,1)S(1)} %get-tuple-element.77), channel_id=1, source_target_pairs={{2,0},{4,2},{6,4},{7,6},{5,7},{3,5},{1,3},{0,1},{10,8},{12,10},{14... | collective-permute-start | bytes 1032200 | tf_op jit(solution)/shard_map/ppermute | solution.py:320
  23.1 10.2 %collective-permute-start = (bf16[96,1792]{1,0:T(8,128)(2,1)S(1)}, bf16[96,1792]{1,0:T(8,128)(2,1)S(1)}, u32[]{:S(2)}, u32[]{:S(2)}) collective-permute-start(bf16[96,1792]{1,0:T(8,128)(2,1)S(1)} %get-tuple-element.51), channel_id=1, source_target_pairs={{0,2},{2,4},{4,6},{6,7},{7,5},{5,3},{3,1},{1,0},{8,10},{10,12},{12... | collective-permute-start | bytes 1032200 | tf_op jit(solution)/shard_map/ppermute | solution.py:319
  27.0 25.3 %collective-permute-start.2 = (bf16[2,512,512]{2,1,0:T(8,128)(2,1)}, bf16[2,512,512]{2,1,0:T(8,128)(2,1)S(1)}, u32[]{:S(2)}, u32[]{:S(2)}) collective-permute-start(bf16[2,512,512]{2,1,0:T(8,128)(2,1)} %get-tuple-element.54), channel_id=1, source_target_pairs={{0,8},{8,0},{16,24},{24,16},{1,9},{9,1},{17,25},{25,17},{2,10},{10... | collective-permute-start | bytes 3145736 | tf_op jit(solution)/shard_map/ppermute | solution.py:330
  27.0 0.7 copy-start.2
  31.8 9.8 %collective-permute-start.10 = (bf16[96,1792]{1,0:T(8,128)(2,1)S(1)}, bf16[96,1792]{1,0:T(8,128)(2,1)S(1)}, u32[]{:S(2)}, u32[]{:S(2)}) collective-permute-start(bf16[96,1792]{1,0:T(8,128)(2,1)S(1)} %add_convert_fusion.5), channel_id=1, source_target_pairs={{2,0},{4,2},{6,4},{7,6},{5,7},{3,5},{1,3},{0,1},{10,8},{12,10},{14... | collective-permute-start | bytes 1032200 | tf_op jit(solution)/shard_map/ppermute | solution.py:320
  33.4 19.4 %copy-start.5 = (bf16[2,512,512]{2,1,0:T(8,128)(2,1)S(1)}, bf16[2,512,512]{2,1,0:T(8,128)(2,1)}, u32[]{:S(2)}) copy-start(bf16[2,512,512]{2,1,0:T(8,128)(2,1)} %get-tuple-element.67) | copy-start | bytes 3145732
  41.7 8.9 %collective-permute-start.11 = (bf16[96,1792]{1,0:T(8,128)(2,1)S(1)}, bf16[96,1792]{1,0:T(8,128)(2,1)S(1)}, u32[]{:S(2)}, u32[]{:S(2)}) collective-permute-start(bf16[96,1792]{1,0:T(8,128)(2,1)S(1)} %add_convert_fusion.4), channel_id=1, source_target_pairs={{2,0},{4,2},{6,4},{7,6},{5,7},{3,5},{1,3},{0,1},{10,8},{12,10},{14... | collective-permute-start | bytes 1032200 | tf_op jit(solution)/shard_map/ppermute | solution.py:320
  43.2 9.0 %collective-permute-start.1 = (bf16[96,1792]{1,0:T(8,128)(2,1)S(1)}, bf16[96,1792]{1,0:T(8,128)(2,1)S(1)}, u32[]{:S(2)}, u32[]{:S(2)}) collective-permute-start(bf16[96,1792]{1,0:T(8,128)(2,1)S(1)} %add_convert_fusion.11), channel_id=1, source_target_pairs={{0,2},{2,4},{4,6},{6,7},{7,5},{5,3},{3,1},{1,0},{8,10},{10,12},{12... | collective-permute-start | bytes 1032200 | tf_op jit(solution)/shard_map/ppermute | solution.py:319
  50.6 10.5 %collective-permute-start.12 = (bf16[96,1792]{1,0:T(8,128)(2,1)S(1)}, bf16[96,1792]{1,0:T(8,128)(2,1)S(1)}, u32[]{:S(2)}, u32[]{:S(2)}) collective-permute-start(bf16[96,1792]{1,0:T(8,128)(2,1)S(1)} %add_convert_fusion.3), channel_id=1, source_target_pairs={{2,0},{4,2},{6,4},{7,6},{5,7},{3,5},{1,3},{0,1},{10,8},{12,10},{14... | collective-permute-start | bytes 1032200 | tf_op jit(solution)/shard_map/ppermute | solution.py:320
  52.3 8.1 %collective-permute-start.3 = (bf16[96,1792]{1,0:T(8,128)(2,1)S(1)}, bf16[96,1792]{1,0:T(8,128)(2,1)S(1)}, u32[]{:S(2)}, u32[]{:S(2)}) collective-permute-start(bf16[96,1792]{1,0:T(8,128)(2,1)S(1)} %add_convert_fusion.10), channel_id=1, source_target_pairs={{0,2},{2,4},{4,6},{6,7},{7,5},{5,3},{3,1},{1,0},{8,10},{10,12},{12... | collective-permute-start | bytes 1032200 | tf_op jit(solution)/shard_map/ppermute | solution.py:319
  53.2 18.0 %collective-permute-start.6 = (bf16[512,512]{1,0:T(8,128)(2,1)S(1)}, bf16[512,512]{1,0:T(8,128)(2,1)S(1)}, u32[]{:S(2)}, u32[]{:S(2)}) collective-permute-start(bf16[512,512]{1,0:T(8,128)(2,1)S(1)} %fusion.10), channel_id=1, source_target_pairs={{0,16},{8,24},{16,0},{24,8},{1,17},{9,25},{17,1},{25,9},{2,18},{10... | collective-permute-start | bytes 1572872 | tf_op jit(solution)/shard_map/ppermute | solution.py:338
  60.5 8.0 %collective-permute-start.4 = (bf16[96,1792]{1,0:T(8,128)(2,1)S(1)}, bf16[96,1792]{1,0:T(8,128)(2,1)S(1)}, u32[]{:S(2)}, u32[]{:S(2)}) collective-permute-start(bf16[96,1792]{1,0:T(8,128)(2,1)S(1)} %add_convert_fusion.9), channel_id=1, source_target_pairs={{0,2},{2,4},{4,6},{6,7},{7,5},{5,3},{3,1},{1,0},{8,10},{10,12},{12... | collective-permute-start | bytes 1032200 | tf_op jit(solution)/shard_map/ppermute | solution.py:319
  61.1 35.7 %slice-start = ((s8[14680064]{0:T(1024)(128)(4,1)}), s8[4194304]{0:T(1024)(128)(4,1)S(1)}, s32[]{:S(2)}) async-start(s8[14680064]{0:T(1024)(128)(4,1)} %bitcast.56), calls=%async_computation.2 | async-start | bytes 8388608
  61.2 34.4 %copy-start = (f32[96,128]{1,0:T(8,128)S(1)}, f32[96,128]{1,0:T(8,128)}, u32[]{:S(2)}) copy-start(f32[96,128]{1,0:T(8,128)} %constant.19.clone.origin_ref) | copy-start | bytes 147460
  61.2 35.6 %slice-start.1 = ((s8[14680064]{0:T(1024)(128)(4,1)}), s8[4194304]{0:T(1024)(128)(4,1)S(1)}, s32[]{:S(2)}) async-start(s8[14680064]{0:T(1024)(128)(4,1)} %bitcast.56), calls=%async_computation.3 | async-start | bytes 8388608
  61.2 35.6 %slice-start.2 = ((s8[14680064]{0:T(1024)(128)(4,1)}), s8[4194304]{0:T(1024)(128)(4,1)S(1)}, s32[]{:S(2)}) async-start(s8[14680064]{0:T(1024)(128)(4,1)} %bitcast.56), calls=%async_computation.4 | async-start | bytes 8388608
  61.2 35.6 %slice-start.3 = ((s8[14680064]{0:T(1024)(128)(4,1)}), s8[2097152]{0:T(1024)(128)(4,1)S(1)}, s32[]{:S(2)}) async-start(s8[14680064]{0:T(1024)(128)(4,1)} %bitcast.56), calls=%async_computation.5 | async-start | bytes 4194304
  61.2 8.5 %collective-permute-start.13 = (bf16[96,1792]{1,0:T(8,128)(2,1)S(1)}, bf16[96,1792]{1,0:T(8,128)(2,1)S(1)}, u32[]{:S(2)}, u32[]{:S(2)}) collective-permute-start(bf16[96,1792]{1,0:T(8,128)(2,1)S(1)} %add_convert_fusion.2), channel_id=1, source_target_pairs={{2,0},{4,2},{6,4},{7,6},{5,7},{3,5},{1,3},{0,1},{10,8},{12,10},{14... | collective-permute-start | bytes 1032200 | tf_op jit(solution)/shard_map/ppermute | solution.py:320
  68.7 8.2 %collective-permute-start.5 = (bf16[96,1792]{1,0:T(8,128)(2,1)S(1)}, bf16[96,1792]{1,0:T(8,128)(2,1)S(1)}, u32[]{:S(2)}, u32[]{:S(2)}) collective-permute-start(bf16[96,1792]{1,0:T(8,128)(2,1)S(1)} %add_convert_fusion.8), channel_id=1, source_target_pairs={{0,2},{2,4},{4,6},{6,7},{7,5},{5,3},{3,1},{1,0},{8,10},{10,12},{12... | collective-permute-start | bytes 1032200 | tf_op jit(solution)/shard_map/ppermute | solution.py:319
  69.8 8.9 %collective-permute-start.14 = (bf16[96,1792]{1,0:T(8,128)(2,1)S(1)}, bf16[96,1792]{1,0:T(8,128)(2,1)S(1)}, u32[]{:S(2)}, u32[]{:S(2)}) collective-permute-start(bf16[96,1792]{1,0:T(8,128)(2,1)S(1)} %add_convert_fusion.1), channel_id=1, source_target_pairs={{2,0},{4,2},{6,4},{7,6},{5,7},{3,5},{1,3},{0,1},{10,8},{12,10},{14... | collective-permute-start | bytes 1032200 | tf_op jit(solution)/shard_map/ppermute | solution.py:320
  77.9 10.1 %collective-permute-start.7 = (bf16[96,1792]{1,0:T(8,128)(2,1)S(1)}, bf16[96,1792]{1,0:T(8,128)(2,1)S(1)}, u32[]{:S(2)}, u32[]{:S(2)}) collective-permute-start(bf16[96,1792]{1,0:T(8,128)(2,1)S(1)} %add_convert_fusion.7), channel_id=1, source_target_pairs={{0,2},{2,4},{4,6},{6,7},{7,5},{5,3},{3,1},{1,0},{8,10},{10,12},{12... | collective-permute-start | bytes 1032200 | tf_op jit(solution)/shard_map/ppermute | solution.py:319
  78.8 10.3 %collective-permute-start.15 = (bf16[96,1792]{1,0:T(8,128)(2,1)S(1)}, bf16[96,1792]{1,0:T(8,128)(2,1)S(1)}, u32[]{:S(2)}, u32[]{:S(2)}) collective-permute-start(bf16[96,1792]{1,0:T(8,128)(2,1)S(1)} %add_convert_fusion), channel_id=1, source_target_pairs={{2,0},{4,2},{6,4},{7,6},{5,7},{3,5},{1,3},{0,1},{10,8},{12,10},{14... | collective-permute-start | bytes 1032200 | tf_op jit(solution)/shard_map/ppermute | solution.py:320
  88.1 7.5 %collective-permute-start.8 = (bf16[96,1792]{1,0:T(8,128)(2,1)S(1)}, bf16[96,1792]{1,0:T(8,128)(2,1)S(1)}, u32[]{:S(2)}, u32[]{:S(2)}) collective-permute-start(bf16[96,1792]{1,0:T(8,128)(2,1)S(1)} %add_convert_fusion.6), channel_id=1, source_target_pairs={{0,2},{2,4},{4,6},{6,7},{7,5},{5,3},{3,1},{1,0},{8,10},{10,12},{12... | collective-permute-start | bytes 1032200 | tf_op jit(solution)/shard_map/ppermute | solution.py:319
  99.6 2.8 %collective-permute-start.16 = (bf16[64,4096]{1,0:T(8,128)(2,1)S(1)}, bf16[64,4096]{1,0:T(8,128)(2,1)S(1)}, u32[]{:S(2)}, u32[]{:S(2)}) collective-permute-start(bf16[64,4096]{1,0:T(8,128)(2,1)S(1)} %fusion.4), channel_id=1, source_target_pairs={{0,8},{8,0},{16,24},{24,16},{1,9},{9,1},{17,25},{25,17},{2,10},{10... | collective-permute-start | bytes 1572872 | tf_op jit(solution)/shard_map/ppermute | solution.py:360
  102.5 6.0 %collective-permute-start.17 = (bf16[2,16,2048]{2,1,0:T(8,128)(2,1)S(1)}, bf16[2,16,2048]{2,1,0:T(8,128)(2,1)S(1)}, u32[]{:S(2)}, u32[]{:S(2)}) collective-permute-start(bf16[2,16,2048]{2,1,0:T(8,128)(2,1)S(1)} %fusion.13), channel_id=1, source_target_pairs={{0,16},{8,24},{16,0},{24,8},{1,17},{9,25},{17,1},{25,9},{2,18},{10... | collective-permute-start | bytes 393224 | tf_op jit(solution)/shard_map/ppermute | solution.py:267
  103.6 5.7 %collective-permute-start.19 = (bf16[2,16,2048]{2,1,0:T(8,128)(2,1)S(1)}, bf16[2,16,2048]{2,1,0:T(8,128)(2,1)S(1)}, u32[]{:S(2)}, u32[]{:S(2)}) collective-permute-start(bf16[2,16,2048]{2,1,0:T(8,128)(2,1)S(1)} %fusion.14), channel_id=1, source_target_pairs={{0,1},{1,0},{2,3},{3,2},{4,5},{5,4},{6,7},{7,6},{8,9},{9,8},{10,11... | collective-permute-start | bytes 393224 | tf_op jit(solution)/shard_map/ppermute | solution.py:267
  108.5 4.3 %collective-permute-start.18 = (bf16[16,2048]{1,0:T(8,128)(2,1)S(1)}, bf16[16,2048]{1,0:T(8,128)(2,1)S(1)}, u32[]{:S(2)}, u32[]{:S(2)}) collective-permute-start(bf16[16,2048]{1,0:T(8,128)(2,1)S(1)} %fusion.19), channel_id=1, source_target_pairs={{0,1},{1,0},{2,3},{3,2},{4,5},{5,4},{6,7},{7,6},{8,9},{9,8},{10,11... | collective-permute-start | bytes 196616 | tf_op jit(solution)/shard_map/ppermute | solution.py:267
  109.4 4.3 %collective-permute-start.20 = (bf16[16,2048]{1,0:T(8,128)(2,1)S(1)}, bf16[16,2048]{1,0:T(8,128)(2,1)S(1)}, u32[]{:S(2)}, u32[]{:S(2)}) collective-permute-start(bf16[16,2048]{1,0:T(8,128)(2,1)S(1)} %fusion.20), channel_id=1, source_target_pairs={{0,16},{8,24},{16,0},{24,8},{1,17},{9,25},{17,1},{25,9},{2,18},{10... | collective-permute-start | bytes 196616 | tf_op jit(solution)/shard_map/ppermute | solution.py:267

commit v9 on v8

--- a/solution.py
+++ b/solution.py
@@ -29,16 +29,6 @@
         line = xs[1:] if i % 2 == 0 else list(reversed(xs[1:]))
         order += [at[(z, x)] for x in line]
     return order
-
-
-def grid_columns(devices):
-    places = [getattr(d, "coords", None) for d in devices]
-    if any(p is None for p in places):
-        return 1
-    columns = len({p[0] for p in places})
-    line = sorted(range(len(places)), key=lambda i: (places[i][2], places[i][0]))
-    whole = len({(p[2], p[0]) for p in places}) == len(places)
-    return columns if whole and line == list(range(len(places))) and len(places) % columns == 0 else 1
 
 
 def core_count(devices):
@@ -184,8 +174,8 @@
 
 
 def hidden_rows(where, gate_in, up_in, gate_own, up_own, tails, origin, sizes, parts):
-    experts, shards, cores, columns, token_count = sizes
-    chips, lines = experts // cores, shards // columns
+    experts, shards, cores, token_count = sizes
+    chips = experts // cores
     total = experts * shards * token_count
     kept = total // cores
     count, slice_width = gate_own.shape
@@ -193,18 +183,12 @@
     chunk = next(c for c in (256, LANES, cut_width) if cut_width % c == 0)
 
     def kernel(where_ref, gate_ref, up_ref, gate_own_ref, up_own_ref, tail_ref, origin_ref, *outs):
-        b, s = where_ref[0], where_ref[1]
-        mine = (
-            lax.rem(b, jnp.int32(cores)), lax.div(b, jnp.int32(cores)),
-            lax.rem(s, jnp.int32(columns)), jnp.int32(0),
-        )
         tail = tail_ref[...].astype(F32)
         number, weight = tail[:, 0:1], tail[:, 1:2] + tail[:, 2:3]
         place = origin_ref[...]
-        target = jnp.zeros((count, 1), F32)
-        for i, size in enumerate((cores, chips, columns, lines)):
-            away = place[:, i : i + 1] - mine[i].astype(F32)
-            target = target * size + jnp.where(away < 0, away + size, away)
+        core = place[:, 0:1] - lax.rem(where_ref[0], jnp.int32(cores)).astype(F32)
+        core = jnp.where(core < 0, core + cores, core)
+        target = (core * chips + place[:, 1:2]) * shards + place[:, 2:3]
         target = target * token_count + number - 1.0
         target = jnp.where(number > 0, target, -1.0).astype(jnp.int32)
         spread = target == lax.broadcasted_iota(jnp.int32, (count, total), 1)
@@ -253,22 +237,7 @@
     ]
 
 
-def shard_target(size, columns, x_step, z_step):
-    lines = size // columns
-    return [
-        (i, (i // columns + z_step) % lines * columns + (i + x_step) % columns)
-        for i in range(size)
-    ]
-
-
-def direct_sum(x, axis_name, target):
-    total = x[0]
-    for k in range(1, x.shape[0]):
-        total = total + lax.ppermute(x[k].astype(BF16), axis_name, target(k)).astype(F32)
-    return total
-
-
-def local(order, cores, columns, tokens, routes, mixing, gate_weight, up_weight, down_weight, key_value):
+def local(order, cores, tokens, routes, mixing, gate_weight, up_weight, down_weight, key_value):
     experts = lax.axis_size("branch")
     shards = lax.axis_size("shard")
     chips = experts // cores
@@ -277,8 +246,7 @@
     depth = gate_weight.shape[1]
     slice_width = down_weight.shape[1]
     count = experts * shards * capacity
-    lines = shards // columns
-    sizes = (experts, shards, cores, columns, token_count)
+    sizes = (experts, shards, cores, token_count)
     where = jnp.stack([lax.axis_index("branch"), lax.axis_index("shard")]).astype(jnp.int32)
 
     place = np.argsort(np.asarray(order))
@@ -294,8 +262,7 @@
     origin = np.zeros((count, LANES), np.float32)
     origin[:, 0] = source // shards % cores
     origin[:, 1] = source // shards // cores
-    origin[:, 2] = source % shards % columns
-    origin[:, 3] = source % shards // columns
+    origin[:, 2] = source % shards
     origin = jnp.asarray(origin)
 
     cells = place_rows(tokens, routes, mixing, experts, capacity, shards)
@@ -320,8 +287,7 @@
         up_in = lax.ppermute(up_sum, "shard", back)
         if sliced and len(gates) < shards:
             more = column_pieces(
-                now, table, rows, gate_weight, up_weight, shards, len(gates),
-                1 if t == 1 else min(2, shards - len(gates)), 1,
+                now, table, rows, gate_weight, up_weight, shards, len(gates), 1, cuts
             )
             gates, ups = gates + more[0], ups + more[1]
         if t == 1:
@@ -364,20 +330,13 @@
     mixed, sent = lax.optimization_barrier((mixed, sent))
     mixed = mixed + sum(x.astype(F32) for x in sent)
 
-    def over_chips(x):
-        return direct_sum(x, "branch", lambda k: branch_target(experts, cores, 0, k))
-
-    def over_columns(x):
-        return direct_sum(x, "shard", lambda k: shard_target(shards, columns, k, 0))
-
-    mixed = mixed.reshape(chips, columns, lines * token_count, width)
-    left = over_chips(mixed[..., : width // 2])
-    right = over_columns(mixed[..., width // 2 :].swapaxes(0, 1))
-    left, right = over_columns(left), over_chips(right)
-    mixed = jnp.concatenate([left, right], axis=1).reshape(lines, token_count, width)
-    groups = [[z * columns + x for z in range(lines)] for x in range(columns)]
+    mixed = mixed.astype(BF16).reshape(chips * shards, token_count, width)
+    groups = [
+        [(chip * cores + core) * shards + s for chip in range(chips) for s in range(shards)]
+        for core in range(cores)
+    ]
     mixed = lax.all_to_all(
-        mixed.astype(BF16), "shard", split_axis=0, concat_axis=0, axis_index_groups=groups, tiled=True
+        mixed, ("branch", "shard"), split_axis=0, concat_axis=0, axis_index_groups=groups, tiled=True
     )
     return jnp.sum(mixed.astype(F32), axis=0).astype(BF16), merged_kv
 
@@ -386,9 +345,8 @@
     grid = mesh.devices
     order = ring_order(list(grid[0, :]))
     cores = core_count(list(grid[:, 0]))
-    columns = grid_columns(list(grid[0, :]))
     return jax.shard_map(
-        functools.partial(local, order, cores, columns),
+        functools.partial(local, order, cores),
         mesh=mesh,
         in_specs=(
             P(("branch", "shard"), None),

time: 124 us -> 115 us (0.927)
  waiting for transfers between devices: 41 us -> 19.4 us
  blocking collectives: 24 us -> 34.5 us
  Pallas kernels: 28.4 us -> 31.1 us
    ppermute x7, waiting for transfers between devices: 21.2 us -> 6.68 us  [local(): gate_in = lax.ppermute(gate_sum, 'shard', forth)]
    all_to_all x1, blocking collectives: 8.79 us -> 19.3 us  [local(): lax.all_to_all(mixed, ('branch', 'shard'), split_axis=0, concat_axis=0, a...]
    ppermute x4 -> x0, waiting for transfers between devices: 8.71 us -> none  [direct_sum(): lax.ppermute(x[k].astype(BF16), axis_name, target(k)).astype(F32)]
    pallas_call x5 -> x8, Pallas kernels: 22.2 us -> 24.9 us  [column_pieces(): pl.pallas_call(kernel, out_shape=[jax.ShapeDtypeStruct((count, width), BF...]
    ppermute x4 -> x0, starting transfers between devices: 2.3 us -> none  [direct_sum(): lax.ppermute(x[k].astype(BF16), axis_name, target(k)).astype(F32)]
    ppermute x7, starting transfers between devices: 4.29 us -> 5.84 us  [local(): gate_in = lax.ppermute(gate_sum, 'shard', forth)]
    ppermute x7, waiting for transfers between devices: 11.1 us -> 12.7 us  [local(): up_in = lax.ppermute(up_sum, 'shard', back)]
  transfers between devices with their start and end apart: 21 -> 17, of which waited for: 13 -> 10; matrix products, arithmetic and copies ran while one was open for 4% -> 4% of each run, Pallas kernels for 18% -> 22%
where the time goes in v9:
time: 115 us
  blocking collectives  34.5 us (30%)
  Pallas kernels  31.1 us (27%)
  waiting for transfers between devices  19.4 us (17%)
  starting transfers between devices  18.3 us (16%)
  matrix products  5.41 us (5%)
  other arithmetic  3.27 us (3%)
  local copies, waits for them, and re-layouts  1.71 us (1%)
    pallas_call x8, Pallas kernels, column_pieces(): pl.pallas_call(kernel, out_shape=[jax.ShapeDtypeStruct((count, width), BF...  24.9 us
    all_to_all x1, blocking collectives, local(): lax.all_to_all(mixed, ('branch', 'shard'), split_axis=0, concat_axis=0, a...  19.3 us
    all_to_all x1, blocking collectives, local(): lax.all_to_all(cells, ('branch', 'shard'), split_axis=0, concat_axis=0, t...  15.2 us
    ppermute x7, waiting for transfers between devices, local(): up_in = lax.ppermute(up_sum, 'shard', back)  12.7 us
    ppermute x7, starting transfers between devices, local(): up_in = lax.ppermute(up_sum, 'shard', back)  11.3 us
    ppermute x7, waiting for transfers between devices, local(): gate_in = lax.ppermute(gate_sum, 'shard', forth)  6.68 us
    ppermute x7, starting transfers between devices, local(): gate_in = lax.ppermute(gate_sum, 'shard', forth)  5.84 us
    dot_general x2, matrix products, down_product(): jnp.dot(h, w, preferred_element_type=F32)  5.41 us
  transfers between devices with their start and end apart: 17, of which 10 were waited for; matrix products, arithmetic and copies ran while one was open for 4% of the time, Pallas kernels for 22%

profile of v9, /device:TPU:0, one launch (start us, length us, event | category | flops | bytes accessed | tf_op | source)
XLA Modules:
  0.0 114.6 jit_solution(9503801580674192458)
XLA Ops:
  0.7 1.7 %place_rows.1 = bf16[32,3,640]{2,1,0:T(4,128)(2,1)} custom-call(bf16[4,4096]{1,0:T(4,128)(2,1)} %tokens_ref.1, s32[2,4]{1,0:T(2,128)} %bitcast.25, f32[2,4]{1,0:T(2,128)} %bitcast.26), custom_call_target="tpu_custom_call" | custom-call | tf_op jit(solution)/shard_map/place_rows/pallas_call | solution.py:84
  2.5 15.2 %all_to_all.10 = bf16[32,3,640]{2,1,0:T(4,128)(2,1)S(1)} all-to-all(bf16[32,3,640]{2,1,0:T(4,128)(2,1)} %place_rows.1), channel_id=1, replica_groups=mesh['branch'=4,'shard'=8] {'branch','shard'}, dimensions={0} | all-to-all | bytes 245760 | tf_op jit(solution)/shard_map/all_to_all | solution.py:270
  17.7 0.1 reshape.11
  17.8 0.6 copy-done.3
  18.5 3.1 %column_pieces.8 = (bf16[96,1792]{1,0:T(8,128)(2,1)S(1)}, bf16[96,1792]{1,0:T(8,128)(2,1)S(1)}) custom-call(s32[2]{0:T(128)S(1)} %pad_add_fusion.where_ref, s32[128]{0:T(128)S(1)} %copy-done.3, bf16[96,512]{1,0:T(8,128)(2,1)S(1)} %slice.17.rows_ref, bf16[1,512,14336]{2,1,0:T(8,128)(2,1)} %refs_0_.17, bf16[1,512,14336]{2,1,0:T(8,128)(2,1)} %refs_1_.17), custom_call_target="tpu_custom_call" | custom-call | flops 352321536 | bytes 3670016 | tf_op jit(solution)/shard_map/column_pieces/pallas_call | solution.py:115
  21.6 1.6 %collective-permute-start.9 = (bf16[96,1792]{1,0:T(8,128)(2,1)S(1)}, bf16[96,1792]{1,0:T(8,128)(2,1)S(1)}, u32[]{:S(2)}, u32[]{:S(2)}) collective-permute-start(bf16[96,1792]{1,0:T(8,128)(2,1)S(1)} %get-tuple-element.82), channel_id=1, source_target_pairs={{2,0},{4,2},{6,4},{7,6},{5,7},{3,5},{1,3},{0,1},{10,8},{12,10},{14... | collective-permute-start | bytes 1032200 | tf_op jit(solution)/shard_map/ppermute | solution.py:287
  23.1 0.5 collective-permute-start
  23.6 3.3 %turn_columns.1 = (bf16[2,512,512]{2,1,0:T(8,128)(2,1)}, bf16[2,512,512]{2,1,0:T(8,128)(2,1)}) custom-call(s32[2]{0:T(128)} %copy-done, bf16[1,512,2048]{2,1,0:T(8,128)(2,1)} %refs_1_.10, bf16[1,512,2048]{2,1,0:T(8,128)(2,1)} %refs_1_.10), custom_call_target="tpu_custom_call" | custom-call | bytes 4194304 | tf_op jit(solution)/shard_map/turn_columns/pallas_call | solution.py:162
  27.0 0.6 copy-done.1
  27.6 3.1 %column_pieces.9 = (bf16[96,1792]{1,0:T(8,128)(2,1)S(1)}, bf16[96,1792]{1,0:T(8,128)(2,1)S(1)}) custom-call(s32[2]{0:T(128)S(1)} %copy-done.1, s32[128]{0:T(128)S(1)} %copy-done.4, bf16[96,512]{1,0:T(8,128)(2,1)S(1)} %slice.17.rows_ref, bf16[1,512,14336]{2,1,0:T(8,128)(2,1)} %refs_0_.17, bf16[1,512,14336]{2,1,0:T(8,128)(2,1)} %refs_1_.17), custom_call_target="tpu_custom_call" | custom-call | flops 352321536 | bytes 3670016 | tf_op jit(solution)/shard_map/column_pieces/pallas_call | solution.py:115
  30.7 1.0 collective-permute-done.9
  31.8 1.5 %collective-permute-start.10 = (bf16[96,1792]{1,0:T(8,128)(2,1)S(1)}, bf16[96,1792]{1,0:T(8,128)(2,1)S(1)}, u32[]{:S(2)}, u32[]{:S(2)}) collective-permute-start(bf16[96,1792]{1,0:T(8,128)(2,1)S(1)} %add_convert_fusion.6), channel_id=1, source_target_pairs={{2,0},{4,2},{6,4},{7,6},{5,7},{3,5},{1,3},{0,1},{10,8},{12,10},{14... | collective-permute-start | bytes 1032200 | tf_op jit(solution)/shard_map/ppermute | solution.py:287
  33.4 0.6 collective-permute-start.1
  34.0 3.1 %column_pieces.10 = (bf16[96,1792]{1,0:T(8,128)(2,1)S(1)}, bf16[96,1792]{1,0:T(8,128)(2,1)S(1)}) custom-call(s32[2]{0:T(128)S(1)} %copy-done.1, s32[128]{0:T(128)S(1)} %copy-done.4, bf16[96,512]{1,0:T(8,128)(2,1)S(1)} %slice.17.rows_ref, bf16[1,512,14336]{2,1,0:T(8,128)(2,1)} %refs_0_.17, bf16[1,512,14336]{2,1,0:T(8,128)(2,1)} %refs_1_.17), custom_call_target="tpu_custom_call" | custom-call | flops 352321536 | bytes 3670016 | tf_op jit(solution)/shard_map/column_pieces/pallas_call | solution.py:115
  37.1 4.2 %collective-permute-done.10 = bf16[96,1792]{1,0:T(8,128)(2,1)S(1)} collective-permute-done((bf16[96,1792]{1,0:T(8,128)(2,1)S(1)}, bf16[96,1792]{1,0:T(8,128)(2,1)S(1)}, u32[]{:S(2)}, u32[]{:S(2)}) %collective-permute-start.10) | collective-permute-done | bytes 344096 | tf_op jit(solution)/shard_map/ppermute | solution.py:287
  41.4 1.6 %collective-permute-start.11 = (bf16[96,1792]{1,0:T(8,128)(2,1)S(1)}, bf16[96,1792]{1,0:T(8,128)(2,1)S(1)}, u32[]{:S(2)}, u32[]{:S(2)}) collective-permute-start(bf16[96,1792]{1,0:T(8,128)(2,1)S(1)} %add_convert_fusion.5), channel_id=1, source_target_pairs={{2,0},{4,2},{6,4},{7,6},{5,7},{3,5},{1,3},{0,1},{10,8},{12,10},{14... | collective-permute-start | bytes 1032200 | tf_op jit(solution)/shard_map/ppermute | solution.py:287
  43.1 0.6 collective-permute-start.3
  43.6 3.1 %column_pieces.11 = (bf16[96,1792]{1,0:T(8,128)(2,1)S(1)}, bf16[96,1792]{1,0:T(8,128)(2,1)S(1)}) custom-call(s32[2]{0:T(128)S(1)} %copy-done.1, s32[128]{0:T(128)S(1)} %copy-done.4, bf16[96,512]{1,0:T(8,128)(2,1)S(1)} %slice.17.rows_ref, bf16[1,512,14336]{2,1,0:T(8,128)(2,1)} %refs_0_.17, bf16[1,512,14336]{2,1,0:T(8,128)(2,1)} %refs_1_.17), custom_call_target="tpu_custom_call" | custom-call | flops 352321536 | bytes 3670016 | tf_op jit(solution)/shard_map/column_pieces/pallas_call | solution.py:115
  46.7 3.3 %collective-permute-done.11 = bf16[96,1792]{1,0:T(8,128)(2,1)S(1)} collective-permute-done((bf16[96,1792]{1,0:T(8,128)(2,1)S(1)}, bf16[96,1792]{1,0:T(8,128)(2,1)S(1)}, u32[]{:S(2)}, u32[]{:S(2)}) %collective-permute-start.11) | collective-permute-done | bytes 344096 | tf_op jit(solution)/shard_map/ppermute | solution.py:287
  50.1 1.6 %collective-permute-start.12 = (bf16[96,1792]{1,0:T(8,128)(2,1)S(1)}, bf16[96,1792]{1,0:T(8,128)(2,1)S(1)}, u32[]{:S(2)}, u32[]{:S(2)}) collective-permute-start(bf16[96,1792]{1,0:T(8,128)(2,1)S(1)} %add_convert_fusion.4), channel_id=1, source_target_pairs={{2,0},{4,2},{6,4},{7,6},{5,7},{3,5},{1,3},{0,1},{10,8},{12,10},{14... | collective-permute-start | bytes 1032200 | tf_op jit(solution)/shard_map/ppermute | solution.py:287
  51.7 0.3 convert_add_fusion
  52.1 1.1 collective-permute-start.6
  53.2 0.7 collective-permute-start.4
  53.9 3.1 %column_pieces.12 = (bf16[96,1792]{1,0:T(8,128)(2,1)S(1)}, bf16[96,1792]{1,0:T(8,128)(2,1)S(1)}) custom-call(s32[2]{0:T(128)S(1)} %copy-done.1, s32[128]{0:T(128)S(1)} %copy-done.4, bf16[96,512]{1,0:T(8,128)(2,1)S(1)} %slice.17.rows_ref, bf16[1,512,14336]{2,1,0:T(8,128)(2,1)} %refs_0_.17, bf16[1,512,14336]{2,1,0:T(8,128)(2,1)} %refs_1_.17), custom_call_target="tpu_custom_call" | custom-call | flops 352321536 | bytes 3670016 | tf_op jit(solution)/shard_map/column_pieces/pallas_call | solution.py:115
  57.0 1.2 %collective-permute-done.12 = bf16[96,1792]{1,0:T(8,128)(2,1)S(1)} collective-permute-done((bf16[96,1792]{1,0:T(8,128)(2,1)S(1)}, bf16[96,1792]{1,0:T(8,128)(2,1)S(1)}, u32[]{:S(2)}, u32[]{:S(2)}) %collective-permute-start.12) | collective-permute-done | bytes 344096 | tf_op jit(solution)/shard_map/ppermute | solution.py:287
  58.3 1.6 %collective-permute-start.13 = (bf16[96,1792]{1,0:T(8,128)(2,1)S(1)}, bf16[96,1792]{1,0:T(8,128)(2,1)S(1)}, u32[]{:S(2)}, u32[]{:S(2)}) collective-permute-start(bf16[96,1792]{1,0:T(8,128)(2,1)S(1)} %add_convert_fusion.3), channel_id=1, source_target_pairs={{2,0},{4,2},{6,4},{7,6},{5,7},{3,5},{1,3},{0,1},{10,8},{12,10},{14... | collective-permute-start | bytes 1032200 | tf_op jit(solution)/shard_map/ppermute | solution.py:287
  59.9 1.5 %collective-permute-done.4 = bf16[96,1792]{1,0:T(8,128)(2,1)S(1)} collective-permute-done((bf16[96,1792]{1,0:T(8,128)(2,1)S(1)}, bf16[96,1792]{1,0:T(8,128)(2,1)S(1)}, u32[]{:S(2)}, u32[]{:S(2)}) %collective-permute-start.4) | collective-permute-done | bytes 344096 | tf_op jit(solution)/shard_map/ppermute | solution.py:286
  61.5 0.8 collective-permute-start.5
  62.3 3.1 %column_pieces.13 = (bf16[96,1792]{1,0:T(8,128)(2,1)S(1)}, bf16[96,1792]{1,0:T(8,128)(2,1)S(1)}) custom-call(s32[2]{0:T(128)S(1)} %copy-done.1, s32[128]{0:T(128)S(1)} %copy-done.4, bf16[96,512]{1,0:T(8,128)(2,1)S(1)} %slice.17.rows_ref, bf16[1,512,14336]{2,1,0:T(8,128)(2,1)} %refs_0_.17, bf16[1,512,14336]{2,1,0:T(8,128)(2,1)} %refs_1_.17), custom_call_target="tpu_custom_call" | custom-call | flops 352321536 | bytes 3670016 | tf_op jit(solution)/shard_map/column_pieces/pallas_call | solution.py:115
  65.4 1.5 %collective-permute-done.13 = bf16[96,1792]{1,0:T(8,128)(2,1)S(1)} collective-permute-done((bf16[96,1792]{1,0:T(8,128)(2,1)S(1)}, bf16[96,1792]{1,0:T(8,128)(2,1)S(1)}, u32[]{:S(2)}, u32[]{:S(2)}) %collective-permute-start.13) | collective-permute-done | bytes 344096 | tf_op jit(solution)/shard_map/ppermute | solution.py:287
  67.0 1.6 %collective-permute-start.14 = (bf16[96,1792]{1,0:T(8,128)(2,1)S(1)}, bf16[96,1792]{1,0:T(8,128)(2,1)S(1)}, u32[]{:S(2)}, u32[]{:S(2)}) collective-permute-start(bf16[96,1792]{1,0:T(8,128)(2,1)S(1)} %add_convert_fusion.2), channel_id=1, source_target_pairs={{2,0},{4,2},{6,4},{7,6},{5,7},{3,5},{1,3},{0,1},{10,8},{12,10},{14... | collective-permute-start | bytes 1032200 | tf_op jit(solution)/shard_map/ppermute | solution.py:287
  68.5 0.8 collective-permute-done.5
  69.3 1.0 fusion.9
  70.4 1.1 collective-permute-start.7
  71.5 3.3 %column_pieces.14 = (bf16[96,1792]{1,0:T(8,128)(2,1)S(1)}, bf16[96,1792]{1,0:T(8,128)(2,1)S(1)}) custom-call(s32[2]{0:T(128)S(1)} %copy-done.1, s32[128]{0:T(128)S(1)} %copy-done.4, bf16[96,512]{1,0:T(8,128)(2,1)S(1)} %slice.17.rows_ref, bf16[1,512,14336]{2,1,0:T(8,128)(2,1)} %refs_0_.17, bf16[1,512,14336]{2,1,0:T(8,128)(2,1)} %refs_1_.17), custom_call_target="tpu_custom_call" | custom-call | flops 352321536 | bytes 3670016 | tf_op jit(solution)/shard_map/column_pieces/pallas_call | solution.py:115
  74.8 1.5 %collective-permute-done.14 = bf16[96,1792]{1,0:T(8,128)(2,1)S(1)} collective-permute-done((bf16[96,1792]{1,0:T(8,128)(2,1)S(1)}, bf16[96,1792]{1,0:T(8,128)(2,1)S(1)}, u32[]{:S(2)}, u32[]{:S(2)}) %collective-permute-start.14) | collective-permute-done | bytes 344096 | tf_op jit(solution)/shard_map/ppermute | solution.py:287
  76.4 1.8 %collective-permute-start.15 = (bf16[96,1792]{1,0:T(8,128)(2,1)S(1)}, bf16[96,1792]{1,0:T(8,128)(2,1)S(1)}, u32[]{:S(2)}, u32[]{:S(2)}) collective-permute-start(bf16[96,1792]{1,0:T(8,128)(2,1)S(1)} %add_convert_fusion.1), channel_id=1, source_target_pairs={{2,0},{4,2},{6,4},{7,6},{5,7},{3,5},{1,3},{0,1},{10,8},{12,10},{14... | collective-permute-start | bytes 1032200 | tf_op jit(solution)/shard_map/ppermute | solution.py:287
  78.2 1.6 %collective-permute-done.7 = bf16[96,1792]{1,0:T(8,128)(2,1)S(1)} collective-permute-done((bf16[96,1792]{1,0:T(8,128)(2,1)S(1)}, bf16[96,1792]{1,0:T(8,128)(2,1)S(1)}, u32[]{:S(2)}, u32[]{:S(2)}) %collective-permute-start.7) | collective-permute-done | bytes 344096 | tf_op jit(solution)/shard_map/ppermute | solution.py:286
  79.9 1.6 %collective-permute-start.8 = (bf16[96,1792]{1,0:T(8,128)(2,1)S(1)}, bf16[96,1792]{1,0:T(8,128)(2,1)S(1)}, u32[]{:S(2)}, u32[]{:S(2)}) collective-permute-start(bf16[96,1792]{1,0:T(8,128)(2,1)S(1)} %add_convert_fusion.7), channel_id=1, source_target_pairs={{0,2},{2,4},{4,6},{6,7},{7,5},{5,3},{3,1},{1,0},{8,10},{10,12},{12... | collective-permute-start | bytes 1032200 | tf_op jit(solution)/shard_map/ppermute | solution.py:286
  81.5 3.1 %column_pieces.15 = (bf16[96,1792]{1,0:T(8,128)(2,1)S(1)}, bf16[96,1792]{1,0:T(8,128)(2,1)S(1)}) custom-call(s32[2]{0:T(128)S(1)} %copy-done.1, s32[128]{0:T(128)S(1)} %copy-done.4, bf16[96,512]{1,0:T(8,128)(2,1)S(1)} %slice.17.rows_ref, bf16[1,512,14336]{2,1,0:T(8,128)(2,1)} %refs_0_.17, bf16[1,512,14336]{2,1,0:T(8,128)(2,1)} %refs_1_.17), custom_call_target="tpu_custom_call" | custom-call | flops 352321536 | bytes 3670016 | tf_op jit(solution)/shard_map/column_pieces/pallas_call | solution.py:115
  84.6 2.8 %collective-permute-done.8.gate_ref = bf16[96,1792]{1,0:T(8,128)(2,1)S(1)} collective-permute-done((bf16[96,1792]{1,0:T(8,128)(2,1)S(1)}, bf16[96,1792]{1,0:T(8,128)(2,1)S(1)}, u32[]{:S(2)}, u32[]{:S(2)}) %collective-permute-start.8) | collective-permute-done | bytes 344096 | tf_op jit(solution)/shard_map/ppermute | solution.py:286
  87.4 1.1 hidden_rows.1
  88.6 2.7 %fusion.4 = bf16[64,4096]{1,0:T(8,128)(2,1)S(1)} fusion(bf16[64,1792]{1,0:T(8,128)(2,1)S(1)} %get-tuple-element.94, bf16[1,1792,4096]{2,1,0:T(8,128)(2,1)S(1)} %bitcast.24), kind=kOutput, calls=%fused_computation.4 | convolution fusion | flops 939786240 | bytes 15433728 | tf_op jit(solution)/shard_map/dot_general | solution.py:229
  91.4 2.7 %fusion.2 = f32[64,4096]{1,0:T(8,128)S(1)} fusion(bf16[64,1792]{1,0:T(8,128)(2,1)S(1)} %get-tuple-element.93, bf16[1,1792,4096]{2,1,0:T(8,128)(2,1)S(1)} %bitcast.24), kind=kOutput, calls=%fused_computation.2 | convolution fusion | flops 939524096 | bytes 15958016 | tf_op jit(solution)/shard_map/dot_general | solution.py:229
  94.1 0.1 add_convert_fusion
  94.3 0.2 reshape.12
  94.5 19.3 %all_to_all.11 = bf16[16,4,4096]{2,1,0:T(4,128)(2,1)S(1)} all-to-all(bf16[16,4,4096]{2,1,0:T(4,128)(2,1)S(1)} %reshape.12), channel_id=1, replica_groups={{0,1,2,3,4,5,6,7,16,17,18,19,20,21,22,23},{8,9,10,11,12,13,14,15,24,25,..., dimensions={0} | all-to-all | bytes 1048576 | tf_op jit(solution)/shard_map/all_to_all | solution.py:338
  113.8 0.8 reduce_sum.12
  (44 shorter events, 1.3 us)
Async XLA Ops:
  0.7 20.8 %copy-start = (s32[2]{0:T(128)}, s32[2]{0:T(128)S(1)}, u32[]{:S(2)}) copy-start(s32[2]{0:T(128)S(1)} %pad_add_fusion.where_ref) | copy-start | bytes 28
  17.8 0.7 copy-start.3
  18.5 8.5 %copy-start.4 = (s32[128]{0:T(128)S(1)}, s32[128]{0:T(128)}, u32[]{:S(2)}) copy-start(s32[128]{0:T(128)} %constant.18.clone.table_ref) | copy-start | bytes 1540
  21.6 10.2 %collective-permute-start.9 = (bf16[96,1792]{1,0:T(8,128)(2,1)S(1)}, bf16[96,1792]{1,0:T(8,128)(2,1)S(1)}, u32[]{:S(2)}, u32[]{:S(2)}) collective-permute-start(bf16[96,1792]{1,0:T(8,128)(2,1)S(1)} %get-tuple-element.82), channel_id=1, source_target_pairs={{2,0},{4,2},{6,4},{7,6},{5,7},{3,5},{1,3},{0,1},{10,8},{12,10},{14... | collective-permute-start | bytes 1032200 | tf_op jit(solution)/shard_map/ppermute | solution.py:287
  23.1 10.2 %collective-permute-start = (bf16[96,1792]{1,0:T(8,128)(2,1)S(1)}, bf16[96,1792]{1,0:T(8,128)(2,1)S(1)}, u32[]{:S(2)}, u32[]{:S(2)}) collective-permute-start(bf16[96,1792]{1,0:T(8,128)(2,1)S(1)} %get-tuple-element.54), channel_id=1, source_target_pairs={{0,2},{2,4},{4,6},{6,7},{7,5},{5,3},{3,1},{1,0},{8,10},{10,12},{12... | collective-permute-start | bytes 1032200 | tf_op jit(solution)/shard_map/ppermute | solution.py:286
  27.0 16.0 %collective-permute-start.2 = (bf16[2,512,512]{2,1,0:T(8,128)(2,1)}, bf16[2,512,512]{2,1,0:T(8,128)(2,1)S(1)}, u32[]{:S(2)}, u32[]{:S(2)}) collective-permute-start(bf16[2,512,512]{2,1,0:T(8,128)(2,1)} %get-tuple-element.57), channel_id=1, source_target_pairs={{0,8},{8,0},{16,24},{24,16},{1,9},{9,1},{17,25},{25,17},{2,10},{10... | collective-permute-start | bytes 3145736 | tf_op jit(solution)/shard_map/ppermute | solution.py:296
  27.0 0.7 copy-start.1
  31.8 9.5 %collective-permute-start.10 = (bf16[96,1792]{1,0:T(8,128)(2,1)S(1)}, bf16[96,1792]{1,0:T(8,128)(2,1)S(1)}, u32[]{:S(2)}, u32[]{:S(2)}) collective-permute-start(bf16[96,1792]{1,0:T(8,128)(2,1)S(1)} %add_convert_fusion.6), channel_id=1, source_target_pairs={{2,0},{4,2},{6,4},{7,6},{5,7},{3,5},{1,3},{0,1},{10,8},{12,10},{14... | collective-permute-start | bytes 1032200 | tf_op jit(solution)/shard_map/ppermute | solution.py:287
  33.4 9.6 %collective-permute-start.1 = (bf16[96,1792]{1,0:T(8,128)(2,1)S(1)}, bf16[96,1792]{1,0:T(8,128)(2,1)S(1)}, u32[]{:S(2)}, u32[]{:S(2)}) collective-permute-start(bf16[96,1792]{1,0:T(8,128)(2,1)S(1)} %add_convert_fusion.12), channel_id=1, source_target_pairs={{0,2},{2,4},{4,6},{6,7},{7,5},{5,3},{3,1},{1,0},{8,10},{10,12},{12... | collective-permute-start | bytes 1032200 | tf_op jit(solution)/shard_map/ppermute | solution.py:286
  41.4 8.6 %collective-permute-start.11 = (bf16[96,1792]{1,0:T(8,128)(2,1)S(1)}, bf16[96,1792]{1,0:T(8,128)(2,1)S(1)}, u32[]{:S(2)}, u32[]{:S(2)}) collective-permute-start(bf16[96,1792]{1,0:T(8,128)(2,1)S(1)} %add_convert_fusion.5), channel_id=1, source_target_pairs={{2,0},{4,2},{6,4},{7,6},{5,7},{3,5},{1,3},{0,1},{10,8},{12,10},{14... | collective-permute-start | bytes 1032200 | tf_op jit(solution)/shard_map/ppermute | solution.py:287
  43.1 8.6 %copy-start.5 = (bf16[2,512,512]{2,1,0:T(8,128)(2,1)S(1)}, bf16[2,512,512]{2,1,0:T(8,128)(2,1)}, u32[]{:S(2)}) copy-start(bf16[2,512,512]{2,1,0:T(8,128)(2,1)} %get-tuple-element.71) | copy-start | bytes 3145732
  43.1 10.1 %collective-permute-start.3 = (bf16[96,1792]{1,0:T(8,128)(2,1)S(1)}, bf16[96,1792]{1,0:T(8,128)(2,1)S(1)}, u32[]{:S(2)}, u32[]{:S(2)}) collective-permute-start(bf16[96,1792]{1,0:T(8,128)(2,1)S(1)} %add_convert_fusion.11), channel_id=1, source_target_pairs={{0,2},{2,4},{4,6},{6,7},{7,5},{5,3},{3,1},{1,0},{8,10},{10,12},{12... | collective-permute-start | bytes 1032200 | tf_op jit(solution)/shard_map/ppermute | solution.py:286
  50.1 8.1 %collective-permute-start.12 = (bf16[96,1792]{1,0:T(8,128)(2,1)S(1)}, bf16[96,1792]{1,0:T(8,128)(2,1)S(1)}, u32[]{:S(2)}, u32[]{:S(2)}) collective-permute-start(bf16[96,1792]{1,0:T(8,128)(2,1)S(1)} %add_convert_fusion.4), channel_id=1, source_target_pairs={{2,0},{4,2},{6,4},{7,6},{5,7},{3,5},{1,3},{0,1},{10,8},{12,10},{14... | collective-permute-start | bytes 1032200 | tf_op jit(solution)/shard_map/ppermute | solution.py:287
  52.1 16.4 %collective-permute-start.6 = (bf16[512,512]{1,0:T(8,128)(2,1)S(1)}, bf16[512,512]{1,0:T(8,128)(2,1)S(1)}, u32[]{:S(2)}, u32[]{:S(2)}) collective-permute-start(bf16[512,512]{1,0:T(8,128)(2,1)S(1)} %fusion.10), channel_id=1, source_target_pairs={{0,16},{8,24},{16,0},{24,8},{1,17},{9,25},{17,1},{25,9},{2,18},{10... | collective-permute-start | bytes 1572872 | tf_op jit(solution)/shard_map/ppermute | solution.py:304
  53.2 8.1 %collective-permute-start.4 = (bf16[96,1792]{1,0:T(8,128)(2,1)S(1)}, bf16[96,1792]{1,0:T(8,128)(2,1)S(1)}, u32[]{:S(2)}, u32[]{:S(2)}) collective-permute-start(bf16[96,1792]{1,0:T(8,128)(2,1)S(1)} %add_convert_fusion.10), channel_id=1, source_target_pairs={{0,2},{2,4},{4,6},{6,7},{7,5},{5,3},{3,1},{1,0},{8,10},{10,12},{12... | collective-permute-start | bytes 1032200 | tf_op jit(solution)/shard_map/ppermute | solution.py:286
  58.3 8.6 %collective-permute-start.13 = (bf16[96,1792]{1,0:T(8,128)(2,1)S(1)}, bf16[96,1792]{1,0:T(8,128)(2,1)S(1)}, u32[]{:S(2)}, u32[]{:S(2)}) collective-permute-start(bf16[96,1792]{1,0:T(8,128)(2,1)S(1)} %add_convert_fusion.3), channel_id=1, source_target_pairs={{2,0},{4,2},{6,4},{7,6},{5,7},{3,5},{1,3},{0,1},{10,8},{12,10},{14... | collective-permute-start | bytes 1032200 | tf_op jit(solution)/shard_map/ppermute | solution.py:287
  61.5 7.9 %collective-permute-start.5 = (bf16[96,1792]{1,0:T(8,128)(2,1)S(1)}, bf16[96,1792]{1,0:T(8,128)(2,1)S(1)}, u32[]{:S(2)}, u32[]{:S(2)}) collective-permute-start(bf16[96,1792]{1,0:T(8,128)(2,1)S(1)} %add_convert_fusion.9), channel_id=1, source_target_pairs={{0,2},{2,4},{4,6},{6,7},{7,5},{5,3},{3,1},{1,0},{8,10},{10,12},{12... | collective-permute-start | bytes 1032200 | tf_op jit(solution)/shard_map/ppermute | solution.py:286
  67.0 9.3 %collective-permute-start.14 = (bf16[96,1792]{1,0:T(8,128)(2,1)S(1)}, bf16[96,1792]{1,0:T(8,128)(2,1)S(1)}, u32[]{:S(2)}, u32[]{:S(2)}) collective-permute-start(bf16[96,1792]{1,0:T(8,128)(2,1)S(1)} %add_convert_fusion.2), channel_id=1, source_target_pairs={{2,0},{4,2},{6,4},{7,6},{5,7},{3,5},{1,3},{0,1},{10,8},{12,10},{14... | collective-permute-start | bytes 1032200 | tf_op jit(solution)/shard_map/ppermute | solution.py:287
  70.4 9.5 %collective-permute-start.7 = (bf16[96,1792]{1,0:T(8,128)(2,1)S(1)}, bf16[96,1792]{1,0:T(8,128)(2,1)S(1)}, u32[]{:S(2)}, u32[]{:S(2)}) collective-permute-start(bf16[96,1792]{1,0:T(8,128)(2,1)S(1)} %add_convert_fusion.8), channel_id=1, source_target_pairs={{0,2},{2,4},{4,6},{6,7},{7,5},{5,3},{3,1},{1,0},{8,10},{10,12},{12... | collective-permute-start | bytes 1032200 | tf_op jit(solution)/shard_map/ppermute | solution.py:286
  71.5 17.1 %slice-start = ((s8[14680064]{0:T(1024)(128)(4,1)}), s8[4194304]{0:T(1024)(128)(4,1)S(1)}, s32[]{:S(2)}) async-start(s8[14680064]{0:T(1024)(128)(4,1)} %bitcast.23), calls=%async_computation.2 | async-start | bytes 8388608
  71.5 17.1 %slice-start.1 = ((s8[14680064]{0:T(1024)(128)(4,1)}), s8[4194304]{0:T(1024)(128)(4,1)S(1)}, s32[]{:S(2)}) async-start(s8[14680064]{0:T(1024)(128)(4,1)} %bitcast.23), calls=%async_computation.3 | async-start | bytes 8388608
  76.4 8.3 %collective-permute-start.15 = (bf16[96,1792]{1,0:T(8,128)(2,1)S(1)}, bf16[96,1792]{1,0:T(8,128)(2,1)S(1)}, u32[]{:S(2)}, u32[]{:S(2)}) collective-permute-start(bf16[96,1792]{1,0:T(8,128)(2,1)S(1)} %add_convert_fusion.1), channel_id=1, source_target_pairs={{2,0},{4,2},{6,4},{7,6},{5,7},{3,5},{1,3},{0,1},{10,8},{12,10},{14... | collective-permute-start | bytes 1032200 | tf_op jit(solution)/shard_map/ppermute | solution.py:287
  79.9 8.7 %slice-start.2 = ((s8[14680064]{0:T(1024)(128)(4,1)}), s8[4194304]{0:T(1024)(128)(4,1)S(1)}, s32[]{:S(2)}) async-start(s8[14680064]{0:T(1024)(128)(4,1)} %bitcast.23), calls=%async_computation.4 | async-start | bytes 8388608
  79.9 7.5 %collective-permute-start.8 = (bf16[96,1792]{1,0:T(8,128)(2,1)S(1)}, bf16[96,1792]{1,0:T(8,128)(2,1)S(1)}, u32[]{:S(2)}, u32[]{:S(2)}) collective-permute-start(bf16[96,1792]{1,0:T(8,128)(2,1)S(1)} %add_convert_fusion.7), channel_id=1, source_target_pairs={{0,2},{2,4},{4,6},{6,7},{7,5},{5,3},{3,1},{1,0},{8,10},{10,12},{12... | collective-permute-start | bytes 1032200 | tf_op jit(solution)/shard_map/ppermute | solution.py:286
  81.5 5.9 %copy-start.2 = (f32[96,128]{1,0:T(8,128)S(1)}, f32[96,128]{1,0:T(8,128)}, u32[]{:S(2)}) copy-start(f32[96,128]{1,0:T(8,128)} %constant.19.clone.origin_ref) | copy-start | bytes 147460
  81.5 7.1 %slice-start.3 = ((s8[14680064]{0:T(1024)(128)(4,1)}), s8[2097152]{0:T(1024)(128)(4,1)S(1)}, s32[]{:S(2)}) async-start(s8[14680064]{0:T(1024)(128)(4,1)} %bitcast.23), calls=%async_computation.5 | async-start | bytes 4194304
  91.3 2.8 %collective-permute-start.16 = (bf16[64,4096]{1,0:T(8,128)(2,1)S(1)}, bf16[64,4096]{1,0:T(8,128)(2,1)S(1)}, u32[]{:S(2)}, u32[]{:S(2)}) collective-permute-start(bf16[64,4096]{1,0:T(8,128)(2,1)S(1)} %fusion.4), channel_id=1, source_target_pairs={{0,8},{8,0},{16,24},{24,16},{1,9},{9,1},{17,25},{25,17},{2,10},{10... | collective-permute-start | bytes 1572872 | tf_op jit(solution)/shard_map/ppermute | solution.py:326

commit v10 on v9

--- a/solution.py
+++ b/solution.py
@@ -94,20 +94,25 @@
     )(tokens, routes.T, mixing.T)
 
 
-def column_pieces(where, table, rows, gate_weight, up_weight, shards, first, pieces, cuts):
+def column_pieces(where, table, rows, gate_weight, up_weight, first, pieces, cuts):
     count, depth = rows.shape
+    cores, shards = table.shape[0], table.shape[2]
     width = gate_weight.shape[2] // shards
     block = width // cuts
 
-    def kernel(where_ref, table_ref, rows_ref, *refs):
+    def kernel(where_ref, rows_ref, *refs):
         weights, outs = refs[: 2 * pieces], refs[2 * pieces :]
         for ref, out in zip(weights, outs):
             value = jnp.dot(rows_ref[...], ref[0], preferred_element_type=F32)
             out[...] = value.astype(BF16)
 
     def weight_map(side, i):
-        def index(j, where_ref, table_ref):
-            return 0, 0, table_ref[(where_ref[1] * 2 + side) * shards + first + i] * cuts + j
+        def index(j, where_ref):
+            key = lax.rem(where_ref[0], jnp.int32(cores)) * shards + where_ref[1]
+            piece = jnp.int32(0)
+            for n, value in enumerate(table[:, side, :, first + i].reshape(-1).tolist()):
+                piece = jnp.where(key == n, jnp.int32(value), piece)
+            return 0, 0, piece * cuts + j
 
         return pl.BlockSpec((1, depth, block), index)
 
@@ -116,7 +121,7 @@
         kernel,
         out_shape=[jax.ShapeDtypeStruct((count, width), BF16)] * len(both),
         grid_spec=pltpu.PrefetchScalarGridSpec(
-            num_scalar_prefetch=2,
+            num_scalar_prefetch=1,
             grid=(cuts,),
             in_specs=[pl.BlockSpec((count, depth), lambda j, *_: (0, 0))]
             + [weight_map(side, i) for side, i in both],
@@ -129,16 +134,17 @@
             transcendentals=0,
         ),
         name="column_pieces",
-    )(where, table, rows, *([gate_weight] * pieces + [up_weight] * pieces))
+    )(where, rows, *([gate_weight] * pieces + [up_weight] * pieces))
     return out[:pieces], out[pieces:]
 
 
-def plain_pieces(where, table, rows, gate_weight, up_weight, shards):
+def plain_pieces(where, table, rows, gate_weight, up_weight):
+    cores, shards = table.shape[0], table.shape[2]
     width = gate_weight.shape[2] // shards
     both = []
     for side, weight in enumerate((gate_weight, up_weight)):
         value = jnp.dot(rows, weight[0], preferred_element_type=F32).astype(BF16)
-        at = table.reshape(shards, 2, shards)[where[1], side] * width
+        at = jnp.asarray(table)[where[0] % cores, side, where[1]] * width
         both.append([lax.dynamic_slice_in_dim(value, at[t], width, 1) for t in range(shards)])
     return both
 
@@ -250,14 +256,16 @@
     where = jnp.stack([lax.axis_index("branch"), lax.axis_index("shard")]).astype(jnp.int32)
 
     place = np.argsort(np.asarray(order))
-    table = np.zeros((shards, 2, shards), np.int32)
-    for s in range(shards):
-        for t in range(shards):
-            table[s, 0, t] = order[(place[s] - 1 - t) % shards]
-            table[s, 1, t] = order[(place[s] + 1 + t) % shards]
-    table = jnp.asarray(table.reshape(-1))
-    forth = [(order[i], order[(i + 1) % shards]) for i in range(shards)]
-    back = [(b, a) for a, b in forth]
+    table = np.zeros((cores, 2, shards, shards), np.int32)
+    pairs = [[], []]
+    for side in range(2):
+        for b in range(experts):
+            core = b % cores
+            way = 1 if (side + core) % 2 == 0 else -1
+            for s in range(shards):
+                for t in range(shards):
+                    table[core, side, s, t] = order[(place[s] - way * (1 + t)) % shards]
+                pairs[side].append((b * shards + s, b * shards + order[(place[s] + way) % shards]))
     source = np.arange(count) // capacity
     origin = np.zeros((count, LANES), np.float32)
     origin[:, 0] = source // shards % cores
@@ -266,7 +274,7 @@
     origin = jnp.asarray(origin)
 
     cells = place_rows(tokens, routes, mixing, experts, capacity, shards)
-    cells, where, table, origin = lax.optimization_barrier((cells, where, table, origin))
+    cells, where, origin = lax.optimization_barrier((cells, where, origin))
     cells = lax.all_to_all(cells, ("branch", "shard"), split_axis=0, concat_axis=0, tiled=True)
     cells = cells.reshape(count, depth + LANES)
     rows, tails = cells[:, :depth], cells[:, depth:]
@@ -274,20 +282,20 @@
     sliced = slice_width % LANES == 0
     if sliced:
         cuts = 2 if slice_width % (2 * LANES) == 0 else 1
-        gates, ups = column_pieces(where, table, rows, gate_weight, up_weight, shards, 0, 1, cuts)
+        gates, ups = column_pieces(where, table, rows, gate_weight, up_weight, 0, 1, cuts)
     else:
-        gates, ups = plain_pieces(where, table, rows, gate_weight, up_weight, shards)
+        gates, ups = plain_pieces(where, table, rows, gate_weight, up_weight)
     gate_sum, up_sum = gates[0], ups[0]
     last = shards - 1
     parts = 1
     weights = [down_weight[0]]
     for t in range(1, shards):
         now, gate_sum = lax.optimization_barrier((where, gate_sum))
-        gate_in = lax.ppermute(gate_sum, "shard", forth)
-        up_in = lax.ppermute(up_sum, "shard", back)
+        gate_in = lax.ppermute(gate_sum, ("branch", "shard"), pairs[0])
+        up_in = lax.ppermute(up_sum, ("branch", "shard"), pairs[1])
         if sliced and len(gates) < shards:
             more = column_pieces(
-                now, table, rows, gate_weight, up_weight, shards, len(gates), 1, cuts
+                now, table, rows, gate_weight, up_weight, len(gates), 1, cuts
             )
             gates, ups = gates + more[0], ups + more[1]
         if t == 1:

time: 115 us -> 119 us (1.035)
  waiting for transfers between devices: 19.4 us -> 25.5 us
  starting transfers between devices: 18.3 us -> 15.3 us
  blocking collectives: 34.5 us -> 35.8 us
    ppermute x14, waiting for transfers between devices: 19.4 us -> 25.5 us  [the longest x7 13.1 us: local(): gate_in = lax.ppermute(gate_sum, ('branch', 'shard'), pairs[0])]
    ppermute x14, starting transfers between devices: 17.2 us -> 13.1 us  [the longest x7 7.09 us: local(): gate_in = lax.ppermute(gate_sum, ('branch', 'shard'), pairs[0])]
    all_to_all x1, blocking collectives: 19.3 us -> 20.6 us  [local(): lax.all_to_all(mixed, ('branch', 'shard'), split_axis=0, concat_axis=0, a...]
  transfers between devices with their start and end apart: 17 -> 17, of which waited for: 10 -> 8; matrix products, arithmetic and copies ran while one was open for 4% -> 4% of each run, Pallas kernels for 22% -> 21%
where the time goes in v10:
time: 119 us
  blocking collectives  35.8 us (30%)
  Pallas kernels  31.2 us (26%)
  waiting for transfers between devices  25.5 us (21%)
  starting transfers between devices  15.3 us (13%)
  matrix products  5.48 us (5%)
  other arithmetic  3.27 us (3%)
    pallas_call x8, Pallas kernels, column_pieces(): pl.pallas_call(kernel, out_shape=[jax.ShapeDtypeStruct((count, width), BF...  25 us
    all_to_all x1, blocking collectives, local(): lax.all_to_all(mixed, ('branch', 'shard'), split_axis=0, concat_axis=0, a...  20.6 us
    all_to_all x1, blocking collectives, local(): lax.all_to_all(cells, ('branch', 'shard'), split_axis=0, concat_axis=0, t...  15.2 us
    ppermute x7, waiting for transfers between devices, local(): gate_in = lax.ppermute(gate_sum, ('branch', 'shard'), pairs[0])  13.1 us
    ppermute x7, waiting for transfers between devices, local(): up_in = lax.ppermute(up_sum, ('branch', 'shard'), pairs[1])  12.5 us
    ppermute x7, starting transfers between devices, local(): gate_in = lax.ppermute(gate_sum, ('branch', 'shard'), pairs[0])  7.09 us
    ppermute x7, starting transfers between devices, local(): up_in = lax.ppermute(up_sum, ('branch', 'shard'), pairs[1])  5.96 us
    dot_general x2, matrix products, down_product(): jnp.dot(h, w, preferred_element_type=F32)  5.48 us
  transfers between devices with their start and end apart: 17, of which 8 were waited for; matrix products, arithmetic and copies ran while one was open for 4% of the time, Pallas kernels for 21%

profile of v10, /device:TPU:0, one launch (start us, length us, event | category | flops | bytes accessed | tf_op | source)
XLA Modules:
  0.0 118.6 jit_solution(2924482482939020653)
XLA Ops:
  0.7 1.7 %place_rows.1 = bf16[32,3,640]{2,1,0:T(4,128)(2,1)} custom-call(bf16[4,4096]{1,0:T(4,128)(2,1)} %tokens_ref.1, s32[2,4]{1,0:T(2,128)} %bitcast.25, f32[2,4]{1,0:T(2,128)} %bitcast.26), custom_call_target="tpu_custom_call" | custom-call | tf_op jit(solution)/shard_map/place_rows/pallas_call | solution.py:84
  2.5 15.2 %all_to_all.10 = bf16[32,3,640]{2,1,0:T(4,128)(2,1)S(1)} all-to-all(bf16[32,3,640]{2,1,0:T(4,128)(2,1)} %place_rows.1), channel_id=1, replica_groups=mesh['branch'=4,'shard'=8] {'branch','shard'}, dimensions={0} | all-to-all | bytes 245760 | tf_op jit(solution)/shard_map/all_to_all | solution.py:278
  17.7 0.1 reshape.11
  17.8 3.1 %column_pieces.8 = (bf16[96,1792]{1,0:T(8,128)(2,1)S(1)}, bf16[96,1792]{1,0:T(8,128)(2,1)S(1)}) custom-call(s32[2]{0:T(128)S(1)} %pad_add_fusion.where_ref, bf16[96,512]{1,0:T(8,128)(2,1)S(1)} %slice.17.rows_ref, bf16[1,512,14336]{2,1,0:T(8,128)(2,1)} %refs_0_.17, bf16[1,512,14336]{2,1,0:T(8,128)(2,1)} %refs_1_.17), custom_call_target="tpu_custom_call" | custom-call | flops 352321536 | bytes 3670016 | tf_op jit(solution)/shard_map/column_pieces/pallas_call | solution.py:120
  20.9 1.6 %collective-permute-start.9 = (bf16[96,1792]{1,0:T(8,128)(2,1)S(1)}, bf16[96,1792]{1,0:T(8,128)(2,1)S(1)}, u32[]{:S(2)}, u32[]{:S(2)}) collective-permute-start(bf16[96,1792]{1,0:T(8,128)(2,1)S(1)} %get-tuple-element.80), channel_id=1, source_target_pairs={{0,1},{1,3},{2,0},{3,5},{4,2},{5,7},{6,4},{7,6},{8,10},{9,8},{10,1... | collective-permute-start | bytes 1032200 | tf_op jit(solution)/shard_map/ppermute | solution.py:295
  22.5 0.5 collective-permute-start
  23.0 3.3 %turn_columns.1 = (bf16[2,512,512]{2,1,0:T(8,128)(2,1)}, bf16[2,512,512]{2,1,0:T(8,128)(2,1)}) custom-call(s32[2]{0:T(128)} %copy-done, bf16[1,512,2048]{2,1,0:T(8,128)(2,1)} %refs_1_.10, bf16[1,512,2048]{2,1,0:T(8,128)(2,1)} %refs_1_.10), custom_call_target="tpu_custom_call" | custom-call | bytes 4194304 | tf_op jit(solution)/shard_map/turn_columns/pallas_call | solution.py:168
  26.3 0.7 copy-done.1
  27.0 3.1 %column_pieces.9 = (bf16[96,1792]{1,0:T(8,128)(2,1)S(1)}, bf16[96,1792]{1,0:T(8,128)(2,1)S(1)}) custom-call(s32[2]{0:T(128)S(1)} %copy-done.1, bf16[96,512]{1,0:T(8,128)(2,1)S(1)} %slice.17.rows_ref, bf16[1,512,14336]{2,1,0:T(8,128)(2,1)} %refs_0_.17, bf16[1,512,14336]{2,1,0:T(8,128)(2,1)} %refs_1_.17), custom_call_target="tpu_custom_call" | custom-call | flops 352321536 | bytes 3670016 | tf_op jit(solution)/shard_map/column_pieces/pallas_call | solution.py:120
  30.1 1.6 %collective-permute-done.9 = bf16[96,1792]{1,0:T(8,128)(2,1)S(1)} collective-permute-done((bf16[96,1792]{1,0:T(8,128)(2,1)S(1)}, bf16[96,1792]{1,0:T(8,128)(2,1)S(1)}, u32[]{:S(2)}, u32[]{:S(2)}) %collective-permute-start.9) | collective-permute-done | bytes 344096 | tf_op jit(solution)/shard_map/ppermute | solution.py:295
  31.7 0.1 add_convert_fusion.6
  31.8 1.3 %collective-permute-start.10 = (bf16[96,1792]{1,0:T(8,128)(2,1)S(1)}, bf16[96,1792]{1,0:T(8,128)(2,1)S(1)}, u32[]{:S(2)}, u32[]{:S(2)}) collective-permute-start(bf16[96,1792]{1,0:T(8,128)(2,1)S(1)} %add_convert_fusion.6), channel_id=1, source_target_pairs={{0,1},{1,3},{2,0},{3,5},{4,2},{5,7},{6,4},{7,6},{8,10},{9,8},{10,1... | collective-permute-start | bytes 1032200 | tf_op jit(solution)/shard_map/ppermute | solution.py:295
  33.0 0.1 add_convert_fusion.12
  33.1 0.9 collective-permute-start.1
  34.0 3.1 %column_pieces.10 = (bf16[96,1792]{1,0:T(8,128)(2,1)S(1)}, bf16[96,1792]{1,0:T(8,128)(2,1)S(1)}) custom-call(s32[2]{0:T(128)S(1)} %copy-done.1, bf16[96,512]{1,0:T(8,128)(2,1)S(1)} %slice.17.rows_ref, bf16[1,512,14336]{2,1,0:T(8,128)(2,1)} %refs_0_.17, bf16[1,512,14336]{2,1,0:T(8,128)(2,1)} %refs_1_.17), custom_call_target="tpu_custom_call" | custom-call | flops 352321536 | bytes 3670016 | tf_op jit(solution)/shard_map/column_pieces/pallas_call | solution.py:120
  37.1 4.8 %collective-permute-done.10 = bf16[96,1792]{1,0:T(8,128)(2,1)S(1)} collective-permute-done((bf16[96,1792]{1,0:T(8,128)(2,1)S(1)}, bf16[96,1792]{1,0:T(8,128)(2,1)S(1)}, u32[]{:S(2)}, u32[]{:S(2)}) %collective-permute-start.10) | collective-permute-done | bytes 344096 | tf_op jit(solution)/shard_map/ppermute | solution.py:295
  42.0 0.8 collective-permute-start.11
  42.9 1.4 %collective-permute-start.3 = (bf16[96,1792]{1,0:T(8,128)(2,1)S(1)}, bf16[96,1792]{1,0:T(8,128)(2,1)S(1)}, u32[]{:S(2)}, u32[]{:S(2)}) collective-permute-start(bf16[96,1792]{1,0:T(8,128)(2,1)S(1)} %add_convert_fusion.11), channel_id=1, source_target_pairs={{0,2},{1,0},{2,4},{3,1},{4,6},{5,3},{6,7},{7,5},{8,9},{9,11},{10,8... | collective-permute-start | bytes 1032200 | tf_op jit(solution)/shard_map/ppermute | solution.py:294
  44.2 3.1 %column_pieces.11 = (bf16[96,1792]{1,0:T(8,128)(2,1)S(1)}, bf16[96,1792]{1,0:T(8,128)(2,1)S(1)}) custom-call(s32[2]{0:T(128)S(1)} %copy-done.1, bf16[96,512]{1,0:T(8,128)(2,1)S(1)} %slice.17.rows_ref, bf16[1,512,14336]{2,1,0:T(8,128)(2,1)} %refs_0_.17, bf16[1,512,14336]{2,1,0:T(8,128)(2,1)} %refs_1_.17), custom_call_target="tpu_custom_call" | custom-call | flops 352321536 | bytes 3670016 | tf_op jit(solution)/shard_map/column_pieces/pallas_call | solution.py:120
  47.3 4.0 %collective-permute-done.11 = bf16[96,1792]{1,0:T(8,128)(2,1)S(1)} collective-permute-done((bf16[96,1792]{1,0:T(8,128)(2,1)S(1)}, bf16[96,1792]{1,0:T(8,128)(2,1)S(1)}, u32[]{:S(2)}, u32[]{:S(2)}) %collective-permute-start.11) | collective-permute-done | bytes 344096 | tf_op jit(solution)/shard_map/ppermute | solution.py:295
  51.4 0.3 collective-permute-start.12
  51.8 0.3 convert_add_fusion
  52.1 2.2 %collective-permute-start.6 = (bf16[512,512]{1,0:T(8,128)(2,1)S(1)}, bf16[512,512]{1,0:T(8,128)(2,1)S(1)}, u32[]{:S(2)}, u32[]{:S(2)}) collective-permute-start(bf16[512,512]{1,0:T(8,128)(2,1)S(1)} %fusion.10), channel_id=1, source_target_pairs={{0,16},{8,24},{16,0},{24,8},{1,17},{9,25},{17,1},{25,9},{2,18},{10... | collective-permute-start | bytes 1572872 | tf_op jit(solution)/shard_map/ppermute | solution.py:312
  54.4 0.3 collective-permute-start.4
  54.7 3.1 %column_pieces.12 = (bf16[96,1792]{1,0:T(8,128)(2,1)S(1)}, bf16[96,1792]{1,0:T(8,128)(2,1)S(1)}) custom-call(s32[2]{0:T(128)S(1)} %copy-done.1, bf16[96,512]{1,0:T(8,128)(2,1)S(1)} %slice.17.rows_ref, bf16[1,512,14336]{2,1,0:T(8,128)(2,1)} %refs_0_.17, bf16[1,512,14336]{2,1,0:T(8,128)(2,1)} %refs_1_.17), custom_call_target="tpu_custom_call" | custom-call | flops 352321536 | bytes 3670016 | tf_op jit(solution)/shard_map/column_pieces/pallas_call | solution.py:120
  57.8 2.0 %collective-permute-done.12 = bf16[96,1792]{1,0:T(8,128)(2,1)S(1)} collective-permute-done((bf16[96,1792]{1,0:T(8,128)(2,1)S(1)}, bf16[96,1792]{1,0:T(8,128)(2,1)S(1)}, u32[]{:S(2)}, u32[]{:S(2)}) %collective-permute-start.12) | collective-permute-done | bytes 344096 | tf_op jit(solution)/shard_map/ppermute | solution.py:295
  59.9 0.3 collective-permute-start.13
  60.3 3.6 %collective-permute-done.4 = bf16[96,1792]{1,0:T(8,128)(2,1)S(1)} collective-permute-done((bf16[96,1792]{1,0:T(8,128)(2,1)S(1)}, bf16[96,1792]{1,0:T(8,128)(2,1)S(1)}, u32[]{:S(2)}, u32[]{:S(2)}) %collective-permute-start.4) | collective-permute-done | bytes 344096 | tf_op jit(solution)/shard_map/ppermute | solution.py:294
  64.0 1.3 %collective-permute-start.5 = (bf16[96,1792]{1,0:T(8,128)(2,1)S(1)}, bf16[96,1792]{1,0:T(8,128)(2,1)S(1)}, u32[]{:S(2)}, u32[]{:S(2)}) collective-permute-start(bf16[96,1792]{1,0:T(8,128)(2,1)S(1)} %add_convert_fusion.9), channel_id=1, source_target_pairs={{0,2},{1,0},{2,4},{3,1},{4,6},{5,3},{6,7},{7,5},{8,9},{9,11},{10,8... | collective-permute-start | bytes 1032200 | tf_op jit(solution)/shard_map/ppermute | solution.py:294
  65.3 3.1 %column_pieces.13 = (bf16[96,1792]{1,0:T(8,128)(2,1)S(1)}, bf16[96,1792]{1,0:T(8,128)(2,1)S(1)}) custom-call(s32[2]{0:T(128)S(1)} %copy-done.1, bf16[96,512]{1,0:T(8,128)(2,1)S(1)} %slice.17.rows_ref, bf16[1,512,14336]{2,1,0:T(8,128)(2,1)} %refs_0_.17, bf16[1,512,14336]{2,1,0:T(8,128)(2,1)} %refs_1_.17), custom_call_target="tpu_custom_call" | custom-call | flops 352321536 | bytes 3670016 | tf_op jit(solution)/shard_map/column_pieces/pallas_call | solution.py:120
  68.4 0.1 add_convert_fusion.2
  68.5 0.8 collective-permute-start.14
  69.3 4.3 %collective-permute-done.5 = bf16[96,1792]{1,0:T(8,128)(2,1)S(1)} collective-permute-done((bf16[96,1792]{1,0:T(8,128)(2,1)S(1)}, bf16[96,1792]{1,0:T(8,128)(2,1)S(1)}, u32[]{:S(2)}, u32[]{:S(2)}) %collective-permute-start.5) | collective-permute-done | bytes 344096 | tf_op jit(solution)/shard_map/ppermute | solution.py:294
  73.6 1.0 fusion.9
  74.7 1.3 %collective-permute-start.7 = (bf16[96,1792]{1,0:T(8,128)(2,1)S(1)}, bf16[96,1792]{1,0:T(8,128)(2,1)S(1)}, u32[]{:S(2)}, u32[]{:S(2)}) collective-permute-start(bf16[96,1792]{1,0:T(8,128)(2,1)S(1)} %add_convert_fusion.8), channel_id=1, source_target_pairs={{0,2},{1,0},{2,4},{3,1},{4,6},{5,3},{6,7},{7,5},{8,9},{9,11},{10,8... | collective-permute-start | bytes 1032200 | tf_op jit(solution)/shard_map/ppermute | solution.py:294
  76.0 3.4 %column_pieces.14 = (bf16[96,1792]{1,0:T(8,128)(2,1)S(1)}, bf16[96,1792]{1,0:T(8,128)(2,1)S(1)}) custom-call(s32[2]{0:T(128)S(1)} %copy-done.1, bf16[96,512]{1,0:T(8,128)(2,1)S(1)} %slice.17.rows_ref, bf16[1,512,14336]{2,1,0:T(8,128)(2,1)} %refs_0_.17, bf16[1,512,14336]{2,1,0:T(8,128)(2,1)} %refs_1_.17), custom_call_target="tpu_custom_call" | custom-call | flops 352321536 | bytes 3670016 | tf_op jit(solution)/shard_map/column_pieces/pallas_call | solution.py:120
  79.4 0.9 collective-permute-start.15
  80.3 2.2 %collective-permute-done.7 = bf16[96,1792]{1,0:T(8,128)(2,1)S(1)} collective-permute-done((bf16[96,1792]{1,0:T(8,128)(2,1)S(1)}, bf16[96,1792]{1,0:T(8,128)(2,1)S(1)}, u32[]{:S(2)}, u32[]{:S(2)}) %collective-permute-start.7) | collective-permute-done | bytes 344096 | tf_op jit(solution)/shard_map/ppermute | solution.py:294
  82.6 1.4 %collective-permute-start.8 = (bf16[96,1792]{1,0:T(8,128)(2,1)S(1)}, bf16[96,1792]{1,0:T(8,128)(2,1)S(1)}, u32[]{:S(2)}, u32[]{:S(2)}) collective-permute-start(bf16[96,1792]{1,0:T(8,128)(2,1)S(1)} %add_convert_fusion.7), channel_id=1, source_target_pairs={{0,2},{1,0},{2,4},{3,1},{4,6},{5,3},{6,7},{7,5},{8,9},{9,11},{10,8... | collective-permute-start | bytes 1032200 | tf_op jit(solution)/shard_map/ppermute | solution.py:294
  84.0 3.1 %column_pieces.15 = (bf16[96,1792]{1,0:T(8,128)(2,1)S(1)}, bf16[96,1792]{1,0:T(8,128)(2,1)S(1)}) custom-call(s32[2]{0:T(128)S(1)} %copy-done.1, bf16[96,512]{1,0:T(8,128)(2,1)S(1)} %slice.17.rows_ref, bf16[1,512,14336]{2,1,0:T(8,128)(2,1)} %refs_0_.17, bf16[1,512,14336]{2,1,0:T(8,128)(2,1)} %refs_1_.17), custom_call_target="tpu_custom_call" | custom-call | flops 352321536 | bytes 3670016 | tf_op jit(solution)/shard_map/column_pieces/pallas_call | solution.py:120
  87.2 2.9 %collective-permute-done.8.gate_ref = bf16[96,1792]{1,0:T(8,128)(2,1)S(1)} collective-permute-done((bf16[96,1792]{1,0:T(8,128)(2,1)S(1)}, bf16[96,1792]{1,0:T(8,128)(2,1)S(1)}, u32[]{:S(2)}, u32[]{:S(2)}) %collective-permute-start.8) | collective-permute-done | bytes 344096 | tf_op jit(solution)/shard_map/ppermute | solution.py:294
  90.1 1.1 hidden_rows.1
  91.3 2.7 %fusion.4 = bf16[64,4096]{1,0:T(8,128)(2,1)S(1)} fusion(bf16[64,1792]{1,0:T(8,128)(2,1)S(1)} %get-tuple-element.92, bf16[1,1792,4096]{2,1,0:T(8,128)(2,1)S(1)} %bitcast.24), kind=kOutput, calls=%fused_computation.4 | convolution fusion | flops 939786240 | bytes 15433728 | tf_op jit(solution)/shard_map/dot_general | solution.py:235
  94.1 2.7 %fusion.2 = f32[64,4096]{1,0:T(8,128)S(1)} fusion(bf16[64,1792]{1,0:T(8,128)(2,1)S(1)} %get-tuple-element.91, bf16[1,1792,4096]{2,1,0:T(8,128)(2,1)S(1)} %bitcast.24), kind=kOutput, calls=%fused_computation.2 | convolution fusion | flops 939524096 | bytes 15958016 | tf_op jit(solution)/shard_map/dot_general | solution.py:235
  96.8 0.1 add_convert_fusion
  97.0 0.2 reshape.12
  97.2 20.6 %all_to_all.11 = bf16[16,4,4096]{2,1,0:T(4,128)(2,1)S(1)} all-to-all(bf16[16,4,4096]{2,1,0:T(4,128)(2,1)S(1)} %reshape.12), channel_id=1, replica_groups={{0,1,2,3,4,5,6,7,16,17,18,19,20,21,22,23},{8,9,10,11,12,13,14,15,24,25,..., dimensions={0} | all-to-all | bytes 1048576 | tf_op jit(solution)/shard_map/all_to_all | solution.py:346
  117.7 0.8 reduce_sum.12
  (40 shorter events, 1.0 us)
Async XLA Ops:
  0.7 20.2 %copy-start = (s32[2]{0:T(128)}, s32[2]{0:T(128)S(1)}, u32[]{:S(2)}) copy-start(s32[2]{0:T(128)S(1)} %pad_add_fusion.where_ref) | copy-start | bytes 28
  20.9 10.8 %collective-permute-start.9 = (bf16[96,1792]{1,0:T(8,128)(2,1)S(1)}, bf16[96,1792]{1,0:T(8,128)(2,1)S(1)}, u32[]{:S(2)}, u32[]{:S(2)}) collective-permute-start(bf16[96,1792]{1,0:T(8,128)(2,1)S(1)} %get-tuple-element.80), channel_id=1, source_target_pairs={{0,1},{1,3},{2,0},{3,5},{4,2},{5,7},{6,4},{7,6},{8,10},{9,8},{10,1... | collective-permute-start | bytes 1032200 | tf_op jit(solution)/shard_map/ppermute | solution.py:295
  22.5 10.5 %collective-permute-start = (bf16[96,1792]{1,0:T(8,128)(2,1)S(1)}, bf16[96,1792]{1,0:T(8,128)(2,1)S(1)}, u32[]{:S(2)}, u32[]{:S(2)}) collective-permute-start(bf16[96,1792]{1,0:T(8,128)(2,1)S(1)} %get-tuple-element.52), channel_id=1, source_target_pairs={{0,2},{1,0},{2,4},{3,1},{4,6},{5,3},{6,7},{7,5},{8,9},{9,11},{10,8... | collective-permute-start | bytes 1032200 | tf_op jit(solution)/shard_map/ppermute | solution.py:294
  26.3 16.5 %collective-permute-start.2 = (bf16[2,512,512]{2,1,0:T(8,128)(2,1)}, bf16[2,512,512]{2,1,0:T(8,128)(2,1)S(1)}, u32[]{:S(2)}, u32[]{:S(2)}) collective-permute-start(bf16[2,512,512]{2,1,0:T(8,128)(2,1)} %get-tuple-element.55), channel_id=1, source_target_pairs={{0,8},{8,0},{16,24},{24,16},{1,9},{9,1},{17,25},{25,17},{2,10},{10... | collective-permute-start | bytes 3145736 | tf_op jit(solution)/shard_map/ppermute | solution.py:304
  26.3 0.7 copy-start.1
  31.8 10.2 %collective-permute-start.10 = (bf16[96,1792]{1,0:T(8,128)(2,1)S(1)}, bf16[96,1792]{1,0:T(8,128)(2,1)S(1)}, u32[]{:S(2)}, u32[]{:S(2)}) collective-permute-start(bf16[96,1792]{1,0:T(8,128)(2,1)S(1)} %add_convert_fusion.6), channel_id=1, source_target_pairs={{0,1},{1,3},{2,0},{3,5},{4,2},{5,7},{6,4},{7,6},{8,10},{9,8},{10,1... | collective-permute-start | bytes 1032200 | tf_op jit(solution)/shard_map/ppermute | solution.py:295
  33.1 9.7 %collective-permute-start.1 = (bf16[96,1792]{1,0:T(8,128)(2,1)S(1)}, bf16[96,1792]{1,0:T(8,128)(2,1)S(1)}, u32[]{:S(2)}, u32[]{:S(2)}) collective-permute-start(bf16[96,1792]{1,0:T(8,128)(2,1)S(1)} %add_convert_fusion.12), channel_id=1, source_target_pairs={{0,2},{1,0},{2,4},{3,1},{4,6},{5,3},{6,7},{7,5},{8,9},{9,11},{10,8... | collective-permute-start | bytes 1032200 | tf_op jit(solution)/shard_map/ppermute | solution.py:294
  42.0 9.3 %collective-permute-start.11 = (bf16[96,1792]{1,0:T(8,128)(2,1)S(1)}, bf16[96,1792]{1,0:T(8,128)(2,1)S(1)}, u32[]{:S(2)}, u32[]{:S(2)}) collective-permute-start(bf16[96,1792]{1,0:T(8,128)(2,1)S(1)} %add_convert_fusion.5), channel_id=1, source_target_pairs={{0,1},{1,3},{2,0},{3,5},{4,2},{5,7},{6,4},{7,6},{8,10},{9,8},{10,1... | collective-permute-start | bytes 1032200 | tf_op jit(solution)/shard_map/ppermute | solution.py:295
  42.9 8.9 %copy-start.3 = (bf16[2,512,512]{2,1,0:T(8,128)(2,1)S(1)}, bf16[2,512,512]{2,1,0:T(8,128)(2,1)}, u32[]{:S(2)}) copy-start(bf16[2,512,512]{2,1,0:T(8,128)(2,1)} %get-tuple-element.69) | copy-start | bytes 3145732
  42.9 11.4 %collective-permute-start.3 = (bf16[96,1792]{1,0:T(8,128)(2,1)S(1)}, bf16[96,1792]{1,0:T(8,128)(2,1)S(1)}, u32[]{:S(2)}, u32[]{:S(2)}) collective-permute-start(bf16[96,1792]{1,0:T(8,128)(2,1)S(1)} %add_convert_fusion.11), channel_id=1, source_target_pairs={{0,2},{1,0},{2,4},{3,1},{4,6},{5,3},{6,7},{7,5},{8,9},{9,11},{10,8... | collective-permute-start | bytes 1032200 | tf_op jit(solution)/shard_map/ppermute | solution.py:294
  51.4 8.4 %collective-permute-start.12 = (bf16[96,1792]{1,0:T(8,128)(2,1)S(1)}, bf16[96,1792]{1,0:T(8,128)(2,1)S(1)}, u32[]{:S(2)}, u32[]{:S(2)}) collective-permute-start(bf16[96,1792]{1,0:T(8,128)(2,1)S(1)} %add_convert_fusion.4), channel_id=1, source_target_pairs={{0,1},{1,3},{2,0},{3,5},{4,2},{5,7},{6,4},{7,6},{8,10},{9,8},{10,1... | collective-permute-start | bytes 1032200 | tf_op jit(solution)/shard_map/ppermute | solution.py:295
  52.1 17.2 %collective-permute-start.6 = (bf16[512,512]{1,0:T(8,128)(2,1)S(1)}, bf16[512,512]{1,0:T(8,128)(2,1)S(1)}, u32[]{:S(2)}, u32[]{:S(2)}) collective-permute-start(bf16[512,512]{1,0:T(8,128)(2,1)S(1)} %fusion.10), channel_id=1, source_target_pairs={{0,16},{8,24},{16,0},{24,8},{1,17},{9,25},{17,1},{25,9},{2,18},{10... | collective-permute-start | bytes 1572872 | tf_op jit(solution)/shard_map/ppermute | solution.py:312
  54.4 9.5 %collective-permute-start.4 = (bf16[96,1792]{1,0:T(8,128)(2,1)S(1)}, bf16[96,1792]{1,0:T(8,128)(2,1)S(1)}, u32[]{:S(2)}, u32[]{:S(2)}) collective-permute-start(bf16[96,1792]{1,0:T(8,128)(2,1)S(1)} %add_convert_fusion.10), channel_id=1, source_target_pairs={{0,2},{1,0},{2,4},{3,1},{4,6},{5,3},{6,7},{7,5},{8,9},{9,11},{10,8... | collective-permute-start | bytes 1032200 | tf_op jit(solution)/shard_map/ppermute | solution.py:294
  59.9 8.4 %collective-permute-start.13 = (bf16[96,1792]{1,0:T(8,128)(2,1)S(1)}, bf16[96,1792]{1,0:T(8,128)(2,1)S(1)}, u32[]{:S(2)}, u32[]{:S(2)}) collective-permute-start(bf16[96,1792]{1,0:T(8,128)(2,1)S(1)} %add_convert_fusion.3), channel_id=1, source_target_pairs={{0,1},{1,3},{2,0},{3,5},{4,2},{5,7},{6,4},{7,6},{8,10},{9,8},{10,1... | collective-permute-start | bytes 1032200 | tf_op jit(solution)/shard_map/ppermute | solution.py:295
  64.0 9.7 %collective-permute-start.5 = (bf16[96,1792]{1,0:T(8,128)(2,1)S(1)}, bf16[96,1792]{1,0:T(8,128)(2,1)S(1)}, u32[]{:S(2)}, u32[]{:S(2)}) collective-permute-start(bf16[96,1792]{1,0:T(8,128)(2,1)S(1)} %add_convert_fusion.9), channel_id=1, source_target_pairs={{0,2},{1,0},{2,4},{3,1},{4,6},{5,3},{6,7},{7,5},{8,9},{9,11},{10,8... | collective-permute-start | bytes 1032200 | tf_op jit(solution)/shard_map/ppermute | solution.py:294
  68.5 10.9 %collective-permute-start.14 = (bf16[96,1792]{1,0:T(8,128)(2,1)S(1)}, bf16[96,1792]{1,0:T(8,128)(2,1)S(1)}, u32[]{:S(2)}, u32[]{:S(2)}) collective-permute-start(bf16[96,1792]{1,0:T(8,128)(2,1)S(1)} %add_convert_fusion.2), channel_id=1, source_target_pairs={{0,1},{1,3},{2,0},{3,5},{4,2},{5,7},{6,4},{7,6},{8,10},{9,8},{10,1... | collective-permute-start | bytes 1032200 | tf_op jit(solution)/shard_map/ppermute | solution.py:295
  74.7 7.8 %collective-permute-start.7 = (bf16[96,1792]{1,0:T(8,128)(2,1)S(1)}, bf16[96,1792]{1,0:T(8,128)(2,1)S(1)}, u32[]{:S(2)}, u32[]{:S(2)}) collective-permute-start(bf16[96,1792]{1,0:T(8,128)(2,1)S(1)} %add_convert_fusion.8), channel_id=1, source_target_pairs={{0,2},{1,0},{2,4},{3,1},{4,6},{5,3},{6,7},{7,5},{8,9},{9,11},{10,8... | collective-permute-start | bytes 1032200 | tf_op jit(solution)/shard_map/ppermute | solution.py:294
  76.0 15.3 %slice-start = ((s8[14680064]{0:T(1024)(128)(4,1)}), s8[4194304]{0:T(1024)(128)(4,1)S(1)}, s32[]{:S(2)}) async-start(s8[14680064]{0:T(1024)(128)(4,1)} %bitcast.23), calls=%async_computation.2 | async-start | bytes 8388608
  76.0 15.3 %slice-start.1 = ((s8[14680064]{0:T(1024)(128)(4,1)}), s8[4194304]{0:T(1024)(128)(4,1)S(1)}, s32[]{:S(2)}) async-start(s8[14680064]{0:T(1024)(128)(4,1)} %bitcast.23), calls=%async_computation.3 | async-start | bytes 8388608
  79.4 7.7 %collective-permute-start.15 = (bf16[96,1792]{1,0:T(8,128)(2,1)S(1)}, bf16[96,1792]{1,0:T(8,128)(2,1)S(1)}, u32[]{:S(2)}, u32[]{:S(2)}) collective-permute-start(bf16[96,1792]{1,0:T(8,128)(2,1)S(1)} %add_convert_fusion.1), channel_id=1, source_target_pairs={{0,1},{1,3},{2,0},{3,5},{4,2},{5,7},{6,4},{7,6},{8,10},{9,8},{10,1... | collective-permute-start | bytes 1032200 | tf_op jit(solution)/shard_map/ppermute | solution.py:295
  82.5 8.7 %slice-start.2 = ((s8[14680064]{0:T(1024)(128)(4,1)}), s8[4194304]{0:T(1024)(128)(4,1)S(1)}, s32[]{:S(2)}) async-start(s8[14680064]{0:T(1024)(128)(4,1)} %bitcast.23), calls=%async_computation.4 | async-start | bytes 8388608
  82.6 7.5 %collective-permute-start.8 = (bf16[96,1792]{1,0:T(8,128)(2,1)S(1)}, bf16[96,1792]{1,0:T(8,128)(2,1)S(1)}, u32[]{:S(2)}, u32[]{:S(2)}) collective-permute-start(bf16[96,1792]{1,0:T(8,128)(2,1)S(1)} %add_convert_fusion.7), channel_id=1, source_target_pairs={{0,2},{1,0},{2,4},{3,1},{4,6},{5,3},{6,7},{7,5},{8,9},{9,11},{10,8... | collective-permute-start | bytes 1032200 | tf_op jit(solution)/shard_map/ppermute | solution.py:294
  84.0 6.0 %copy-start.2 = (f32[96,128]{1,0:T(8,128)S(1)}, f32[96,128]{1,0:T(8,128)}, u32[]{:S(2)}) copy-start(f32[96,128]{1,0:T(8,128)} %constant.16.clone.origin_ref) | copy-start | bytes 147460
  84.0 7.2 %slice-start.3 = ((s8[14680064]{0:T(1024)(128)(4,1)}), s8[2097152]{0:T(1024)(128)(4,1)S(1)}, s32[]{:S(2)}) async-start(s8[14680064]{0:T(1024)(128)(4,1)} %bitcast.23), calls=%async_computation.5 | async-start | bytes 4194304
  94.0 2.8 %collective-permute-start.16 = (bf16[64,4096]{1,0:T(8,128)(2,1)S(1)}, bf16[64,4096]{1,0:T(8,128)(2,1)S(1)}, u32[]{:S(2)}, u32[]{:S(2)}) collective-permute-start(bf16[64,4096]{1,0:T(8,128)(2,1)S(1)} %fusion.4), channel_id=1, source_target_pairs={{0,8},{8,0},{16,24},{24,16},{1,9},{9,1},{17,25},{25,17},{2,10},{10... | collective-permute-start | bytes 1572872 | tf_op jit(solution)/shard_map/ppermute | solution.py:334

commit v11 on v10

--- a/solution.py
+++ b/solution.py
@@ -96,7 +96,7 @@
 
 def column_pieces(where, table, rows, gate_weight, up_weight, first, pieces, cuts):
     count, depth = rows.shape
-    cores, shards = table.shape[0], table.shape[2]
+    shards = table.shape[1]
     width = gate_weight.shape[2] // shards
     block = width // cuts
 
@@ -108,10 +108,9 @@
 
     def weight_map(side, i):
         def index(j, where_ref):
-            key = lax.rem(where_ref[0], jnp.int32(cores)) * shards + where_ref[1]
             piece = jnp.int32(0)
-            for n, value in enumerate(table[:, side, :, first + i].reshape(-1).tolist()):
-                piece = jnp.where(key == n, jnp.int32(value), piece)
+            for s, value in enumerate(table[side, :, first + i].tolist()):
+                piece = jnp.where(where_ref[1] == s, jnp.int32(value), piece)
             return 0, 0, piece * cuts + j
 
         return pl.BlockSpec((1, depth, block), index)
@@ -139,12 +138,12 @@
 
 
 def plain_pieces(where, table, rows, gate_weight, up_weight):
-    cores, shards = table.shape[0], table.shape[2]
+    shards = table.shape[1]
     width = gate_weight.shape[2] // shards
     both = []
     for side, weight in enumerate((gate_weight, up_weight)):
         value = jnp.dot(rows, weight[0], preferred_element_type=F32).astype(BF16)
-        at = jnp.asarray(table)[where[0] % cores, side, where[1]] * width
+        at = jnp.asarray(table)[side, where[1]] * width
         both.append([lax.dynamic_slice_in_dim(value, at[t], width, 1) for t in range(shards)])
     return both
 
@@ -256,16 +255,13 @@
     where = jnp.stack([lax.axis_index("branch"), lax.axis_index("shard")]).astype(jnp.int32)
 
     place = np.argsort(np.asarray(order))
-    table = np.zeros((cores, 2, shards, shards), np.int32)
-    pairs = [[], []]
-    for side in range(2):
-        for b in range(experts):
-            core = b % cores
-            way = 1 if (side + core) % 2 == 0 else -1
-            for s in range(shards):
-                for t in range(shards):
-                    table[core, side, s, t] = order[(place[s] - way * (1 + t)) % shards]
-                pairs[side].append((b * shards + s, b * shards + order[(place[s] + way) % shards]))
+    table = np.zeros((2, shards, shards), np.int32)
+    pairs = []
+    for side, way in enumerate((1, -1)):
+        for s in range(shards):
+            for t in range(shards):
+                table[side, s, t] = order[(place[s] - way * (1 + t)) % shards]
+        pairs.append([(s, order[(place[s] + way) % shards]) for s in range(shards)])
     source = np.arange(count) // capacity
     origin = np.zeros((count, LANES), np.float32)
     origin[:, 0] = source // shards % cores
@@ -291,21 +287,21 @@
     weights = [down_weight[0]]
     for t in range(1, shards):
         now, gate_sum = lax.optimization_barrier((where, gate_sum))
-        gate_in = lax.ppermute(gate_sum, ("branch", "shard"), pairs[0])
-        up_in = lax.ppermute(up_sum, ("branch", "shard"), pairs[1])
+        gate_in = lax.ppermute(gate_sum, "shard", pairs[0])
+        up_in = lax.ppermute(up_sum, "shard", pairs[1])
         if sliced and len(gates) < shards:
             more = column_pieces(
                 now, table, rows, gate_weight, up_weight, len(gates), 1, cuts
             )
             gates, ups = gates + more[0], ups + more[1]
-        if t == 1:
+        if t == min(2, last):
             kv = turn_columns(now, key_value, cores, chips)
             kv_core = [
                 lax.ppermute(kv[k], "branch", branch_target(experts, cores, k, 0))
                 for k in range(1, cores)
             ]
             gate_in, kv = lax.optimization_barrier((gate_in, kv))
-        if t == min(2, last):
+        if t == min(3, last):
             gate_in, kv_core = lax.optimization_barrier((gate_in, kv_core))
             kv_sum = kv[0].astype(F32) + sum(x.astype(F32) for x in kv_core)
             kv_chip = [
@@ -314,7 +310,7 @@
                 )
                 for k in range(1, chips)
             ]
-        if t == min(5, last):
+        if t == min(6, last):
             gate_in, kv_chip = lax.optimization_barrier((gate_in, kv_chip))
             kv_sum = kv_sum[0] + sum(x.astype(F32) for x in kv_chip)
             merged_kv = (kv_sum / experts).astype(BF16)

time: 119 us -> 115 us (0.966)
  waiting for transfers between devices: 25.5 us -> 22.2 us
  starting transfers between devices: 15.3 us -> 16.9 us
  blocking collectives: 35.8 us -> 34.2 us
    ppermute x14, waiting for transfers between devices: 25.5 us -> 22.2 us  [the longest x7 18.9 us: local(): up_in = lax.ppermute(up_sum, 'shard', pairs[1])]
    ppermute x14, starting transfers between devices: 13.1 us -> 16.2 us  [the longest x7 10.8 us: local(): up_in = lax.ppermute(up_sum, 'shard', pairs[1])]
    all_to_all x1, blocking collectives: 20.6 us -> 19 us  [local(): lax.all_to_all(mixed, ('branch', 'shard'), split_axis=0, concat_axis=0, a...]
    ppermute x1, starting transfers between devices: 2.16 us -> 0.67 us  [local(): lax.ppermute(kv_sum[k].astype(BF16), 'branch', branch_target(experts, cor...]
  transfers between devices with their start and end apart: 17 -> 17, of which waited for: 8 -> 9; matrix products, arithmetic and copies ran while one was open for 4% -> 4% of each run, Pallas kernels for 21% -> 22%
where the time goes in v11:
time: 115 us
  blocking collectives  34.2 us (30%)
  Pallas kernels  31 us (27%)
  waiting for transfers between devices  22.2 us (19%)
  starting transfers between devices  16.9 us (15%)
  matrix products  5.41 us (5%)
  other arithmetic  3.27 us (3%)
    pallas_call x8, Pallas kernels, column_pieces(): pl.pallas_call(kernel, out_shape=[jax.ShapeDtypeStruct((count, width), BF...  24.8 us
    all_to_all x1, blocking collectives, local(): lax.all_to_all(mixed, ('branch', 'shard'), split_axis=0, concat_axis=0, a...  19 us
    ppermute x7, waiting for transfers between devices, local(): up_in = lax.ppermute(up_sum, 'shard', pairs[1])  18.9 us
    all_to_all x1, blocking collectives, local(): lax.all_to_all(cells, ('branch', 'shard'), split_axis=0, concat_axis=0, t...  15.2 us
    ppermute x7, starting transfers between devices, local(): up_in = lax.ppermute(up_sum, 'shard', pairs[1])  10.8 us
    dot_general x2, matrix products, down_product(): jnp.dot(h, w, preferred_element_type=F32)  5.41 us
    ppermute x7, starting transfers between devices, local(): gate_in = lax.ppermute(gate_sum, 'shard', pairs[0])  5.4 us
    ppermute x7, waiting for transfers between devices, local(): gate_in = lax.ppermute(gate_sum, 'shard', pairs[0])  3.34 us
  transfers between devices with their start and end apart: 17, of which 9 were waited for; matrix products, arithmetic and copies ran while one was open for 4% of the time, Pallas kernels for 22%

profile of v11, /device:TPU:0, one launch (start us, length us, event | category | flops | bytes accessed | tf_op | source)
XLA Modules:
  0.0 115.0 jit_solution(5060548981581324654)
XLA Ops:
  0.7 1.7 %place_rows.1 = bf16[32,3,640]{2,1,0:T(4,128)(2,1)} custom-call(bf16[4,4096]{1,0:T(4,128)(2,1)} %tokens_ref.1, s32[2,4]{1,0:T(2,128)} %bitcast.25, f32[2,4]{1,0:T(2,128)} %bitcast.26), custom_call_target="tpu_custom_call" | custom-call | tf_op jit(solution)/shard_map/place_rows/pallas_call | solution.py:84
  2.5 15.2 %all_to_all.10 = bf16[32,3,640]{2,1,0:T(4,128)(2,1)S(1)} all-to-all(bf16[32,3,640]{2,1,0:T(4,128)(2,1)} %place_rows.1), channel_id=1, replica_groups=mesh['branch'=4,'shard'=8] {'branch','shard'}, dimensions={0} | all-to-all | bytes 245760 | tf_op jit(solution)/shard_map/all_to_all | solution.py:274
  17.7 0.1 reshape.11
  17.8 3.1 %column_pieces.8 = (bf16[96,1792]{1,0:T(8,128)(2,1)S(1)}, bf16[96,1792]{1,0:T(8,128)(2,1)S(1)}) custom-call(s32[2]{0:T(128)S(1)} %pad_add_fusion.where_ref, bf16[96,512]{1,0:T(8,128)(2,1)S(1)} %slice.17.rows_ref, bf16[1,512,14336]{2,1,0:T(8,128)(2,1)} %refs_0_.17, bf16[1,512,14336]{2,1,0:T(8,128)(2,1)} %refs_1_.17), custom_call_target="tpu_custom_call" | custom-call | flops 352321536 | bytes 3670016 | tf_op jit(solution)/shard_map/column_pieces/pallas_call | solution.py:119
  20.9 1.6 %collective-permute-start.9 = (bf16[96,1792]{1,0:T(8,128)(2,1)S(1)}, bf16[96,1792]{1,0:T(8,128)(2,1)S(1)}, u32[]{:S(2)}, u32[]{:S(2)}) collective-permute-start(bf16[96,1792]{1,0:T(8,128)(2,1)S(1)} %get-tuple-element.80), channel_id=1, source_target_pairs={{0,1},{1,3},{2,0},{3,5},{4,2},{5,7},{6,4},{7,6},{8,9},{9,11},{10,8... | collective-permute-start | bytes 1032200 | tf_op jit(solution)/shard_map/ppermute | solution.py:291
  22.5 0.5 collective-permute-start
  23.0 3.1 %column_pieces.9 = (bf16[96,1792]{1,0:T(8,128)(2,1)S(1)}, bf16[96,1792]{1,0:T(8,128)(2,1)S(1)}) custom-call(s32[2]{0:T(128)S(1)} %pad_add_fusion.where_ref, bf16[96,512]{1,0:T(8,128)(2,1)S(1)} %slice.17.rows_ref, bf16[1,512,14336]{2,1,0:T(8,128)(2,1)} %refs_0_.17, bf16[1,512,14336]{2,1,0:T(8,128)(2,1)} %refs_1_.17), custom_call_target="tpu_custom_call" | custom-call | flops 352321536 | bytes 3670016 | tf_op jit(solution)/shard_map/column_pieces/pallas_call | solution.py:119
  26.0 5.0 %collective-permute-done.9 = bf16[96,1792]{1,0:T(8,128)(2,1)S(1)} collective-permute-done((bf16[96,1792]{1,0:T(8,128)(2,1)S(1)}, bf16[96,1792]{1,0:T(8,128)(2,1)S(1)}, u32[]{:S(2)}, u32[]{:S(2)}) %collective-permute-start.9) | collective-permute-done | bytes 344096 | tf_op jit(solution)/shard_map/ppermute | solution.py:291
  31.1 1.5 %collective-permute-start.10 = (bf16[96,1792]{1,0:T(8,128)(2,1)S(1)}, bf16[96,1792]{1,0:T(8,128)(2,1)S(1)}, u32[]{:S(2)}, u32[]{:S(2)}) collective-permute-start(bf16[96,1792]{1,0:T(8,128)(2,1)S(1)} %add_convert_fusion.6), channel_id=1, source_target_pairs={{0,1},{1,3},{2,0},{3,5},{4,2},{5,7},{6,4},{7,6},{8,9},{9,11},{10,8... | collective-permute-start | bytes 1032200 | tf_op jit(solution)/shard_map/ppermute | solution.py:291
  32.7 0.1 add_convert_fusion.12
  32.8 0.6 collective-permute-start.1
  33.4 3.3 %turn_columns.1 = (bf16[2,512,512]{2,1,0:T(8,128)(2,1)}, bf16[2,512,512]{2,1,0:T(8,128)(2,1)}) custom-call(s32[2]{0:T(128)} %copy-done, bf16[1,512,2048]{2,1,0:T(8,128)(2,1)} %refs_1_.11, bf16[1,512,2048]{2,1,0:T(8,128)(2,1)} %refs_1_.11), custom_call_target="tpu_custom_call" | custom-call | bytes 4194304 | tf_op jit(solution)/shard_map/turn_columns/pallas_call | solution.py:167
  36.7 0.7 copy-done.1
  37.3 3.1 %column_pieces.10 = (bf16[96,1792]{1,0:T(8,128)(2,1)S(1)}, bf16[96,1792]{1,0:T(8,128)(2,1)S(1)}) custom-call(s32[2]{0:T(128)S(1)} %copy-done.1, bf16[96,512]{1,0:T(8,128)(2,1)S(1)} %slice.17.rows_ref, bf16[1,512,14336]{2,1,0:T(8,128)(2,1)} %refs_0_.17, bf16[1,512,14336]{2,1,0:T(8,128)(2,1)} %refs_1_.17), custom_call_target="tpu_custom_call" | custom-call | flops 352321536 | bytes 3670016 | tf_op jit(solution)/shard_map/column_pieces/pallas_call | solution.py:119
  40.6 1.5 %collective-permute-start.11 = (bf16[96,1792]{1,0:T(8,128)(2,1)S(1)}, bf16[96,1792]{1,0:T(8,128)(2,1)S(1)}, u32[]{:S(2)}, u32[]{:S(2)}) collective-permute-start(bf16[96,1792]{1,0:T(8,128)(2,1)S(1)} %add_convert_fusion.5), channel_id=1, source_target_pairs={{0,1},{1,3},{2,0},{3,5},{4,2},{5,7},{6,4},{7,6},{8,9},{9,11},{10,8... | collective-permute-start | bytes 1032200 | tf_op jit(solution)/shard_map/ppermute | solution.py:291
  42.1 0.1 add_convert_fusion.11
  42.1 0.6 collective-permute-start.2
  42.8 3.1 %column_pieces.11 = (bf16[96,1792]{1,0:T(8,128)(2,1)S(1)}, bf16[96,1792]{1,0:T(8,128)(2,1)S(1)}) custom-call(s32[2]{0:T(128)S(1)} %copy-done.1, bf16[96,512]{1,0:T(8,128)(2,1)S(1)} %slice.17.rows_ref, bf16[1,512,14336]{2,1,0:T(8,128)(2,1)} %refs_0_.17, bf16[1,512,14336]{2,1,0:T(8,128)(2,1)} %refs_1_.17), custom_call_target="tpu_custom_call" | custom-call | flops 352321536 | bytes 3670016 | tf_op jit(solution)/shard_map/column_pieces/pallas_call | solution.py:119
  45.9 5.2 %collective-permute-done.11 = bf16[96,1792]{1,0:T(8,128)(2,1)S(1)} collective-permute-done((bf16[96,1792]{1,0:T(8,128)(2,1)S(1)}, bf16[96,1792]{1,0:T(8,128)(2,1)S(1)}, u32[]{:S(2)}, u32[]{:S(2)}) %collective-permute-start.11) | collective-permute-done | bytes 344096 | tf_op jit(solution)/shard_map/ppermute | solution.py:291
  51.0 0.1 add_convert_fusion.4
  51.1 1.5 %collective-permute-start.12 = (bf16[96,1792]{1,0:T(8,128)(2,1)S(1)}, bf16[96,1792]{1,0:T(8,128)(2,1)S(1)}, u32[]{:S(2)}, u32[]{:S(2)}) collective-permute-start(bf16[96,1792]{1,0:T(8,128)(2,1)S(1)} %add_convert_fusion.4), channel_id=1, source_target_pairs={{0,1},{1,3},{2,0},{3,5},{4,2},{5,7},{6,4},{7,6},{8,9},{9,11},{10,8... | collective-permute-start | bytes 1032200 | tf_op jit(solution)/shard_map/ppermute | solution.py:291
  52.7 0.6 collective-permute-start.4
  53.4 3.1 %column_pieces.12 = (bf16[96,1792]{1,0:T(8,128)(2,1)S(1)}, bf16[96,1792]{1,0:T(8,128)(2,1)S(1)}) custom-call(s32[2]{0:T(128)S(1)} %copy-done.1, bf16[96,512]{1,0:T(8,128)(2,1)S(1)} %slice.17.rows_ref, bf16[1,512,14336]{2,1,0:T(8,128)(2,1)} %refs_0_.17, bf16[1,512,14336]{2,1,0:T(8,128)(2,1)} %refs_1_.17), custom_call_target="tpu_custom_call" | custom-call | flops 352321536 | bytes 3670016 | tf_op jit(solution)/shard_map/column_pieces/pallas_call | solution.py:119
  56.4 4.4 %collective-permute-done.12 = bf16[96,1792]{1,0:T(8,128)(2,1)S(1)} collective-permute-done((bf16[96,1792]{1,0:T(8,128)(2,1)S(1)}, bf16[96,1792]{1,0:T(8,128)(2,1)S(1)}, u32[]{:S(2)}, u32[]{:S(2)}) %collective-permute-start.12) | collective-permute-done | bytes 344096 | tf_op jit(solution)/shard_map/ppermute | solution.py:291
  60.9 1.5 %collective-permute-start.13 = (bf16[96,1792]{1,0:T(8,128)(2,1)S(1)}, bf16[96,1792]{1,0:T(8,128)(2,1)S(1)}, u32[]{:S(2)}, u32[]{:S(2)}) collective-permute-start(bf16[96,1792]{1,0:T(8,128)(2,1)S(1)} %add_convert_fusion.3), channel_id=1, source_target_pairs={{0,1},{1,3},{2,0},{3,5},{4,2},{5,7},{6,4},{7,6},{8,9},{9,11},{10,8... | collective-permute-start | bytes 1032200 | tf_op jit(solution)/shard_map/ppermute | solution.py:291
  62.5 0.3 convert_add_fusion
  62.8 0.7 collective-permute-start.7
  63.6 1.2 %collective-permute-start.5 = (bf16[96,1792]{1,0:T(8,128)(2,1)S(1)}, bf16[96,1792]{1,0:T(8,128)(2,1)S(1)}, u32[]{:S(2)}, u32[]{:S(2)}) collective-permute-start(bf16[96,1792]{1,0:T(8,128)(2,1)S(1)} %add_convert_fusion.9), channel_id=1, source_target_pairs={{0,2},{1,0},{2,4},{3,1},{4,6},{5,3},{6,7},{7,5},{8,10},{9,8},{10,1... | collective-permute-start | bytes 1032200 | tf_op jit(solution)/shard_map/ppermute | solution.py:290
  64.8 3.1 %column_pieces.13 = (bf16[96,1792]{1,0:T(8,128)(2,1)S(1)}, bf16[96,1792]{1,0:T(8,128)(2,1)S(1)}) custom-call(s32[2]{0:T(128)S(1)} %copy-done.1, bf16[96,512]{1,0:T(8,128)(2,1)S(1)} %slice.17.rows_ref, bf16[1,512,14336]{2,1,0:T(8,128)(2,1)} %refs_0_.17, bf16[1,512,14336]{2,1,0:T(8,128)(2,1)} %refs_1_.17), custom_call_target="tpu_custom_call" | custom-call | flops 352321536 | bytes 3670016 | tf_op jit(solution)/shard_map/column_pieces/pallas_call | solution.py:119
  67.8 1.9 %collective-permute-done.13 = bf16[96,1792]{1,0:T(8,128)(2,1)S(1)} collective-permute-done((bf16[96,1792]{1,0:T(8,128)(2,1)S(1)}, bf16[96,1792]{1,0:T(8,128)(2,1)S(1)}, u32[]{:S(2)}, u32[]{:S(2)}) %collective-permute-start.13) | collective-permute-done | bytes 344096 | tf_op jit(solution)/shard_map/ppermute | solution.py:291
  69.8 1.6 %collective-permute-start.14 = (bf16[96,1792]{1,0:T(8,128)(2,1)S(1)}, bf16[96,1792]{1,0:T(8,128)(2,1)S(1)}, u32[]{:S(2)}, u32[]{:S(2)}) collective-permute-start(bf16[96,1792]{1,0:T(8,128)(2,1)S(1)} %add_convert_fusion.2), channel_id=1, source_target_pairs={{0,1},{1,3},{2,0},{3,5},{4,2},{5,7},{6,4},{7,6},{8,9},{9,11},{10,8... | collective-permute-start | bytes 1032200 | tf_op jit(solution)/shard_map/ppermute | solution.py:291
  71.4 0.5 collective-permute-done.5
  72.0 1.0 collective-permute-start.6
  73.0 3.1 %column_pieces.14 = (bf16[96,1792]{1,0:T(8,128)(2,1)S(1)}, bf16[96,1792]{1,0:T(8,128)(2,1)S(1)}) custom-call(s32[2]{0:T(128)S(1)} %copy-done.1, bf16[96,512]{1,0:T(8,128)(2,1)S(1)} %slice.17.rows_ref, bf16[1,512,14336]{2,1,0:T(8,128)(2,1)} %refs_0_.17, bf16[1,512,14336]{2,1,0:T(8,128)(2,1)} %refs_1_.17), custom_call_target="tpu_custom_call" | custom-call | flops 352321536 | bytes 3670016 | tf_op jit(solution)/shard_map/column_pieces/pallas_call | solution.py:119
  76.1 1.9 %collective-permute-done.14 = bf16[96,1792]{1,0:T(8,128)(2,1)S(1)} collective-permute-done((bf16[96,1792]{1,0:T(8,128)(2,1)S(1)}, bf16[96,1792]{1,0:T(8,128)(2,1)S(1)}, u32[]{:S(2)}, u32[]{:S(2)}) %collective-permute-start.14) | collective-permute-done | bytes 344096 | tf_op jit(solution)/shard_map/ppermute | solution.py:291
  78.0 1.6 %collective-permute-start.15 = (bf16[96,1792]{1,0:T(8,128)(2,1)S(1)}, bf16[96,1792]{1,0:T(8,128)(2,1)S(1)}, u32[]{:S(2)}, u32[]{:S(2)}) collective-permute-start(bf16[96,1792]{1,0:T(8,128)(2,1)S(1)} %add_convert_fusion.1), channel_id=1, source_target_pairs={{0,1},{1,3},{2,0},{3,5},{4,2},{5,7},{6,4},{7,6},{8,9},{9,11},{10,8... | collective-permute-start | bytes 1032200 | tf_op jit(solution)/shard_map/ppermute | solution.py:291
  79.6 1.0 fusion.9
  80.7 0.9 collective-permute-start.8
  81.5 3.3 %column_pieces.15 = (bf16[96,1792]{1,0:T(8,128)(2,1)S(1)}, bf16[96,1792]{1,0:T(8,128)(2,1)S(1)}) custom-call(s32[2]{0:T(128)S(1)} %copy-done.1, bf16[96,512]{1,0:T(8,128)(2,1)S(1)} %slice.17.rows_ref, bf16[1,512,14336]{2,1,0:T(8,128)(2,1)} %refs_0_.17, bf16[1,512,14336]{2,1,0:T(8,128)(2,1)} %refs_1_.17), custom_call_target="tpu_custom_call" | custom-call | flops 352321536 | bytes 3670016 | tf_op jit(solution)/shard_map/column_pieces/pallas_call | solution.py:119
  84.8 0.5 collective-permute-done.15.up_ref
  85.3 2.8 %collective-permute-done.8.gate_ref = bf16[96,1792]{1,0:T(8,128)(2,1)S(1)} collective-permute-done((bf16[96,1792]{1,0:T(8,128)(2,1)S(1)}, bf16[96,1792]{1,0:T(8,128)(2,1)S(1)}, u32[]{:S(2)}, u32[]{:S(2)}) %collective-permute-start.8) | collective-permute-done | bytes 344096 | tf_op jit(solution)/shard_map/ppermute | solution.py:290
  88.1 1.1 hidden_rows.1
  89.3 2.7 %fusion.4 = bf16[64,4096]{1,0:T(8,128)(2,1)S(1)} fusion(bf16[64,1792]{1,0:T(8,128)(2,1)S(1)} %get-tuple-element.92, bf16[1,1792,4096]{2,1,0:T(8,128)(2,1)S(1)} %bitcast.24), kind=kOutput, calls=%fused_computation.4 | convolution fusion | flops 939786240 | bytes 15433728 | tf_op jit(solution)/shard_map/dot_general | solution.py:234
  92.1 2.7 %fusion.2 = f32[64,4096]{1,0:T(8,128)S(1)} fusion(bf16[64,1792]{1,0:T(8,128)(2,1)S(1)} %get-tuple-element.91, bf16[1,1792,4096]{2,1,0:T(8,128)(2,1)S(1)} %bitcast.24), kind=kOutput, calls=%fused_computation.2 | convolution fusion | flops 939524096 | bytes 15958016 | tf_op jit(solution)/shard_map/dot_general | solution.py:234
  94.9 0.1 add_convert_fusion
  95.0 0.2 reshape.12
  95.2 19.0 %all_to_all.11 = bf16[16,4,4096]{2,1,0:T(4,128)(2,1)S(1)} all-to-all(bf16[16,4,4096]{2,1,0:T(4,128)(2,1)S(1)} %reshape.12), channel_id=1, replica_groups={{0,1,2,3,4,5,6,7,16,17,18,19,20,21,22,23},{8,9,10,11,12,13,14,15,24,25,..., dimensions={0} | all-to-all | bytes 1048576 | tf_op jit(solution)/shard_map/all_to_all | solution.py:342
  114.2 0.8 reduce_sum.12
  (40 shorter events, 1.1 us)
Async XLA Ops:
  0.7 22.3 %copy-start = (s32[2]{0:T(128)}, s32[2]{0:T(128)S(1)}, u32[]{:S(2)}) copy-start(s32[2]{0:T(128)S(1)} %pad_add_fusion.where_ref) | copy-start | bytes 28
  20.9 10.2 %collective-permute-start.9 = (bf16[96,1792]{1,0:T(8,128)(2,1)S(1)}, bf16[96,1792]{1,0:T(8,128)(2,1)S(1)}, u32[]{:S(2)}, u32[]{:S(2)}) collective-permute-start(bf16[96,1792]{1,0:T(8,128)(2,1)S(1)} %get-tuple-element.80), channel_id=1, source_target_pairs={{0,1},{1,3},{2,0},{3,5},{4,2},{5,7},{6,4},{7,6},{8,9},{9,11},{10,8... | collective-permute-start | bytes 1032200 | tf_op jit(solution)/shard_map/ppermute | solution.py:291
  22.5 10.2 %collective-permute-start = (bf16[96,1792]{1,0:T(8,128)(2,1)S(1)}, bf16[96,1792]{1,0:T(8,128)(2,1)S(1)}, u32[]{:S(2)}, u32[]{:S(2)}) collective-permute-start(bf16[96,1792]{1,0:T(8,128)(2,1)S(1)} %get-tuple-element.52), channel_id=1, source_target_pairs={{0,2},{1,0},{2,4},{3,1},{4,6},{5,3},{6,7},{7,5},{8,10},{9,8},{10,1... | collective-permute-start | bytes 1032200 | tf_op jit(solution)/shard_map/ppermute | solution.py:290
  31.1 9.3 %collective-permute-start.10 = (bf16[96,1792]{1,0:T(8,128)(2,1)S(1)}, bf16[96,1792]{1,0:T(8,128)(2,1)S(1)}, u32[]{:S(2)}, u32[]{:S(2)}) collective-permute-start(bf16[96,1792]{1,0:T(8,128)(2,1)S(1)} %add_convert_fusion.6), channel_id=1, source_target_pairs={{0,1},{1,3},{2,0},{3,5},{4,2},{5,7},{6,4},{7,6},{8,9},{9,11},{10,8... | collective-permute-start | bytes 1032200 | tf_op jit(solution)/shard_map/ppermute | solution.py:291
  32.8 9.3 %collective-permute-start.1 = (bf16[96,1792]{1,0:T(8,128)(2,1)S(1)}, bf16[96,1792]{1,0:T(8,128)(2,1)S(1)}, u32[]{:S(2)}, u32[]{:S(2)}) collective-permute-start(bf16[96,1792]{1,0:T(8,128)(2,1)S(1)} %add_convert_fusion.12), channel_id=1, source_target_pairs={{0,2},{1,0},{2,4},{3,1},{4,6},{5,3},{6,7},{7,5},{8,10},{9,8},{10,1... | collective-permute-start | bytes 1032200 | tf_op jit(solution)/shard_map/ppermute | solution.py:290
  36.7 16.0 %collective-permute-start.3 = (bf16[2,512,512]{2,1,0:T(8,128)(2,1)}, bf16[2,512,512]{2,1,0:T(8,128)(2,1)S(1)}, u32[]{:S(2)}, u32[]{:S(2)}) collective-permute-start(bf16[2,512,512]{2,1,0:T(8,128)(2,1)} %get-tuple-element.58), channel_id=1, source_target_pairs={{0,8},{8,0},{16,24},{24,16},{1,9},{9,1},{17,25},{25,17},{2,10},{10... | collective-permute-start | bytes 3145736 | tf_op jit(solution)/shard_map/ppermute | solution.py:300
  36.7 0.7 copy-start.1
  40.6 10.5 %collective-permute-start.11 = (bf16[96,1792]{1,0:T(8,128)(2,1)S(1)}, bf16[96,1792]{1,0:T(8,128)(2,1)S(1)}, u32[]{:S(2)}, u32[]{:S(2)}) collective-permute-start(bf16[96,1792]{1,0:T(8,128)(2,1)S(1)} %add_convert_fusion.5), channel_id=1, source_target_pairs={{0,1},{1,3},{2,0},{3,5},{4,2},{5,7},{6,4},{7,6},{8,9},{9,11},{10,8... | collective-permute-start | bytes 1032200 | tf_op jit(solution)/shard_map/ppermute | solution.py:291
  42.1 10.5 %collective-permute-start.2 = (bf16[96,1792]{1,0:T(8,128)(2,1)S(1)}, bf16[96,1792]{1,0:T(8,128)(2,1)S(1)}, u32[]{:S(2)}, u32[]{:S(2)}) collective-permute-start(bf16[96,1792]{1,0:T(8,128)(2,1)S(1)} %add_convert_fusion.11), channel_id=1, source_target_pairs={{0,2},{1,0},{2,4},{3,1},{4,6},{5,3},{6,7},{7,5},{8,10},{9,8},{10,1... | collective-permute-start | bytes 1032200 | tf_op jit(solution)/shard_map/ppermute | solution.py:290
  51.1 9.7 %collective-permute-start.12 = (bf16[96,1792]{1,0:T(8,128)(2,1)S(1)}, bf16[96,1792]{1,0:T(8,128)(2,1)S(1)}, u32[]{:S(2)}, u32[]{:S(2)}) collective-permute-start(bf16[96,1792]{1,0:T(8,128)(2,1)S(1)} %add_convert_fusion.4), channel_id=1, source_target_pairs={{0,1},{1,3},{2,0},{3,5},{4,2},{5,7},{6,4},{7,6},{8,9},{9,11},{10,8... | collective-permute-start | bytes 1032200 | tf_op jit(solution)/shard_map/ppermute | solution.py:291
  52.7 9.7 %copy-start.3 = (bf16[2,512,512]{2,1,0:T(8,128)(2,1)S(1)}, bf16[2,512,512]{2,1,0:T(8,128)(2,1)}, u32[]{:S(2)}) copy-start(bf16[2,512,512]{2,1,0:T(8,128)(2,1)} %get-tuple-element.72) | copy-start | bytes 3145732
  52.7 10.8 %collective-permute-start.4 = (bf16[96,1792]{1,0:T(8,128)(2,1)S(1)}, bf16[96,1792]{1,0:T(8,128)(2,1)S(1)}, u32[]{:S(2)}, u32[]{:S(2)}) collective-permute-start(bf16[96,1792]{1,0:T(8,128)(2,1)S(1)} %add_convert_fusion.10), channel_id=1, source_target_pairs={{0,2},{1,0},{2,4},{3,1},{4,6},{5,3},{6,7},{7,5},{8,10},{9,8},{10,1... | collective-permute-start | bytes 1032200 | tf_op jit(solution)/shard_map/ppermute | solution.py:290
  60.9 8.8 %collective-permute-start.13 = (bf16[96,1792]{1,0:T(8,128)(2,1)S(1)}, bf16[96,1792]{1,0:T(8,128)(2,1)S(1)}, u32[]{:S(2)}, u32[]{:S(2)}) collective-permute-start(bf16[96,1792]{1,0:T(8,128)(2,1)S(1)} %add_convert_fusion.3), channel_id=1, source_target_pairs={{0,1},{1,3},{2,0},{3,5},{4,2},{5,7},{6,4},{7,6},{8,9},{9,11},{10,8... | collective-permute-start | bytes 1032200 | tf_op jit(solution)/shard_map/ppermute | solution.py:291
  62.8 16.8 %collective-permute-start.7 = (bf16[512,512]{1,0:T(8,128)(2,1)S(1)}, bf16[512,512]{1,0:T(8,128)(2,1)S(1)}, u32[]{:S(2)}, u32[]{:S(2)}) collective-permute-start(bf16[512,512]{1,0:T(8,128)(2,1)S(1)} %fusion.10), channel_id=1, source_target_pairs={{0,16},{8,24},{16,0},{24,8},{1,17},{9,25},{17,1},{25,9},{2,18},{10... | collective-permute-start | bytes 1572872 | tf_op jit(solution)/shard_map/ppermute | solution.py:308
  63.6 8.3 %collective-permute-start.5 = (bf16[96,1792]{1,0:T(8,128)(2,1)S(1)}, bf16[96,1792]{1,0:T(8,128)(2,1)S(1)}, u32[]{:S(2)}, u32[]{:S(2)}) collective-permute-start(bf16[96,1792]{1,0:T(8,128)(2,1)S(1)} %add_convert_fusion.9), channel_id=1, source_target_pairs={{0,2},{1,0},{2,4},{3,1},{4,6},{5,3},{6,7},{7,5},{8,10},{9,8},{10,1... | collective-permute-start | bytes 1032200 | tf_op jit(solution)/shard_map/ppermute | solution.py:290
  69.8 8.1 %collective-permute-start.14 = (bf16[96,1792]{1,0:T(8,128)(2,1)S(1)}, bf16[96,1792]{1,0:T(8,128)(2,1)S(1)}, u32[]{:S(2)}, u32[]{:S(2)}) collective-permute-start(bf16[96,1792]{1,0:T(8,128)(2,1)S(1)} %add_convert_fusion.2), channel_id=1, source_target_pairs={{0,1},{1,3},{2,0},{3,5},{4,2},{5,7},{6,4},{7,6},{8,9},{9,11},{10,8... | collective-permute-start | bytes 1032200 | tf_op jit(solution)/shard_map/ppermute | solution.py:291
  72.0 7.6 %collective-permute-start.6 = (bf16[96,1792]{1,0:T(8,128)(2,1)S(1)}, bf16[96,1792]{1,0:T(8,128)(2,1)S(1)}, u32[]{:S(2)}, u32[]{:S(2)}) collective-permute-start(bf16[96,1792]{1,0:T(8,128)(2,1)S(1)} %add_convert_fusion.8), channel_id=1, source_target_pairs={{0,2},{1,0},{2,4},{3,1},{4,6},{5,3},{6,7},{7,5},{8,10},{9,8},{10,1... | collective-permute-start | bytes 1032200 | tf_op jit(solution)/shard_map/ppermute | solution.py:290
  78.0 7.3 %collective-permute-start.15 = (bf16[96,1792]{1,0:T(8,128)(2,1)S(1)}, bf16[96,1792]{1,0:T(8,128)(2,1)S(1)}, u32[]{:S(2)}, u32[]{:S(2)}) collective-permute-start(bf16[96,1792]{1,0:T(8,128)(2,1)S(1)} %add_convert_fusion.1), channel_id=1, source_target_pairs={{0,1},{1,3},{2,0},{3,5},{4,2},{5,7},{6,4},{7,6},{8,9},{9,11},{10,8... | collective-permute-start | bytes 1032200 | tf_op jit(solution)/shard_map/ppermute | solution.py:291
  79.6 9.7 %slice-start = ((s8[14680064]{0:T(1024)(128)(4,1)}), s8[4194304]{0:T(1024)(128)(4,1)S(1)}, s32[]{:S(2)}) async-start(s8[14680064]{0:T(1024)(128)(4,1)} %bitcast.23), calls=%async_computation.2 | async-start | bytes 8388608
  80.7 7.5 %collective-permute-start.8 = (bf16[96,1792]{1,0:T(8,128)(2,1)S(1)}, bf16[96,1792]{1,0:T(8,128)(2,1)S(1)}, u32[]{:S(2)}, u32[]{:S(2)}) collective-permute-start(bf16[96,1792]{1,0:T(8,128)(2,1)S(1)} %add_convert_fusion.7), channel_id=1, source_target_pairs={{0,2},{1,0},{2,4},{3,1},{4,6},{5,3},{6,7},{7,5},{8,10},{9,8},{10,1... | collective-permute-start | bytes 1032200 | tf_op jit(solution)/shard_map/ppermute | solution.py:290
  81.5 6.6 %copy-start.2 = (f32[96,128]{1,0:T(8,128)S(1)}, f32[96,128]{1,0:T(8,128)}, u32[]{:S(2)}) copy-start(f32[96,128]{1,0:T(8,128)} %constant.16.clone.origin_ref) | copy-start | bytes 147460
  81.5 7.8 %slice-start.1 = ((s8[14680064]{0:T(1024)(128)(4,1)}), s8[4194304]{0:T(1024)(128)(4,1)S(1)}, s32[]{:S(2)}) async-start(s8[14680064]{0:T(1024)(128)(4,1)} %bitcast.23), calls=%async_computation.3 | async-start | bytes 8388608
  81.5 7.8 %slice-start.2 = ((s8[14680064]{0:T(1024)(128)(4,1)}), s8[4194304]{0:T(1024)(128)(4,1)S(1)}, s32[]{:S(2)}) async-start(s8[14680064]{0:T(1024)(128)(4,1)} %bitcast.23), calls=%async_computation.4 | async-start | bytes 8388608
  81.5 7.8 %slice-start.3 = ((s8[14680064]{0:T(1024)(128)(4,1)}), s8[2097152]{0:T(1024)(128)(4,1)S(1)}, s32[]{:S(2)}) async-start(s8[14680064]{0:T(1024)(128)(4,1)} %bitcast.23), calls=%async_computation.5 | async-start | bytes 4194304
  92.1 2.8 %collective-permute-start.16 = (bf16[64,4096]{1,0:T(8,128)(2,1)S(1)}, bf16[64,4096]{1,0:T(8,128)(2,1)S(1)}, u32[]{:S(2)}, u32[]{:S(2)}) collective-permute-start(bf16[64,4096]{1,0:T(8,128)(2,1)S(1)} %fusion.4), channel_id=1, source_target_pairs={{0,8},{8,0},{16,24},{24,16},{1,9},{9,1},{17,25},{25,17},{2,10},{10... | collective-permute-start | bytes 1572872 | tf_op jit(solution)/shard_map/ppermute | solution.py:330

commit v12 on v11

--- a/solution.py
+++ b/solution.py
@@ -294,14 +294,14 @@
                 now, table, rows, gate_weight, up_weight, len(gates), 1, cuts
             )
             gates, ups = gates + more[0], ups + more[1]
-        if t == min(2, last):
+        if t == 1:
             kv = turn_columns(now, key_value, cores, chips)
             kv_core = [
                 lax.ppermute(kv[k], "branch", branch_target(experts, cores, k, 0))
                 for k in range(1, cores)
             ]
             gate_in, kv = lax.optimization_barrier((gate_in, kv))
-        if t == min(3, last):
+        if t == min(2, last):
             gate_in, kv_core = lax.optimization_barrier((gate_in, kv_core))
             kv_sum = kv[0].astype(F32) + sum(x.astype(F32) for x in kv_core)
             kv_chip = [
@@ -310,7 +310,7 @@
                 )
                 for k in range(1, chips)
             ]
-        if t == min(6, last):
+        if t == min(5, last):
             gate_in, kv_chip = lax.optimization_barrier((gate_in, kv_chip))
             kv_sum = kv_sum[0] + sum(x.astype(F32) for x in kv_chip)
             merged_kv = (kv_sum / experts).astype(BF16)

time: 115 us -> 114 us (level)
  waiting for transfers between devices: 22.2 us -> 18.9 us
  starting transfers between devices: 16.9 us -> 18.8 us
    ppermute x7, waiting for transfers between devices: 18.9 us -> 12.5 us  [local(): up_in = lax.ppermute(up_sum, 'shard', pairs[1])]
    ppermute x7, waiting for transfers between devices: 3.34 us -> 6.41 us  [local(): gate_in = lax.ppermute(gate_sum, 'shard', pairs[0])]
  transfers between devices with their start and end apart: 17 -> 17, of which waited for: 9 -> 10; matrix products, arithmetic and copies ran while one was open for 4% -> 4% of each run, Pallas kernels for 22% -> 22%
where the time goes in v12:
time: 114 us
  blocking collectives  34.6 us (30%)
  Pallas kernels  31 us (27%)
  waiting for transfers between devices  18.9 us (17%)
  starting transfers between devices  18.8 us (16%)
  matrix products  5.48 us (5%)
  other arithmetic  3.26 us (3%)
    pallas_call x8, Pallas kernels, column_pieces(): pl.pallas_call(kernel, out_shape=[jax.ShapeDtypeStruct((count, width), BF...  24.9 us
    all_to_all x1, blocking collectives, local(): lax.all_to_all(mixed, ('branch', 'shard'), split_axis=0, concat_axis=0, a...  19.4 us
    all_to_all x1, blocking collectives, local(): lax.all_to_all(cells, ('branch', 'shard'), split_axis=0, concat_axis=0, t...  15.2 us
    ppermute x7, waiting for transfers between devices, local(): up_in = lax.ppermute(up_sum, 'shard', pairs[1])  12.5 us
    ppermute x7, starting transfers between devices, local(): up_in = lax.ppermute(up_sum, 'shard', pairs[1])  11.3 us
    ppermute x7, waiting for transfers between devices, local(): gate_in = lax.ppermute(gate_sum, 'shard', pairs[0])  6.41 us
    ppermute x7, starting transfers between devices, local(): gate_in = lax.ppermute(gate_sum, 'shard', pairs[0])  6.29 us
    dot_general x2, matrix products, down_product(): jnp.dot(h, w, preferred_element_type=F32)  5.48 us
  transfers between devices with their start and end apart: 17, of which 10 were waited for; matrix products, arithmetic and copies ran while one was open for 4% of the time, Pallas kernels for 22%

profile of v12, /device:TPU:0, one launch (start us, length us, event | category | flops | bytes accessed | tf_op | source)
XLA Modules:
  0.0 114.1 jit_solution(7130811032845394647)
XLA Ops:
  0.7 1.7 %place_rows.1 = bf16[32,3,640]{2,1,0:T(4,128)(2,1)} custom-call(bf16[4,4096]{1,0:T(4,128)(2,1)} %tokens_ref.1, s32[2,4]{1,0:T(2,128)} %bitcast.25, f32[2,4]{1,0:T(2,128)} %bitcast.26), custom_call_target="tpu_custom_call" | custom-call | tf_op jit(solution)/shard_map/place_rows/pallas_call | solution.py:84
  2.5 15.2 %all_to_all.10 = bf16[32,3,640]{2,1,0:T(4,128)(2,1)S(1)} all-to-all(bf16[32,3,640]{2,1,0:T(4,128)(2,1)} %place_rows.1), channel_id=1, replica_groups=mesh['branch'=4,'shard'=8] {'branch','shard'}, dimensions={0} | all-to-all | bytes 245760 | tf_op jit(solution)/shard_map/all_to_all | solution.py:274
  17.7 0.1 reshape.11
  17.8 3.1 %column_pieces.8 = (bf16[96,1792]{1,0:T(8,128)(2,1)S(1)}, bf16[96,1792]{1,0:T(8,128)(2,1)S(1)}) custom-call(s32[2]{0:T(128)S(1)} %pad_add_fusion.where_ref, bf16[96,512]{1,0:T(8,128)(2,1)S(1)} %slice.17.rows_ref, bf16[1,512,14336]{2,1,0:T(8,128)(2,1)} %refs_0_.17, bf16[1,512,14336]{2,1,0:T(8,128)(2,1)} %refs_1_.17), custom_call_target="tpu_custom_call" | custom-call | flops 352321536 | bytes 3670016 | tf_op jit(solution)/shard_map/column_pieces/pallas_call | solution.py:119
  20.9 1.6 %collective-permute-start.9 = (bf16[96,1792]{1,0:T(8,128)(2,1)S(1)}, bf16[96,1792]{1,0:T(8,128)(2,1)S(1)}, u32[]{:S(2)}, u32[]{:S(2)}) collective-permute-start(bf16[96,1792]{1,0:T(8,128)(2,1)S(1)} %get-tuple-element.80), channel_id=1, source_target_pairs={{0,1},{1,3},{2,0},{3,5},{4,2},{5,7},{6,4},{7,6},{8,9},{9,11},{10,8... | collective-permute-start | bytes 1032200 | tf_op jit(solution)/shard_map/ppermute | solution.py:291
  22.5 0.5 collective-permute-start
  23.0 3.3 %turn_columns.1 = (bf16[2,512,512]{2,1,0:T(8,128)(2,1)}, bf16[2,512,512]{2,1,0:T(8,128)(2,1)}) custom-call(s32[2]{0:T(128)} %copy-done, bf16[1,512,2048]{2,1,0:T(8,128)(2,1)} %refs_1_.10, bf16[1,512,2048]{2,1,0:T(8,128)(2,1)} %refs_1_.10), custom_call_target="tpu_custom_call" | custom-call | bytes 4194304 | tf_op jit(solution)/shard_map/turn_columns/pallas_call | solution.py:167
  26.3 0.7 copy-done.1
  26.9 3.1 %column_pieces.9 = (bf16[96,1792]{1,0:T(8,128)(2,1)S(1)}, bf16[96,1792]{1,0:T(8,128)(2,1)S(1)}) custom-call(s32[2]{0:T(128)S(1)} %copy-done.1, bf16[96,512]{1,0:T(8,128)(2,1)S(1)} %slice.17.rows_ref, bf16[1,512,14336]{2,1,0:T(8,128)(2,1)} %refs_0_.17, bf16[1,512,14336]{2,1,0:T(8,128)(2,1)} %refs_1_.17), custom_call_target="tpu_custom_call" | custom-call | flops 352321536 | bytes 3670016 | tf_op jit(solution)/shard_map/column_pieces/pallas_call | solution.py:119
  30.0 1.1 collective-permute-done.9
  31.2 1.5 %collective-permute-start.10 = (bf16[96,1792]{1,0:T(8,128)(2,1)S(1)}, bf16[96,1792]{1,0:T(8,128)(2,1)S(1)}, u32[]{:S(2)}, u32[]{:S(2)}) collective-permute-start(bf16[96,1792]{1,0:T(8,128)(2,1)S(1)} %add_convert_fusion.6), channel_id=1, source_target_pairs={{0,1},{1,3},{2,0},{3,5},{4,2},{5,7},{6,4},{7,6},{8,9},{9,11},{10,8... | collective-permute-start | bytes 1032200 | tf_op jit(solution)/shard_map/ppermute | solution.py:291
  32.7 0.1 add_convert_fusion.12
  32.8 0.6 collective-permute-start.1
  33.4 3.1 %column_pieces.10 = (bf16[96,1792]{1,0:T(8,128)(2,1)S(1)}, bf16[96,1792]{1,0:T(8,128)(2,1)S(1)}) custom-call(s32[2]{0:T(128)S(1)} %copy-done.1, bf16[96,512]{1,0:T(8,128)(2,1)S(1)} %slice.17.rows_ref, bf16[1,512,14336]{2,1,0:T(8,128)(2,1)} %refs_0_.17, bf16[1,512,14336]{2,1,0:T(8,128)(2,1)} %refs_1_.17), custom_call_target="tpu_custom_call" | custom-call | flops 352321536 | bytes 3670016 | tf_op jit(solution)/shard_map/column_pieces/pallas_call | solution.py:119
  36.5 4.2 %collective-permute-done.10 = bf16[96,1792]{1,0:T(8,128)(2,1)S(1)} collective-permute-done((bf16[96,1792]{1,0:T(8,128)(2,1)S(1)}, bf16[96,1792]{1,0:T(8,128)(2,1)S(1)}, u32[]{:S(2)}, u32[]{:S(2)}) %collective-permute-start.10) | collective-permute-done | bytes 344096 | tf_op jit(solution)/shard_map/ppermute | solution.py:291
  40.7 1.6 %collective-permute-start.11 = (bf16[96,1792]{1,0:T(8,128)(2,1)S(1)}, bf16[96,1792]{1,0:T(8,128)(2,1)S(1)}, u32[]{:S(2)}, u32[]{:S(2)}) collective-permute-start(bf16[96,1792]{1,0:T(8,128)(2,1)S(1)} %add_convert_fusion.5), channel_id=1, source_target_pairs={{0,1},{1,3},{2,0},{3,5},{4,2},{5,7},{6,4},{7,6},{8,9},{9,11},{10,8... | collective-permute-start | bytes 1032200 | tf_op jit(solution)/shard_map/ppermute | solution.py:291
  42.4 0.6 collective-permute-start.3
  43.0 3.1 %column_pieces.11 = (bf16[96,1792]{1,0:T(8,128)(2,1)S(1)}, bf16[96,1792]{1,0:T(8,128)(2,1)S(1)}) custom-call(s32[2]{0:T(128)S(1)} %copy-done.1, bf16[96,512]{1,0:T(8,128)(2,1)S(1)} %slice.17.rows_ref, bf16[1,512,14336]{2,1,0:T(8,128)(2,1)} %refs_0_.17, bf16[1,512,14336]{2,1,0:T(8,128)(2,1)} %refs_1_.17), custom_call_target="tpu_custom_call" | custom-call | flops 352321536 | bytes 3670016 | tf_op jit(solution)/shard_map/column_pieces/pallas_call | solution.py:119
  46.0 3.3 %collective-permute-done.11 = bf16[96,1792]{1,0:T(8,128)(2,1)S(1)} collective-permute-done((bf16[96,1792]{1,0:T(8,128)(2,1)S(1)}, bf16[96,1792]{1,0:T(8,128)(2,1)S(1)}, u32[]{:S(2)}, u32[]{:S(2)}) %collective-permute-start.11) | collective-permute-done | bytes 344096 | tf_op jit(solution)/shard_map/ppermute | solution.py:291
  49.4 1.6 %collective-permute-start.12 = (bf16[96,1792]{1,0:T(8,128)(2,1)S(1)}, bf16[96,1792]{1,0:T(8,128)(2,1)S(1)}, u32[]{:S(2)}, u32[]{:S(2)}) collective-permute-start(bf16[96,1792]{1,0:T(8,128)(2,1)S(1)} %add_convert_fusion.4), channel_id=1, source_target_pairs={{0,1},{1,3},{2,0},{3,5},{4,2},{5,7},{6,4},{7,6},{8,9},{9,11},{10,8... | collective-permute-start | bytes 1032200 | tf_op jit(solution)/shard_map/ppermute | solution.py:291
  51.0 0.3 convert_add_fusion
  51.4 1.1 collective-permute-start.6
  52.5 0.7 collective-permute-start.4
  53.3 3.1 %column_pieces.12 = (bf16[96,1792]{1,0:T(8,128)(2,1)S(1)}, bf16[96,1792]{1,0:T(8,128)(2,1)S(1)}) custom-call(s32[2]{0:T(128)S(1)} %copy-done.1, bf16[96,512]{1,0:T(8,128)(2,1)S(1)} %slice.17.rows_ref, bf16[1,512,14336]{2,1,0:T(8,128)(2,1)} %refs_0_.17, bf16[1,512,14336]{2,1,0:T(8,128)(2,1)} %refs_1_.17), custom_call_target="tpu_custom_call" | custom-call | flops 352321536 | bytes 3670016 | tf_op jit(solution)/shard_map/column_pieces/pallas_call | solution.py:119
  56.3 1.2 %collective-permute-done.12 = bf16[96,1792]{1,0:T(8,128)(2,1)S(1)} collective-permute-done((bf16[96,1792]{1,0:T(8,128)(2,1)S(1)}, bf16[96,1792]{1,0:T(8,128)(2,1)S(1)}, u32[]{:S(2)}, u32[]{:S(2)}) %collective-permute-start.12) | collective-permute-done | bytes 344096 | tf_op jit(solution)/shard_map/ppermute | solution.py:291
  57.6 1.6 %collective-permute-start.13 = (bf16[96,1792]{1,0:T(8,128)(2,1)S(1)}, bf16[96,1792]{1,0:T(8,128)(2,1)S(1)}, u32[]{:S(2)}, u32[]{:S(2)}) collective-permute-start(bf16[96,1792]{1,0:T(8,128)(2,1)S(1)} %add_convert_fusion.3), channel_id=1, source_target_pairs={{0,1},{1,3},{2,0},{3,5},{4,2},{5,7},{6,4},{7,6},{8,9},{9,11},{10,8... | collective-permute-start | bytes 1032200 | tf_op jit(solution)/shard_map/ppermute | solution.py:291
  59.2 1.4 %collective-permute-done.4 = bf16[96,1792]{1,0:T(8,128)(2,1)S(1)} collective-permute-done((bf16[96,1792]{1,0:T(8,128)(2,1)S(1)}, bf16[96,1792]{1,0:T(8,128)(2,1)S(1)}, u32[]{:S(2)}, u32[]{:S(2)}) %collective-permute-start.4) | collective-permute-done | bytes 344096 | tf_op jit(solution)/shard_map/ppermute | solution.py:290
  60.7 1.0 collective-permute-start.5
  61.7 3.1 %column_pieces.13 = (bf16[96,1792]{1,0:T(8,128)(2,1)S(1)}, bf16[96,1792]{1,0:T(8,128)(2,1)S(1)}) custom-call(s32[2]{0:T(128)S(1)} %copy-done.1, bf16[96,512]{1,0:T(8,128)(2,1)S(1)} %slice.17.rows_ref, bf16[1,512,14336]{2,1,0:T(8,128)(2,1)} %refs_0_.17, bf16[1,512,14336]{2,1,0:T(8,128)(2,1)} %refs_1_.17), custom_call_target="tpu_custom_call" | custom-call | flops 352321536 | bytes 3670016 | tf_op jit(solution)/shard_map/column_pieces/pallas_call | solution.py:119
  64.8 1.4 %collective-permute-done.13 = bf16[96,1792]{1,0:T(8,128)(2,1)S(1)} collective-permute-done((bf16[96,1792]{1,0:T(8,128)(2,1)S(1)}, bf16[96,1792]{1,0:T(8,128)(2,1)S(1)}, u32[]{:S(2)}, u32[]{:S(2)}) %collective-permute-start.13) | collective-permute-done | bytes 344096 | tf_op jit(solution)/shard_map/ppermute | solution.py:291
  66.3 1.6 %collective-permute-start.14 = (bf16[96,1792]{1,0:T(8,128)(2,1)S(1)}, bf16[96,1792]{1,0:T(8,128)(2,1)S(1)}, u32[]{:S(2)}, u32[]{:S(2)}) collective-permute-start(bf16[96,1792]{1,0:T(8,128)(2,1)S(1)} %add_convert_fusion.2), channel_id=1, source_target_pairs={{0,1},{1,3},{2,0},{3,5},{4,2},{5,7},{6,4},{7,6},{8,9},{9,11},{10,8... | collective-permute-start | bytes 1032200 | tf_op jit(solution)/shard_map/ppermute | solution.py:291
  67.8 0.8 collective-permute-done.5
  68.6 1.0 fusion.9
  69.7 1.2 %collective-permute-start.7 = (bf16[96,1792]{1,0:T(8,128)(2,1)S(1)}, bf16[96,1792]{1,0:T(8,128)(2,1)S(1)}, u32[]{:S(2)}, u32[]{:S(2)}) collective-permute-start(bf16[96,1792]{1,0:T(8,128)(2,1)S(1)} %add_convert_fusion.8), channel_id=1, source_target_pairs={{0,2},{1,0},{2,4},{3,1},{4,6},{5,3},{6,7},{7,5},{8,10},{9,8},{10,1... | collective-permute-start | bytes 1032200 | tf_op jit(solution)/shard_map/ppermute | solution.py:290
  70.9 3.3 %column_pieces.14 = (bf16[96,1792]{1,0:T(8,128)(2,1)S(1)}, bf16[96,1792]{1,0:T(8,128)(2,1)S(1)}) custom-call(s32[2]{0:T(128)S(1)} %copy-done.1, bf16[96,512]{1,0:T(8,128)(2,1)S(1)} %slice.17.rows_ref, bf16[1,512,14336]{2,1,0:T(8,128)(2,1)} %refs_0_.17, bf16[1,512,14336]{2,1,0:T(8,128)(2,1)} %refs_1_.17), custom_call_target="tpu_custom_call" | custom-call | flops 352321536 | bytes 3670016 | tf_op jit(solution)/shard_map/column_pieces/pallas_call | solution.py:119
  74.2 1.4 %collective-permute-done.14 = bf16[96,1792]{1,0:T(8,128)(2,1)S(1)} collective-permute-done((bf16[96,1792]{1,0:T(8,128)(2,1)S(1)}, bf16[96,1792]{1,0:T(8,128)(2,1)S(1)}, u32[]{:S(2)}, u32[]{:S(2)}) %collective-permute-start.14) | collective-permute-done | bytes 344096 | tf_op jit(solution)/shard_map/ppermute | solution.py:291
  75.7 1.8 %collective-permute-start.15 = (bf16[96,1792]{1,0:T(8,128)(2,1)S(1)}, bf16[96,1792]{1,0:T(8,128)(2,1)S(1)}, u32[]{:S(2)}, u32[]{:S(2)}) collective-permute-start(bf16[96,1792]{1,0:T(8,128)(2,1)S(1)} %add_convert_fusion.1), channel_id=1, source_target_pairs={{0,1},{1,3},{2,0},{3,5},{4,2},{5,7},{6,4},{7,6},{8,9},{9,11},{10,8... | collective-permute-start | bytes 1032200 | tf_op jit(solution)/shard_map/ppermute | solution.py:291
  77.6 1.6 %collective-permute-done.7 = bf16[96,1792]{1,0:T(8,128)(2,1)S(1)} collective-permute-done((bf16[96,1792]{1,0:T(8,128)(2,1)S(1)}, bf16[96,1792]{1,0:T(8,128)(2,1)S(1)}, u32[]{:S(2)}, u32[]{:S(2)}) %collective-permute-start.7) | collective-permute-done | bytes 344096 | tf_op jit(solution)/shard_map/ppermute | solution.py:290
  79.2 1.7 %collective-permute-start.8 = (bf16[96,1792]{1,0:T(8,128)(2,1)S(1)}, bf16[96,1792]{1,0:T(8,128)(2,1)S(1)}, u32[]{:S(2)}, u32[]{:S(2)}) collective-permute-start(bf16[96,1792]{1,0:T(8,128)(2,1)S(1)} %add_convert_fusion.7), channel_id=1, source_target_pairs={{0,2},{1,0},{2,4},{3,1},{4,6},{5,3},{6,7},{7,5},{8,10},{9,8},{10,1... | collective-permute-start | bytes 1032200 | tf_op jit(solution)/shard_map/ppermute | solution.py:290
  80.9 3.1 %column_pieces.15 = (bf16[96,1792]{1,0:T(8,128)(2,1)S(1)}, bf16[96,1792]{1,0:T(8,128)(2,1)S(1)}) custom-call(s32[2]{0:T(128)S(1)} %copy-done.1, bf16[96,512]{1,0:T(8,128)(2,1)S(1)} %slice.17.rows_ref, bf16[1,512,14336]{2,1,0:T(8,128)(2,1)} %refs_0_.17, bf16[1,512,14336]{2,1,0:T(8,128)(2,1)} %refs_1_.17), custom_call_target="tpu_custom_call" | custom-call | flops 352321536 | bytes 3670016 | tf_op jit(solution)/shard_map/column_pieces/pallas_call | solution.py:119
  84.1 2.6 %collective-permute-done.8.gate_ref = bf16[96,1792]{1,0:T(8,128)(2,1)S(1)} collective-permute-done((bf16[96,1792]{1,0:T(8,128)(2,1)S(1)}, bf16[96,1792]{1,0:T(8,128)(2,1)S(1)}, u32[]{:S(2)}, u32[]{:S(2)}) %collective-permute-start.8) | collective-permute-done | bytes 344096 | tf_op jit(solution)/shard_map/ppermute | solution.py:290
  86.7 1.1 %hidden_rows.1 = (bf16[64,1792]{1,0:T(8,128)(2,1)S(1)}, bf16[64,1792]{1,0:T(8,128)(2,1)S(1)}) custom-call(s32[2]{0:T(128)S(1)} %copy-done.1, bf16[96,1792]{1,0:T(8,128)(2,1)S(1)} %collective-permute-done.8.gate_ref, bf16[96,1792]{1,0:T(8,128)(2,1)S(1)} %collective-permute-done.15.up_ref, bf16[96,1792]{1,0:T(8,128)(2,1)S(1)} %get-tuple-element.88.gate_own_ref, ...), custom_call_target="tpu_custom_call" | custom-call | flops 44040192 | bytes 1376256 | tf_op jit(solution)/shard_map/hidden_rows/pallas_call | solution.py:217
  87.9 2.7 %fusion.4 = bf16[64,4096]{1,0:T(8,128)(2,1)S(1)} fusion(bf16[64,1792]{1,0:T(8,128)(2,1)S(1)} %get-tuple-element.92, bf16[1,1792,4096]{2,1,0:T(8,128)(2,1)S(1)} %bitcast.24), kind=kOutput, calls=%fused_computation.4 | convolution fusion | flops 939786240 | bytes 15433728 | tf_op jit(solution)/shard_map/dot_general | solution.py:234
  90.7 2.7 %fusion.2 = f32[64,4096]{1,0:T(8,128)S(1)} fusion(bf16[64,1792]{1,0:T(8,128)(2,1)S(1)} %get-tuple-element.91, bf16[1,1792,4096]{2,1,0:T(8,128)(2,1)S(1)} %bitcast.24), kind=kOutput, calls=%fused_computation.2 | convolution fusion | flops 939524096 | bytes 15958016 | tf_op jit(solution)/shard_map/dot_general | solution.py:234
  93.5 0.1 add_convert_fusion
  93.6 0.2 reshape.12
  93.8 19.4 %all_to_all.11 = bf16[16,4,4096]{2,1,0:T(4,128)(2,1)S(1)} all-to-all(bf16[16,4,4096]{2,1,0:T(4,128)(2,1)S(1)} %reshape.12), channel_id=1, replica_groups={{0,1,2,3,4,5,6,7,16,17,18,19,20,21,22,23},{8,9,10,11,12,13,14,15,24,25,..., dimensions={0} | all-to-all | bytes 1048576 | tf_op jit(solution)/shard_map/all_to_all | solution.py:342
  113.2 0.8 reduce_sum.12
  (40 shorter events, 1.2 us)
Async XLA Ops:
  0.7 20.2 %copy-start = (s32[2]{0:T(128)}, s32[2]{0:T(128)S(1)}, u32[]{:S(2)}) copy-start(s32[2]{0:T(128)S(1)} %pad_add_fusion.where_ref) | copy-start | bytes 28
  20.9 10.2 %collective-permute-start.9 = (bf16[96,1792]{1,0:T(8,128)(2,1)S(1)}, bf16[96,1792]{1,0:T(8,128)(2,1)S(1)}, u32[]{:S(2)}, u32[]{:S(2)}) collective-permute-start(bf16[96,1792]{1,0:T(8,128)(2,1)S(1)} %get-tuple-element.80), channel_id=1, source_target_pairs={{0,1},{1,3},{2,0},{3,5},{4,2},{5,7},{6,4},{7,6},{8,9},{9,11},{10,8... | collective-permute-start | bytes 1032200 | tf_op jit(solution)/shard_map/ppermute | solution.py:291
  22.5 10.2 %collective-permute-start = (bf16[96,1792]{1,0:T(8,128)(2,1)S(1)}, bf16[96,1792]{1,0:T(8,128)(2,1)S(1)}, u32[]{:S(2)}, u32[]{:S(2)}) collective-permute-start(bf16[96,1792]{1,0:T(8,128)(2,1)S(1)} %get-tuple-element.52), channel_id=1, source_target_pairs={{0,2},{1,0},{2,4},{3,1},{4,6},{5,3},{6,7},{7,5},{8,10},{9,8},{10,1... | collective-permute-start | bytes 1032200 | tf_op jit(solution)/shard_map/ppermute | solution.py:290
  26.3 16.0 %collective-permute-start.2 = (bf16[2,512,512]{2,1,0:T(8,128)(2,1)}, bf16[2,512,512]{2,1,0:T(8,128)(2,1)S(1)}, u32[]{:S(2)}, u32[]{:S(2)}) collective-permute-start(bf16[2,512,512]{2,1,0:T(8,128)(2,1)} %get-tuple-element.55), channel_id=1, source_target_pairs={{0,8},{8,0},{16,24},{24,16},{1,9},{9,1},{17,25},{25,17},{2,10},{10... | collective-permute-start | bytes 3145736 | tf_op jit(solution)/shard_map/ppermute | solution.py:300
  26.3 0.7 copy-start.1
  31.2 9.5 %collective-permute-start.10 = (bf16[96,1792]{1,0:T(8,128)(2,1)S(1)}, bf16[96,1792]{1,0:T(8,128)(2,1)S(1)}, u32[]{:S(2)}, u32[]{:S(2)}) collective-permute-start(bf16[96,1792]{1,0:T(8,128)(2,1)S(1)} %add_convert_fusion.6), channel_id=1, source_target_pairs={{0,1},{1,3},{2,0},{3,5},{4,2},{5,7},{6,4},{7,6},{8,9},{9,11},{10,8... | collective-permute-start | bytes 1032200 | tf_op jit(solution)/shard_map/ppermute | solution.py:291
  32.8 9.5 %collective-permute-start.1 = (bf16[96,1792]{1,0:T(8,128)(2,1)S(1)}, bf16[96,1792]{1,0:T(8,128)(2,1)S(1)}, u32[]{:S(2)}, u32[]{:S(2)}) collective-permute-start(bf16[96,1792]{1,0:T(8,128)(2,1)S(1)} %add_convert_fusion.12), channel_id=1, source_target_pairs={{0,2},{1,0},{2,4},{3,1},{4,6},{5,3},{6,7},{7,5},{8,10},{9,8},{10,1... | collective-permute-start | bytes 1032200 | tf_op jit(solution)/shard_map/ppermute | solution.py:290
  40.7 8.6 %collective-permute-start.11 = (bf16[96,1792]{1,0:T(8,128)(2,1)S(1)}, bf16[96,1792]{1,0:T(8,128)(2,1)S(1)}, u32[]{:S(2)}, u32[]{:S(2)}) collective-permute-start(bf16[96,1792]{1,0:T(8,128)(2,1)S(1)} %add_convert_fusion.5), channel_id=1, source_target_pairs={{0,1},{1,3},{2,0},{3,5},{4,2},{5,7},{6,4},{7,6},{8,9},{9,11},{10,8... | collective-permute-start | bytes 1032200 | tf_op jit(solution)/shard_map/ppermute | solution.py:291
  42.4 8.6 %copy-start.3 = (bf16[2,512,512]{2,1,0:T(8,128)(2,1)S(1)}, bf16[2,512,512]{2,1,0:T(8,128)(2,1)}, u32[]{:S(2)}) copy-start(bf16[2,512,512]{2,1,0:T(8,128)(2,1)} %get-tuple-element.69) | copy-start | bytes 3145732
  42.4 10.0 %collective-permute-start.3 = (bf16[96,1792]{1,0:T(8,128)(2,1)S(1)}, bf16[96,1792]{1,0:T(8,128)(2,1)S(1)}, u32[]{:S(2)}, u32[]{:S(2)}) collective-permute-start(bf16[96,1792]{1,0:T(8,128)(2,1)S(1)} %add_convert_fusion.11), channel_id=1, source_target_pairs={{0,2},{1,0},{2,4},{3,1},{4,6},{5,3},{6,7},{7,5},{8,10},{9,8},{10,1... | collective-permute-start | bytes 1032200 | tf_op jit(solution)/shard_map/ppermute | solution.py:290
  49.4 8.1 %collective-permute-start.12 = (bf16[96,1792]{1,0:T(8,128)(2,1)S(1)}, bf16[96,1792]{1,0:T(8,128)(2,1)S(1)}, u32[]{:S(2)}, u32[]{:S(2)}) collective-permute-start(bf16[96,1792]{1,0:T(8,128)(2,1)S(1)} %add_convert_fusion.4), channel_id=1, source_target_pairs={{0,1},{1,3},{2,0},{3,5},{4,2},{5,7},{6,4},{7,6},{8,9},{9,11},{10,8... | collective-permute-start | bytes 1032200 | tf_op jit(solution)/shard_map/ppermute | solution.py:291
  51.4 16.5 %collective-permute-start.6 = (bf16[512,512]{1,0:T(8,128)(2,1)S(1)}, bf16[512,512]{1,0:T(8,128)(2,1)S(1)}, u32[]{:S(2)}, u32[]{:S(2)}) collective-permute-start(bf16[512,512]{1,0:T(8,128)(2,1)S(1)} %fusion.10), channel_id=1, source_target_pairs={{0,16},{8,24},{16,0},{24,8},{1,17},{9,25},{17,1},{25,9},{2,18},{10... | collective-permute-start | bytes 1572872 | tf_op jit(solution)/shard_map/ppermute | solution.py:308
  52.5 8.1 %collective-permute-start.4 = (bf16[96,1792]{1,0:T(8,128)(2,1)S(1)}, bf16[96,1792]{1,0:T(8,128)(2,1)S(1)}, u32[]{:S(2)}, u32[]{:S(2)}) collective-permute-start(bf16[96,1792]{1,0:T(8,128)(2,1)S(1)} %add_convert_fusion.10), channel_id=1, source_target_pairs={{0,2},{1,0},{2,4},{3,1},{4,6},{5,3},{6,7},{7,5},{8,10},{9,8},{10,1... | collective-permute-start | bytes 1032200 | tf_op jit(solution)/shard_map/ppermute | solution.py:290
  57.6 8.6 %collective-permute-start.13 = (bf16[96,1792]{1,0:T(8,128)(2,1)S(1)}, bf16[96,1792]{1,0:T(8,128)(2,1)S(1)}, u32[]{:S(2)}, u32[]{:S(2)}) collective-permute-start(bf16[96,1792]{1,0:T(8,128)(2,1)S(1)} %add_convert_fusion.3), channel_id=1, source_target_pairs={{0,1},{1,3},{2,0},{3,5},{4,2},{5,7},{6,4},{7,6},{8,9},{9,11},{10,8... | collective-permute-start | bytes 1032200 | tf_op jit(solution)/shard_map/ppermute | solution.py:291
  60.7 7.9 %collective-permute-start.5 = (bf16[96,1792]{1,0:T(8,128)(2,1)S(1)}, bf16[96,1792]{1,0:T(8,128)(2,1)S(1)}, u32[]{:S(2)}, u32[]{:S(2)}) collective-permute-start(bf16[96,1792]{1,0:T(8,128)(2,1)S(1)} %add_convert_fusion.9), channel_id=1, source_target_pairs={{0,2},{1,0},{2,4},{3,1},{4,6},{5,3},{6,7},{7,5},{8,10},{9,8},{10,1... | collective-permute-start | bytes 1032200 | tf_op jit(solution)/shard_map/ppermute | solution.py:290
  66.3 9.4 %collective-permute-start.14 = (bf16[96,1792]{1,0:T(8,128)(2,1)S(1)}, bf16[96,1792]{1,0:T(8,128)(2,1)S(1)}, u32[]{:S(2)}, u32[]{:S(2)}) collective-permute-start(bf16[96,1792]{1,0:T(8,128)(2,1)S(1)} %add_convert_fusion.2), channel_id=1, source_target_pairs={{0,1},{1,3},{2,0},{3,5},{4,2},{5,7},{6,4},{7,6},{8,9},{9,11},{10,8... | collective-permute-start | bytes 1032200 | tf_op jit(solution)/shard_map/ppermute | solution.py:291
  69.7 9.5 %collective-permute-start.7 = (bf16[96,1792]{1,0:T(8,128)(2,1)S(1)}, bf16[96,1792]{1,0:T(8,128)(2,1)S(1)}, u32[]{:S(2)}, u32[]{:S(2)}) collective-permute-start(bf16[96,1792]{1,0:T(8,128)(2,1)S(1)} %add_convert_fusion.8), channel_id=1, source_target_pairs={{0,2},{1,0},{2,4},{3,1},{4,6},{5,3},{6,7},{7,5},{8,10},{9,8},{10,1... | collective-permute-start | bytes 1032200 | tf_op jit(solution)/shard_map/ppermute | solution.py:290
  70.9 17.0 %slice-start = ((s8[14680064]{0:T(1024)(128)(4,1)}), s8[4194304]{0:T(1024)(128)(4,1)S(1)}, s32[]{:S(2)}) async-start(s8[14680064]{0:T(1024)(128)(4,1)} %bitcast.23), calls=%async_computation.2 | async-start | bytes 8388608
  70.9 17.0 %slice-start.1 = ((s8[14680064]{0:T(1024)(128)(4,1)}), s8[4194304]{0:T(1024)(128)(4,1)S(1)}, s32[]{:S(2)}) async-start(s8[14680064]{0:T(1024)(128)(4,1)} %bitcast.23), calls=%async_computation.3 | async-start | bytes 8388608
  75.7 8.3 %collective-permute-start.15 = (bf16[96,1792]{1,0:T(8,128)(2,1)S(1)}, bf16[96,1792]{1,0:T(8,128)(2,1)S(1)}, u32[]{:S(2)}, u32[]{:S(2)}) collective-permute-start(bf16[96,1792]{1,0:T(8,128)(2,1)S(1)} %add_convert_fusion.1), channel_id=1, source_target_pairs={{0,1},{1,3},{2,0},{3,5},{4,2},{5,7},{6,4},{7,6},{8,9},{9,11},{10,8... | collective-permute-start | bytes 1032200 | tf_op jit(solution)/shard_map/ppermute | solution.py:291
  79.1 8.7 %slice-start.2 = ((s8[14680064]{0:T(1024)(128)(4,1)}), s8[4194304]{0:T(1024)(128)(4,1)S(1)}, s32[]{:S(2)}) async-start(s8[14680064]{0:T(1024)(128)(4,1)} %bitcast.23), calls=%async_computation.4 | async-start | bytes 8388608
  79.2 7.5 %collective-permute-start.8 = (bf16[96,1792]{1,0:T(8,128)(2,1)S(1)}, bf16[96,1792]{1,0:T(8,128)(2,1)S(1)}, u32[]{:S(2)}, u32[]{:S(2)}) collective-permute-start(bf16[96,1792]{1,0:T(8,128)(2,1)S(1)} %add_convert_fusion.7), channel_id=1, source_target_pairs={{0,2},{1,0},{2,4},{3,1},{4,6},{5,3},{6,7},{7,5},{8,10},{9,8},{10,1... | collective-permute-start | bytes 1032200 | tf_op jit(solution)/shard_map/ppermute | solution.py:290
  80.9 5.8 %copy-start.2 = (f32[96,128]{1,0:T(8,128)S(1)}, f32[96,128]{1,0:T(8,128)}, u32[]{:S(2)}) copy-start(f32[96,128]{1,0:T(8,128)} %constant.16.clone.origin_ref) | copy-start | bytes 147460
  80.9 7.0 %slice-start.3 = ((s8[14680064]{0:T(1024)(128)(4,1)}), s8[2097152]{0:T(1024)(128)(4,1)S(1)}, s32[]{:S(2)}) async-start(s8[14680064]{0:T(1024)(128)(4,1)} %bitcast.23), calls=%async_computation.5 | async-start | bytes 4194304
  90.7 2.8 %collective-permute-start.16 = (bf16[64,4096]{1,0:T(8,128)(2,1)S(1)}, bf16[64,4096]{1,0:T(8,128)(2,1)S(1)}, u32[]{:S(2)}, u32[]{:S(2)}) collective-permute-start(bf16[64,4096]{1,0:T(8,128)(2,1)S(1)} %fusion.4), channel_id=1, source_target_pairs={{0,8},{8,0},{16,24},{24,16},{1,9},{9,1},{17,25},{25,17},{2,10},{10... | collective-permute-start | bytes 1572872 | tf_op jit(solution)/shard_map/ppermute | solution.py:330
